TPU v7x, 32 devices: a whole 2x2x4 slice. The times are simulated.
32 devices in a mesh: seq: 16 (over z, x, core), expert: 2 (over y).
Axes of the slice: x: 2, y: 2, z: 4, core: 2. Of those that a mesh axis runs over, the one named last changes fastest.
Arguments:
- query_cols: bfloat16 [256, 32768], P('expert', 'seq'), may hold values from -16 to 16
- key_cols: bfloat16 [256, 32768], P('expert', 'seq'), may hold values from -6 to 6
- value_cols: bfloat16 [256, 32768], P('expert', 'seq'), may hold values from -12 to 12
- block_list: int32 [256, 4], P('seq'), may hold values from 0 to 255, as said below
- residual: bfloat16 [32768, 256], P(('seq', 'expert')), may hold values from -6 to 6
- out_proj: bfloat16 [256, 256], replicated, may hold values from -0.375 to 0.375
- norm_gain: float32 [256], replicated, may hold values from 0.1 to 1.9
- router_weight: bfloat16 [256, 16], replicated, may hold values from -0.375 to 0.375
- expert_ids: int32 [32768, 2], P(('seq', 'expert')), may hold values from 0 to 15, all different within a row; in each aligned block of 1024 rows (0 to 1023, 1024 to 2047, ...) at most 256 rows name the same one
- expert_in: bfloat16 [16, 256, 512], P('expert'), may hold values from -0.375 to 0.375
- expert_out: bfloat16 [16, 512, 256], P('expert'), may hold values from -0.25 to 0.25
- cotangent: bfloat16 [32768, 256], P(('seq', 'expert')), may hold values from -6 to 6
Outputs:
- layer_out: bfloat16 [32768, 256], P(('seq', 'expert'))
- grad_stream: bfloat16 [32768, 256], P(('seq', 'expert'))
- grad_w_in: float32 [16, 256, 512], P('expert')
- grad_w_out: float32 [16, 512, 256], P('expert')
Inputs may be any that keep to these rules, and one draw needn't show every extreme that they name: `block_list`: global key block ids. Among the entries of the 16 query blocks of one seq index, no owner index (id // 16) appears more than 8 times, and one owner, the same for every seq index, appears exactly 8 times. A row may repeat a block. `expert_ids`: each row names 2 different experts; in each aligned block of 1024 rows (the rows of one device) no expert is named more than 256 times.
All inputs are finite; a program needn't handle non-finite values.
Results may differ from a plain program's by a relative error of at most 0.0081.
Values may be sent and summed in bfloat16 or wider, within the bound.
No kernel may reach another device: no remote copies, remote signals or barrier semaphores. Data moves between devices by JAX's collectives and lax.ppermute only.
A program may use at most 128 MiB of HBM per device.

v0:
```python
import math

import jax
import jax.numpy as jnp
from jax import lax
from jax.sharding import PartitionSpec as P

HD = 32


norm_eps = 1e-05
root_two_pi = 0.7978845608028654
cubic_term = 0.044715


def gelu_value(preact):
    inside = root_two_pi * (preact + cubic_term * preact * preact * preact)
    return 0.5 * preact * (1.0 + jnp.tanh(inside))


def gelu_slope(preact):
    inside = root_two_pi * (preact + cubic_term * preact * preact * preact)
    tanh_value = jnp.tanh(inside)
    return 0.5 * (1.0 + tanh_value) + 0.5 * preact * (
        1.0 - tanh_value * tanh_value
    ) * root_two_pi * (1.0 + 3.0 * cubic_term * preact * preact)


def attention(query_cols, key_cols, value_cols, block_list):
    seq_count = lax.axis_size("seq")
    feat_dev, node_seq = query_cols.shape
    blk_seq, degree = block_list.shape
    block_len = node_seq // blk_seq
    heads_dev = feat_dev // HD
    pair_count = blk_seq * degree
    capacity = 2 * pair_count // seq_count
    owner_ids = (block_list // blk_seq).reshape(-1)
    local_ids = (block_list % blk_seq).reshape(-1)
    owner_hot = (owner_ids[:, None] == jnp.arange(seq_count, dtype=jnp.int32)[None, :]).astype(
        jnp.int32
    )
    slot_rank = jnp.sum((jnp.cumsum(owner_hot, 0) - owner_hot) * owner_hot, 1)
    slot_index = owner_ids * capacity + slot_rank
    wanted = jnp.zeros((seq_count * capacity,), jnp.int32).at[slot_index].set(local_ids)
    incoming = lax.all_to_all(
        wanted.reshape(seq_count, capacity), "seq", split_axis=0, concat_axis=0, tiled=True
    )
    local_pairs = jnp.concatenate([key_cols, value_cols], 0).reshape(
        2 * feat_dev, blk_seq, block_len
    )
    replies = jnp.take(local_pairs, incoming.reshape(-1), axis=1)
    fetched = lax.all_to_all(replies, "seq", split_axis=1, concat_axis=1, tiled=True)
    chosen = jnp.take(fetched, slot_index, axis=1).reshape(
        2, heads_dev, HD, blk_seq, degree * block_len
    )
    queries = query_cols.reshape(heads_dev, HD, blk_seq, block_len)
    scores = jnp.einsum(
        "hdbn,hdbj->hbnj", queries, chosen[0], preferred_element_type=jnp.float32
    ) * (1.0 / math.sqrt(HD))
    row_max = jnp.max(scores, -1, keepdims=True)
    weights = jnp.exp(scores - row_max)
    row_sum = jnp.sum(weights, -1)
    attended = jnp.einsum(
        "hbnj,hdbj->hdbn",
        weights.astype(jnp.bfloat16),
        chosen[1],
        preferred_element_type=jnp.float32,
    )
    return (attended / row_sum[:, None]).astype(jnp.bfloat16).reshape(feat_dev, node_seq)


def shards(
    query_cols,
    key_cols,
    value_cols,
    block_list,
    residual,
    out_proj,
    norm_gain,
    router_weight,
    expert_ids,
    expert_in,
    expert_out,
    cotangent,
):
    exp_count = lax.axis_size("expert")
    attended = attention(query_cols, key_cols, value_cols, block_list)
    feat_dev, node_seq = attended.shape
    tok_dev = node_seq // exp_count
    head_rows = lax.dynamic_slice_in_dim(out_proj, lax.axis_index("expert") * feat_dev, feat_dev, 0)
    projected = lax.psum_scatter(
        jnp.einsum("fn,fe->ne", attended, head_rows, preferred_element_type=jnp.float32),
        "expert",
        scatter_dimension=0,
        tiled=True,
    )
    stream = (residual.astype(jnp.float32) + projected).astype(jnp.bfloat16)
    stream_float = stream.astype(jnp.float32)
    inverse_rms = lax.rsqrt(jnp.mean(stream_float * stream_float, -1, keepdims=True) + norm_eps)
    normed = (stream_float * inverse_rms * norm_gain).astype(jnp.bfloat16)
    logits = jnp.dot(normed, router_weight, preferred_element_type=jnp.float32)
    expert_total = router_weight.shape[1]
    topk_count = expert_ids.shape[1]
    feature_width = normed.shape[1]
    id_hot = expert_ids[:, :, None] == jnp.arange(expert_total, dtype=jnp.int32)[None, None, :]
    gate_values = jax.nn.sigmoid(jnp.sum(jnp.where(id_hot, logits[:, None, :], 0.0), -1))
    flat_hot = id_hot.reshape(tok_dev * topk_count, expert_total).astype(jnp.int32)
    slot_rank = jnp.sum((jnp.cumsum(flat_hot, 0) - flat_hot) * flat_hot, 1)
    flat_ids = expert_ids.reshape(-1)
    exp_dev = expert_total // exp_count
    capacity = 2 * tok_dev * topk_count // expert_total
    position = (flat_ids % exp_dev * exp_count + flat_ids // exp_dev) * capacity + slot_rank
    buffer_rows = exp_dev * exp_count * capacity

    def pack_rows(source_rows):
        filled = jnp.zeros((buffer_rows, feature_width), jnp.bfloat16).at[position].set(source_rows)
        return filled.reshape(exp_dev, exp_count, capacity, feature_width)

    def unpack_rows(buffer):
        return jnp.take(buffer.reshape(buffer_rows, feature_width), position, axis=0).reshape(
            tok_dev, topk_count, feature_width
        )

    cot_float = cotangent.astype(jnp.float32)
    sent_rows = pack_rows(jnp.repeat(normed, topk_count, 0))
    scaled = (
        (gate_values[:, :, None] * cot_float[:, None, :])
        .astype(jnp.bfloat16)
        .reshape(tok_dev * topk_count, feature_width)
    )
    arrived = lax.all_to_all(sent_rows, "expert", split_axis=1, concat_axis=1, tiled=True)
    rows_in = arrived.reshape(exp_dev, exp_count * capacity, feature_width)
    preact = jnp.einsum("jrd,jdf->jrf", rows_in, expert_in, preferred_element_type=jnp.float32)
    hidden = gelu_value(preact).astype(jnp.bfloat16)
    produced = jnp.einsum(
        "jrf,jfd->jrd", hidden, expert_out, preferred_element_type=jnp.float32
    ).astype(jnp.bfloat16)
    rows_in, preact, hidden, produced = (
        rows_in,
        preact,
        hidden,
        produced.reshape(exp_dev, exp_count, capacity, feature_width),
    )
    produced_home = lax.all_to_all(produced, "expert", split_axis=1, concat_axis=1, tiled=True)
    arrived_cot = lax.all_to_all(
        pack_rows(scaled), "expert", split_axis=1, concat_axis=1, tiled=True
    )
    cot_rows = arrived_cot.reshape(exp_dev, exp_count * capacity, feature_width)
    grad_out = jnp.einsum("jrf,jrd->jfd", hidden, cot_rows, preferred_element_type=jnp.float32)
    grad_hidden = jnp.einsum(
        "jrd,jfd->jrf", cot_rows, expert_out, preferred_element_type=jnp.float32
    )
    grad_pre = (grad_hidden * gelu_slope(preact)).astype(jnp.bfloat16)
    grad_in = jnp.einsum("jrd,jrf->jdf", rows_in, grad_pre, preferred_element_type=jnp.float32)
    grad_back = jnp.einsum(
        "jrf,jdf->jrd", grad_pre, expert_in, preferred_element_type=jnp.float32
    ).astype(jnp.bfloat16)
    grad_in, grad_out, grad_back = (
        grad_in,
        grad_out,
        grad_back.reshape(exp_dev, exp_count, capacity, feature_width),
    )
    back_home = lax.all_to_all(grad_back, "expert", split_axis=1, concat_axis=1, tiled=True)
    grad_w_in, grad_w_out = lax.psum((grad_in, grad_out), "seq")
    expert_rows = unpack_rows(produced_home).astype(jnp.float32)
    layer_out = (stream_float + jnp.sum(gate_values[:, :, None] * expert_rows, 1)).astype(
        jnp.bfloat16
    )
    grad_gate = jnp.sum(cot_float[:, None, :] * expert_rows, -1)
    grad_logit = grad_gate * gate_values * (1.0 - gate_values)
    logit_table = jnp.sum(jnp.where(id_hot, grad_logit[:, :, None], 0.0), 1)
    router_term = jnp.dot(
        logit_table, router_weight.astype(jnp.float32).T, precision=lax.Precision.HIGHEST
    )
    grad_normed = jnp.sum(unpack_rows(back_home).astype(jnp.float32), 1) + router_term
    gained = grad_normed * norm_gain
    grad_stream = (
        cot_float
        + inverse_rms * gained
        - stream_float * inverse_rms**3 * jnp.mean(stream_float * gained, -1, keepdims=True)
    )
    return (layer_out, grad_stream.astype(jnp.bfloat16), grad_w_in, grad_w_out)


def solution(mesh):
    return jax.shard_map(
        shards,
        mesh=mesh,
        in_specs=(
            P("expert", "seq"),
            P("expert", "seq"),
            P("expert", "seq"),
            P("seq", None),
            P(("seq", "expert"), None),
            P(),
            P(),
            P(),
            P(("seq", "expert"), None),
            P("expert", None, None),
            P("expert", None, None),
            P(("seq", "expert"), None),
        ),
        out_specs=(
            P(("seq", "expert"), None),
            P(("seq", "expert"), None),
            P("expert", None, None),
            P("expert", None, None),
        ),
        check_vma=False,
    )
```

profile of v0, /device:TPU:0, one launch (start us, length us, event | category | flops | bytes accessed | tf_op | source)
XLA Modules:
  0.0 664.3 jit_solution(7389052124910228881)
XLA Ops:
  10.4 7.4 %all-to-all-start = ((s32[16,1,8]{2,1,0:T(1,128)}), s32[16,1,8]{2,1,0:T(1,128)S(1)}, u32[]{:S(2)}, u32[]{:S(2)}) async-start(s32[16,1,8]{2,1,0:T(1,128)} %bitcast.2), calls=%async_computation | async-start | bytes 16384 | tf_op jit(solution)/shard_map/all_to_all | solution.py:45
  25.5 6.4 gather_fusion
  31.9 7.4 %select_bitcast_fusion = bf16[256,128,128]{2,0,1:T(8,128)(2,1)} fusion(bf16[128,256,128]{2,1,0:T(8,128)(2,1)} %gather_fusion, pred[128]{0:T(512)(128)(4,1)S(1)} %compare_and_fusion.1), kind=kLoop, calls=%fused_computation.22 | loop fusion | flops 4194304 | bytes 16777344 | tf_op jit(solution)/shard_map/jit(_take)/select_n | solution.py:51
  39.3 5.2 all-to-all-start.1
  44.7 150.5 %all-to-all-done.1 = bf16[256,128,128]{2,0,1:T(8,128)(2,1)} async-done(((bf16[256,128,128]{2,0,1:T(8,128)(2,1)}), bf16[256,128,128]{2,0,1:T(8,128)(2,1)}, u32[]{:S(2)}, u32[]{:S(2)}) %all-to-all-start.1) | async-done | bytes 8388640 | tf_op jit(solution)/shard_map/all_to_all | solution.py:52
  195.2 6.5 gather_fusion.1
  201.7 2.6 select_bitcast_fusion.1
  206.1 2.7 copy.131
  208.7 4.9 squeeze.7
  213.6 4.3 copy.130
  217.9 4.3 squeeze.6
  222.2 11.5 %bitcast_reduce_fusion = (f32[4,16,128]{2,1,0:T(8,128)S(1)}, f32[4,16,512,128]{3,2,1,0:T(8,128)}) fusion(bf16[4,32,16,128]{3,2,1,0:T(8,128)(2,1)S(1)} %bitcast.90, bf16[4,32,16,512]{3,2,1,0:T(8,128)(2,1)} %squeeze.7), kind=kOutput, calls=%fused_computation.8 | convolution fusion | flops 276815872 | bytes 19431424 | tf_op jit(solution)/shard_map/hdbn,hdbj->hbnj/dot_general | solution.py:57
  233.7 9.3 %fusion.1 = f32[4,16,128]{2,1,0:T(8,128)S(1)} fusion(f32[4,16,512,128]{3,2,1,0:T(8,128)} %get-tuple-element.25, f32[4,16,128]{2,1,0:T(8,128)S(1)} %get-tuple-element.24), kind=kLoop, calls=%fused_computation.10 | loop fusion | flops 12574720 | bytes 16842752 | tf_op jit(solution)/shard_map/reduce_sum | solution.py:62
  243.1 8.0 %fusion.35 = bf16[4,32,16,128]{3,1,2,0:T(8,128)(2,1)S(1)} fusion(f32[4,16,512,128]{3,2,1,0:T(8,128)} %get-tuple-element.25, f32[4,16,128]{2,1,0:T(8,128)S(1)} %get-tuple-element.24, bf16[4,32,16,512]{3,2,1,0:T(8,128)(2,1)S(1)} %copy-done.12, f32[4,16,128]{2,1,0:T(8,128)S(1)} %fusion.1), kind=kOutput, calls=%fused_computation.60 | convolution fusion | flops 281542656 | bytes 19464192 | tf_op jit(solution)/shard_map/hbnj,hdbj->hdbn/dot_general | solution.py:63
  251.3 1.8 fusion.40
  254.3 4.5 reduce-window.6
  259.7 57.3 %reduce-scatter.2.cloned.1.call-done = f32[1024,256]{1,0:T(8,128)} async-done(((f32[2048,256]{1,0:T(8,128)}), f32[1024,256]{1,0:T(8,128)}) %reduce-scatter.2.cloned.1.call-update) | async-done | bytes 1048592 | tf_op jit(solution)/shard_map/reduce_scatter | solution.py:91
  320.9 2.2 reshape.403
  323.2 11.2 %scatter_custom_fusion.1 = bf16[4096,256]{1,0:T(8,128)(2,1)} fusion(s32[2048]{0:T(1024)S(1)} %bitcast.101, bf16[2048,256]{1,0:T(8,128)(2,1)} %reshape.403, bf16[]{:T(256)} %constant.134.clone.1), kind=kCustom, calls=%fused_computation.56 | custom fusion | bytes 2097664 | tf_op jit(solution)/shard_map/scatter | solution.py:116
  336.2 27.8 %all_to_all.34 = bf16[8,2,256,256]{3,2,0,1:T(8,128)(2,1)S(1)} all-to-all(bf16[8,2,256,256]{3,2,0,1:T(8,128)(2,1)S(1)} %copy.141), channel_id=1, replica_groups=mesh['seq'=16,'expert'=2] {'expert'}, dimensions={1} | all-to-all | bytes 4194304 | tf_op jit(solution)/shard_map/all_to_all | solution.py:131
  366.8 3.0 convolution_convert_fusion.1
  371.5 4.9 all-to-all-start.3
  376.7 1.9 mul.252
  378.6 3.6 mul.253
  382.5 18.2 %all-to-all-done.3 = bf16[8,2,256,256]{3,2,0,1:T(8,128)(2,1)} async-done(((bf16[8,2,256,256]{3,2,0,1:T(8,128)(2,1)}), bf16[8,2,256,256]{3,2,0,1:T(8,128)(2,1)}, u32[]{:S(2)}, u32[]{:S(2)}) %all-to-all-start.3) | async-done | bytes 2097184 | tf_op jit(solution)/shard_map/all_to_all | solution.py:144
  400.7 3.1 copy.144
  403.8 8.5 %gather_fusion.2 = bf16[2048,256]{1,0:T(8,128)(2,1)S(1)} fusion(bf16[4096,256]{1,0:T(8,128)(2,1)} %bitcast.82, s32[2048]{0:T(1024)S(1)} %broadcast_clamp_fusion), kind=kCustom, calls=%fused_computation.clone | custom fusion | bytes 2105344 | tf_op jit(solution)/shard_map/jit(_take)/gather | solution.py:120
  412.3 2.0 multiply_reduce_fusion
  419.2 12.3 %scatter_custom_fusion.2 = bf16[4096,256]{1,0:T(8,128)(2,1)} fusion(s32[2048]{0:T(1024)S(1)} %bitcast.102, f32[2048,256]{1,0:T(8,128)} %mul.253, f32[2048]{0:T(1024)S(1)} %div.77, bf16[]{:T(256)} %constant.134.clone.1), kind=kCustom, calls=%fused_computation.50 | custom fusion | flops 1048576 | bytes 4202498 | tf_op jit(solution)/shard_map/scatter | solution.py:116
  433.2 26.1 %all_to_all.35 = bf16[8,2,256,256]{3,2,0,1:T(8,128)(2,1)S(1)} all-to-all(bf16[8,2,256,256]{3,2,0,1:T(8,128)(2,1)S(1)} %copy.146), channel_id=1, replica_groups=mesh['seq'=16,'expert'=2] {'expert'}, dimensions={1} | all-to-all | bytes 4194304 | tf_op jit(solution)/shard_map/all_to_all | solution.py:145
  459.5 8.7 %fusion.67 = f32[8,512,256]{2,1,0:T(8,128)} fusion(bf16[8,512,256]{2,1,0:T(8,128)(2,1)S(1)} %bitcast.91, f32[8,512,512]{2,1,0:T(8,128)} %copy-done.3), kind=kOutput, calls=%fused_computation.135 | convolution fusion | flops 1092616192 | bytes 14680064 | tf_op jit(solution)/shard_map/jrf,jrd->jfd/dot_general | solution.py:149
  468.3 5.8 fusion.9
  474.1 2.0 copy-done.9
  476.1 3.3 fusion.71
  479.5 4.2 convolution_convert_fusion
  485.1 5.2 all-to-all-start.5
  490.4 22.4 %all-to-all-done.5 = bf16[8,2,256,256]{3,2,0,1:T(8,128)(2,1)} async-done(((bf16[8,2,256,256]{3,2,0,1:T(8,128)(2,1)}), bf16[8,2,256,256]{3,2,0,1:T(8,128)(2,1)}, u32[]{:S(2)}, u32[]{:S(2)}) %all-to-all-start.5) | async-done | bytes 2097184 | tf_op jit(solution)/shard_map/all_to_all | solution.py:163
  512.8 3.1 copy.149
  515.9 10.3 %gather_fusion.3 = bf16[2048,256]{1,0:T(8,128)(2,1)} fusion(bf16[4096,256]{1,0:T(8,128)(2,1)} %bitcast.81, s32[2048]{0:T(1024)S(1)} %broadcast_clamp_fusion), kind=kCustom, calls=%fused_computation.1.clone | custom fusion | bytes 2105344 | tf_op jit(solution)/shard_map/jit(_take)/gather | solution.py:120
  526.3 3.3 select_convert_fusion
  529.6 3.5 reshape.357
  533.1 3.6 reshape.358
  536.7 5.1 reduce_sum.104
  541.8 2.1 fusion.25
  543.9 6.8 %multiply_reduce_fusion.1 = f32[1024,256]{1,0:T(8,128)S(1)} fusion(f32[1024,2,256]{2,1,0:T(2,128)} %reshape.357, f32[1024,2]{1,0:T(8,128)S(1)} %copy-done.7), kind=kLoop, calls=%fused_computation.32 | loop fusion | flops 786432 | bytes 3153920 | tf_op jit(solution)/shard_map/reduce_sum | solution.py:166
  552.1 98.0 %all-reduce.3.cloned.1.call-done = (f32[8,256,512]{2,1,0:T(8,128)}, f32[8,512,256]{2,1,0:T(8,128)}) async-done(((f32[8,256,512]{2,1,0:T(8,128)}, f32[8,512,256]{2,1,0:T(8,128)}), (f32[8,256,512]{2,1,0:T(8,128)}, f32[8,512,256]{2,1,0:T(8,128)})) %all-reduce.3.cloned.1.call-update) | async-done | bytes 8388624 | tf_op jit(solution)/shard_map/psum | solution.py:164
  650.1 4.8 copy.182
  654.9 2.0 copy.183
  (109 shorter events, 35.5 us)
Async XLA Ops:
  7.2 359.6 %copy-start = (bf16[8,512,256]{2,1,0:T(8,128)(2,1)S(1)}, bf16[8,512,256]{2,1,0:T(8,128)(2,1)}, u32[]{:S(2)}) copy-start(bf16[8,512,256]{2,1,0:T(8,128)(2,1)} %param.24) | copy-start | bytes 6291460
  10.4 13.7 %all-to-all-start = ((s32[16,1,8]{2,1,0:T(1,128)}), s32[16,1,8]{2,1,0:T(1,128)S(1)}, u32[]{:S(2)}, u32[]{:S(2)}) async-start(s32[16,1,8]{2,1,0:T(1,128)} %bitcast.2), calls=%async_computation | async-start | bytes 16384 | tf_op jit(solution)/shard_map/all_to_all | solution.py:45
  39.3 5.3 copy-start.13
  39.3 155.9 %all-to-all-start.1 = ((bf16[256,128,128]{2,0,1:T(8,128)(2,1)}), bf16[256,128,128]{2,0,1:T(8,128)(2,1)}, u32[]{:S(2)}, u32[]{:S(2)}) async-start(bf16[256,128,128]{2,0,1:T(8,128)(2,1)} %select_bitcast_fusion), calls=%async_computation.1 | async-start | bytes 16777216 | tf_op jit(solution)/shard_map/all_to_all | solution.py:52
  44.5 272.4 %reduce-scatter.2.cloned.1.call-start = ((), (), s32[]{:S(2)}) async-start(), calls=%async_computation.7 | async-start | bytes 3145728 | tf_op jit(solution)/shard_map/reduce_scatter | solution.py:91
  233.7 9.3 %copy-start.12 = (bf16[4,32,16,512]{3,2,1,0:T(8,128)(2,1)S(1)}, bf16[4,32,16,512]{3,2,1,0:T(8,128)(2,1)}, u32[]{:S(2)}) copy-start(bf16[4,32,16,512]{3,2,1,0:T(8,128)(2,1)} %squeeze.6) | copy-start | bytes 6291460
  243.0 8.3 %copy-start.17 = (bf16[256,256]{1,0:T(8,128)(2,1)S(1)}, bf16[256,256]{1,0:T(8,128)(2,1)}, u32[]{:S(2)}) copy-start(bf16[256,256]{1,0:T(8,128)(2,1)} %param.19) | copy-start | bytes 393220
  251.1 2.1 copy-start.15
  251.3 65.7 %copy-start.14 = (bf16[1024,256]{1,0:T(8,128)(2,1)S(1)}, bf16[1024,256]{1,0:T(8,128)(2,1)}, u32[]{:S(2)}) copy-start(bf16[1024,256]{1,0:T(8,128)(2,1)} %param.18) | copy-start | bytes 1572868
  253.1 66.1 %copy-start.18 = (f32[256]{0:T(256)S(1)}, f32[256]{0:T(256)}, u32[]{:S(2)}) copy-start(f32[256]{0:T(256)} %param.20) | copy-start | bytes 3076
  318.4 0.8 copy-start.4
  336.1 29.4 %copy-start.6 = (bf16[8,256,512]{2,1,0:T(8,128)(2,1)S(1)}, bf16[8,256,512]{2,1,0:T(8,128)(2,1)}, u32[]{:S(2)}) copy-start(bf16[8,256,512]{2,1,0:T(8,128)(2,1)} %param.23) | copy-start | bytes 6291460
  364.2 1.4 copy-start.1
  366.8 3.2 copy-start.3
  370.0 6.7 %copy-start.10 = (bf16[1024,256]{1,0:T(8,128)(2,1)S(1)}, bf16[1024,256]{1,0:T(8,128)(2,1)}, u32[]{:S(2)}) copy-start(bf16[1024,256]{1,0:T(8,128)(2,1)} %param.25) | copy-start | bytes 1572868
  371.5 29.2 %all-to-all-start.3 = ((bf16[8,2,256,256]{3,2,0,1:T(8,128)(2,1)}), bf16[8,2,256,256]{3,2,0,1:T(8,128)(2,1)}, u32[]{:S(2)}, u32[]{:S(2)}) async-start(bf16[8,2,256,256]{3,2,0,1:T(8,128)(2,1)} %copy.143), calls=%async_computation.4 | async-start | bytes 4194304 | tf_op jit(solution)/shard_map/all_to_all | solution.py:144
  376.4 5.8 copy-start.16
  376.4 273.7 %all-reduce.3.cloned.1.call-start = ((), (), s32[]{:S(2)}) async-start(), calls=%async_computation.8 | async-start | bytes 16777216 | tf_op jit(solution)/shard_map/psum | solution.py:164
  459.3 8.9 %slice-start = ((s8[8388608]{0:T(1024)(128)(4,1)}), s8[4194304]{0:T(1024)(128)(4,1)S(1)}, s32[]{:S(2)}) async-start(s8[8388608]{0:T(1024)(128)(4,1)} %bitcast.85), calls=%async_computation.9 | async-start | bytes 8388608
  459.5 8.8 %slice-start.1 = ((s8[8388608]{0:T(1024)(128)(4,1)}), s8[4194304]{0:T(1024)(128)(4,1)S(1)}, s32[]{:S(2)}) async-start(s8[8388608]{0:T(1024)(128)(4,1)} %bitcast.85), calls=%async_computation.10 | async-start | bytes 8388608
  468.3 7.9 %copy-start.2 = (bf16[8,2,256,256]{3,2,1,0:T(8,128)(2,1)S(1)}, bf16[8,2,256,256]{3,2,1,0:T(8,128)(2,1)}, u32[]{:S(2)}) copy-start(bf16[8,2,256,256]{3,2,1,0:T(8,128)(2,1)} %copy-done.1) | copy-start | bytes 6291460
  474.1 2.0 copy-start.9
  485.1 27.7 %all-to-all-start.5 = ((bf16[8,2,256,256]{3,2,0,1:T(8,128)(2,1)}), bf16[8,2,256,256]{3,2,0,1:T(8,128)(2,1)}, u32[]{:S(2)}, u32[]{:S(2)}) async-start(bf16[8,2,256,256]{3,2,0,1:T(8,128)(2,1)} %copy.148), calls=%async_computation.6 | async-start | bytes 4194304 | tf_op jit(solution)/shard_map/all_to_all | solution.py:163
  533.1 8.7 %copy-start.5 = (bf16[1024,256]{1,0:T(8,128)(2,1)S(1)}, bf16[1024,256]{1,0:T(8,128)(2,1)}, u32[]{:S(2)}) copy-start(bf16[1024,256]{1,0:T(8,128)(2,1)} %copy-done.4) | copy-start | bytes 1572868
  533.1 10.7 %copy-start.7 = (f32[1024,2]{1,0:T(8,128)S(1)}, f32[1024,2]{1,0:T(8,128)}, u32[]{:S(2)}) copy-start(f32[1024,2]{1,0:T(8,128)} %copy.137) | copy-start | bytes 24580
  541.8 8.9 %copy-start.11 = (bf16[1024,256]{1,0:T(8,128)(2,1)S(1)}, bf16[1024,256]{1,0:T(8,128)(2,1)}, u32[]{:S(2)}) copy-start(bf16[1024,256]{1,0:T(8,128)(2,1)} %param.25) | copy-start | bytes 1572868
  650.1 4.8 copy-start.8
Sparse Core Ops, SparseCore 0:
  253.3 63.6 reduce-scatter.1
  479.6 170.4 all-reduce.2
where the time goes:
time: 671 us; the launch traced here: 664 us
  waiting for transfers between devices  347 us (52%)
  local copies, waits for them, and re-layouts  115 us (17%)
  other arithmetic  60 us (9%)
  blocking collectives  53.9 us (8%)
  matrix products  49.9 us (7%)
  starting transfers between devices  22.9 us (3%)
  between operations  15.1 us (2%)
    all_to_all x1, waiting for transfers between devices, attention(): lax.all_to_all(replies, 'seq', split_axis=1, concat_axis=1, tiled=True)  150 us
    psum x1, waiting for transfers between devices, shards(): grad_w_in, grad_w_out = lax.psum((grad_in, grad_out), 'seq')  98 us
    reduce_scatter x1, waiting for transfers between devices, shards(): lax.psum_scatter(jnp.einsum('fn,fe->ne', attended, head_rows, preferred_e...  57.3 us
    all_to_all x1, blocking collectives, shards(): lax.all_to_all(sent_rows, 'expert', split_axis=1, concat_axis=1, tiled=True)  27.8 us
    all_to_all x1, blocking collectives, shards(): lax.all_to_all(pack_rows(scaled), 'expert', split_axis=1, concat_axis=1,...  26.1 us
    all_to_all x1, waiting for transfers between devices, shards(): lax.all_to_all(grad_back, 'expert', split_axis=1, concat_axis=1, tiled=True)  22.4 us
    gather x2, local copies, waits for them, and re-layouts, unpack_rows(): jnp.take(buffer.reshape(buffer_rows, feature_width), position, axis=0)  18.8 us
    all_to_all x1, waiting for transfers between devices, shards(): lax.all_to_all(produced, 'expert', split_axis=1, concat_axis=1, tiled=True)  18.2 us
  transfers between devices with their start and end apart: 6, of which 6 were waited for; matrix products, arithmetic and copies ran while one was open for 9% of the time, Pallas kernels for 0%

commit v1 on v0

v1 whole, which is shorter than its diff:
```python
import functools
import math

import jax
import jax.numpy as jnp
from jax import lax
from jax.experimental import pallas as pl
from jax.experimental.pallas import tpu as pltpu
from jax.sharding import PartitionSpec as P

HD = 32
WINDOW = 128
TILE = 128

norm_eps = 1e-05
root_two_pi = 0.7978845608028654
cubic_term = 0.044715

bf16 = jnp.bfloat16
f32 = jnp.float32
VMEM_BYTES = 48 * 1024 * 1024


def params(**kw):
    return pltpu.CompilerParams(vmem_limit_bytes=VMEM_BYTES, **kw)


def contract(a, b, da, db):
    return lax.dot_general(a, b, (((da,), (db,)), ((), ())), preferred_element_type=f32)


def ring_order(seq_count):
    rows = max(1, seq_count // 4)
    if seq_count % 4:
        return list(range(seq_count // 2))
    return [2 * z for z in range(rows)] + [2 * z + 1 for z in reversed(range(rows))]


def ring_pairs(seq_count, step):
    order = ring_order(seq_count)
    n = len(order)
    return [(2 * order[i] + c, 2 * order[(i + step) % n] + c) for i in range(n) for c in range(2)]


def sibling_pairs(seq_count):
    return [(s, s ^ 1) for s in range(seq_count)]


def shift_pairs(count, d):
    return [(i, (i + d) % count) for i in range(count)]


def gather_expert_axis(x, exp_count, axis=0):
    me = lax.axis_index("expert")
    size = x.shape[axis]
    shape = list(x.shape)
    shape[axis] = size * exp_count
    out = jnp.zeros(shape, x.dtype)
    out = lax.dynamic_update_slice_in_dim(out, x, me * size, axis)
    for d in range(1, exp_count):
        got = lax.ppermute(x, "expert", shift_pairs(exp_count, d))
        out = lax.dynamic_update_slice_in_dim(out, got, lax.rem(me + exp_count - d, exp_count) * size, axis)
    return out


def own_slots_kernel(k_ref, v_ref, kbuf_ref, vbuf_ref, sems):
    copies = [
        pltpu.make_async_copy(k_ref, kbuf_ref.at[0], sems.at[0]),
        pltpu.make_async_copy(v_ref, vbuf_ref.at[0], sems.at[1]),
    ]
    for copy in copies:
        copy.start()
    for copy in copies:
        copy.wait()


def own_slots(keys, values, slots):
    shape = jax.ShapeDtypeStruct((slots,) + keys.shape, keys.dtype)
    return pl.pallas_call(
        own_slots_kernel,
        in_specs=[pl.BlockSpec(memory_space=pl.ANY)] * 2,
        out_specs=[pl.BlockSpec(memory_space=pl.ANY)] * 2,
        out_shape=[shape, shape],
        scratch_shapes=[pltpu.SemaphoreType.DMA((2,))],
        name="own_slots",
    )(keys, values)


def ring_gather(keys, values, seq_count):
    n = seq_count // 2
    feat, nodes = keys.shape
    parts = 2 if feat >= 2 * HD else 1
    rows = feat // parts
    kbuf, vbuf = own_slots(keys, values, 2 * n)
    fwd, bwd, sib = ring_pairs(seq_count, 1), ring_pairs(seq_count, -1), sibling_pairs(seq_count)
    held = [(keys[i * rows : (i + 1) * rows], values[i * rows : (i + 1) * rows]) for i in range(parts)]
    for t in range(n):
        nxt = []
        for i, (k, v) in enumerate(held):
            if t > 0:
                k = lax.ppermute(k, "seq", fwd)
                v = lax.ppermute(v, "seq", bwd)
            nxt.append((k, v))
            if t > 0:
                kbuf = lax.dynamic_update_slice(kbuf, k[None], (t, i * rows, 0))
                vbuf = lax.dynamic_update_slice(vbuf, v[None], (t, i * rows, 0))
            ks = lax.ppermute(k, "seq", sib)
            vs = lax.ppermute(v, "seq", sib)
            kbuf = lax.dynamic_update_slice(kbuf, ks[None], (n + t, i * rows, 0))
            vbuf = lax.dynamic_update_slice(vbuf, vs[None], (n + t, i * rows, 0))
        held = nxt
    return kbuf, vbuf


def block_places(block_list, blk_seq, seq_count):
    order = ring_order(seq_count)
    n = len(order)
    inverse = [0] * n
    for i, chip in enumerate(order):
        inverse[chip] = i
    inverse = jnp.asarray(inverse, jnp.int32)
    me = lax.axis_index("seq")
    place = inverse[me // 2]
    owner = block_list // blk_seq
    local = block_list % blk_seq
    other = inverse[owner // 2]
    flag = ((owner ^ me) & 1) * n
    kslot = flag + lax.rem(place - other + n, n)
    vslot = flag + lax.rem(other - place + n, n)
    return kslot, vslot, local


def attention_kernel(degree, heads, kslot, vslot, local, q_ref, *refs):
    k_refs, v_refs, out_ref = refs[:degree], refs[degree : 2 * degree], refs[2 * degree]
    factor = math.log2(math.e) / math.sqrt(HD)
    cols = []
    for h in range(heads):
        rows = slice(h * HD, (h + 1) * HD)
        q = q_ref[rows, :]
        k = jnp.concatenate([r[0, rows, :] for r in k_refs], 1)
        v = jnp.concatenate([r[0, rows, :] for r in v_refs], 1)
        scores = contract(k, q, 0, 0)
        top = jnp.max(scores, 0, keepdims=True)
        probs = jnp.exp2((scores - top) * factor)
        total = jnp.sum(probs, 0, keepdims=True)
        out = jnp.dot(v, probs.astype(bf16), preferred_element_type=f32)
        cols.append(out / total)
    att = jnp.concatenate(cols, 0)
    out_ref[...] = att.T.astype(bf16)


def attention(queries, kbuf, vbuf, places, first, count, block_len):
    kslot, vslot, local = places
    degree = kslot.shape[1]
    feat = queries.shape[0]

    def kv_spec(slots_at, j):
        def index(b, ks, vs, lo):
            return ((ks, vs)[slots_at][b + first, j], 0, lo[b + first, j])

        return pl.BlockSpec((1, feat, block_len), index)

    return pl.pallas_call(
        functools.partial(attention_kernel, degree, feat // HD),
        grid_spec=pltpu.PrefetchScalarGridSpec(
            num_scalar_prefetch=3,
            grid=(count,),
            in_specs=[pl.BlockSpec((feat, block_len), lambda b, *_: (0, b + first))]
            + [kv_spec(0, j) for j in range(degree)]
            + [kv_spec(1, j) for j in range(degree)],
            out_specs=pl.BlockSpec((block_len, feat), lambda b, *_: (b, 0)),
        ),
        out_shape=jax.ShapeDtypeStruct((count * block_len, feat), bf16),
        compiler_params=params(),
        cost_estimate=pl.CostEstimate(
            flops=4 * count * block_len * degree * block_len * feat,
            bytes_accessed=2 * count * feat * block_len * (2 * degree + 2),
            transcendentals=count * block_len * degree * block_len * feat // HD,
        ),
        name="attention",
    )(kslot, vslot, local, queries, *([kbuf] * degree), *([vbuf] * degree))


def window_base(starts, i, e):
    return pl.multiple_of((starts[i, e] // 16) * 16, 16)


def stack_hot(starts, rank_ref, i, experts):
    nodes = rank_ref.shape[1]
    place = lax.broadcasted_iota(jnp.int32, (WINDOW, nodes), 0)
    hots = []
    for e in range(experts):
        rank = rank_ref[e : e + 1, :] - window_base(starts, i, e)
        hots.append(jnp.where(place == rank, 1.0, 0.0).astype(bf16))
    return jnp.concatenate(hots, 0)


def one_hot(rank_row, base):
    place = lax.broadcasted_iota(jnp.int32, (WINDOW, rank_row.shape[1]), 0)
    return jnp.where(place == rank_row - base, 1.0, 0.0).astype(bf16)


def extra_windows(starts, i, e):
    left = starts[i + 1, e] - window_base(starts, i, e)
    return jnp.maximum((left + WINDOW - 1) // WINDOW, 1)


def dispatch_kernel(experts, pieces, starts, rank_ref, res_ref, cot_ref, gain_ref, *refs):
    atts, projs, stream_ref, slots_ref = refs[:pieces], refs[pieces : 2 * pieces], refs[-2], refs[-1]
    i = pl.program_id(0)

    @pl.when(i == 0)
    def _():
        slots_ref[...] = jnp.zeros_like(slots_ref)

    acc = res_ref[...].astype(f32)
    projected = jnp.dot(atts[0][...], projs[0][...], preferred_element_type=f32)
    for a, w in zip(atts[1:], projs[1:]):
        projected = projected + jnp.dot(a[...], w[...], preferred_element_type=f32)
    stream = (acc + projected).astype(bf16)
    stream_ref[...] = stream
    wide = stream.astype(f32)
    inverse_rms = lax.rsqrt(jnp.mean(wide * wide, -1, keepdims=True) + norm_eps)
    normed = (wide * inverse_rms * gain_ref[...]).astype(bf16)
    rows = jnp.concatenate([normed, cot_ref[...]], 1)
    hot = stack_hot(starts, rank_ref, i, experts)
    packed = jnp.dot(hot, rows, preferred_element_type=f32).astype(bf16)
    for e in range(experts):
        at = pl.ds(window_base(starts, i, e), WINDOW)
        slots_ref[e, at, :] = slots_ref[e, at, :] + packed[e * WINDOW : (e + 1) * WINDOW]

    for e in range(experts):

        def more(w, carry, e=e):
            base = pl.multiple_of(window_base(starts, i, e) + w * WINDOW, 16)
            got = jnp.dot(one_hot(rank_ref[e : e + 1, :], base), rows, preferred_element_type=f32)
            at = pl.ds(base, WINDOW)
            slots_ref[e, at, :] = slots_ref[e, at, :] + got.astype(bf16)
            return carry

        lax.fori_loop(1, extra_windows(starts, i, e), more, 0)


def dispatch(starts, rank, residual, cotangent, gain, atts, projs, slot_rows, chunk):
    experts, nodes = rank.shape
    width = residual.shape[1]
    rows = lambda w: pl.BlockSpec((chunk, w), lambda i, s: (i, 0))
    whole = lambda a: pl.BlockSpec(a.shape, lambda i, s: (0,) * a.ndim)
    return pl.pallas_call(
        functools.partial(dispatch_kernel, experts, len(atts)),
        grid_spec=pltpu.PrefetchScalarGridSpec(
            num_scalar_prefetch=1,
            grid=(nodes // chunk,),
            in_specs=[
                pl.BlockSpec((experts, chunk), lambda i, s: (0, i)),
                rows(width),
                rows(width),
                whole(gain),
            ]
            + [rows(a.shape[1]) for a in atts]
            + [whole(w) for w in projs],
            out_specs=[rows(width), pl.BlockSpec((experts, slot_rows, 2 * width), lambda i, s: (0, 0, 0))],
        ),
        out_shape=[
            jax.ShapeDtypeStruct((nodes, width), bf16),
            jax.ShapeDtypeStruct((experts, slot_rows, 2 * width), bf16),
        ],
        compiler_params=params(),
        cost_estimate=pl.CostEstimate(
            flops=4 * nodes * experts * WINDOW * 2 * width,
            bytes_accessed=4 * nodes * width * 2 + 2 * experts * slot_rows * width * 2,
            transcendentals=nodes,
        ),
        name="dispatch",
    )(starts, rank, residual, cotangent, gain, *atts, *projs)


def expert_kernel(first, width, counts, ids, slots_ref, win_ref, wout_ref, router_ref, rcol_ref, rows_ref, grad_ref, acc_in, acc_out):
    step = pl.program_id(0)
    e = step + first
    count = counts[e]
    tiles = (count + TILE - 1) // TILE
    slot_rows = slots_ref.shape[1]
    acc_in[...] = jnp.zeros_like(acc_in)
    acc_out[...] = jnp.zeros_like(acc_out)
    w_in = win_ref[0]
    w_out = wout_ref[0]
    lane = lax.broadcasted_iota(jnp.int32, (TILE, router_ref.shape[1]), 1)
    mine = lane == ids[e]
    column = rcol_ref[0]

    def one(t, carry):
        at = pl.ds(pl.multiple_of(t * TILE, TILE), TILE)
        x = slots_ref[0, at, :width]
        cot = slots_ref[0, at, width:]
        cot_wide = cot.astype(f32)
        logits = jnp.dot(x, router_ref[...], preferred_element_type=f32)
        logit = jnp.sum(jnp.where(mine, logits, 0.0), 1, keepdims=True)
        gate = 1.0 / (1.0 + jnp.exp(-logit))
        scaled = (gate * cot_wide).astype(bf16)
        a = jnp.dot(x, w_in, preferred_element_type=f32)
        grad_hidden = contract(scaled, w_out, 1, 1)
        a2 = a * a
        t1 = jnp.tanh(root_two_pi * (a + cubic_term * a * a2))
        half = 0.5 + 0.5 * t1
        hidden = (a * half).astype(bf16)
        slope = half + (0.5 * root_two_pi) * a * (1.0 - t1 * t1) * (1.0 + (3.0 * cubic_term) * a2)
        grad_pre = (grad_hidden * slope).astype(bf16)
        acc_out[...] += contract(hidden, scaled, 0, 0)
        acc_in[...] += contract(x, grad_pre, 0, 0)
        produced = jnp.dot(hidden, w_out, preferred_element_type=f32).astype(bf16).astype(f32)
        grad_rows = contract(grad_pre, w_in, 1, 1).astype(bf16).astype(f32)
        grad_logit = jnp.sum(cot_wide * produced, 1, keepdims=True) * gate * (1.0 - gate)
        rows_ref[0, at, :width] = (gate * produced).astype(bf16)
        rows_ref[0, at, width:] = (grad_rows + grad_logit * column).astype(bf16)
        return carry

    lax.fori_loop(0, tiles, one, 0)

    def blank(t, carry):
        at = pl.ds(pl.multiple_of(t * TILE, TILE), TILE)
        rows_ref[0, at, :] = jnp.zeros((TILE, 2 * width), bf16)
        return carry

    lax.fori_loop(tiles, slot_rows // TILE, blank, 0)
    ff = acc_in.shape[1]
    grad_ref[0, :width, :] = acc_in[...].astype(bf16)
    parts = ff // width
    for j in range(parts):
        grad_ref[0, width:, j * width : (j + 1) * width] = acc_out[j * width : (j + 1) * width, :].astype(bf16)


def experts_step(counts, ids, slots, w_in, w_out, router, columns, first, count):
    experts, slot_rows, double = slots.shape
    width, ff = w_in.shape[1], w_in.shape[2]
    block = lambda *shape: pl.BlockSpec((1,) + shape, lambda i, *_: (i + first, 0, 0))
    fresh = lambda *shape: pl.BlockSpec((1,) + shape, lambda i, *_: (i, 0, 0))
    return pl.pallas_call(
        functools.partial(expert_kernel, first, width),
        grid_spec=pltpu.PrefetchScalarGridSpec(
            num_scalar_prefetch=2,
            grid=(count,),
            in_specs=[
                block(slot_rows, double),
                block(width, ff),
                block(ff, width),
                pl.BlockSpec(router.shape, lambda i, *_: (0, 0)),
                block(1, width),
            ],
            out_specs=[fresh(slot_rows, double), fresh(2 * width, ff)],
            scratch_shapes=[pltpu.VMEM((width, ff), f32), pltpu.VMEM((ff, width), f32)],
        ),
        out_shape=[
            jax.ShapeDtypeStruct((count, slot_rows, double), bf16),
            jax.ShapeDtypeStruct((count, 2 * width, ff), bf16),
        ],
        compiler_params=params(),
        cost_estimate=pl.CostEstimate(
            flops=count * slot_rows * width * ff * 12,
            bytes_accessed=count * (2 * slot_rows * double + 4 * width * ff) * 2,
            transcendentals=count * slot_rows * ff,
        ),
        name="experts",
    )(counts, ids, slots, w_in, w_out, router, columns)


def combined(starts, rank_ref, rows_refs, i, experts):
    hot = stack_hot(starts, rank_ref, i, experts)
    windows = []
    where = []
    for r in rows_refs:
        for j in range(r.shape[0]):
            where.append((r, j))
    for e, (r, j) in enumerate(where):
        windows.append(r[j, pl.ds(window_base(starts, i, e), WINDOW), :])
    total = contract(hot, jnp.concatenate(windows, 0), 0, 0)
    for e, (r, j) in enumerate(where):

        def more(w, acc, e=e, r=r, j=j):
            base = pl.multiple_of(window_base(starts, i, e) + w * WINDOW, 16)
            return acc + contract(one_hot(rank_ref[e : e + 1, :], base), r[j, pl.ds(base, WINDOW), :], 0, 0)

        total = lax.fori_loop(1, extra_windows(starts, i, e), more, total)
    return total


def send_kernel(experts, parts, chunks, starts, order, rank_ref, *refs):
    i = order[pl.program_id(0)]
    refs[parts][...] = combined(starts, rank_ref, refs[:parts], i, experts).astype(bf16)


def home_kernel(experts, parts, got, starts, order, rank_ref, stream_ref, cot_ref, gain_ref, *refs):
    i = order[pl.program_id(0)]
    rows_refs, got_refs = refs[:parts], refs[parts : parts + got]
    layer_ref, grad_ref = refs[parts + got :]
    total = combined(starts, rank_ref, rows_refs, i, experts)
    for g in got_refs:
        total = total + g[...].astype(f32)
    width = stream_ref.shape[1]
    stream = stream_ref[...].astype(f32)
    inverse_rms = lax.rsqrt(jnp.mean(stream * stream, -1, keepdims=True) + norm_eps)
    layer_ref[...] = (stream + total[:, :width]).astype(bf16)
    gained = total[:, width:] * gain_ref[...]
    mean = jnp.mean(stream * gained, -1, keepdims=True)
    grad = cot_ref[...].astype(f32) + inverse_rms * gained - stream * (inverse_rms * inverse_rms * inverse_rms) * mean
    grad_ref[...] = grad.astype(bf16)


def send_home(starts, order, rank, rows_parts, chunk):
    experts = rank.shape[0]
    count = order.shape[0]
    double = rows_parts[0].shape[2]
    return pl.pallas_call(
        functools.partial(send_kernel, experts, len(rows_parts), count),
        grid_spec=pltpu.PrefetchScalarGridSpec(
            num_scalar_prefetch=2,
            grid=(count,),
            in_specs=[pl.BlockSpec((experts, chunk), lambda i, s, o: (0, o[i]))]
            + [pl.BlockSpec(r.shape, lambda i, s, o: (0, 0, 0)) for r in rows_parts],
            out_specs=pl.BlockSpec((chunk, double), lambda i, s, o: (i, 0)),
        ),
        out_shape=jax.ShapeDtypeStruct((count * chunk, double), bf16),
        compiler_params=params(),
        cost_estimate=pl.CostEstimate(
            flops=2 * count * chunk * experts * WINDOW * double,
            bytes_accessed=sum(r.size for r in rows_parts) * 2 + count * chunk * double * 2,
            transcendentals=0,
        ),
        name="send_home",
    )(starts, order, rank, *rows_parts)


def at_home(starts, order, rank, stream, cotangent, gain, rows_parts, got, chunk):
    experts = rank.shape[0]
    count = order.shape[0]
    double = rows_parts[0].shape[2]
    width = double // 2
    fresh = lambda w: pl.BlockSpec((chunk, w), lambda i, s, o: (i, 0))
    return pl.pallas_call(
        functools.partial(home_kernel, experts, len(rows_parts), len(got)),
        grid_spec=pltpu.PrefetchScalarGridSpec(
            num_scalar_prefetch=2,
            grid=(count,),
            in_specs=[
                pl.BlockSpec((experts, chunk), lambda i, s, o: (0, o[i])),
                pl.BlockSpec((chunk, width), lambda i, s, o: (o[i], 0)),
                fresh(width),
                pl.BlockSpec(gain.shape, lambda i, s, o: (0, 0)),
            ]
            + [pl.BlockSpec(r.shape, lambda i, s, o: (0, 0, 0)) for r in rows_parts]
            + [fresh(double) for _ in got],
            out_specs=[fresh(width), fresh(width)],
        ),
        out_shape=[jax.ShapeDtypeStruct((count * chunk, width), bf16)] * 2,
        compiler_params=params(),
        cost_estimate=pl.CostEstimate(
            flops=2 * count * chunk * experts * WINDOW * double,
            bytes_accessed=sum(r.size for r in rows_parts) * 2 + count * chunk * double * 4,
            transcendentals=0,
        ),
        name="at_home",
    )(starts, order, rank, stream, cotangent, gain, *rows_parts, *got)


def line_pairs(seq_count, d):
    lines = seq_count // 4
    return [(z * 4 + r, ((z + d) % lines) * 4 + r) for z in range(lines) for r in range(4)]


def sum_over_seq(grads, seq_count):
    lines = seq_count // 4
    s = lax.axis_index("seq")
    core, column, line = s % 2, (s // 2) % 2, s // 4
    sib = sibling_pairs(seq_count)
    cross = [(i, i ^ 2) for i in range(seq_count)]

    def halve(a, which, pairs):
        h = a.shape[0] // 2
        mine = lax.dynamic_slice_in_dim(a, which * h, h, 0)
        other = lax.dynamic_slice_in_dim(a, (1 - which) * h, h, 0)
        got = lax.ppermute(other, "seq", pairs)
        return (mine.astype(f32) + got.astype(f32)).astype(bf16)

    a = halve(halve(grads, core, sib), column, cross)
    q = a.shape[0] // lines
    total = lax.dynamic_slice_in_dim(a, line * q, q, 0).astype(f32)
    for d in range(1, lines):
        part = lax.dynamic_slice_in_dim(a, lax.rem(line + d, lines) * q, q, 0)
        total = total + lax.ppermute(part, "seq", line_pairs(seq_count, d)).astype(f32)
    shard = total.astype(bf16)

    out = jnp.zeros((q * lines,) + a.shape[1:], bf16)
    out = lax.dynamic_update_slice_in_dim(out, shard, line * q, 0)
    for d in range(1, lines):
        got = lax.ppermute(shard, "seq", line_pairs(seq_count, d))
        out = lax.dynamic_update_slice_in_dim(out, got, lax.rem(line - d + lines, lines) * q, 0)

    def double(a, which, pairs):
        got = lax.ppermute(a, "seq", pairs)
        return jnp.where(which == 0, jnp.concatenate([a, got], 0), jnp.concatenate([got, a], 0))

    return double(double(out, column, cross), core, sib)


def shards(
    query_cols,
    key_cols,
    value_cols,
    block_list,
    residual,
    out_proj,
    norm_gain,
    router_weight,
    expert_ids,
    expert_in,
    expert_out,
    cotangent,
):
    seq_count = lax.axis_size("seq")
    exp_count = lax.axis_size("expert")
    me = lax.axis_index("expert")
    feat, nodes = query_cols.shape
    blk_seq, degree = block_list.shape
    block_len = nodes // blk_seq
    tok_dev, width = residual.shape
    expert_total = router_weight.shape[1]
    experts = expert_in.shape[0]
    ff = expert_in.shape[2]
    topk = expert_ids.shape[1]
    chunk = min(256, tok_dev)
    capacity = 2 * tok_dev * topk // expert_total * exp_count
    slot_rows = capacity + WINDOW

    kbuf, vbuf = ring_gather(key_cols, value_cols, seq_count)
    places = block_places(block_list, blk_seq, seq_count)

    residual_all = gather_expert_axis(residual, exp_count)
    cotangent_all = gather_expert_axis(cotangent, exp_count)
    ids_all = gather_expert_axis(expert_ids.T, exp_count, 1)
    gain = norm_gain.reshape(1, width)
    local_ids = me * experts + jnp.arange(experts, dtype=jnp.int32)
    hot = jnp.sum((ids_all[None, :, :] == local_ids[:, None, None]).astype(jnp.int32), 1)
    running = jnp.cumsum(hot, 1)
    rank = jnp.where(hot > 0, running - 1, -(1 << 20))
    ends = running[:, chunk - 1 :: chunk]
    starts = jnp.concatenate([jnp.zeros((experts, 1), jnp.int32), ends], 1).T
    counts = running[:, -1]
    router = jnp.pad(router_weight, ((0, 0), (0, -expert_total % 128)))
    columns = lax.dynamic_slice_in_dim(router_weight.T, me * experts, experts, 0).astype(f32).reshape(experts, 1, width)
    projs = [
        lax.dynamic_slice_in_dim(out_proj, lax.rem(me + exp_count - d, exp_count) * feat, feat, 0)
        for d in range(exp_count)
    ]
    chunks_dev = tok_dev // chunk
    in_chunk = jnp.arange(chunks_dev, dtype=jnp.int32)
    own_order = me * chunks_dev + in_chunk

    calls = 2 if blk_seq % 2 == 0 else 1
    per_call = blk_seq // calls
    pieces = [[] for _ in range(exp_count)]
    for c in range(calls):
        part = attention(query_cols, kbuf, vbuf, places, c * per_call, per_call, block_len)
        pieces[0].append(part)
        for d in range(1, exp_count):
            pieces[d].append(lax.ppermute(part, "expert", shift_pairs(exp_count, d)))
    atts = [jnp.concatenate(p, 0) for p in pieces]

    stream, slots = dispatch(starts, rank, residual_all, cotangent_all, gain, atts, projs, slot_rows, chunk)

    groups = 2 if experts % 2 == 0 else 1
    per_group = experts // groups
    rows_parts, sums = [], []
    for g in range(groups):
        rows, grads = experts_step(counts, local_ids, slots, expert_in, expert_out, router, columns, g * per_group, per_group)
        rows_parts.append(rows)
        sums.append(sum_over_seq(grads.reshape(per_group * 2 * width, ff), seq_count).reshape(per_group, 2 * width, ff))

    got = []
    for d in range(1, exp_count):
        target = lax.rem(me + d, exp_count)
        partial = send_home(starts, target * chunks_dev + in_chunk, rank, rows_parts, chunk)
        got.append(lax.ppermute(partial, "expert", shift_pairs(exp_count, d)))
    layer_out, grad_stream = at_home(starts, own_order, rank, stream, cotangent, gain, rows_parts, got, chunk)

    total = jnp.concatenate(sums, 0).astype(f32)
    grad_w_in = total[:, :width, :]
    grad_w_out = jnp.concatenate(
        [total[:, width:, j * width : (j + 1) * width] for j in range(ff // width)], 1
    )
    return layer_out, grad_stream, grad_w_in, grad_w_out


def solution(mesh):
    return jax.shard_map(
        shards,
        mesh=mesh,
        in_specs=(
            P("expert", "seq"),
            P("expert", "seq"),
            P("expert", "seq"),
            P("seq", None),
            P(("seq", "expert"), None),
            P(),
            P(),
            P(),
            P(("seq", "expert"), None),
            P("expert", None, None),
            P("expert", None, None),
            P(("seq", "expert"), None),
        ),
        out_specs=(
            P(("seq", "expert"), None),
            P(("seq", "expert"), None),
            P("expert", None, None),
            P("expert", None, None),
        ),
        check_vma=False,
    )
```

time: 671 us -> 372 us (0.55); the launches traced: 664 us -> 373 us
  waiting for transfers between devices: 347 us -> 99.4 us
  Pallas kernels: 0 us -> 108 us
  blocking collectives: 53.9 us -> 0 us
  matrix products: 49.9 us -> 0 us
  starting transfers between devices: 22.9 us -> 66.3 us
  local copies, waits for them, and re-layouts: 115 us -> 72 us
  other arithmetic: 60 us -> 26.1 us
  between operations: 15.1 us -> 1.25 us
    all_to_all x4 -> x0, waiting for transfers between devices: 192 us -> none  [the longest x1 150 us: attention(): lax.all_to_all(replies, 'seq', split_axis=1, concat_axis=1, tiled=True)]
    pallas_call x0 -> x8, Pallas kernels: none -> 108 us  [the longest x1 32.9 us: own_slots(): pl.pallas_call(own_slots_kernel, in_specs=[pl.BlockSpec(memory_space=pl.A...]
    ppermute x0 -> x86, waiting for transfers between devices: none -> 99.4 us  [the longest x14 39.1 us: ring_gather(): k = lax.ppermute(k, 'seq', fwd)]
    psum x1 -> x0, waiting for transfers between devices: 98 us -> none  [shards(): grad_w_in, grad_w_out = lax.psum((grad_in, grad_out), 'seq')]
    ppermute x0 -> x86, starting transfers between devices: none -> 66.3 us  [the longest x14 19.1 us: ring_gather(): v = lax.ppermute(v, 'seq', bwd)]
    reduce_scatter x1 -> x0, waiting for transfers between devices: 57.3 us -> none  [shards(): lax.psum_scatter(jnp.einsum('fn,fe->ne', attended, head_rows, preferred_e...]
    all_to_all x2 -> x0, blocking collectives: 53.9 us -> none  [the longest x1 27.8 us: shards(): lax.all_to_all(sent_rows, 'expert', split_axis=1, concat_axis=1, tiled=True)]
    dynamic_update_slice x0 -> x72, local copies, waits for them, and re-layouts: none -> 51.2 us  [the longest x16 13.4 us: ring_gather(): vbuf = lax.dynamic_update_slice(vbuf, vs[None], (n + t, i * rows, 0))]
  transfers between devices with their start and end apart: 6 -> 86, of which waited for: 6 -> 24; matrix products, arithmetic and copies ran while one was open for 9% -> 22% of each run, Pallas kernels for 0% -> 23%
where the time goes in v1:
time: 372 us; the launch traced here: 373 us
  Pallas kernels  108 us (29%)
  waiting for transfers between devices  99.4 us (27%)
  local copies, waits for them, and re-layouts  72 us (19%)
  starting transfers between devices  66.3 us (18%)
  other arithmetic  26.1 us (7%)
    ppermute x14, waiting for transfers between devices, ring_gather(): k = lax.ppermute(k, 'seq', fwd)  39.1 us
    pallas_call x1, Pallas kernels, own_slots(): pl.pallas_call(own_slots_kernel, in_specs=[pl.BlockSpec(memory_space=pl.A...  32.9 us
    pallas_call x2, Pallas kernels, attention(): pl.pallas_call(functools.partial(attention_kernel, degree, feat // HD), g...  26.1 us
    pallas_call x2, Pallas kernels, experts_step(): pl.pallas_call(functools.partial(expert_kernel, first, width), grid_spec=...  23.8 us
    ppermute x14, starting transfers between devices, ring_gather(): v = lax.ppermute(v, 'seq', bwd)  19.1 us
    ppermute x4, waiting for transfers between devices, halve(): got = lax.ppermute(other, 'seq', pairs)  14 us
    dynamic_update_slice x16, local copies, waits for them, and re-layouts, ring_gather(): vbuf = lax.dynamic_update_slice(vbuf, vs[None], (n + t, i * rows, 0))  13.4 us
    dynamic_update_slice x16, local copies, waits for them, and re-layouts, ring_gather(): kbuf = lax.dynamic_update_slice(kbuf, ks[None], (n + t, i * rows, 0))  12.5 us
  transfers between devices with their start and end apart: 86, of which 24 were waited for; matrix products, arithmetic and copies ran while one was open for 22% of the time, Pallas kernels for 23%

profile of v1, /device:TPU:0, one launch (start us, length us, event | category | flops | bytes accessed | tf_op | source)
XLA Modules:
  0.0 372.7 jit_solution(5047235668423862554)
XLA Ops:
  0.7 2.0 fusion.8
  3.1 2.5 collective-permute-start.35
  14.6 32.9 %own_slots.1 = (bf16[16,128,2048]{2,1,0:T(8,128)(2,1)}, bf16[16,128,2048]{2,1,0:T(8,128)(2,1)}) custom-call(bf16[128,2048]{1,0:T(8,128)(2,1)} %k_ref.1, bf16[128,2048]{1,0:T(8,128)(2,1)} %v_ref.1), custom_call_target="tpu_custom_call" | custom-call | tf_op jit(solution)/shard_map/own_slots/pallas_call | solution.py:79
  47.9 2.3 reduce-window.6
  51.7 1.7 bitcast_dynamic-update-slice_fusion.29
  53.6 1.6 bitcast_dynamic-update-slice_fusion.28
  55.8 1.7 bitcast_dynamic-update-slice_fusion.27
  57.8 1.7 bitcast_dynamic-update-slice_fusion.59
  59.5 1.7 collective-permute-start.2
  70.5 4.1 %collective-permute-done.39 = bf16[64,2048]{1,0:T(8,128)(2,1)S(1)} collective-permute-done((bf16[64,2048]{1,0:T(8,128)(2,1)}, bf16[64,2048]{1,0:T(8,128)(2,1)S(1)}, u32[]{:S(2)}, u32[]{:S(2)}) %collective-permute-start.39) | collective-permute-done | bytes 262176 | tf_op jit(solution)/shard_map/ppermute | solution.py:102
  79.2 4.6 %collective-permute-done.9 = bf16[64,2048]{1,0:T(8,128)(2,1)S(1)} collective-permute-done((bf16[64,2048]{1,0:T(8,128)(2,1)S(1)}, bf16[64,2048]{1,0:T(8,128)(2,1)S(1)}, u32[]{:S(2)}, u32[]{:S(2)}) %collective-permute-start.9) | collective-permute-done | bytes 262176 | tf_op jit(solution)/shard_map/ppermute | solution.py:101
  96.7 3.6 collective-permute-done.13
  111.5 6.1 %collective-permute-done.17 = bf16[64,2048]{1,0:T(8,128)(2,1)S(1)} collective-permute-done((bf16[64,2048]{1,0:T(8,128)(2,1)S(1)}, bf16[64,2048]{1,0:T(8,128)(2,1)S(1)}, u32[]{:S(2)}, u32[]{:S(2)}) %collective-permute-start.17) | collective-permute-done | bytes 262176 | tf_op jit(solution)/shard_map/ppermute | solution.py:101
  129.0 6.0 %collective-permute-done.21 = bf16[64,2048]{1,0:T(8,128)(2,1)S(1)} collective-permute-done((bf16[64,2048]{1,0:T(8,128)(2,1)S(1)}, bf16[64,2048]{1,0:T(8,128)(2,1)S(1)}, u32[]{:S(2)}, u32[]{:S(2)}) %collective-permute-start.21) | collective-permute-done | bytes 262176 | tf_op jit(solution)/shard_map/ppermute | solution.py:101
  138.4 1.8 collective-permute-done.23
  146.3 5.2 %collective-permute-done.25 = bf16[64,2048]{1,0:T(8,128)(2,1)S(1)} collective-permute-done((bf16[64,2048]{1,0:T(8,128)(2,1)S(1)}, bf16[64,2048]{1,0:T(8,128)(2,1)S(1)}, u32[]{:S(2)}, u32[]{:S(2)}) %collective-permute-start.25) | collective-permute-done | bytes 262176 | tf_op jit(solution)/shard_map/ppermute | solution.py:101
  154.8 2.0 collective-permute-done.27
  163.0 1.8 collective-permute-done.61
  165.2 2.7 collective-permute-done.29
  167.9 5.2 %collective-permute-done.31 = bf16[64,2048]{1,0:T(8,128)(2,1)S(1)} collective-permute-done((bf16[64,2048]{1,0:T(8,128)(2,1)S(1)}, bf16[64,2048]{1,0:T(8,128)(2,1)S(1)}, u32[]{:S(2)}, u32[]{:S(2)}) %collective-permute-start.31) | collective-permute-done | bytes 262176 | tf_op jit(solution)/shard_map/ppermute | solution.py:101
  178.9 13.0 %attention.2 = bf16[1024,128]{1,0:T(8,128)(2,1)S(1)} custom-call(s32[16,4]{1,0:T(8,128)S(1)} %get-tuple-element.45.kslot, s32[16,4]{1,0:T(8,128)S(1)} %get-tuple-element.44.vslot, s32[16,4]{1,0:T(8,128)S(1)} %get-tuple-element.42.local, bf16[128,2048]{1,0:T(8,128)(2,1)S(1)} %copy-done.1, ...), custom_call_target="tpu_custom_call" | custom-call | flops 268435456 | bytes 2621440 | tf_op jit(solution)/shard_map/attention/pallas_call | solution.py:163
  192.5 13.1 %attention.3 = bf16[1024,128]{1,0:T(8,128)(2,1)S(1)} custom-call(s32[16,4]{1,0:T(8,128)S(1)} %get-tuple-element.45.kslot, s32[16,4]{1,0:T(8,128)S(1)} %get-tuple-element.44.vslot, s32[16,4]{1,0:T(8,128)S(1)} %get-tuple-element.42.local, bf16[128,2048]{1,0:T(8,128)(2,1)S(1)} %copy-done.1, ...), custom_call_target="tpu_custom_call" | custom-call | flops 268435456 | bytes 2621440 | tf_op jit(solution)/shard_map/attention/pallas_call | solution.py:163
  207.3 6.8 %collective-permute-done.64 = bf16[1024,128]{1,0:T(8,128)(2,1)S(1)} collective-permute-done((bf16[1024,128]{1,0:T(8,128)(2,1)S(1)}, bf16[1024,128]{1,0:T(8,128)(2,1)S(1)}, u32[]{:S(2)}, u32[]{:S(2)}) %collective-permute-start.64) | collective-permute-done | bytes 262176 | tf_op jit(solution)/shard_map/ppermute | solution.py:565
  214.2 10.4 %dispatch.1 = (bf16[2048,256]{1,0:T(8,128)(2,1)S(1)}, bf16[8,640,512]{2,1,0:T(8,128)(2,1)}) custom-call(s32[9,8]{1,0:T(8,128)S(1)} %copy.43.starts, s32[8,2048]{1,0:T(8,128)S(1)} %add_select_fusion.rank_ref, bf16[2048,256]{1,0:T(8,128)(2,1)S(1)} %constant_dynamic-update-slice_fusion.10.res_ref, ...), custom_call_target="tpu_custom_call" | custom-call | flops 4294967296 | bytes 9437184 | tf_op jit(solution)/shard_map/dispatch/pallas_call | solution.py:249
  225.5 12.7 %experts.2 = (bf16[4,640,512]{2,1,0:T(8,128)(2,1)}, bf16[4,512,512]{2,1,0:T(8,128)(2,1)S(1)}) custom-call(s32[8]{0:T(128)S(1)} %slice_reduce_fusion.1.counts, s32[8]{0:T(128)S(1)} %iota_add_fusion.2.ids, bf16[8,640,512]{2,1,0:T(8,128)(2,1)} %get-tuple-element.17.slots_ref, bf16[8,256,512]{2,1,0:T(8,128)(2,1)S(1)} %copy-done.8, ...), custom_call_target="tpu_custom_call" | custom-call | flops 4026531840 | bytes 9437184 | tf_op jit(solution)/shard_map/experts/pallas_call | solution.py:338
  239.9 11.2 %experts.3 = (bf16[4,640,512]{2,1,0:T(8,128)(2,1)}, bf16[4,512,512]{2,1,0:T(8,128)(2,1)S(1)}) custom-call(s32[8]{0:T(128)S(1)} %slice_reduce_fusion.1.counts, s32[8]{0:T(128)S(1)} %iota_add_fusion.2.ids, bf16[8,640,512]{2,1,0:T(8,128)(2,1)} %get-tuple-element.17.slots_ref, bf16[8,256,512]{2,1,0:T(8,128)(2,1)S(1)} %copy-done.8, ...), custom_call_target="tpu_custom_call" | custom-call | flops 4026531840 | bytes 9437184 | tf_op jit(solution)/shard_map/experts/pallas_call | solution.py:338
  253.5 2.0 add_convert_fusion.1
  256.8 1.8 add_convert_fusion
  262.0 9.4 %collective-permute-done.67 = bf16[512,512]{1,0:T(8,128)(2,1)} collective-permute-done((bf16[512,512]{1,0:T(8,128)(2,1)}, bf16[512,512]{1,0:T(8,128)(2,1)}, u32[]{:S(2)}, u32[]{:S(2)}) %collective-permute-start.67) | collective-permute-done | bytes 524320 | tf_op jit(solution)/shard_map/ppermute | solution.py:481
  275.0 2.7 collective-permute-start.70
  277.7 4.6 %collective-permute-done.77 = bf16[512,512]{1,0:T(8,128)(2,1)} collective-permute-done((bf16[512,512]{1,0:T(8,128)(2,1)}, bf16[512,512]{1,0:T(8,128)(2,1)}, u32[]{:S(2)}, u32[]{:S(2)}) %collective-permute-start.77) | collective-permute-done | bytes 524320 | tf_op jit(solution)/shard_map/ppermute | solution.py:481
  285.9 2.5 collective-permute-start.80
  289.9 1.7 collective-permute-start.72
  292.0 2.1 collective-permute-start.73
  294.1 6.7 %collective-permute-done.79 = bf16[128,512]{1,0:T(8,128)(2,1)S(1)} collective-permute-done((bf16[128,512]{1,0:T(8,128)(2,1)S(1)}, bf16[128,512]{1,0:T(8,128)(2,1)S(1)}, u32[]{:S(2)}, u32[]{:S(2)}) %collective-permute-start.79) | collective-permute-done | bytes 131104 | tf_op jit(solution)/shard_map/ppermute | solution.py:489
  302.3 6.0 %collective-permute-start.81 = (bf16[128,512]{1,0:T(8,128)(2,1)S(1)}, bf16[128,512]{1,0:T(8,128)(2,1)S(1)}, u32[]{:S(2)}, u32[]{:S(2)}) collective-permute-start(bf16[128,512]{1,0:T(8,128)(2,1)S(1)} %get-tuple-element.27), channel_id=1, source_target_pairs={{0,8},{2,10},{4,12},{6,14},{8,16},{10,18},{12,20},{14,22},{16,24},... | collective-permute-start | bytes 393224 | tf_op jit(solution)/shard_map/ppermute | solution.py:495
  308.9 1.7 collective-permute-start.83
  313.4 5.4 %collective-permute-done.82 = bf16[128,512]{1,0:T(8,128)(2,1)S(1)} collective-permute-done((bf16[128,512]{1,0:T(8,128)(2,1)S(1)}, bf16[128,512]{1,0:T(8,128)(2,1)S(1)}, u32[]{:S(2)}, u32[]{:S(2)}) %collective-permute-start.82) | collective-permute-done | bytes 131104 | tf_op jit(solution)/shard_map/ppermute | solution.py:495
  320.2 6.9 %send_home.1 = bf16[1024,512]{1,0:T(8,128)(2,1)} custom-call(s32[9,8]{1,0:T(8,128)S(1)} %copy.43.starts, s32[4]{0:T(128)S(1)} %iota_add_fusion.order, s32[8,2048]{1,0:T(8,128)S(1)} %add_select_fusion.rank_ref, bf16[4,640,512]{2,1,0:T(8,128)(2,1)S(1)} %copy-done, bf16[4,640,512]{2,1,0:T(8,128)(2,1)} %get-tuple-element.19.refs_1_), custom_call_target="tpu_custom_call" | custom-call | flops 1073741824 | bytes 6291456 | tf_op jit(solution)/shard_map/send_home/pallas_call | solution.py:413
  327.8 2.8 maximum_select_fusion.2
  330.6 6.5 %collective-permute-done.84 = bf16[512,512]{1,0:T(8,128)(2,1)} collective-permute-done((bf16[512,512]{1,0:T(8,128)(2,1)}, bf16[512,512]{1,0:T(8,128)(2,1)}, u32[]{:S(2)}, u32[]{:S(2)}) %collective-permute-start.84) | collective-permute-done | bytes 524320 | tf_op jit(solution)/shard_map/ppermute | solution.py:499
  337.1 2.8 maximum_select_fusion.3
  339.9 12.4 %collective-permute-done.65.refs_2_ = bf16[1024,512]{1,0:T(8,128)(2,1)} collective-permute-done((bf16[1024,512]{1,0:T(8,128)(2,1)}, bf16[1024,512]{1,0:T(8,128)(2,1)}, u32[]{:S(2)}, u32[]{:S(2)}) %collective-permute-start.65) | collective-permute-done | bytes 1048608 | tf_op jit(solution)/shard_map/ppermute | solution.py:582
  353.5 7.5 %at_home.1 = (bf16[1024,256]{1,0:T(8,128)(2,1)}, bf16[1024,256]{1,0:T(8,128)(2,1)}) custom-call(s32[9,8]{1,0:T(8,128)S(1)} %copy.43.starts, s32[4]{0:T(128)S(1)} %iota_add_fusion.1.order, s32[8,2048]{1,0:T(8,128)S(1)} %add_select_fusion.rank_ref, bf16[2048,256]{1,0:T(8,128)(2,1)S(1)} %copy-done.6, bf16[1024,256]{1,0:T(8,128)(2,1)S(1)} %copy-done.4, ...), custom_call_target="tpu_custom_call" | custom-call | flops 1073741824 | bytes 7340032 | tf_op jit(solution)/shard_map/at_home/pallas_call | solution.py:439
  361.1 3.0 maximum_select_fusion
  364.0 2.8 maximum_select_fusion.1
  367.9 2.5 slice.48
  370.4 2.3 pad_maximum_fusion
  (295 shorter events, 117.6 us)
Async XLA Ops:
  2.7 48.6 %collective-permute-start.33 = (bf16[64,2048]{1,0:T(8,128)(2,1)}, bf16[64,2048]{1,0:T(8,128)(2,1)}, u32[]{:S(2)}, u32[]{:S(2)}) collective-permute-start(bf16[64,2048]{1,0:T(8,128)(2,1)} %get-tuple-element.37), channel_id=1, source_target_pairs={{0,2},{2,0},{4,6},{6,4},{8,10},{10,8},{12,14},{14,12},{16,18},{18,... | collective-permute-start | bytes 786440 | tf_op jit(solution)/shard_map/ppermute | solution.py:108
  3.1 52.1 %collective-permute-start.35 = (bf16[64,2048]{1,0:T(8,128)(2,1)}, bf16[64,2048]{1,0:T(8,128)(2,1)}, u32[]{:S(2)}, u32[]{:S(2)}) collective-permute-start(bf16[64,2048]{1,0:T(8,128)(2,1)} %get-tuple-element.37), channel_id=1, source_target_pairs={{0,4},{2,6},{8,0},{10,2},{16,8},{18,10},{24,16},{26,18},{28,24},{3... | collective-permute-start | bytes 786440 | tf_op jit(solution)/shard_map/ppermute | solution.py:102
  5.6 47.8 %collective-permute-start.34 = (bf16[64,2048]{1,0:T(8,128)(2,1)}, bf16[64,2048]{1,0:T(8,128)(2,1)}, u32[]{:S(2)}, u32[]{:S(2)}) collective-permute-start(bf16[64,2048]{1,0:T(8,128)(2,1)} %get-tuple-element.36), channel_id=1, source_target_pairs={{0,2},{2,0},{4,6},{6,4},{8,10},{10,8},{12,14},{14,12},{16,18},{18,... | collective-permute-start | bytes 786440 | tf_op jit(solution)/shard_map/ppermute | solution.py:108
  5.9 56.7 %collective-permute-start.37 = (bf16[64,2048]{1,0:T(8,128)(2,1)}, bf16[64,2048]{1,0:T(8,128)(2,1)S(1)}, u32[]{:S(2)}, u32[]{:S(2)}) collective-permute-start(bf16[64,2048]{1,0:T(8,128)(2,1)} %get-tuple-element.36), channel_id=1, source_target_pairs={{0,4},{2,6},{8,0},{10,2},{16,8},{18,10},{24,16},{26,18},{28,24},{3... | collective-permute-start | bytes 786440 | tf_op jit(solution)/shard_map/ppermute | solution.py:102
  7.4 40.3 %collective-permute-start = (s32[2,1024]{1,0:T(2,128)}, s32[2,1024]{1,0:T(2,128)S(1)}, u32[]{:S(2)}, u32[]{:S(2)}) collective-permute-start(s32[2,1024]{1,0:T(2,128)} %bitcast.155), channel_id=1, source_target_pairs={{0,1},{1,0},{2,3},{3,2},{4,5},{5,4},{6,7},{7,6},{8,9},{9,8},{10,11... | collective-permute-start | bytes 24584 | tf_op jit(solution)/shard_map/ppermute | solution.py:61
  47.7 9.8 %collective-permute-start.3 = (bf16[64,2048]{1,0:T(8,128)(2,1)}, bf16[64,2048]{1,0:T(8,128)(2,1)}, u32[]{:S(2)}, u32[]{:S(2)}) collective-permute-start(bf16[64,2048]{1,0:T(8,128)(2,1)} %get-tuple-element.39), channel_id=1, source_target_pairs={{0,2},{2,0},{4,6},{6,4},{8,10},{10,8},{12,14},{14,12},{16,18},{18,... | collective-permute-start | bytes 786440 | tf_op jit(solution)/shard_map/ppermute | solution.py:107
  51.2 10.6 %collective-permute-start.5 = (bf16[64,2048]{1,0:T(8,128)(2,1)}, bf16[64,2048]{1,0:T(8,128)(2,1)S(1)}, u32[]{:S(2)}, u32[]{:S(2)}) collective-permute-start(bf16[64,2048]{1,0:T(8,128)(2,1)} %get-tuple-element.39), channel_id=1, source_target_pairs={{0,8},{2,10},{8,16},{10,18},{16,24},{18,26},{24,28},{26,30},{28,20... | collective-permute-start | bytes 786440 | tf_op jit(solution)/shard_map/ppermute | solution.py:101
  55.3 12.2 %collective-permute-start.7 = (bf16[64,2048]{1,0:T(8,128)(2,1)}, bf16[64,2048]{1,0:T(8,128)(2,1)S(1)}, u32[]{:S(2)}, u32[]{:S(2)}) collective-permute-start(bf16[64,2048]{1,0:T(8,128)(2,1)} %get-tuple-element.38), channel_id=1, source_target_pairs={{0,8},{2,10},{8,16},{10,18},{16,24},{18,26},{24,28},{26,30},{28,20... | collective-permute-start | bytes 786440 | tf_op jit(solution)/shard_map/ppermute | solution.py:101
  57.5 27.1 %collective-permute-start.1 = (bf16[1024,256]{1,0:T(8,128)(2,1)}, bf16[1024,256]{1,0:T(8,128)(2,1)S(1)}, u32[]{:S(2)}, u32[]{:S(2)}) collective-permute-start(bf16[1024,256]{1,0:T(8,128)(2,1)} %param.17), channel_id=1, source_target_pairs={{0,1},{1,0},{2,3},{3,2},{4,5},{5,4},{6,7},{7,6},{8,9},{9,8},{10,11... | collective-permute-start | bytes 1572872 | tf_op jit(solution)/shard_map/ppermute | solution.py:61
  59.5 147.7 %collective-permute-start.2 = (bf16[1024,256]{1,0:T(8,128)(2,1)S(1)}, bf16[1024,256]{1,0:T(8,128)(2,1)S(1)}, u32[]{:S(2)}, u32[]{:S(2)}) collective-permute-start(bf16[1024,256]{1,0:T(8,128)(2,1)S(1)} %copy-done.4), channel_id=1, source_target_pairs={{0,1},{1,0},{2,3},{3,2},{4,5},{5,4},{6,7},{7,6},{8,9},{9,8},{10,11... | collective-permute-start | bytes 1572872 | tf_op jit(solution)/shard_map/ppermute | solution.py:61
  65.2 9.3 %collective-permute-start.39 = (bf16[64,2048]{1,0:T(8,128)(2,1)}, bf16[64,2048]{1,0:T(8,128)(2,1)S(1)}, u32[]{:S(2)}, u32[]{:S(2)}) collective-permute-start(bf16[64,2048]{1,0:T(8,128)(2,1)} %collective-permute-done.35), channel_id=1, source_target_pairs={{0,4},{2,6},{8,0},{10,2},{16,8},{18,10},{24,16},{26,18},{28,24},{3... | collective-permute-start | bytes 786440 | tf_op jit(solution)/shard_map/ppermute | solution.py:102
  67.4 18.6 %collective-permute-start.41 = (bf16[64,2048]{1,0:T(8,128)(2,1)S(1)}, bf16[64,2048]{1,0:T(8,128)(2,1)S(1)}, u32[]{:S(2)}, u32[]{:S(2)}) collective-permute-start(bf16[64,2048]{1,0:T(8,128)(2,1)S(1)} %collective-permute-done.37), channel_id=1, source_target_pairs={{0,4},{2,6},{8,0},{10,2},{16,8},{18,10},{24,16},{26,18},{28,24},{3... | collective-permute-start | bytes 786440 | tf_op jit(solution)/shard_map/ppermute | solution.py:102
  76.9 11.2 %collective-permute-start.11 = (bf16[64,2048]{1,0:T(8,128)(2,1)S(1)}, bf16[64,2048]{1,0:T(8,128)(2,1)S(1)}, u32[]{:S(2)}, u32[]{:S(2)}) collective-permute-start(bf16[64,2048]{1,0:T(8,128)(2,1)S(1)} %collective-permute-done.7), channel_id=1, source_target_pairs={{0,8},{2,10},{8,16},{10,18},{16,24},{18,26},{24,28},{26,30},{28,20... | collective-permute-start | bytes 786440 | tf_op jit(solution)/shard_map/ppermute | solution.py:101
  88.1 14.4 %collective-permute-start.45 = (bf16[64,2048]{1,0:T(8,128)(2,1)S(1)}, bf16[64,2048]{1,0:T(8,128)(2,1)S(1)}, u32[]{:S(2)}, u32[]{:S(2)}) collective-permute-start(bf16[64,2048]{1,0:T(8,128)(2,1)S(1)} %collective-permute-done.41), channel_id=1, source_target_pairs={{0,4},{2,6},{8,0},{10,2},{16,8},{18,10},{24,16},{26,18},{28,24},{3... | collective-permute-start | bytes 786440 | tf_op jit(solution)/shard_map/ppermute | solution.py:102
  93.6 11.9 %collective-permute-start.15 = (bf16[64,2048]{1,0:T(8,128)(2,1)S(1)}, bf16[64,2048]{1,0:T(8,128)(2,1)S(1)}, u32[]{:S(2)}, u32[]{:S(2)}) collective-permute-start(bf16[64,2048]{1,0:T(8,128)(2,1)S(1)} %collective-permute-done.11), channel_id=1, source_target_pairs={{0,8},{2,10},{8,16},{10,18},{16,24},{18,26},{24,28},{26,30},{28,20... | collective-permute-start | bytes 786440 | tf_op jit(solution)/shard_map/ppermute | solution.py:101
  100.3 9.4 %collective-permute-start.47 = (bf16[64,2048]{1,0:T(8,128)(2,1)S(1)}, bf16[64,2048]{1,0:T(8,128)(2,1)S(1)}, u32[]{:S(2)}, u32[]{:S(2)}) collective-permute-start(bf16[64,2048]{1,0:T(8,128)(2,1)S(1)} %collective-permute-done.43), channel_id=1, source_target_pairs={{0,4},{2,6},{8,0},{10,2},{16,8},{18,10},{24,16},{26,18},{28,24},{3... | collective-permute-start | bytes 786440 | tf_op jit(solution)/shard_map/ppermute | solution.py:102
  105.5 14.4 %collective-permute-start.49 = (bf16[64,2048]{1,0:T(8,128)(2,1)S(1)}, bf16[64,2048]{1,0:T(8,128)(2,1)S(1)}, u32[]{:S(2)}, u32[]{:S(2)}) collective-permute-start(bf16[64,2048]{1,0:T(8,128)(2,1)S(1)} %collective-permute-done.45), channel_id=1, source_target_pairs={{0,4},{2,6},{8,0},{10,2},{16,8},{18,10},{24,16},{26,18},{28,24},{3... | collective-permute-start | bytes 786440 | tf_op jit(solution)/shard_map/ppermute | solution.py:102
  109.7 13.2 %collective-permute-start.19 = (bf16[64,2048]{1,0:T(8,128)(2,1)S(1)}, bf16[64,2048]{1,0:T(8,128)(2,1)S(1)}, u32[]{:S(2)}, u32[]{:S(2)}) collective-permute-start(bf16[64,2048]{1,0:T(8,128)(2,1)S(1)} %collective-permute-done.15), channel_id=1, source_target_pairs={{0,8},{2,10},{8,16},{10,18},{16,24},{18,26},{24,28},{26,30},{28,20... | collective-permute-start | bytes 786440 | tf_op jit(solution)/shard_map/ppermute | solution.py:101
  117.6 9.4 %collective-permute-start.51 = (bf16[64,2048]{1,0:T(8,128)(2,1)S(1)}, bf16[64,2048]{1,0:T(8,128)(2,1)S(1)}, u32[]{:S(2)}, u32[]{:S(2)}) collective-permute-start(bf16[64,2048]{1,0:T(8,128)(2,1)S(1)} %collective-permute-done.47), channel_id=1, source_target_pairs={{0,4},{2,6},{8,0},{10,2},{16,8},{18,10},{24,16},{26,18},{28,24},{3... | collective-permute-start | bytes 786440 | tf_op jit(solution)/shard_map/ppermute | solution.py:102
  122.8 13.6 %collective-permute-start.53 = (bf16[64,2048]{1,0:T(8,128)(2,1)S(1)}, bf16[64,2048]{1,0:T(8,128)(2,1)S(1)}, u32[]{:S(2)}, u32[]{:S(2)}) collective-permute-start(bf16[64,2048]{1,0:T(8,128)(2,1)S(1)} %collective-permute-done.49), channel_id=1, source_target_pairs={{0,4},{2,6},{8,0},{10,2},{16,8},{18,10},{24,16},{26,18},{28,24},{3... | collective-permute-start | bytes 786440 | tf_op jit(solution)/shard_map/ppermute | solution.py:102
  127.0 13.2 %collective-permute-start.23 = (bf16[64,2048]{1,0:T(8,128)(2,1)S(1)}, bf16[64,2048]{1,0:T(8,128)(2,1)S(1)}, u32[]{:S(2)}, u32[]{:S(2)}) collective-permute-start(bf16[64,2048]{1,0:T(8,128)(2,1)S(1)} %collective-permute-done.19), channel_id=1, source_target_pairs={{0,8},{2,10},{8,16},{10,18},{16,24},{18,26},{24,28},{26,30},{28,20... | collective-permute-start | bytes 786440 | tf_op jit(solution)/shard_map/ppermute | solution.py:101
  134.9 9.5 %collective-permute-start.55 = (bf16[64,2048]{1,0:T(8,128)(2,1)S(1)}, bf16[64,2048]{1,0:T(8,128)(2,1)S(1)}, u32[]{:S(2)}, u32[]{:S(2)}) collective-permute-start(bf16[64,2048]{1,0:T(8,128)(2,1)S(1)} %collective-permute-done.51), channel_id=1, source_target_pairs={{0,4},{2,6},{8,0},{10,2},{16,8},{18,10},{24,16},{26,18},{28,24},{3... | collective-permute-start | bytes 786440 | tf_op jit(solution)/shard_map/ppermute | solution.py:102
  140.2 12.6 %collective-permute-start.57 = (bf16[64,2048]{1,0:T(8,128)(2,1)S(1)}, bf16[64,2048]{1,0:T(8,128)(2,1)S(1)}, u32[]{:S(2)}, u32[]{:S(2)}) collective-permute-start(bf16[64,2048]{1,0:T(8,128)(2,1)S(1)} %collective-permute-done.53), channel_id=1, source_target_pairs={{0,4},{2,6},{8,0},{10,2},{16,8},{18,10},{24,16},{26,18},{28,24},{3... | collective-permute-start | bytes 786440 | tf_op jit(solution)/shard_map/ppermute | solution.py:102
  144.4 12.4 %collective-permute-start.27 = (bf16[64,2048]{1,0:T(8,128)(2,1)S(1)}, bf16[64,2048]{1,0:T(8,128)(2,1)S(1)}, u32[]{:S(2)}, u32[]{:S(2)}) collective-permute-start(bf16[64,2048]{1,0:T(8,128)(2,1)S(1)} %collective-permute-done.23), channel_id=1, source_target_pairs={{0,8},{2,10},{8,16},{10,18},{16,24},{18,26},{24,28},{26,30},{28,20... | collective-permute-start | bytes 786440 | tf_op jit(solution)/shard_map/ppermute | solution.py:101
  151.5 9.4 %collective-permute-start.59 = (bf16[64,2048]{1,0:T(8,128)(2,1)S(1)}, bf16[64,2048]{1,0:T(8,128)(2,1)S(1)}, u32[]{:S(2)}, u32[]{:S(2)}) collective-permute-start(bf16[64,2048]{1,0:T(8,128)(2,1)S(1)} %collective-permute-done.55), channel_id=1, source_target_pairs={{0,4},{2,6},{8,0},{10,2},{16,8},{18,10},{24,16},{26,18},{28,24},{3... | collective-permute-start | bytes 786440 | tf_op jit(solution)/shard_map/ppermute | solution.py:102
  161.0 12.1 %collective-permute-start.31 = (bf16[64,2048]{1,0:T(8,128)(2,1)S(1)}, bf16[64,2048]{1,0:T(8,128)(2,1)S(1)}, u32[]{:S(2)}, u32[]{:S(2)}) collective-permute-start(bf16[64,2048]{1,0:T(8,128)(2,1)S(1)} %collective-permute-done.27), channel_id=1, source_target_pairs={{0,8},{2,10},{8,16},{10,18},{16,24},{18,26},{24,28},{26,30},{28,20... | collective-permute-start | bytes 786440 | tf_op jit(solution)/shard_map/ppermute | solution.py:101
  164.7 9.9 %collective-permute-start.60 = (bf16[64,2048]{1,0:T(8,128)(2,1)S(1)}, bf16[64,2048]{1,0:T(8,128)(2,1)S(1)}, u32[]{:S(2)}, u32[]{:S(2)}) collective-permute-start(bf16[64,2048]{1,0:T(8,128)(2,1)S(1)} %collective-permute-done.59), channel_id=1, source_target_pairs={{0,2},{2,0},{4,6},{6,4},{8,10},{10,8},{12,14},{14,12},{16,18},{18,... | collective-permute-start | bytes 786440 | tf_op jit(solution)/shard_map/ppermute | solution.py:108
  164.7 12.7 %collective-permute-start.62 = (bf16[64,2048]{1,0:T(8,128)(2,1)S(1)}, bf16[64,2048]{1,0:T(8,128)(2,1)S(1)}, u32[]{:S(2)}, u32[]{:S(2)}) collective-permute-start(bf16[64,2048]{1,0:T(8,128)(2,1)S(1)} %collective-permute-done.61), channel_id=1, source_target_pairs={{0,2},{2,0},{4,6},{6,4},{8,10},{10,8},{12,14},{14,12},{16,18},{18,... | collective-permute-start | bytes 786440 | tf_op jit(solution)/shard_map/ppermute | solution.py:108
  192.0 15.3 %collective-permute-start.63 = (bf16[1024,128]{1,0:T(8,128)(2,1)S(1)}, bf16[1024,128]{1,0:T(8,128)(2,1)S(1)}, u32[]{:S(2)}, u32[]{:S(2)}) collective-permute-start(bf16[1024,128]{1,0:T(8,128)(2,1)S(1)} %attention.2), channel_id=1, source_target_pairs={{0,1},{1,0},{2,3},{3,2},{4,5},{5,4},{6,7},{7,6},{8,9},{9,8},{10,11... | collective-permute-start | bytes 786440 | tf_op jit(solution)/shard_map/ppermute | solution.py:565
  239.9 13.6 %collective-permute-start.66 = (bf16[1024,512]{1,0:T(8,128)(2,1)}, bf16[1024,512]{1,0:T(8,128)(2,1)}, u32[]{:S(2)}, u32[]{:S(2)}) collective-permute-start(bf16[1024,512]{1,0:T(8,128)(2,1)} %constant_dynamic-slice_fusion.9), channel_id=1, source_target_pairs={{0,2},{2,0},{4,6},{6,4},{8,10},{10,8},{12,14},{14,12},{16,18},{18,... | collective-permute-start | bytes 3145736 | tf_op jit(solution)/shard_map/ppermute | solution.py:481
  256.4 15.0 %collective-permute-start.67 = (bf16[512,512]{1,0:T(8,128)(2,1)}, bf16[512,512]{1,0:T(8,128)(2,1)}, u32[]{:S(2)}, u32[]{:S(2)}) collective-permute-start(bf16[512,512]{1,0:T(8,128)(2,1)} %constant_dynamic-slice_fusion.8), channel_id=1, source_target_pairs={{0,4},{2,6},{4,0},{6,2},{8,12},{10,14},{12,8},{14,10},{16,20},{18,... | collective-permute-start | bytes 1572872 | tf_op jit(solution)/shard_map/ppermute | solution.py:481
  260.5 21.8 %collective-permute-start.77 = (bf16[512,512]{1,0:T(8,128)(2,1)}, bf16[512,512]{1,0:T(8,128)(2,1)}, u32[]{:S(2)}, u32[]{:S(2)}) collective-permute-start(bf16[512,512]{1,0:T(8,128)(2,1)} %constant_dynamic-slice_fusion.3), channel_id=1, source_target_pairs={{0,4},{2,6},{4,0},{6,2},{8,12},{10,14},{12,8},{14,10},{16,20},{18,... | collective-permute-start | bytes 1572872 | tf_op jit(solution)/shard_map/ppermute | solution.py:481
  272.8 13.1 %collective-permute-start.68 = (bf16[128,512]{1,0:T(8,128)(2,1)S(1)}, bf16[128,512]{1,0:T(8,128)(2,1)S(1)}, u32[]{:S(2)}, u32[]{:S(2)}) collective-permute-start(bf16[128,512]{1,0:T(8,128)(2,1)S(1)} %get-tuple-element.30), channel_id=1, source_target_pairs={{0,8},{2,10},{4,12},{6,14},{8,16},{10,18},{12,20},{14,22},{16,24},... | collective-permute-start | bytes 393224 | tf_op jit(solution)/shard_map/ppermute | solution.py:489
  274.0 14.3 %collective-permute-start.69 = (bf16[128,512]{1,0:T(8,128)(2,1)S(1)}, bf16[128,512]{1,0:T(8,128)(2,1)S(1)}, u32[]{:S(2)}, u32[]{:S(2)}) collective-permute-start(bf16[128,512]{1,0:T(8,128)(2,1)S(1)} %get-tuple-element.32), channel_id=1, source_target_pairs={{0,16},{2,18},{4,20},{6,22},{8,24},{10,26},{12,28},{14,30},{16,0},... | collective-permute-start | bytes 393224 | tf_op jit(solution)/shard_map/ppermute | solution.py:489
  275.0 13.3 %collective-permute-start.70 = (bf16[128,512]{1,0:T(8,128)(2,1)S(1)}, bf16[128,512]{1,0:T(8,128)(2,1)S(1)}, u32[]{:S(2)}, u32[]{:S(2)}) collective-permute-start(bf16[128,512]{1,0:T(8,128)(2,1)S(1)} %get-tuple-element.31), channel_id=1, source_target_pairs={{0,24},{2,26},{4,28},{6,30},{8,0},{10,2},{12,4},{14,6},{16,8},{18,... | collective-permute-start | bytes 393224 | tf_op jit(solution)/shard_map/ppermute | solution.py:489
  284.9 15.8 %collective-permute-start.79 = (bf16[128,512]{1,0:T(8,128)(2,1)S(1)}, bf16[128,512]{1,0:T(8,128)(2,1)S(1)}, u32[]{:S(2)}, u32[]{:S(2)}) collective-permute-start(bf16[128,512]{1,0:T(8,128)(2,1)S(1)} %get-tuple-element.35), channel_id=1, source_target_pairs={{0,16},{2,18},{4,20},{6,22},{8,24},{10,26},{12,28},{14,30},{16,0},... | collective-permute-start | bytes 393224 | tf_op jit(solution)/shard_map/ppermute | solution.py:489
  285.9 14.8 %collective-permute-start.80 = (bf16[128,512]{1,0:T(8,128)(2,1)S(1)}, bf16[128,512]{1,0:T(8,128)(2,1)S(1)}, u32[]{:S(2)}, u32[]{:S(2)}) collective-permute-start(bf16[128,512]{1,0:T(8,128)(2,1)S(1)} %get-tuple-element.34), channel_id=1, source_target_pairs={{0,24},{2,26},{4,28},{6,30},{8,0},{10,2},{12,4},{14,6},{16,8},{18,... | collective-permute-start | bytes 393224 | tf_op jit(solution)/shard_map/ppermute | solution.py:489
  289.9 19.0 %collective-permute-start.71 = (bf16[128,512]{1,0:T(8,128)(2,1)S(1)}, bf16[128,512]{1,0:T(8,128)(2,1)S(1)}, u32[]{:S(2)}, u32[]{:S(2)}) collective-permute-start(bf16[128,512]{1,0:T(8,128)(2,1)S(1)} %get-tuple-element.25), channel_id=1, source_target_pairs={{0,8},{2,10},{4,12},{6,14},{8,16},{10,18},{12,20},{14,22},{16,24},... | collective-permute-start | bytes 393224 | tf_op jit(solution)/shard_map/ppermute | solution.py:495
  289.9 21.4 %collective-permute-start.72 = (bf16[128,512]{1,0:T(8,128)(2,1)S(1)}, bf16[128,512]{1,0:T(8,128)(2,1)S(1)}, u32[]{:S(2)}, u32[]{:S(2)}) collective-permute-start(bf16[128,512]{1,0:T(8,128)(2,1)S(1)} %get-tuple-element.25), channel_id=1, source_target_pairs={{0,16},{2,18},{4,20},{6,22},{8,24},{10,26},{12,28},{14,30},{16,0},... | collective-permute-start | bytes 393224 | tf_op jit(solution)/shard_map/ppermute | solution.py:495
  292.0 20.0 %collective-permute-start.73 = (bf16[128,512]{1,0:T(8,128)(2,1)S(1)}, bf16[128,512]{1,0:T(8,128)(2,1)S(1)}, u32[]{:S(2)}, u32[]{:S(2)}) collective-permute-start(bf16[128,512]{1,0:T(8,128)(2,1)S(1)} %get-tuple-element.25), channel_id=1, source_target_pairs={{0,24},{2,26},{4,28},{6,30},{8,0},{10,2},{12,4},{14,6},{16,8},{18,... | collective-permute-start | bytes 393224 | tf_op jit(solution)/shard_map/ppermute | solution.py:495
  302.3 10.5 %collective-permute-start.81 = (bf16[128,512]{1,0:T(8,128)(2,1)S(1)}, bf16[128,512]{1,0:T(8,128)(2,1)S(1)}, u32[]{:S(2)}, u32[]{:S(2)}) collective-permute-start(bf16[128,512]{1,0:T(8,128)(2,1)S(1)} %get-tuple-element.27), channel_id=1, source_target_pairs={{0,8},{2,10},{4,12},{6,14},{8,16},{10,18},{12,20},{14,22},{16,24},... | collective-permute-start | bytes 393224 | tf_op jit(solution)/shard_map/ppermute | solution.py:495
  308.3 10.5 %collective-permute-start.82 = (bf16[128,512]{1,0:T(8,128)(2,1)S(1)}, bf16[128,512]{1,0:T(8,128)(2,1)S(1)}, u32[]{:S(2)}, u32[]{:S(2)}) collective-permute-start(bf16[128,512]{1,0:T(8,128)(2,1)S(1)} %get-tuple-element.27), channel_id=1, source_target_pairs={{0,16},{2,18},{4,20},{6,22},{8,24},{10,26},{12,28},{14,30},{16,0},... | collective-permute-start | bytes 393224 | tf_op jit(solution)/shard_map/ppermute | solution.py:495
  308.9 10.6 %collective-permute-start.83 = (bf16[128,512]{1,0:T(8,128)(2,1)S(1)}, bf16[128,512]{1,0:T(8,128)(2,1)S(1)}, u32[]{:S(2)}, u32[]{:S(2)}) collective-permute-start(bf16[128,512]{1,0:T(8,128)(2,1)S(1)} %get-tuple-element.27), channel_id=1, source_target_pairs={{0,24},{2,26},{4,28},{6,30},{8,0},{10,2},{12,4},{14,6},{16,8},{18,... | collective-permute-start | bytes 393224 | tf_op jit(solution)/shard_map/ppermute | solution.py:495
  312.6 15.2 %collective-permute-start.74 = (bf16[512,512]{1,0:T(8,128)(2,1)}, bf16[512,512]{1,0:T(8,128)(2,1)}, u32[]{:S(2)}, u32[]{:S(2)}) collective-permute-start(bf16[512,512]{1,0:T(8,128)(2,1)} %constant_dynamic-update-slice_fusion.4), channel_id=1, source_target_pairs={{0,4},{2,6},{4,0},{6,2},{8,12},{10,14},{12,8},{14,10},{16,20},{18,... | collective-permute-start | bytes 1572872 | tf_op jit(solution)/shard_map/ppermute | solution.py:499
  320.1 17.0 %collective-permute-start.84 = (bf16[512,512]{1,0:T(8,128)(2,1)}, bf16[512,512]{1,0:T(8,128)(2,1)}, u32[]{:S(2)}, u32[]{:S(2)}) collective-permute-start(bf16[512,512]{1,0:T(8,128)(2,1)} %constant_dynamic-update-slice_fusion), channel_id=1, source_target_pairs={{0,4},{2,6},{4,0},{6,2},{8,12},{10,14},{12,8},{14,10},{16,20},{18,... | collective-permute-start | bytes 1572872 | tf_op jit(solution)/shard_map/ppermute | solution.py:499
  327.1 25.2 %collective-permute-start.65 = (bf16[1024,512]{1,0:T(8,128)(2,1)}, bf16[1024,512]{1,0:T(8,128)(2,1)}, u32[]{:S(2)}, u32[]{:S(2)}) collective-permute-start(bf16[1024,512]{1,0:T(8,128)(2,1)} %send_home.1), channel_id=1, source_target_pairs={{0,1},{1,0},{2,3},{3,2},{4,5},{5,4},{6,7},{7,6},{8,9},{9,8},{10,11... | collective-permute-start | bytes 3145736 | tf_op jit(solution)/shard_map/ppermute | solution.py:582
  330.6 30.4 %collective-permute-start.75 = (bf16[1024,512]{1,0:T(8,128)(2,1)}, bf16[1024,512]{1,0:T(8,128)(2,1)}, u32[]{:S(2)}, u32[]{:S(2)}) collective-permute-start(bf16[1024,512]{1,0:T(8,128)(2,1)} %maximum_select_fusion.2), channel_id=1, source_target_pairs={{0,2},{2,0},{4,6},{6,4},{8,10},{10,8},{12,14},{14,12},{16,18},{18,... | collective-permute-start | bytes 3145736 | tf_op jit(solution)/shard_map/ppermute | solution.py:499
  339.9 24.1 %collective-permute-start.85 = (bf16[1024,512]{1,0:T(8,128)(2,1)}, bf16[1024,512]{1,0:T(8,128)(2,1)}, u32[]{:S(2)}, u32[]{:S(2)}) collective-permute-start(bf16[1024,512]{1,0:T(8,128)(2,1)} %maximum_select_fusion.3), channel_id=1, source_target_pairs={{0,2},{2,0},{4,6},{6,4},{8,10},{10,8},{12,14},{14,12},{16,18},{18,... | collective-permute-start | bytes 3145736 | tf_op jit(solution)/shard_map/ppermute | solution.py:499
  (54 other events, 503.0 us)

commit v2 on v1

--- a/solution.py
+++ b/solution.py
@@ -63,56 +63,33 @@
     return out
 
 
-def own_slots_kernel(k_ref, v_ref, kbuf_ref, vbuf_ref, sems):
-    copies = [
-        pltpu.make_async_copy(k_ref, kbuf_ref.at[0], sems.at[0]),
-        pltpu.make_async_copy(v_ref, vbuf_ref.at[0], sems.at[1]),
-    ]
-    for copy in copies:
-        copy.start()
-    for copy in copies:
-        copy.wait()
-
-
-def own_slots(keys, values, slots):
-    shape = jax.ShapeDtypeStruct((slots,) + keys.shape, keys.dtype)
-    return pl.pallas_call(
-        own_slots_kernel,
-        in_specs=[pl.BlockSpec(memory_space=pl.ANY)] * 2,
-        out_specs=[pl.BlockSpec(memory_space=pl.ANY)] * 2,
-        out_shape=[shape, shape],
-        scratch_shapes=[pltpu.SemaphoreType.DMA((2,))],
-        name="own_slots",
-    )(keys, values)
-
-
 def ring_gather(keys, values, seq_count):
     n = seq_count // 2
-    feat, nodes = keys.shape
-    parts = 2 if feat >= 2 * HD else 1
-    rows = feat // parts
-    kbuf, vbuf = own_slots(keys, values, 2 * n)
     fwd, bwd, sib = ring_pairs(seq_count, 1), ring_pairs(seq_count, -1), sibling_pairs(seq_count)
-    held = [(keys[i * rows : (i + 1) * rows], values[i * rows : (i + 1) * rows]) for i in range(parts)]
+    k, v = keys, values
+    own, other = ([], []), ([], [])
     for t in range(n):
-        nxt = []
-        for i, (k, v) in enumerate(held):
-            if t > 0:
-                k = lax.ppermute(k, "seq", fwd)
-                v = lax.ppermute(v, "seq", bwd)
-            nxt.append((k, v))
-            if t > 0:
-                kbuf = lax.dynamic_update_slice(kbuf, k[None], (t, i * rows, 0))
-                vbuf = lax.dynamic_update_slice(vbuf, v[None], (t, i * rows, 0))
-            ks = lax.ppermute(k, "seq", sib)
-            vs = lax.ppermute(v, "seq", sib)
-            kbuf = lax.dynamic_update_slice(kbuf, ks[None], (n + t, i * rows, 0))
-            vbuf = lax.dynamic_update_slice(vbuf, vs[None], (n + t, i * rows, 0))
-        held = nxt
-    return kbuf, vbuf
-
-
-def block_places(block_list, blk_seq, seq_count):
+        if t > 0:
+            k = lax.ppermute(k, "seq", fwd)
+            v = lax.ppermute(v, "seq", bwd)
+        own[0].append(k)
+        own[1].append(v)
+        other[0].append(lax.ppermute(k, "seq", sib))
+        other[1].append(lax.ppermute(v, "seq", sib))
+    return own[0] + other[0], own[1] + other[1]
+
+
+def sorted_entries(slot, slots):
+    count = slot.shape[-1]
+    at = jnp.arange(count, dtype=jnp.int32)
+    before = (slot[:, None, :] < slot[:, :, None]) | ((slot[:, None, :] == slot[:, :, None]) & (at[None, None, :] < at[None, :, None]))
+    rank = jnp.sum(before.astype(jnp.int32), 2)
+    order = jnp.sum(jnp.where(rank[:, None, :] == at[None, :, None], at[None, None, :], 0), 2)
+    begin = jnp.sum((slot[:, None, :] < jnp.arange(slots + 1, dtype=jnp.int32)[None, :, None]).astype(jnp.int32), 2)
+    return order, begin
+
+
+def block_tables(block_list, blk_seq, seq_count, calls):
     order = ring_order(seq_count)
     n = len(order)
     inverse = [0] * n
@@ -122,53 +99,65 @@
     me = lax.axis_index("seq")
     place = inverse[me // 2]
     owner = block_list // blk_seq
-    local = block_list % blk_seq
+    local = (block_list % blk_seq).reshape(calls, -1)
     other = inverse[owner // 2]
     flag = ((owner ^ me) & 1) * n
-    kslot = flag + lax.rem(place - other + n, n)
-    vslot = flag + lax.rem(other - place + n, n)
-    return kslot, vslot, local
-
-
-def attention_kernel(degree, heads, kslot, vslot, local, q_ref, *refs):
-    k_refs, v_refs, out_ref = refs[:degree], refs[degree : 2 * degree], refs[2 * degree]
+    kslot = (flag + lax.rem(place - other + n, n)).reshape(calls, -1)
+    vslot = (flag + lax.rem(other - place + n, n)).reshape(calls, -1)
+    return (local,) + sorted_entries(kslot, 2 * n) + sorted_entries(vslot, 2 * n)
+
+
+def attention_kernel(degree, heads, sources, local, korder, kbegin, vorder, vbegin, q_ref, *refs):
+    k_refs, v_refs = refs[:sources], refs[sources : 2 * sources]
+    out_ref, k_all, v_all, sems = refs[2 * sources :]
+    block_len = k_all.shape[2] // degree
+
+    def fetch(source, dest, order, begin, s, sem):
+        def one(r, carry):
+            e = order[r]
+            at = pl.ds(pl.multiple_of(local[e] * block_len, block_len), block_len)
+            to = pl.ds(pl.multiple_of(lax.rem(e, degree) * block_len, block_len), block_len)
+            pltpu.make_async_copy(source.at[:, at], dest.at[lax.div(e, degree), :, to], sem).start()
+            return carry
+
+        lax.fori_loop(begin[s], begin[s + 1], one, 0)
+
+    for s in range(sources):
+        fetch(k_refs[s], k_all, korder, kbegin, s, sems.at[0])
+    for s in range(sources):
+        fetch(v_refs[s], v_all, vorder, vbegin, s, sems.at[1])
+    pltpu.make_async_copy(k_all, k_all, sems.at[0]).wait()
+    pltpu.make_async_copy(v_all, v_all, sems.at[1]).wait()
     factor = math.log2(math.e) / math.sqrt(HD)
-    cols = []
-    for h in range(heads):
-        rows = slice(h * HD, (h + 1) * HD)
-        q = q_ref[rows, :]
-        k = jnp.concatenate([r[0, rows, :] for r in k_refs], 1)
-        v = jnp.concatenate([r[0, rows, :] for r in v_refs], 1)
-        scores = contract(k, q, 0, 0)
-        top = jnp.max(scores, 0, keepdims=True)
-        probs = jnp.exp2((scores - top) * factor)
-        total = jnp.sum(probs, 0, keepdims=True)
-        out = jnp.dot(v, probs.astype(bf16), preferred_element_type=f32)
-        cols.append(out / total)
-    att = jnp.concatenate(cols, 0)
-    out_ref[...] = att.T.astype(bf16)
-
-
-def attention(queries, kbuf, vbuf, places, first, count, block_len):
-    kslot, vslot, local = places
-    degree = kslot.shape[1]
+
+    def one_block(b, carry):
+        nodes = pl.ds(pl.multiple_of(b * block_len, block_len), block_len)
+        cols = []
+        for h in range(heads):
+            rows = slice(h * HD, (h + 1) * HD)
+            scores = contract(k_all[b, rows, :], q_ref[rows, nodes], 0, 0)
+            top = jnp.max(scores, 0, keepdims=True)
+            probs = jnp.exp2((scores - top) * factor)
+            total = jnp.sum(probs, 0, keepdims=True)
+            out = jnp.dot(v_all[b, rows, :], probs.astype(bf16), preferred_element_type=f32)
+            cols.append(out / total)
+        out_ref[nodes, :] = jnp.concatenate(cols, 0).T.astype(bf16)
+        return carry
+
+    lax.fori_loop(0, k_all.shape[0], one_block, 0)
+
+
+def attention(queries, keys, values, tables, call, count, block_len, degree):
     feat = queries.shape[0]
-
-    def kv_spec(slots_at, j):
-        def index(b, ks, vs, lo):
-            return ((ks, vs)[slots_at][b + first, j], 0, lo[b + first, j])
-
-        return pl.BlockSpec((1, feat, block_len), index)
-
     return pl.pallas_call(
-        functools.partial(attention_kernel, degree, feat // HD),
+        functools.partial(attention_kernel, degree, feat // HD, len(keys)),
         grid_spec=pltpu.PrefetchScalarGridSpec(
-            num_scalar_prefetch=3,
-            grid=(count,),
-            in_specs=[pl.BlockSpec((feat, block_len), lambda b, *_: (0, b + first))]
-            + [kv_spec(0, j) for j in range(degree)]
-            + [kv_spec(1, j) for j in range(degree)],
-            out_specs=pl.BlockSpec((block_len, feat), lambda b, *_: (b, 0)),
+            num_scalar_prefetch=5,
+            grid=(1,),
+            in_specs=[pl.BlockSpec((feat, count * block_len), lambda i, *_: (0, call))]
+            + [pl.BlockSpec(memory_space=pl.ANY)] * (2 * len(keys)),
+            out_specs=pl.BlockSpec((count * block_len, feat), lambda i, *_: (0, 0)),
+            scratch_shapes=[pltpu.VMEM((count, feat, degree * block_len), bf16)] * 2 + [pltpu.SemaphoreType.DMA((2,))],
         ),
         out_shape=jax.ShapeDtypeStruct((count * block_len, feat), bf16),
         compiler_params=params(),
@@ -178,7 +167,7 @@
             transcendentals=count * block_len * degree * block_len * feat // HD,
         ),
         name="attention",
-    )(kslot, vslot, local, queries, *([kbuf] * degree), *([vbuf] * degree))
+    )(*[t[call] for t in tables], queries, *keys, *values)
 
 
 def window_base(starts, i, e):
@@ -531,8 +520,9 @@
     capacity = 2 * tok_dev * topk // expert_total * exp_count
     slot_rows = capacity + WINDOW
 
-    kbuf, vbuf = ring_gather(key_cols, value_cols, seq_count)
-    places = block_places(block_list, blk_seq, seq_count)
+    calls = 2 if blk_seq % 2 == 0 else 1
+    keys, values = ring_gather(key_cols, value_cols, seq_count)
+    tables = block_tables(block_list, blk_seq, seq_count, calls)
 
     residual_all = gather_expert_axis(residual, exp_count)
     cotangent_all = gather_expert_axis(cotangent, exp_count)
@@ -555,11 +545,10 @@
     in_chunk = jnp.arange(chunks_dev, dtype=jnp.int32)
     own_order = me * chunks_dev + in_chunk
 
-    calls = 2 if blk_seq % 2 == 0 else 1
     per_call = blk_seq // calls
     pieces = [[] for _ in range(exp_count)]
     for c in range(calls):
-        part = attention(query_cols, kbuf, vbuf, places, c * per_call, per_call, block_len)
+        part = attention(query_cols, keys, values, tables, c, per_call, block_len, degree)
         pieces[0].append(part)
         for d in range(1, exp_count):
             pieces[d].append(lax.ppermute(part, "expert", shift_pairs(exp_count, d)))

time: 372 us -> 285 us (0.77)
  local copies, waits for them, and re-layouts: 72 us -> 27.4 us
  Pallas kernels: 108 us -> 72.8 us
  starting transfers between devices: 66.3 us -> 49.2 us
    dynamic_update_slice x60 -> x0, local copies, waits for them, and re-layouts: 47 us -> none  [the longest x16 13.4 us: ring_gather(): vbuf = lax.dynamic_update_slice(vbuf, vs[None], (n + t, i * rows, 0))]
    pallas_call x3 -> x2, Pallas kernels: 59 us -> 25 us  [attention(): pl.pallas_call(functools.partial(attention_kernel, degree, feat // HD, le...]
    ppermute x14 -> x7, starting transfers between devices: 19.1 us -> 4.59 us  [ring_gather(): v = lax.ppermute(v, 'seq', bwd)]
    ppermute x14 -> x7, waiting for transfers between devices: 39.1 us -> 47.4 us  [ring_gather(): k = lax.ppermute(k, 'seq', fwd)]
    ppermute x14 -> x7, waiting for transfers between devices: 7.2 us -> 0.79 us  [ring_gather(): v = lax.ppermute(v, 'seq', bwd)]
    ppermute x14 -> x7, starting transfers between devices: 12.5 us -> 10.9 us  [ring_gather(): k = lax.ppermute(k, 'seq', fwd)]
  transfers between devices with their start and end apart: 86 -> 56, of which waited for: 24 -> 16; matrix products, arithmetic and copies ran while one was open for 22% -> 15% of each run, Pallas kernels for 23% -> 18%
where the time goes in v2:
time: 285 us; the launch traced here: 283 us
  waiting for transfers between devices  103 us (36%)
  Pallas kernels  72.8 us (26%)
  starting transfers between devices  49.2 us (17%)
  other arithmetic  29 us (10%)
  local copies, waits for them, and re-layouts  27.4 us (10%)
    ppermute x7, waiting for transfers between devices, ring_gather(): k = lax.ppermute(k, 'seq', fwd)  47.4 us
    pallas_call x2, Pallas kernels, attention(): pl.pallas_call(functools.partial(attention_kernel, degree, feat // HD, le...  25 us
    pallas_call x2, Pallas kernels, experts_step(): pl.pallas_call(functools.partial(expert_kernel, first, width), grid_spec=...  23 us
    ppermute x4, waiting for transfers between devices, halve(): got = lax.ppermute(other, 'seq', pairs)  15.3 us
    ppermute x1, waiting for transfers between devices, shards(): got.append(lax.ppermute(partial, 'expert', shift_pairs(exp_count, d)))  14.1 us
    ppermute x6, starting transfers between devices, sum_over_seq(): got = lax.ppermute(shard, 'seq', line_pairs(seq_count, d))  12.3 us
    select_n x4, other arithmetic, double(): jnp.where(which == 0, jnp.concatenate([a, got], 0), jnp.concatenate([got,...  11.3 us
    ppermute x7, starting transfers between devices, ring_gather(): k = lax.ppermute(k, 'seq', fwd)  10.9 us
  transfers between devices with their start and end apart: 56, of which 16 were waited for; matrix products, arithmetic and copies ran while one was open for 15% of the time, Pallas kernels for 18%

profile of v2, /device:TPU:0, one launch (start us, length us, event | category | flops | bytes accessed | tf_op | source)
XLA Modules:
  0.0 283.0 jit_solution(12766567354502415320)
XLA Ops:
  0.6 3.1 %collective-permute-start.3 = (bf16[128,2048]{1,0:T(8,128)(2,1)}, bf16[128,2048]{1,0:T(8,128)(2,1)S(1)}, u32[]{:S(2)}, u32[]{:S(2)}) collective-permute-start(bf16[128,2048]{1,0:T(8,128)(2,1)} %refs_0_.3), channel_id=1, source_target_pairs={{0,8},{2,10},{8,16},{10,18},{16,24},{18,26},{24,28},{26,30},{28,20... | collective-permute-start | bytes 1572872 | tf_op jit(solution)/shard_map/ppermute | solution.py:73
  3.7 2.0 collective-permute-start
  8.0 7.7 %collective-permute-done.3.refs_1_ = bf16[128,2048]{1,0:T(8,128)(2,1)S(1)} collective-permute-done((bf16[128,2048]{1,0:T(8,128)(2,1)}, bf16[128,2048]{1,0:T(8,128)(2,1)S(1)}, u32[]{:S(2)}, u32[]{:S(2)}) %collective-permute-start.3) | collective-permute-done | bytes 524320 | tf_op jit(solution)/shard_map/ppermute | solution.py:73
  15.8 1.8 collective-permute-start.4
  19.2 9.8 %collective-permute-done.4.refs_2_ = bf16[128,2048]{1,0:T(8,128)(2,1)S(1)} collective-permute-done((bf16[128,2048]{1,0:T(8,128)(2,1)S(1)}, bf16[128,2048]{1,0:T(8,128)(2,1)S(1)}, u32[]{:S(2)}, u32[]{:S(2)}) %collective-permute-start.4) | collective-permute-done | bytes 524320 | tf_op jit(solution)/shard_map/ppermute | solution.py:73
  29.0 1.5 collective-permute-start.5
  32.2 9.0 %collective-permute-done.5.refs_3_ = bf16[128,2048]{1,0:T(8,128)(2,1)S(1)} collective-permute-done((bf16[128,2048]{1,0:T(8,128)(2,1)S(1)}, bf16[128,2048]{1,0:T(8,128)(2,1)S(1)}, u32[]{:S(2)}, u32[]{:S(2)}) %collective-permute-start.5) | collective-permute-done | bytes 524320 | tf_op jit(solution)/shard_map/ppermute | solution.py:73
  46.0 1.5 constant_dynamic-update-slice_fusion.9
  48.3 4.9 %collective-permute-done.6.refs_4_ = bf16[128,2048]{1,0:T(8,128)(2,1)} collective-permute-done((bf16[128,2048]{1,0:T(8,128)(2,1)S(1)}, bf16[128,2048]{1,0:T(8,128)(2,1)}, u32[]{:S(2)}, u32[]{:S(2)}) %collective-permute-start.6) | collective-permute-done | bytes 524320 | tf_op jit(solution)/shard_map/ppermute | solution.py:73
  56.3 8.9 %collective-permute-done.7.refs_5_ = bf16[128,2048]{1,0:T(8,128)(2,1)} collective-permute-done((bf16[128,2048]{1,0:T(8,128)(2,1)}, bf16[128,2048]{1,0:T(8,128)(2,1)}, u32[]{:S(2)}, u32[]{:S(2)}) %collective-permute-start.7) | collective-permute-done | bytes 524320 | tf_op jit(solution)/shard_map/ppermute | solution.py:73
  68.2 4.2 %reduce-window.6 = s32[8,16,128]{2,1,0:T(8,128)S(1)} reduce-window(s32[8,16,128]{2,1,0:T(8,128)} %copy.44, s32[]{:T(128)} %constant.138.clone.1), window={size=1x1x128 pad=0_0x0_0x127_0}, to_apply=%region_1.2 | reduce-window | flops 2080768 | bytes 131076 | tf_op jit(solution)/shard_map/reduce-window
  73.1 2.3 collective-permute-done.8.refs_6_
  82.8 4.8 %collective-permute-done.9.refs_7_ = bf16[128,2048]{1,0:T(8,128)(2,1)} collective-permute-done((bf16[128,2048]{1,0:T(8,128)(2,1)}, bf16[128,2048]{1,0:T(8,128)(2,1)}, u32[]{:S(2)}, u32[]{:S(2)}) %collective-permute-start.9) | collective-permute-done | bytes 524320 | tf_op jit(solution)/shard_map/ppermute | solution.py:73
  89.3 1.9 constant_dynamic-update-slice_fusion.10.res_ref
  92.6 12.5 %attention.3 = bf16[1024,128]{1,0:T(8,128)(2,1)S(1)} custom-call(s32[32]{0:T(128)S(1)} %squeeze.42.local, s32[32]{0:T(128)S(1)} %get-tuple-element.48.korder, s32[17]{0:T(128)S(1)} %get-tuple-element.53.kbegin, s32[32]{0:T(128)S(1)} %get-tuple-element.46.vorder, s32[17]{0:T(128)S(1)} %get-tuple-element.21.vbegin, bf16[128,2048]{1,0:T(8,128)(2,1)S(1)} %copy-done.1, ...), custom_call_target="tpu_custom_call" | custom-call | flops 268435456 | bytes 2621440 | tf_op jit(solution)/shard_map/attention/pallas_call | solution.py:152
  105.1 1.6 collective-permute-start.34
  106.7 12.5 %attention.2 = bf16[1024,128]{1,0:T(8,128)(2,1)S(1)} custom-call(s32[32]{0:T(128)S(1)} %squeeze.36.local, s32[32]{0:T(128)S(1)} %get-tuple-element.47.korder, s32[17]{0:T(128)S(1)} %get-tuple-element.54.kbegin, s32[32]{0:T(128)S(1)} %get-tuple-element.45.vorder, s32[17]{0:T(128)S(1)} %get-tuple-element.20.vbegin, bf16[128,2048]{1,0:T(8,128)(2,1)S(1)} %copy-done.1, ...), custom_call_target="tpu_custom_call" | custom-call | flops 268435456 | bytes 2621440 | tf_op jit(solution)/shard_map/attention/pallas_call | solution.py:152
  119.9 7.8 %collective-permute-done.33 = bf16[1024,128]{1,0:T(8,128)(2,1)S(1)} collective-permute-done((bf16[1024,128]{1,0:T(8,128)(2,1)S(1)}, bf16[1024,128]{1,0:T(8,128)(2,1)S(1)}, u32[]{:S(2)}, u32[]{:S(2)}) %collective-permute-start.33) | collective-permute-done | bytes 262176 | tf_op jit(solution)/shard_map/ppermute | solution.py:554
  127.8 10.4 %dispatch.1 = (bf16[2048,256]{1,0:T(8,128)(2,1)S(1)}, bf16[8,640,512]{2,1,0:T(8,128)(2,1)}) custom-call(s32[9,8]{1,0:T(8,128)S(1)} %copy.52.starts, s32[8,2048]{1,0:T(8,128)S(1)} %add_select_fusion.rank_ref, bf16[2048,256]{1,0:T(8,128)(2,1)S(1)} %copy-done.8, bf16[2048,256]{1,0:T(8,128)(2,1)S(1)} %constant_dynamic-update-slice_fusion.8.cot_ref, ...), custom_call_target="tpu_custom_call" | custom-call | flops 4294967296 | bytes 9437184 | tf_op jit(solution)/shard_map/dispatch/pallas_call | solution.py:238
  139.2 11.9 %experts.3 = (bf16[4,640,512]{2,1,0:T(8,128)(2,1)}, bf16[4,512,512]{2,1,0:T(8,128)(2,1)S(1)}) custom-call(s32[8]{0:T(128)S(1)} %slice_reduce_fusion.5.counts, s32[8]{0:T(128)S(1)} %iota_add_fusion.2.ids, bf16[8,640,512]{2,1,0:T(8,128)(2,1)} %get-tuple-element.13.slots_ref, bf16[8,256,512]{2,1,0:T(8,128)(2,1)S(1)} %copy-done.12, ...), custom_call_target="tpu_custom_call" | custom-call | flops 4026531840 | bytes 9437184 | tf_op jit(solution)/shard_map/experts/pallas_call | solution.py:327
  151.2 1.3 copy-done.3
  152.5 11.1 %experts.2 = (bf16[4,640,512]{2,1,0:T(8,128)(2,1)}, bf16[4,512,512]{2,1,0:T(8,128)(2,1)S(1)}) custom-call(s32[8]{0:T(128)S(1)} %slice_reduce_fusion.5.counts, s32[8]{0:T(128)S(1)} %iota_add_fusion.2.ids, bf16[8,640,512]{2,1,0:T(8,128)(2,1)} %get-tuple-element.13.slots_ref, bf16[8,256,512]{2,1,0:T(8,128)(2,1)S(1)} %copy-done.12, ...), custom_call_target="tpu_custom_call" | custom-call | flops 4026531840 | bytes 9437184 | tf_op jit(solution)/shard_map/experts/pallas_call | solution.py:327
  165.2 1.8 add_convert_fusion
  168.7 1.5 add_convert_fusion.1
  170.2 1.4 collective-permute-start.37
  171.6 11.4 %collective-permute-done.47 = bf16[512,512]{1,0:T(8,128)(2,1)} collective-permute-done((bf16[512,512]{1,0:T(8,128)(2,1)}, bf16[512,512]{1,0:T(8,128)(2,1)}, u32[]{:S(2)}, u32[]{:S(2)}) %collective-permute-start.47) | collective-permute-done | bytes 524320 | tf_op jit(solution)/shard_map/ppermute | solution.py:470
  183.1 1.3 add_convert_fusion.2
  184.5 4.3 %collective-permute-start.50 = (bf16[128,512]{1,0:T(8,128)(2,1)S(1)}, bf16[128,512]{1,0:T(8,128)(2,1)S(1)}, u32[]{:S(2)}, u32[]{:S(2)}) collective-permute-start(bf16[128,512]{1,0:T(8,128)(2,1)S(1)} %get-tuple-element.36), channel_id=1, source_target_pairs={{0,24},{2,26},{4,28},{6,30},{8,0},{10,2},{12,4},{14,6},{16,8},{18,... | collective-permute-start | bytes 393224 | tf_op jit(solution)/shard_map/ppermute | solution.py:478
  189.4 3.8 %collective-permute-done.37 = bf16[512,512]{1,0:T(8,128)(2,1)S(1)} collective-permute-done((bf16[512,512]{1,0:T(8,128)(2,1)S(1)}, bf16[512,512]{1,0:T(8,128)(2,1)S(1)}, u32[]{:S(2)}, u32[]{:S(2)}) %collective-permute-start.37) | collective-permute-done | bytes 524320 | tf_op jit(solution)/shard_map/ppermute | solution.py:470
  193.4 4.3 %collective-permute-start.40 = (bf16[128,512]{1,0:T(8,128)(2,1)S(1)}, bf16[128,512]{1,0:T(8,128)(2,1)S(1)}, u32[]{:S(2)}, u32[]{:S(2)}) collective-permute-start(bf16[128,512]{1,0:T(8,128)(2,1)S(1)} %get-tuple-element.33), channel_id=1, source_target_pairs={{0,24},{2,26},{4,28},{6,30},{8,0},{10,2},{12,4},{14,6},{16,8},{18,... | collective-permute-start | bytes 393224 | tf_op jit(solution)/shard_map/ppermute | solution.py:478
  198.4 3.5 %collective-permute-done.49 = bf16[128,512]{1,0:T(8,128)(2,1)S(1)} collective-permute-done((bf16[128,512]{1,0:T(8,128)(2,1)S(1)}, bf16[128,512]{1,0:T(8,128)(2,1)S(1)}, u32[]{:S(2)}, u32[]{:S(2)}) %collective-permute-start.49) | collective-permute-done | bytes 131104 | tf_op jit(solution)/shard_map/ppermute | solution.py:478
  203.4 2.7 collective-permute-start.51
  206.1 2.4 collective-permute-start.52
  208.6 2.9 %collective-permute-start.53 = (bf16[128,512]{1,0:T(8,128)(2,1)S(1)}, bf16[128,512]{1,0:T(8,128)(2,1)S(1)}, u32[]{:S(2)}, u32[]{:S(2)}) collective-permute-start(bf16[128,512]{1,0:T(8,128)(2,1)S(1)} %get-tuple-element.29), channel_id=1, source_target_pairs={{0,24},{2,26},{4,28},{6,30},{8,0},{10,2},{12,4},{14,6},{16,8},{18,... | collective-permute-start | bytes 393224 | tf_op jit(solution)/shard_map/ppermute | solution.py:484
  211.5 5.8 %collective-permute-done.39 = bf16[128,512]{1,0:T(8,128)(2,1)S(1)} collective-permute-done((bf16[128,512]{1,0:T(8,128)(2,1)S(1)}, bf16[128,512]{1,0:T(8,128)(2,1)S(1)}, u32[]{:S(2)}, u32[]{:S(2)}) %collective-permute-start.39) | collective-permute-done | bytes 131104 | tf_op jit(solution)/shard_map/ppermute | solution.py:478
  218.8 1.4 collective-permute-start.42
  220.2 2.9 %collective-permute-start.43 = (bf16[128,512]{1,0:T(8,128)(2,1)S(1)}, bf16[128,512]{1,0:T(8,128)(2,1)S(1)}, u32[]{:S(2)}, u32[]{:S(2)}) collective-permute-start(bf16[128,512]{1,0:T(8,128)(2,1)S(1)} %get-tuple-element.27), channel_id=1, source_target_pairs={{0,24},{2,26},{4,28},{6,30},{8,0},{10,2},{12,4},{14,6},{16,8},{18,... | collective-permute-start | bytes 393224 | tf_op jit(solution)/shard_map/ppermute | solution.py:484
  226.5 4.8 %collective-permute-done.42 = bf16[128,512]{1,0:T(8,128)(2,1)S(1)} collective-permute-done((bf16[128,512]{1,0:T(8,128)(2,1)S(1)}, bf16[128,512]{1,0:T(8,128)(2,1)S(1)}, u32[]{:S(2)}, u32[]{:S(2)}) %collective-permute-start.42) | collective-permute-done | bytes 131104 | tf_op jit(solution)/shard_map/ppermute | solution.py:484
  232.6 6.9 %send_home.1 = bf16[1024,512]{1,0:T(8,128)(2,1)} custom-call(s32[9,8]{1,0:T(8,128)S(1)} %copy.52.starts, s32[4]{0:T(128)S(1)} %iota_add_fusion.order, s32[8,2048]{1,0:T(8,128)S(1)} %add_select_fusion.rank_ref, bf16[4,640,512]{2,1,0:T(8,128)(2,1)S(1)} %copy-done, bf16[4,640,512]{2,1,0:T(8,128)(2,1)} %get-tuple-element.15.refs_1_), custom_call_target="tpu_custom_call" | custom-call | flops 1073741824 | bytes 6291456 | tf_op jit(solution)/shard_map/send_home/pallas_call | solution.py:402
  239.5 2.9 %maximum_select_fusion.3 = bf16[1024,512]{1,0:T(8,128)(2,1)} fusion(bf16[512,512]{1,0:T(8,128)(2,1)} %collective-permute-done.54, bf16[512,512]{1,0:T(8,128)(2,1)} %constant_dynamic-update-slice_fusion, pred[]{:T(512)S(6)} %eq.87), kind=kLoop, calls=%fused_computation.10 | loop fusion | flops 4718592 | bytes 2097153 | tf_op jit(solution)/shard_map/jit(_where)/select_n | solution.py:489
  242.4 3.5 %collective-permute-done.44 = bf16[512,512]{1,0:T(8,128)(2,1)} collective-permute-done((bf16[512,512]{1,0:T(8,128)(2,1)}, bf16[512,512]{1,0:T(8,128)(2,1)}, u32[]{:S(2)}, u32[]{:S(2)}) %collective-permute-start.44) | collective-permute-done | bytes 524320 | tf_op jit(solution)/shard_map/ppermute | solution.py:488
  245.9 2.8 maximum_select_fusion.2
  248.6 14.1 %collective-permute-done.35.refs_2_ = bf16[1024,512]{1,0:T(8,128)(2,1)} collective-permute-done((bf16[1024,512]{1,0:T(8,128)(2,1)}, bf16[1024,512]{1,0:T(8,128)(2,1)}, u32[]{:S(2)}, u32[]{:S(2)}) %collective-permute-start.35) | collective-permute-done | bytes 1048608 | tf_op jit(solution)/shard_map/ppermute | solution.py:571
  264.0 7.5 %at_home.1 = (bf16[1024,256]{1,0:T(8,128)(2,1)}, bf16[1024,256]{1,0:T(8,128)(2,1)}) custom-call(s32[9,8]{1,0:T(8,128)S(1)} %copy.52.starts, s32[4]{0:T(128)S(1)} %iota_add_fusion.1.order, s32[8,2048]{1,0:T(8,128)S(1)} %add_select_fusion.rank_ref, bf16[2048,256]{1,0:T(8,128)(2,1)S(1)} %copy-done.6, bf16[1024,256]{1,0:T(8,128)(2,1)S(1)} %copy-done.4, ...), custom_call_target="tpu_custom_call" | custom-call | flops 1073741824 | bytes 7340032 | tf_op jit(solution)/shard_map/at_home/pallas_call | solution.py:428
  271.6 2.8 maximum_select_fusion.1
  274.3 2.8 %maximum_select_fusion = bf16[2048,512]{1,0:T(8,128)(2,1)S(1)} fusion(bf16[1024,512]{1,0:T(8,128)(2,1)} %collective-permute-done.45, bf16[1024,512]{1,0:T(8,128)(2,1)} %maximum_select_fusion.2, pred[]{:T(512)S(6)} %eq.86), kind=kLoop, calls=%fused_computation.3 | loop fusion | flops 9437184 | bytes 4194305 | tf_op jit(solution)/shard_map/jit(_where)/select_n | solution.py:489
  278.2 2.5 slice.80
  280.7 2.3 pad_maximum_fusion
  (213 shorter events, 44.8 us)
Async XLA Ops:
  0.6 15.1 %collective-permute-start.3 = (bf16[128,2048]{1,0:T(8,128)(2,1)}, bf16[128,2048]{1,0:T(8,128)(2,1)S(1)}, u32[]{:S(2)}, u32[]{:S(2)}) collective-permute-start(bf16[128,2048]{1,0:T(8,128)(2,1)} %refs_0_.3), channel_id=1, source_target_pairs={{0,8},{2,10},{8,16},{10,18},{16,24},{18,26},{24,28},{26,30},{28,20... | collective-permute-start | bytes 1572872 | tf_op jit(solution)/shard_map/ppermute | solution.py:73
  3.7 13.9 %collective-permute-start.18 = (bf16[128,2048]{1,0:T(8,128)(2,1)}, bf16[128,2048]{1,0:T(8,128)(2,1)S(1)}, u32[]{:S(2)}, u32[]{:S(2)}) collective-permute-start(bf16[128,2048]{1,0:T(8,128)(2,1)} %refs_16_.3), channel_id=1, source_target_pairs={{0,4},{2,6},{8,0},{10,2},{16,8},{18,10},{24,16},{26,18},{28,24},{3... | collective-permute-start | bytes 1572872 | tf_op jit(solution)/shard_map/ppermute | solution.py:74
  3.7 43.9 %collective-permute-start.10 = (bf16[128,2048]{1,0:T(8,128)(2,1)}, bf16[128,2048]{1,0:T(8,128)(2,1)S(1)}, u32[]{:S(2)}, u32[]{:S(2)}) collective-permute-start(bf16[128,2048]{1,0:T(8,128)(2,1)} %refs_0_.3), channel_id=1, source_target_pairs={{0,2},{2,0},{4,6},{6,4},{8,10},{10,8},{12,14},{14,12},{16,18},{18,... | collective-permute-start | bytes 1572872 | tf_op jit(solution)/shard_map/ppermute | solution.py:77
  3.7 27.9 %collective-permute-start = (s32[2,1024]{1,0:T(2,128)}, s32[2,1024]{1,0:T(2,128)S(1)}, u32[]{:S(2)}, u32[]{:S(2)}) collective-permute-start(s32[2,1024]{1,0:T(2,128)} %bitcast.43), channel_id=1, source_target_pairs={{0,1},{1,0},{2,3},{3,2},{4,5},{5,4},{6,7},{7,6},{8,9},{9,8},{10,11... | collective-permute-start | bytes 24584 | tf_op jit(solution)/shard_map/ppermute | solution.py:61
  5.7 26.0 %collective-permute-start.1 = (bf16[1024,256]{1,0:T(8,128)(2,1)}, bf16[1024,256]{1,0:T(8,128)(2,1)}, u32[]{:S(2)}, u32[]{:S(2)}) collective-permute-start(bf16[1024,256]{1,0:T(8,128)(2,1)} %param.17), channel_id=1, source_target_pairs={{0,1},{1,0},{2,3},{3,2},{4,5},{5,4},{6,7},{7,6},{8,9},{9,8},{10,11... | collective-permute-start | bytes 1572872 | tf_op jit(solution)/shard_map/ppermute | solution.py:61
  15.8 13.2 %collective-permute-start.4 = (bf16[128,2048]{1,0:T(8,128)(2,1)S(1)}, bf16[128,2048]{1,0:T(8,128)(2,1)S(1)}, u32[]{:S(2)}, u32[]{:S(2)}) collective-permute-start(bf16[128,2048]{1,0:T(8,128)(2,1)S(1)} %collective-permute-done.3.refs_1_), channel_id=1, source_target_pairs={{0,8},{2,10},{8,16},{10,18},{16,24},{18,26},{24,28},{26,30},{28,20... | collective-permute-start | bytes 1572872 | tf_op jit(solution)/shard_map/ppermute | solution.py:73
  17.6 12.9 %collective-permute-start.19 = (bf16[128,2048]{1,0:T(8,128)(2,1)S(1)}, bf16[128,2048]{1,0:T(8,128)(2,1)S(1)}, u32[]{:S(2)}, u32[]{:S(2)}) collective-permute-start(bf16[128,2048]{1,0:T(8,128)(2,1)S(1)} %collective-permute-done.18.refs_17_), channel_id=1, source_target_pairs={{0,4},{2,6},{8,0},{10,2},{16,8},{18,10},{24,16},{26,18},{28,24},{3... | collective-permute-start | bytes 1572872 | tf_op jit(solution)/shard_map/ppermute | solution.py:74
  29.0 12.3 %collective-permute-start.5 = (bf16[128,2048]{1,0:T(8,128)(2,1)S(1)}, bf16[128,2048]{1,0:T(8,128)(2,1)S(1)}, u32[]{:S(2)}, u32[]{:S(2)}) collective-permute-start(bf16[128,2048]{1,0:T(8,128)(2,1)S(1)} %collective-permute-done.4.refs_2_), channel_id=1, source_target_pairs={{0,8},{2,10},{8,16},{10,18},{16,24},{18,26},{24,28},{26,30},{28,20... | collective-permute-start | bytes 1572872 | tf_op jit(solution)/shard_map/ppermute | solution.py:73
  30.5 12.0 %collective-permute-start.20 = (bf16[128,2048]{1,0:T(8,128)(2,1)S(1)}, bf16[128,2048]{1,0:T(8,128)(2,1)}, u32[]{:S(2)}, u32[]{:S(2)}) collective-permute-start(bf16[128,2048]{1,0:T(8,128)(2,1)S(1)} %collective-permute-done.19.refs_18_), channel_id=1, source_target_pairs={{0,4},{2,6},{8,0},{10,2},{16,8},{18,10},{24,16},{26,18},{28,24},{3... | collective-permute-start | bytes 1572872 | tf_op jit(solution)/shard_map/ppermute | solution.py:74
  31.7 16.0 %collective-permute-start.25 = (bf16[128,2048]{1,0:T(8,128)(2,1)}, bf16[128,2048]{1,0:T(8,128)(2,1)}, u32[]{:S(2)}, u32[]{:S(2)}) collective-permute-start(bf16[128,2048]{1,0:T(8,128)(2,1)} %refs_16_.3), channel_id=1, source_target_pairs={{0,2},{2,0},{4,6},{6,4},{8,10},{10,8},{12,14},{14,12},{16,18},{18,... | collective-permute-start | bytes 1572872 | tf_op jit(solution)/shard_map/ppermute | solution.py:78
  31.7 16.4 %collective-permute-start.11 = (bf16[128,2048]{1,0:T(8,128)(2,1)S(1)}, bf16[128,2048]{1,0:T(8,128)(2,1)}, u32[]{:S(2)}, u32[]{:S(2)}) collective-permute-start(bf16[128,2048]{1,0:T(8,128)(2,1)S(1)} %collective-permute-done.3.refs_1_), channel_id=1, source_target_pairs={{0,2},{2,0},{4,6},{6,4},{8,10},{10,8},{12,14},{14,12},{16,18},{18,... | collective-permute-start | bytes 1572872 | tf_op jit(solution)/shard_map/ppermute | solution.py:77
  41.3 11.9 %collective-permute-start.6 = (bf16[128,2048]{1,0:T(8,128)(2,1)S(1)}, bf16[128,2048]{1,0:T(8,128)(2,1)}, u32[]{:S(2)}, u32[]{:S(2)}) collective-permute-start(bf16[128,2048]{1,0:T(8,128)(2,1)S(1)} %collective-permute-done.5.refs_3_), channel_id=1, source_target_pairs={{0,8},{2,10},{8,16},{10,18},{16,24},{18,26},{24,28},{26,30},{28,20... | collective-permute-start | bytes 1572872 | tf_op jit(solution)/shard_map/ppermute | solution.py:73
  42.5 11.9 %collective-permute-start.21 = (bf16[128,2048]{1,0:T(8,128)(2,1)}, bf16[128,2048]{1,0:T(8,128)(2,1)}, u32[]{:S(2)}, u32[]{:S(2)}) collective-permute-start(bf16[128,2048]{1,0:T(8,128)(2,1)} %collective-permute-done.20.refs_19_), channel_id=1, source_target_pairs={{0,4},{2,6},{8,0},{10,2},{16,8},{18,10},{24,16},{26,18},{28,24},{3... | collective-permute-start | bytes 1572872 | tf_op jit(solution)/shard_map/ppermute | solution.py:74
  53.2 12.1 %collective-permute-start.7 = (bf16[128,2048]{1,0:T(8,128)(2,1)}, bf16[128,2048]{1,0:T(8,128)(2,1)}, u32[]{:S(2)}, u32[]{:S(2)}) collective-permute-start(bf16[128,2048]{1,0:T(8,128)(2,1)} %collective-permute-done.6.refs_4_), channel_id=1, source_target_pairs={{0,8},{2,10},{8,16},{10,18},{16,24},{18,26},{24,28},{26,30},{28,20... | collective-permute-start | bytes 1572872 | tf_op jit(solution)/shard_map/ppermute | solution.py:73
  54.4 12.1 %collective-permute-start.22 = (bf16[128,2048]{1,0:T(8,128)(2,1)}, bf16[128,2048]{1,0:T(8,128)(2,1)}, u32[]{:S(2)}, u32[]{:S(2)}) collective-permute-start(bf16[128,2048]{1,0:T(8,128)(2,1)} %collective-permute-done.21.refs_20_), channel_id=1, source_target_pairs={{0,4},{2,6},{8,0},{10,2},{16,8},{18,10},{24,16},{26,18},{28,24},{3... | collective-permute-start | bytes 1572872 | tf_op jit(solution)/shard_map/ppermute | solution.py:74
  55.6 16.8 %collective-permute-start.13 = (bf16[128,2048]{1,0:T(8,128)(2,1)S(1)}, bf16[128,2048]{1,0:T(8,128)(2,1)}, u32[]{:S(2)}, u32[]{:S(2)}) collective-permute-start(bf16[128,2048]{1,0:T(8,128)(2,1)S(1)} %collective-permute-done.5.refs_3_), channel_id=1, source_target_pairs={{0,2},{2,0},{4,6},{6,4},{8,10},{10,8},{12,14},{14,12},{16,18},{18,... | collective-permute-start | bytes 1572872 | tf_op jit(solution)/shard_map/ppermute | solution.py:77
  55.7 16.8 %collective-permute-start.28 = (bf16[128,2048]{1,0:T(8,128)(2,1)}, bf16[128,2048]{1,0:T(8,128)(2,1)}, u32[]{:S(2)}, u32[]{:S(2)}) collective-permute-start(bf16[128,2048]{1,0:T(8,128)(2,1)} %collective-permute-done.20.refs_19_), channel_id=1, source_target_pairs={{0,2},{2,0},{4,6},{6,4},{8,10},{10,8},{12,14},{14,12},{16,18},{18,... | collective-permute-start | bytes 1572872 | tf_op jit(solution)/shard_map/ppermute | solution.py:78
  56.2 16.8 %collective-permute-start.14 = (bf16[128,2048]{1,0:T(8,128)(2,1)}, bf16[128,2048]{1,0:T(8,128)(2,1)}, u32[]{:S(2)}, u32[]{:S(2)}) collective-permute-start(bf16[128,2048]{1,0:T(8,128)(2,1)} %collective-permute-done.6.refs_4_), channel_id=1, source_target_pairs={{0,2},{2,0},{4,6},{6,4},{8,10},{10,8},{12,14},{14,12},{16,18},{18,... | collective-permute-start | bytes 1572872 | tf_op jit(solution)/shard_map/ppermute | solution.py:77
  65.2 10.1 %collective-permute-start.8 = (bf16[128,2048]{1,0:T(8,128)(2,1)}, bf16[128,2048]{1,0:T(8,128)(2,1)}, u32[]{:S(2)}, u32[]{:S(2)}) collective-permute-start(bf16[128,2048]{1,0:T(8,128)(2,1)} %collective-permute-done.7.refs_5_), channel_id=1, source_target_pairs={{0,8},{2,10},{8,16},{10,18},{16,24},{18,26},{24,28},{26,30},{28,20... | collective-permute-start | bytes 1572872 | tf_op jit(solution)/shard_map/ppermute | solution.py:73
  66.4 9.8 %collective-permute-start.23 = (bf16[128,2048]{1,0:T(8,128)(2,1)}, bf16[128,2048]{1,0:T(8,128)(2,1)}, u32[]{:S(2)}, u32[]{:S(2)}) collective-permute-start(bf16[128,2048]{1,0:T(8,128)(2,1)} %collective-permute-done.22.refs_21_), channel_id=1, source_target_pairs={{0,4},{2,6},{8,0},{10,2},{16,8},{18,10},{24,16},{26,18},{28,24},{3... | collective-permute-start | bytes 1572872 | tf_op jit(solution)/shard_map/ppermute | solution.py:74
  72.4 9.0 %collective-permute-start.29 = (bf16[128,2048]{1,0:T(8,128)(2,1)}, bf16[128,2048]{1,0:T(8,128)(2,1)}, u32[]{:S(2)}, u32[]{:S(2)}) collective-permute-start(bf16[128,2048]{1,0:T(8,128)(2,1)} %collective-permute-done.21.refs_20_), channel_id=1, source_target_pairs={{0,2},{2,0},{4,6},{6,4},{8,10},{10,8},{12,14},{14,12},{16,18},{18,... | collective-permute-start | bytes 1572872 | tf_op jit(solution)/shard_map/ppermute | solution.py:78
  72.5 9.8 %collective-permute-start.15 = (bf16[128,2048]{1,0:T(8,128)(2,1)}, bf16[128,2048]{1,0:T(8,128)(2,1)}, u32[]{:S(2)}, u32[]{:S(2)}) collective-permute-start(bf16[128,2048]{1,0:T(8,128)(2,1)} %collective-permute-done.7.refs_5_), channel_id=1, source_target_pairs={{0,2},{2,0},{4,6},{6,4},{8,10},{10,8},{12,14},{14,12},{16,18},{18,... | collective-permute-start | bytes 1572872 | tf_op jit(solution)/shard_map/ppermute | solution.py:77
  73.0 9.3 %collective-permute-start.30 = (bf16[128,2048]{1,0:T(8,128)(2,1)}, bf16[128,2048]{1,0:T(8,128)(2,1)}, u32[]{:S(2)}, u32[]{:S(2)}) collective-permute-start(bf16[128,2048]{1,0:T(8,128)(2,1)} %collective-permute-done.22.refs_21_), channel_id=1, source_target_pairs={{0,2},{2,0},{4,6},{6,4},{8,10},{10,8},{12,14},{14,12},{16,18},{18,... | collective-permute-start | bytes 1572872 | tf_op jit(solution)/shard_map/ppermute | solution.py:78
  75.3 12.3 %collective-permute-start.9 = (bf16[128,2048]{1,0:T(8,128)(2,1)}, bf16[128,2048]{1,0:T(8,128)(2,1)}, u32[]{:S(2)}, u32[]{:S(2)}) collective-permute-start(bf16[128,2048]{1,0:T(8,128)(2,1)} %collective-permute-done.8.refs_6_), channel_id=1, source_target_pairs={{0,8},{2,10},{8,16},{10,18},{16,24},{18,26},{24,28},{26,30},{28,20... | collective-permute-start | bytes 1572872 | tf_op jit(solution)/shard_map/ppermute | solution.py:73
  76.3 12.1 %collective-permute-start.24 = (bf16[128,2048]{1,0:T(8,128)(2,1)}, bf16[128,2048]{1,0:T(8,128)(2,1)}, u32[]{:S(2)}, u32[]{:S(2)}) collective-permute-start(bf16[128,2048]{1,0:T(8,128)(2,1)} %collective-permute-done.23.refs_22_), channel_id=1, source_target_pairs={{0,4},{2,6},{8,0},{10,2},{16,8},{18,10},{24,16},{26,18},{28,24},{3... | collective-permute-start | bytes 1572872 | tf_op jit(solution)/shard_map/ppermute | solution.py:74
  81.4 38.4 %collective-permute-start.2 = (bf16[1024,256]{1,0:T(8,128)(2,1)}, bf16[1024,256]{1,0:T(8,128)(2,1)S(1)}, u32[]{:S(2)}, u32[]{:S(2)}) collective-permute-start(bf16[1024,256]{1,0:T(8,128)(2,1)} %cot_ref.1), channel_id=1, source_target_pairs={{0,1},{1,0},{2,3},{3,2},{4,5},{5,4},{6,7},{7,6},{8,9},{9,8},{10,11... | collective-permute-start | bytes 1572872 | tf_op jit(solution)/shard_map/ppermute | solution.py:61
  82.3 8.9 %collective-permute-start.16 = (bf16[128,2048]{1,0:T(8,128)(2,1)}, bf16[128,2048]{1,0:T(8,128)(2,1)S(1)}, u32[]{:S(2)}, u32[]{:S(2)}) collective-permute-start(bf16[128,2048]{1,0:T(8,128)(2,1)} %collective-permute-done.8.refs_6_), channel_id=1, source_target_pairs={{0,2},{2,0},{4,6},{6,4},{8,10},{10,8},{12,14},{14,12},{16,18},{18,... | collective-permute-start | bytes 1572872 | tf_op jit(solution)/shard_map/ppermute | solution.py:77
  82.3 8.9 %collective-permute-start.31 = (bf16[128,2048]{1,0:T(8,128)(2,1)}, bf16[128,2048]{1,0:T(8,128)(2,1)S(1)}, u32[]{:S(2)}, u32[]{:S(2)}) collective-permute-start(bf16[128,2048]{1,0:T(8,128)(2,1)} %collective-permute-done.23.refs_22_), channel_id=1, source_target_pairs={{0,2},{2,0},{4,6},{6,4},{8,10},{10,8},{12,14},{14,12},{16,18},{18,... | collective-permute-start | bytes 1572872 | tf_op jit(solution)/shard_map/ppermute | solution.py:78
  105.1 14.8 %collective-permute-start.34 = (bf16[1024,128]{1,0:T(8,128)(2,1)S(1)}, bf16[1024,128]{1,0:T(8,128)(2,1)S(1)}, u32[]{:S(2)}, u32[]{:S(2)}) collective-permute-start(bf16[1024,128]{1,0:T(8,128)(2,1)S(1)} %attention.3), channel_id=1, source_target_pairs={{0,1},{1,0},{2,3},{3,2},{4,5},{5,4},{6,7},{7,6},{8,9},{9,8},{10,11... | collective-permute-start | bytes 786440 | tf_op jit(solution)/shard_map/ppermute | solution.py:554
  152.5 12.7 %collective-permute-start.46 = (bf16[1024,512]{1,0:T(8,128)(2,1)S(1)}, bf16[1024,512]{1,0:T(8,128)(2,1)}, u32[]{:S(2)}, u32[]{:S(2)}) collective-permute-start(bf16[1024,512]{1,0:T(8,128)(2,1)S(1)} %constant_dynamic-slice_fusion.4), channel_id=1, source_target_pairs={{0,2},{2,0},{4,6},{6,4},{8,10},{10,8},{12,14},{14,12},{16,18},{18,... | collective-permute-start | bytes 3145736 | tf_op jit(solution)/shard_map/ppermute | solution.py:470
  168.0 15.1 %collective-permute-start.47 = (bf16[512,512]{1,0:T(8,128)(2,1)}, bf16[512,512]{1,0:T(8,128)(2,1)}, u32[]{:S(2)}, u32[]{:S(2)}) collective-permute-start(bf16[512,512]{1,0:T(8,128)(2,1)} %constant_dynamic-slice_fusion.3), channel_id=1, source_target_pairs={{0,4},{2,6},{4,0},{6,2},{8,12},{10,14},{12,8},{14,10},{16,20},{18,... | collective-permute-start | bytes 1572872 | tf_op jit(solution)/shard_map/ppermute | solution.py:470
  170.2 23.0 %collective-permute-start.37 = (bf16[512,512]{1,0:T(8,128)(2,1)S(1)}, bf16[512,512]{1,0:T(8,128)(2,1)S(1)}, u32[]{:S(2)}, u32[]{:S(2)}) collective-permute-start(bf16[512,512]{1,0:T(8,128)(2,1)S(1)} %constant_dynamic-slice_fusion.8), channel_id=1, source_target_pairs={{0,4},{2,6},{4,0},{6,2},{8,12},{10,14},{12,8},{14,10},{16,20},{18,... | collective-permute-start | bytes 1572872 | tf_op jit(solution)/shard_map/ppermute | solution.py:470
  184.5 13.2 %collective-permute-start.50 = (bf16[128,512]{1,0:T(8,128)(2,1)S(1)}, bf16[128,512]{1,0:T(8,128)(2,1)S(1)}, u32[]{:S(2)}, u32[]{:S(2)}) collective-permute-start(bf16[128,512]{1,0:T(8,128)(2,1)S(1)} %get-tuple-element.36), channel_id=1, source_target_pairs={{0,24},{2,26},{4,28},{6,30},{8,0},{10,2},{12,4},{14,6},{16,8},{18,... | collective-permute-start | bytes 393224 | tf_op jit(solution)/shard_map/ppermute | solution.py:478
  188.7 13.2 %collective-permute-start.49 = (bf16[128,512]{1,0:T(8,128)(2,1)S(1)}, bf16[128,512]{1,0:T(8,128)(2,1)S(1)}, u32[]{:S(2)}, u32[]{:S(2)}) collective-permute-start(bf16[128,512]{1,0:T(8,128)(2,1)S(1)} %get-tuple-element.37), channel_id=1, source_target_pairs={{0,16},{2,18},{4,20},{6,22},{8,24},{10,26},{12,28},{14,30},{16,0},... | collective-permute-start | bytes 393224 | tf_op jit(solution)/shard_map/ppermute | solution.py:478
  188.7 13.2 %collective-permute-start.48 = (bf16[128,512]{1,0:T(8,128)(2,1)S(1)}, bf16[128,512]{1,0:T(8,128)(2,1)S(1)}, u32[]{:S(2)}, u32[]{:S(2)}) collective-permute-start(bf16[128,512]{1,0:T(8,128)(2,1)S(1)} %get-tuple-element.35), channel_id=1, source_target_pairs={{0,8},{2,10},{4,12},{6,14},{8,16},{10,18},{12,20},{14,22},{16,24},... | collective-permute-start | bytes 393224 | tf_op jit(solution)/shard_map/ppermute | solution.py:478
  193.4 15.1 %collective-permute-start.40 = (bf16[128,512]{1,0:T(8,128)(2,1)S(1)}, bf16[128,512]{1,0:T(8,128)(2,1)S(1)}, u32[]{:S(2)}, u32[]{:S(2)}) collective-permute-start(bf16[128,512]{1,0:T(8,128)(2,1)S(1)} %get-tuple-element.33), channel_id=1, source_target_pairs={{0,24},{2,26},{4,28},{6,30},{8,0},{10,2},{12,4},{14,6},{16,8},{18,... | collective-permute-start | bytes 393224 | tf_op jit(solution)/shard_map/ppermute | solution.py:478
  197.7 19.6 %collective-permute-start.39 = (bf16[128,512]{1,0:T(8,128)(2,1)S(1)}, bf16[128,512]{1,0:T(8,128)(2,1)S(1)}, u32[]{:S(2)}, u32[]{:S(2)}) collective-permute-start(bf16[128,512]{1,0:T(8,128)(2,1)S(1)} %get-tuple-element.34), channel_id=1, source_target_pairs={{0,16},{2,18},{4,20},{6,22},{8,24},{10,26},{12,28},{14,30},{16,0},... | collective-permute-start | bytes 393224 | tf_op jit(solution)/shard_map/ppermute | solution.py:478
  197.7 19.6 %collective-permute-start.38 = (bf16[128,512]{1,0:T(8,128)(2,1)S(1)}, bf16[128,512]{1,0:T(8,128)(2,1)S(1)}, u32[]{:S(2)}, u32[]{:S(2)}) collective-permute-start(bf16[128,512]{1,0:T(8,128)(2,1)S(1)} %get-tuple-element.32), channel_id=1, source_target_pairs={{0,8},{2,10},{4,12},{6,14},{8,16},{10,18},{12,20},{14,22},{16,24},... | collective-permute-start | bytes 393224 | tf_op jit(solution)/shard_map/ppermute | solution.py:478
  203.4 16.8 %collective-permute-start.51 = (bf16[128,512]{1,0:T(8,128)(2,1)S(1)}, bf16[128,512]{1,0:T(8,128)(2,1)S(1)}, u32[]{:S(2)}, u32[]{:S(2)}) collective-permute-start(bf16[128,512]{1,0:T(8,128)(2,1)S(1)} %get-tuple-element.29), channel_id=1, source_target_pairs={{0,8},{2,10},{4,12},{6,14},{8,16},{10,18},{12,20},{14,22},{16,24},... | collective-permute-start | bytes 393224 | tf_op jit(solution)/shard_map/ppermute | solution.py:484
  206.1 17.7 %collective-permute-start.52 = (bf16[128,512]{1,0:T(8,128)(2,1)S(1)}, bf16[128,512]{1,0:T(8,128)(2,1)S(1)}, u32[]{:S(2)}, u32[]{:S(2)}) collective-permute-start(bf16[128,512]{1,0:T(8,128)(2,1)S(1)} %get-tuple-element.29), channel_id=1, source_target_pairs={{0,16},{2,18},{4,20},{6,22},{8,24},{10,26},{12,28},{14,30},{16,0},... | collective-permute-start | bytes 393224 | tf_op jit(solution)/shard_map/ppermute | solution.py:484
  208.6 15.9 %collective-permute-start.53 = (bf16[128,512]{1,0:T(8,128)(2,1)S(1)}, bf16[128,512]{1,0:T(8,128)(2,1)S(1)}, u32[]{:S(2)}, u32[]{:S(2)}) collective-permute-start(bf16[128,512]{1,0:T(8,128)(2,1)S(1)} %get-tuple-element.29), channel_id=1, source_target_pairs={{0,24},{2,26},{4,28},{6,30},{8,0},{10,2},{12,4},{14,6},{16,8},{18,... | collective-permute-start | bytes 393224 | tf_op jit(solution)/shard_map/ppermute | solution.py:484
  218.8 12.4 %collective-permute-start.42 = (bf16[128,512]{1,0:T(8,128)(2,1)S(1)}, bf16[128,512]{1,0:T(8,128)(2,1)S(1)}, u32[]{:S(2)}, u32[]{:S(2)}) collective-permute-start(bf16[128,512]{1,0:T(8,128)(2,1)S(1)} %get-tuple-element.27), channel_id=1, source_target_pairs={{0,16},{2,18},{4,20},{6,22},{8,24},{10,26},{12,28},{14,30},{16,0},... | collective-permute-start | bytes 393224 | tf_op jit(solution)/shard_map/ppermute | solution.py:484
  220.2 11.7 %collective-permute-start.43 = (bf16[128,512]{1,0:T(8,128)(2,1)S(1)}, bf16[128,512]{1,0:T(8,128)(2,1)S(1)}, u32[]{:S(2)}, u32[]{:S(2)}) collective-permute-start(bf16[128,512]{1,0:T(8,128)(2,1)S(1)} %get-tuple-element.27), channel_id=1, source_target_pairs={{0,24},{2,26},{4,28},{6,30},{8,0},{10,2},{12,4},{14,6},{16,8},{18,... | collective-permute-start | bytes 393224 | tf_op jit(solution)/shard_map/ppermute | solution.py:484
  225.1 14.3 %collective-permute-start.54 = (bf16[512,512]{1,0:T(8,128)(2,1)}, bf16[512,512]{1,0:T(8,128)(2,1)}, u32[]{:S(2)}, u32[]{:S(2)}) collective-permute-start(bf16[512,512]{1,0:T(8,128)(2,1)} %constant_dynamic-update-slice_fusion), channel_id=1, source_target_pairs={{0,4},{2,6},{4,0},{6,2},{8,12},{10,14},{12,8},{14,10},{16,20},{18,... | collective-permute-start | bytes 1572872 | tf_op jit(solution)/shard_map/ppermute | solution.py:488
  232.6 13.3 %collective-permute-start.44 = (bf16[512,512]{1,0:T(8,128)(2,1)}, bf16[512,512]{1,0:T(8,128)(2,1)}, u32[]{:S(2)}, u32[]{:S(2)}) collective-permute-start(bf16[512,512]{1,0:T(8,128)(2,1)} %constant_dynamic-update-slice_fusion.4), channel_id=1, source_target_pairs={{0,4},{2,6},{4,0},{6,2},{8,12},{10,14},{12,8},{14,10},{16,20},{18,... | collective-permute-start | bytes 1572872 | tf_op jit(solution)/shard_map/ppermute | solution.py:488
  239.5 23.3 %collective-permute-start.35 = (bf16[1024,512]{1,0:T(8,128)(2,1)}, bf16[1024,512]{1,0:T(8,128)(2,1)}, u32[]{:S(2)}, u32[]{:S(2)}) collective-permute-start(bf16[1024,512]{1,0:T(8,128)(2,1)} %send_home.1), channel_id=1, source_target_pairs={{0,1},{1,0},{2,3},{3,2},{4,5},{5,4},{6,7},{7,6},{8,9},{9,8},{10,11... | collective-permute-start | bytes 3145736 | tf_op jit(solution)/shard_map/ppermute | solution.py:571
  242.4 29.2 %collective-permute-start.55 = (bf16[1024,512]{1,0:T(8,128)(2,1)}, bf16[1024,512]{1,0:T(8,128)(2,1)}, u32[]{:S(2)}, u32[]{:S(2)}) collective-permute-start(bf16[1024,512]{1,0:T(8,128)(2,1)} %maximum_select_fusion.3), channel_id=1, source_target_pairs={{0,2},{2,0},{4,6},{6,4},{8,10},{10,8},{12,14},{14,12},{16,18},{18,... | collective-permute-start | bytes 3145736 | tf_op jit(solution)/shard_map/ppermute | solution.py:488
  248.6 25.7 %collective-permute-start.45 = (bf16[1024,512]{1,0:T(8,128)(2,1)}, bf16[1024,512]{1,0:T(8,128)(2,1)}, u32[]{:S(2)}, u32[]{:S(2)}) collective-permute-start(bf16[1024,512]{1,0:T(8,128)(2,1)} %maximum_select_fusion.2), channel_id=1, source_target_pairs={{0,2},{2,0},{4,6},{6,4},{8,10},{10,8},{12,14},{14,12},{16,18},{18,... | collective-permute-start | bytes 3145736 | tf_op jit(solution)/shard_map/ppermute | solution.py:488
  (38 other events, 430.6 us)

commit v3 on v2

v3 whole, which is shorter than its diff:
```python
import functools
import math

import jax
import jax.numpy as jnp
from jax import lax
from jax.experimental import pallas as pl
from jax.experimental.pallas import tpu as pltpu
from jax.sharding import PartitionSpec as P

HD = 32
WINDOW = 128
TILE = 256
EAGER = 32

norm_eps = 1e-05
root_two_pi = 0.7978845608028654
cubic_term = 0.044715

bf16 = jnp.bfloat16
f32 = jnp.float32
VMEM_BYTES = 48 * 1024 * 1024


def params(**kw):
    return pltpu.CompilerParams(vmem_limit_bytes=VMEM_BYTES, **kw)


def contract(a, b, da, db):
    return lax.dot_general(a, b, (((da,), (db,)), ((), ())), preferred_element_type=f32)


def ring_order(seq_count):
    rows = max(1, seq_count // 4)
    if seq_count % 4:
        return list(range(seq_count // 2))
    return [2 * z for z in range(rows)] + [2 * z + 1 for z in reversed(range(rows))]


def ring_pairs(seq_count, step):
    order = ring_order(seq_count)
    n = len(order)
    return [(2 * order[i] + c, 2 * order[(i + step) % n] + c) for i in range(n) for c in range(2)]


def sibling_pairs(seq_count):
    return [(s, s ^ 1) for s in range(seq_count)]


def shift_pairs(count, d):
    return [(i, (i + d) % count) for i in range(count)]


def gather_expert_axis(x, exp_count, axis=0):
    me = lax.axis_index("expert")
    size = x.shape[axis]
    shape = list(x.shape)
    shape[axis] = size * exp_count
    out = jnp.zeros(shape, x.dtype)
    out = lax.dynamic_update_slice_in_dim(out, x, me * size, axis)
    for d in range(1, exp_count):
        got = lax.ppermute(x, "expert", shift_pairs(exp_count, d))
        out = lax.dynamic_update_slice_in_dim(out, got, lax.rem(me + exp_count - d, exp_count) * size, axis)
    return out


def ring_gather(keys, values, seq_count):
    n = seq_count // 2
    fwd, bwd, sib = ring_pairs(seq_count, 1), ring_pairs(seq_count, -1), sibling_pairs(seq_count)
    k, v = keys, values
    own, other = ([], []), ([], [])
    for t in range(n):
        if t > 0:
            k = lax.ppermute(k, "seq", fwd)
            v = lax.ppermute(v, "seq", bwd)
        own[0].append(k)
        own[1].append(v)
        other[0].append(lax.ppermute(k, "seq", sib))
        other[1].append(lax.ppermute(v, "seq", sib))
    return own[0] + other[0], own[1] + other[1]


def sorted_entries(slot, slots):
    count = slot.shape[-1]
    at = jnp.arange(count, dtype=jnp.int32)
    before = (slot[:, None, :] < slot[:, :, None]) | ((slot[:, None, :] == slot[:, :, None]) & (at[None, None, :] < at[None, :, None]))
    rank = jnp.sum(before.astype(jnp.int32), 2)
    order = jnp.sum(jnp.where(rank[:, None, :] == at[None, :, None], at[None, None, :], 0), 2)
    begin = jnp.sum((slot[:, None, :] < jnp.arange(slots + 1, dtype=jnp.int32)[None, :, None]).astype(jnp.int32), 2)
    return order, begin


def block_tables(block_list, blk_seq, seq_count, calls):
    order = ring_order(seq_count)
    n = len(order)
    inverse = [0] * n
    for i, chip in enumerate(order):
        inverse[chip] = i
    inverse = jnp.asarray(inverse, jnp.int32)
    me = lax.axis_index("seq")
    place = inverse[me // 2]
    owner = block_list // blk_seq
    local = (block_list % blk_seq).reshape(calls, -1)
    other = inverse[owner // 2]
    flag = ((owner ^ me) & 1) * n
    kslot = (flag + lax.rem(place - other + n, n)).reshape(calls, -1)
    vslot = (flag + lax.rem(other - place + n, n)).reshape(calls, -1)
    return (local,) + sorted_entries(kslot, 2 * n) + sorted_entries(vslot, 2 * n)


def attention_kernel(degree, heads, sources, local, korder, kbegin, vorder, vbegin, q_ref, *refs):
    k_refs, v_refs = refs[:sources], refs[sources : 2 * sources]
    out_ref, k_all, v_all, sems = refs[2 * sources :]
    block_len = k_all.shape[2] // degree

    def fetch(source, dest, order, begin, s, sem):
        def one(r, carry):
            e = order[r]
            at = pl.ds(pl.multiple_of(local[e] * block_len, block_len), block_len)
            to = pl.ds(pl.multiple_of(lax.rem(e, degree) * block_len, block_len), block_len)
            pltpu.make_async_copy(source.at[:, at], dest.at[lax.div(e, degree), :, to], sem).start()
            return carry

        lax.fori_loop(begin[s], begin[s + 1], one, 0)

    for s in range(sources):
        fetch(k_refs[s], k_all, korder, kbegin, s, sems.at[0])
    for s in range(sources):
        fetch(v_refs[s], v_all, vorder, vbegin, s, sems.at[1])
    pltpu.make_async_copy(k_all, k_all, sems.at[0]).wait()
    pltpu.make_async_copy(v_all, v_all, sems.at[1]).wait()
    factor = math.log2(math.e) / math.sqrt(HD)

    feat = heads * HD
    head_row = lax.broadcasted_iota(jnp.int32, (feat, heads * block_len), 0) // HD
    head_col = lax.broadcasted_iota(jnp.int32, (feat, heads * block_len), 1) // block_len
    diagonal = head_row == head_col

    def one_block(b, carry):
        nodes = pl.ds(pl.multiple_of(b * block_len, block_len), block_len)
        q = jnp.concatenate([q_ref[:, nodes]] * heads, 1)
        scores = contract(k_all[b], jnp.where(diagonal, q, jnp.zeros_like(q)), 0, 0)
        top = jnp.max(scores, 0, keepdims=True)
        probs = jnp.exp2((scores - top) * factor)
        total = jnp.sum(probs, 0, keepdims=True)
        probs = probs.astype(bf16)
        cols = []
        for h in range(heads):
            rows, own = slice(h * HD, (h + 1) * HD), slice(h * block_len, (h + 1) * block_len)
            cols.append(jnp.dot(v_all[b, rows, :], probs[:, own], preferred_element_type=f32) / total[:, own])
        out_ref[nodes, :] = jnp.concatenate(cols, 0).T.astype(bf16)
        return carry

    count = k_all.shape[0]
    lax.fori_loop(0, count, one_block, 0, unroll=4 if count % 4 == 0 else 1)


def attention(queries, keys, values, tables, call, count, block_len, degree):
    feat = queries.shape[0]
    return pl.pallas_call(
        functools.partial(attention_kernel, degree, feat // HD, len(keys)),
        grid_spec=pltpu.PrefetchScalarGridSpec(
            num_scalar_prefetch=5,
            grid=(1,),
            in_specs=[pl.BlockSpec((feat, count * block_len), lambda i, *_: (0, call))]
            + [pl.BlockSpec(memory_space=pl.ANY)] * (2 * len(keys)),
            out_specs=pl.BlockSpec((count * block_len, feat), lambda i, *_: (0, 0)),
            scratch_shapes=[pltpu.VMEM((count, feat, degree * block_len), bf16)] * 2 + [pltpu.SemaphoreType.DMA((2,))],
        ),
        out_shape=jax.ShapeDtypeStruct((count * block_len, feat), bf16),
        compiler_params=params(),
        cost_estimate=pl.CostEstimate(
            flops=4 * count * block_len * degree * block_len * feat,
            bytes_accessed=2 * count * feat * block_len * (2 * degree + 2),
            transcendentals=count * block_len * degree * block_len * feat // HD,
        ),
        name="attention",
    )(*[t[call] for t in tables], queries, *keys, *values)


def window_base(starts, i, e):
    return pl.multiple_of((starts[i, e] // 16) * 16, 16)


def further_windows(starts, i, e):
    left = starts[i + 1, e] - window_base(starts, i, e)
    return jnp.maximum((left + WINDOW - 1) // WINDOW, 1)


def any_further(starts, i, first, count):
    most = further_windows(starts, i, first)
    for e in range(first + 1, first + count):
        most = jnp.maximum(most, further_windows(starts, i, e))
    return most > 1


def one_hot(rank_row, base):
    place = lax.broadcasted_iota(jnp.int32, (WINDOW, rank_row.shape[1]), 0)
    return jnp.where(place == rank_row - base, 1.0, 0.0).astype(bf16)


def stack_hot(starts, rank, i, first, count):
    return jnp.concatenate([one_hot(rank[e : e + 1, :], window_base(starts, i, e)) for e in range(first, first + count)], 0)


def group_kernel(first, count, pieces, chunk, lines, owners, counts, ids, perm, starts, order, line, *refs):
    refs = list(refs)
    rank_ref, cot_ref, gain_ref, router_ref, win_ref, wout_ref, rcol_ref = [refs.pop(0) for _ in range(7)]
    if pieces:
        res_ref = refs.pop(0)
        atts = [refs.pop(0) for _ in range(pieces)]
        projs = [refs.pop(0) for _ in range(pieces)]
        stream_ref = None
    else:
        stream_ref = refs.pop(0)
        partial_refs = [refs.pop(0) for _ in range(owners)]
        refs.pop(0)
    if pieces:
        out_stream = refs.pop(0)
    out_refs = [refs.pop(0) for _ in range(owners)]
    grad_refs, (rows_ref, slots, acc_in, acc_out) = refs[:-4], refs[-4:]
    nodes, width = cot_ref.shape
    step = pl.program_id(0)

    @pl.when(step == 0)
    def _():
        slots[...] = jnp.zeros_like(slots)

        def place(i, carry):
            at = pl.ds(pl.multiple_of(i * chunk, chunk), chunk)
            if pieces:
                projected = jnp.dot(atts[0][at, :], projs[0][...], preferred_element_type=f32)
                for a, w in zip(atts[1:], projs[1:]):
                    projected = projected + jnp.dot(a[at, :], w[...], preferred_element_type=f32)
                stream = (res_ref[at, :].astype(f32) + projected).astype(bf16)
                out_stream[at, :] = stream
            else:
                stream = stream_ref[at, :]
            wide = stream.astype(f32)
            inverse_rms = lax.rsqrt(jnp.mean(wide * wide, -1, keepdims=True) + norm_eps)
            rows_ref[:, :width] = (wide * inverse_rms * gain_ref[...]).astype(bf16)
            rows_ref[:, width:] = cot_ref[at, :]
            rank = rank_ref[:, at]
            packed = jnp.dot(stack_hot(starts, rank, i, first, count), rows_ref[...], preferred_element_type=f32).astype(bf16)
            for e in range(count):
                to = pl.ds(window_base(starts, i, first + e), WINDOW)
                slots[e, to, :] = slots[e, to, :] + packed[e * WINDOW : (e + 1) * WINDOW]

            @pl.when(any_further(starts, i, first, count))
            def _():
                for e in range(count):

                    def more(w, carry, e=e):
                        base = pl.multiple_of(window_base(starts, i, first + e) + w * WINDOW, 16)
                        hot = one_hot(rank[first + e : first + e + 1, :], base)
                        got = jnp.dot(hot, rows_ref[...], preferred_element_type=f32)
                        to = pl.ds(base, WINDOW)
                        slots[e, to, :] = slots[e, to, :] + got.astype(bf16)
                        return carry

                    lax.fori_loop(1, further_windows(starts, i, first + e), more, 0)

            return carry

        lax.fori_loop(0, nodes // chunk, place, 0)

    e = step + first
    tiles = (counts[e] + TILE - 1) // TILE
    acc_in[...] = jnp.zeros_like(acc_in)
    acc_out[...] = jnp.zeros_like(acc_out)
    w_in = win_ref[0]
    w_out = wout_ref[0]
    mine = lax.broadcasted_iota(jnp.int32, (TILE, router_ref.shape[1]), 1) == ids[e]
    column = rcol_ref[0]

    def one(t, carry):
        at = pl.ds(pl.multiple_of(t * TILE, TILE), TILE)
        x = slots[step, at, :width]
        cot = slots[step, at, width:]
        cot_wide = cot.astype(f32)
        logits = jnp.dot(x, router_ref[...], preferred_element_type=f32)
        logit = jnp.sum(jnp.where(mine, logits, 0.0), 1, keepdims=True)
        gate = 1.0 / (1.0 + jnp.exp(-logit))
        scaled = (gate * cot_wide).astype(bf16)
        a = jnp.dot(x, w_in, preferred_element_type=f32)
        grad_hidden = contract(scaled, w_out, 1, 1)
        a2 = a * a
        t1 = jnp.tanh(a * (root_two_pi + (root_two_pi * cubic_term) * a2))
        half = 0.5 + 0.5 * t1
        hidden = (a * half).astype(bf16)
        slope = half + (a * (1.0 - t1 * t1)) * (0.5 * root_two_pi + (1.5 * root_two_pi * cubic_term) * a2)
        grad_pre = (grad_hidden * slope).astype(bf16)
        acc_out[...] += contract(hidden, scaled, 0, 0)
        acc_in[...] += contract(x, grad_pre, 0, 0)
        produced = jnp.dot(hidden, w_out, preferred_element_type=f32).astype(bf16).astype(f32)
        grad_rows = contract(grad_pre, w_in, 1, 1).astype(bf16).astype(f32)
        grad_logit = jnp.sum(cot_wide * produced, 1, keepdims=True) * gate * (1.0 - gate)
        slots[step, at, :width] = (gate * produced).astype(bf16)
        slots[step, at, width:] = (grad_rows + grad_logit * column).astype(bf16)
        return carry

    lax.fori_loop(0, tiles, one, 0)

    ff = acc_in.shape[1]
    part = 2 * width // lines

    def write(grad_ref):
        for p in range(lines):
            where = lax.rem(p - line[0] + lines, lines)
            at = pl.ds(pl.multiple_of(where * part, part), part)
            low = p * part
            if low < width:
                grad_ref[0, at, :] = acc_in[low : low + part, :].astype(bf16)
            else:
                low = low - width
                for j in range(ff // width):
                    cols = slice(j * width, (j + 1) * width)
                    grad_ref[0, at, cols] = acc_out[j * width + low : j * width + low + part, :].astype(bf16)

    each = count // len(grad_refs)
    for k, grad_ref in enumerate(grad_refs):
        pl.when((step >= k * each) & (step < (k + 1) * each))(functools.partial(write, grad_ref))

    @pl.when(step == count - 1)
    def _():
        chunks = nodes // chunk // owners

        for d in range(owners):

            def gather(c, carry, d=d):
                i = order[d] * chunks + c
                rank = rank_ref[:, pl.ds(pl.multiple_of(i * chunk, chunk), chunk)]
                windows = [slots[e, pl.ds(window_base(starts, i, first + e), WINDOW), :] for e in range(count)]
                total = contract(stack_hot(starts, rank, i, first, count), jnp.concatenate(windows, 0), 0, 0)

                def further(total):
                    for e in range(count):

                        def more(w, acc, e=e):
                            base = pl.multiple_of(window_base(starts, i, first + e) + w * WINDOW, 16)
                            hot = one_hot(rank[first + e : first + e + 1, :], base)
                            return acc + contract(hot, slots[e, pl.ds(base, WINDOW), :], 0, 0)

                        total = lax.fori_loop(1, further_windows(starts, i, first + e), more, total)
                    return total

                total = lax.cond(any_further(starts, i, first, count), further, lambda total: total, total)
                at = pl.ds(pl.multiple_of(c * chunk, chunk), chunk)
                if not pieces:
                    total = total + partial_refs[d][at, :].astype(f32)
                out_refs[d][at, :] = total.astype(bf16)
                return carry

            lax.fori_loop(0, chunks, gather, 0)


def expert_group(scalars, common, weights, first, count, head, tail, lines, slot_rows, chunk):
    counts, ids, perm, starts, order, line = scalars
    rank, cotangent, gain, router = common
    w_in, w_out, columns = weights
    nodes, width = cotangent.shape
    ff = w_in.shape[2]
    owners = order.shape[0]
    whole = lambda a: pl.BlockSpec(a.shape, lambda i, *_: (0,) * a.ndim)
    listed = lambda *shape: pl.BlockSpec((1,) + shape, lambda i, c, d, perm, *_: (perm[i + first], 0, 0))
    args = [rank, cotangent, gain, router, w_in, w_out, columns]
    specs = [whole(a) for a in args[:4]] + [listed(width, ff), listed(ff, width), listed(1, width)]
    out_shape, out_specs = [], []
    if head:
        residual, atts, projs = head
        extra = [residual, *atts, *projs]
        specs += [whole(a) for a in extra]
        out_shape.append(jax.ShapeDtypeStruct((nodes, width), bf16))
        pieces = len(atts)
    else:
        stream, partials, after = tail
        extra = [stream, *partials, after]
        specs += [whole(stream)] + [whole(p) for p in partials] + [pl.BlockSpec(memory_space=pl.ANY)]
        pieces = 0
    out_shape += [jax.ShapeDtypeStruct((nodes // owners, 2 * width), bf16)] * owners
    out_specs = [pl.BlockSpec(o.shape, lambda i, *_: (0, 0)) for o in out_shape]
    parts = 4 if count % 4 == 0 else count
    each = count // parts
    out_shape += [jax.ShapeDtypeStruct((each, 2 * width, ff), bf16)] * parts
    for k in range(parts):
        out_specs.append(
            pl.BlockSpec((1, 2 * width, ff), lambda i, *_, k=k: (jnp.clip(i - k * each, 0, each - 1), 0, 0))
        )
    return pl.pallas_call(
        functools.partial(group_kernel, first, count, pieces, chunk, lines, owners),
        grid_spec=pltpu.PrefetchScalarGridSpec(
            num_scalar_prefetch=6,
            grid=(count,),
            in_specs=specs,
            out_specs=out_specs,
            scratch_shapes=[
                pltpu.VMEM((chunk, 2 * width), bf16),
                pltpu.VMEM((count, slot_rows, 2 * width), bf16),
                pltpu.VMEM((width, ff), f32),
                pltpu.VMEM((ff, width), f32),
            ],
        ),
        out_shape=out_shape,
        compiler_params=params(),
        cost_estimate=pl.CostEstimate(flops=1000, bytes_accessed=1000, transcendentals=0),
        name="experts",
    )(counts, ids, perm, starts, order, line, *args, *extra)


def home_kernel(parts, stream_ref, cot_ref, gain_ref, *refs):
    layer_ref, grad_ref = refs[parts:]
    total = refs[0][...].astype(f32)
    for g in refs[1:parts]:
        total = total + g[...].astype(f32)
    width = stream_ref.shape[1]
    stream = stream_ref[...].astype(f32)
    inverse_rms = lax.rsqrt(jnp.mean(stream * stream, -1, keepdims=True) + norm_eps)
    layer_ref[...] = (stream + total[:, :width]).astype(bf16)
    gained = total[:, width:] * gain_ref[...]
    mean = jnp.mean(stream * gained, -1, keepdims=True)
    grad = cot_ref[...].astype(f32) + inverse_rms * gained - stream * (inverse_rms * inverse_rms * inverse_rms) * mean
    grad_ref[...] = grad.astype(bf16)


def at_home(me, stream, cotangent, gain, parts, chunk):
    tok_dev, width = cotangent.shape
    steps = tok_dev // chunk
    fresh = lambda w: pl.BlockSpec((chunk, w), lambda i, me: (i, 0))
    return pl.pallas_call(
        lambda me, *refs: home_kernel(len(parts), *refs),
        grid_spec=pltpu.PrefetchScalarGridSpec(
            num_scalar_prefetch=1,
            grid=(steps,),
            in_specs=[
                pl.BlockSpec((chunk, width), lambda i, me: (me[0] * steps + i, 0)),
                fresh(width),
                pl.BlockSpec(gain.shape, lambda i, me: (0, 0)),
            ]
            + [fresh(2 * width) for _ in parts],
            out_specs=[fresh(width), fresh(width)],
        ),
        out_shape=[jax.ShapeDtypeStruct((tok_dev, width), bf16)] * 2,
        compiler_params=params(),
        cost_estimate=pl.CostEstimate(
            flops=EAGER * tok_dev * width * 1000, bytes_accessed=tok_dev * width * 16, transcendentals=0
        ),
        name="at_home",
    )(me.reshape(1), stream, cotangent, gain, *parts)


def line_pairs(seq_count, d):
    lines = seq_count // 4
    return [(z * 4 + r, ((z + d) % lines) * 4 + r) for z in range(lines) for r in range(4)]


def seq_place():
    s = lax.axis_index("seq")
    return s % 2, (s // 2) % 2, s // 4


def add_bf16(*terms):
    total = terms[0].astype(f32)
    for t in terms[1:]:
        total = total + t.astype(f32)
    return total.astype(bf16)


def token_spec():
    return pl.BlockSpec((8, 128), lambda i: (0, 0)), jax.ShapeDtypeStruct((8, 128), f32)


def sum_kernel(terms, cuts, *refs):
    outs = refs[-1 - cuts : -1]
    total = refs[0][...].astype(f32)
    for r in refs[1:terms]:
        total = total + r[...].astype(f32)
    total = total.astype(bf16)
    part = total.shape[1] // cuts
    for k, out in enumerate(outs):
        out[...] = total[:, k * part : (k + 1) * part]
    refs[-1][...] = jnp.zeros_like(refs[-1])


def sum_blocks(terms, cuts, after, name):
    shape = terms[0].shape
    whole = lambda s: pl.BlockSpec(s, lambda i: (0, 0, 0))
    piece = (shape[0], shape[1] // cuts, shape[2])
    token, token_shape = token_spec()
    found = pl.pallas_call(
        functools.partial(sum_kernel, len(terms), cuts),
        grid=(1,),
        in_specs=[whole(shape)] * len(terms) + [pl.BlockSpec(memory_space=pl.ANY)] * len(after),
        out_specs=[whole(piece)] * cuts + [token],
        out_shape=[jax.ShapeDtypeStruct(piece, bf16)] * cuts + [token_shape],
        compiler_params=params(),
        cost_estimate=pl.CostEstimate(flops=1000, bytes_accessed=1000, transcendentals=0),
        name=name,
    )(*terms, *after)
    return found[:-1], found[-1]


def stack_kernel(count, *refs):
    for k in range(count):
        refs[-1][k] = refs[k][...]


def stack_pieces(pieces, after):
    shape = pieces[0].shape
    return pl.pallas_call(
        functools.partial(stack_kernel, len(pieces)),
        grid=(1,),
        in_specs=[pl.BlockSpec(shape, lambda i: (0, 0, 0))] * len(pieces) + [pl.BlockSpec(memory_space=pl.ANY)] * len(after),
        out_specs=pl.BlockSpec((len(pieces),) + shape, lambda i: (0, 0, 0, 0)),
        out_shape=jax.ShapeDtypeStruct((len(pieces),) + shape, bf16),
        compiler_params=params(),
        cost_estimate=pl.CostEstimate(flops=1000, bytes_accessed=1000, transcendentals=0),
        name="stack_pieces",
    )(*pieces, *after)


class SeqSum:
    def __init__(self, grads, seq_count):
        self.grads, self.seq_count, self.lines = grads, seq_count, seq_count // 4
        self.sib = sibling_pairs(seq_count)
        self.cross = [(i, i ^ 2) for i in range(seq_count)]

    def over_core(self, after):
        self.got = [lax.ppermute(g, "seq", self.sib) for g in self.grads[:2]]
        (first,), token = sum_blocks([self.grads[2], self.got[0]], 1, after, "sum_core")
        self.crossed = lax.ppermute(first, "seq", self.cross)
        return token

    def over_x(self):
        self.parts, token = sum_blocks([self.grads[3], self.got[1], self.crossed], self.lines, [], "sum_x")
        return token

    def over_lines(self):
        shard = self.parts[0].astype(f32)
        for d in range(1, self.lines):
            shard = shard + lax.ppermute(self.parts[d], "seq", line_pairs(self.seq_count, d)).astype(f32)
        self.shard = shard.astype(bf16)

    def back(self, after):
        pieces = [self.shard]
        for d in range(1, self.lines):
            pieces.append(lax.ppermute(self.shard, "seq", line_pairs(self.seq_count, d)))
        own = stack_pieces(pieces, after)
        other = lax.ppermute(own, "seq", self.cross)
        return [own, other, lax.ppermute(own, "seq", self.sib), lax.ppermute(other, "seq", self.sib)]


def unpack_kernel(lines, each, width, where, line, *refs):
    win_ref, wout_ref = refs[-2:]
    step = pl.program_id(0)
    for a in range(4):
        for i in range(each):

            @pl.when(step == a * each + i)
            def _(a=a, i=i):
                for p in range(lines):
                    block = refs[a][lax.rem(line[0] - p + lines, lines), i].astype(f32)
                    part, ff = block.shape
                    low = p * part
                    if low < width:
                        win_ref[0, low : low + part, :] = block
                    else:
                        low = low - width
                        for j in range(ff // width):
                            wout_ref[0, j * width + low : j * width + low + part, :] = block[:, j * width : (j + 1) * width]


def unpack(where, line, blocks, experts, width, ff, into):
    lines, each = blocks[0].shape[:2]
    whole = pl.BlockSpec(blocks[0].shape, lambda i, *_: (0, 0, 0, 0))
    out = lambda *shape: pl.BlockSpec((1,) + shape, lambda i, where, line: (where[i], 0, 0))
    return pl.pallas_call(
        functools.partial(unpack_kernel, lines, each, width),
        grid_spec=pltpu.PrefetchScalarGridSpec(
            num_scalar_prefetch=2,
            grid=(4 * each,),
            in_specs=[whole] * 4 + [pl.BlockSpec(memory_space=pl.ANY)] * len(into),
            out_specs=[out(width, ff), out(ff, width)],
        ),
        out_shape=[
            jax.ShapeDtypeStruct((experts, width, ff), f32),
            jax.ShapeDtypeStruct((experts, ff, width), f32),
        ],
        input_output_aliases={6 + i: i for i in range(len(into))},
        compiler_params=params(),
        cost_estimate=pl.CostEstimate(flops=EAGER * 4 * each * 2 * width * ff * 6, bytes_accessed=4 * each * 2 * width * ff * 6, transcendentals=0),
        name="unpack",
    )(where, line, *blocks, *into)


def sum_any(grads, seq_count):
    lines = seq_count // 4
    core, column, line = seq_place()
    sib = sibling_pairs(seq_count)
    cross = [(i, i ^ 2) for i in range(seq_count)]

    def halve(a, which, pairs):
        h = a.shape[0] // 2
        mine = lax.dynamic_slice_in_dim(a, which * h, h, 0)
        other = lax.dynamic_slice_in_dim(a, (1 - which) * h, h, 0)
        return add_bf16(mine, lax.ppermute(other, "seq", pairs))

    a = halve(halve(grads, core, sib), column, cross)
    q = a.shape[0] // lines
    total = lax.dynamic_slice_in_dim(a, line * q, q, 0).astype(f32)
    for d in range(1, lines):
        part = lax.dynamic_slice_in_dim(a, lax.rem(line + d, lines) * q, q, 0)
        total = total + lax.ppermute(part, "seq", line_pairs(seq_count, d)).astype(f32)
    shard = total.astype(bf16)

    out = jnp.zeros((q * lines,) + a.shape[1:], bf16)
    out = lax.dynamic_update_slice_in_dim(out, shard, line * q, 0)
    for d in range(1, lines):
        got = lax.ppermute(shard, "seq", line_pairs(seq_count, d))
        out = lax.dynamic_update_slice_in_dim(out, got, lax.rem(line - d + lines, lines) * q, 0)

    def double(a, which, pairs):
        got = lax.ppermute(a, "seq", pairs)
        return jnp.where(which == 0, jnp.concatenate([a, got], 0), jnp.concatenate([got, a], 0))

    return double(double(out, column, cross), core, sib)


def shards(
    query_cols,
    key_cols,
    value_cols,
    block_list,
    residual,
    out_proj,
    norm_gain,
    router_weight,
    expert_ids,
    expert_in,
    expert_out,
    cotangent,
):
    seq_count = lax.axis_size("seq")
    exp_count = lax.axis_size("expert")
    me = lax.axis_index("expert")
    feat, nodes = query_cols.shape
    blk_seq, degree = block_list.shape
    block_len = nodes // blk_seq
    tok_dev, width = residual.shape
    expert_total = router_weight.shape[1]
    experts = expert_in.shape[0]
    ff = expert_in.shape[2]
    topk = expert_ids.shape[1]
    chunk = min(256, tok_dev)
    capacity = 2 * tok_dev * topk // expert_total * exp_count
    slot_rows = capacity + WINDOW

    calls = 2 if blk_seq % 2 == 0 else 1
    keys, values = ring_gather(key_cols, value_cols, seq_count)
    tables = block_tables(block_list, blk_seq, seq_count, calls)

    residual_all = gather_expert_axis(residual, exp_count)
    cotangent_all = gather_expert_axis(cotangent, exp_count)
    ids_all = gather_expert_axis(expert_ids.T, exp_count, 1)
    gain = norm_gain.reshape(1, width)
    core, column, line_at = seq_place()
    lines = seq_count // 4
    line = line_at.reshape(1).astype(jnp.int32)
    groups = 2 if experts % 8 == 0 else 1
    per_group = experts // groups
    tuned = per_group % 4 == 0 and (2 * width) % (16 * lines) == 0 and lines > 1
    each = per_group // 4
    at = jnp.arange(experts, dtype=jnp.int32)
    first_of = lambda dest, i: at // per_group * per_group + dest * each + i
    dests = jnp.stack([(1 - core) * 2 + 1 - column, (1 - core) * 2 + column, core * 2 + 1 - column, core * 2 + column])
    outs = jnp.stack([core * 2 + column, core * 2 + 1 - column, (1 - core) * 2 + column, (1 - core) * 2 + 1 - column])
    if tuned:
        perm = first_of(jnp.tile(jnp.repeat(dests, each), groups), at % each).astype(jnp.int32)
        where = first_of(jnp.tile(jnp.repeat(outs, each), groups), at % each).astype(jnp.int32)
    else:
        perm = at
        line = jnp.zeros_like(line)
    local_ids = me * experts + perm
    hot = jnp.sum((ids_all[None, :, :] == local_ids[:, None, None]).astype(jnp.int32), 1)
    running = jnp.cumsum(hot, 1)
    rank = jnp.where(hot > 0, running - 1, -(1 << 20))
    ends = running[:, chunk - 1 :: chunk]
    starts = jnp.concatenate([jnp.zeros((experts, 1), jnp.int32), ends], 1).T
    counts = running[:, -1]
    router = jnp.pad(router_weight, ((0, 0), (0, -expert_total % 128)))
    columns = lax.dynamic_slice_in_dim(router_weight.T, me * experts, experts, 0).astype(f32).reshape(experts, 1, width)
    projs = [
        lax.dynamic_slice_in_dim(out_proj, lax.rem(me + exp_count - d, exp_count) * feat, feat, 0)
        for d in range(exp_count)
    ]
    owner_order = lax.rem(me + jnp.arange(exp_count, dtype=jnp.int32), exp_count)

    per_call = blk_seq // calls
    pieces = [[] for _ in range(exp_count)]
    for c in range(calls):
        part = attention(query_cols, keys, values, tables, c, per_call, block_len, degree)
        pieces[0].append(part)
        for d in range(1, exp_count):
            pieces[d].append(lax.ppermute(part, "expert", shift_pairs(exp_count, d)))
    atts = [jnp.concatenate(p, 0) for p in pieces]

    scalars = (counts, local_ids, perm, starts, owner_order, line)
    common = (rank, cotangent_all, gain, router)
    weights = (expert_in, expert_out, columns)
    into, sums, after, stream, partials = [], [], None, None, None
    for g in range(groups):
        head = (residual_all, atts, projs) if g == 0 else None
        tail = (stream, partials, after)
        found = list(
            expert_group(scalars, common, weights, g * per_group, per_group, head, tail, lines, slot_rows, chunk)
        )
        if g == 0:
            stream = found.pop(0)
        partials, grads = found[:exp_count], found[exp_count:]
        if tuned:
            sums.append(SeqSum(grads, seq_count))
            after = sums[-1].over_core([sums[-2].over_x()] if g > 0 else [])
        else:
            into.append(sum_any(jnp.concatenate(grads, 0).reshape(per_group * 2 * width, ff), seq_count))
    parts = partials[:1] + [lax.ppermute(partials[d], "expert", shift_pairs(exp_count, d)) for d in range(1, exp_count)]
    layer_out, grad_stream = at_home(me, stream, cotangent, gain, parts, chunk)
    if tuned:
        sums[-1].over_x()
        for g, each_sum in enumerate(sums):
            each_sum.over_lines()
            blocks = each_sum.back([layer_out] if g == 0 else [])
            into = unpack(where[g * per_group : (g + 1) * per_group], line, blocks, experts, width, ff, into)
    if tuned:
        grad_w_in, grad_w_out = into
    else:
        total = jnp.concatenate(into, 0).reshape(experts, 2 * width, ff).astype(f32)
        grad_w_in = total[:, :width, :]
        grad_w_out = jnp.concatenate([total[:, width:, j * width : (j + 1) * width] for j in range(ff // width)], 1)

    return layer_out, grad_stream, grad_w_in, grad_w_out


def solution(mesh):
    return jax.shard_map(
        shards,
        mesh=mesh,
        in_specs=(
            P("expert", "seq"),
            P("expert", "seq"),
            P("expert", "seq"),
            P("seq", None),
            P(("seq", "expert"), None),
            P(),
            P(),
            P(),
            P(("seq", "expert"), None),
            P("expert", None, None),
            P("expert", None, None),
            P(("seq", "expert"), None),
        ),
        out_specs=(
            P(("seq", "expert"), None),
            P(("seq", "expert"), None),
            P("expert", None, None),
            P("expert", None, None),
        ),
        check_vma=False,
    )
```

time: 285 us -> 240 us (0.84)
  other arithmetic: 29 us -> 7.64 us
  Pallas kernels: 72.8 us -> 57.9 us
  local copies, waits for them, and re-layouts: 27.4 us -> 16 us
  starting transfers between devices: 49.2 us -> 59.2 us
  waiting for transfers between devices: 103 us -> 97.5 us
    select_n x4 -> x0, other arithmetic: 11.3 us -> none  [double(): jnp.where(which == 0, jnp.concatenate([a, got], 0), jnp.concatenate([got,...]
    pallas_call x2, Pallas kernels: 25 us -> 14.1 us  [attention(): pl.pallas_call(functools.partial(attention_kernel, degree, feat // HD, le...]
    ppermute x21 -> x25, starting transfers between devices: 25.5 us -> 35.5 us  [the longest x6 17.1 us: back(): lax.ppermute(self.shard, 'seq', line_pairs(self.seq_count, d))]
    ppermute x21 -> x25, waiting for transfers between devices: 47.1 us -> 37.7 us  [the longest x2 17 us: back(): other = lax.ppermute(own, 'seq', self.cross)]
    convert_element_type x5 -> x2, other arithmetic: 5.35 us -> 0.14 us  [over_lines(): self.shard = shard.astype(bf16)]
    pallas_call x5 -> x11, Pallas kernels: 47.8 us -> 43.8 us  [the longest x2 33 us: expert_group(): pl.pallas_call(functools.partial(group_kernel, first, count, pieces, chun...]
    dynamic_update_slice x6 -> x0, local copies, waits for them, and re-layouts: 3.98 us -> none  [sum_over_seq(): lax.dynamic_update_slice_in_dim(out, got, lax.rem(line - d + lines, lines...]
    unnamed x63 -> x65, local copies, waits for them, and re-layouts: 6.52 us -> 6.48 us
  transfers between devices with their start and end apart: 56 -> 60, of which waited for: 16 -> 20; matrix products, arithmetic and copies ran while one was open for 15% -> 8% of each run, Pallas kernels for 18% -> 15%
where the time goes in v3:
time: 240 us
  waiting for transfers between devices  97.5 us (41%)
  starting transfers between devices  59.2 us (25%)
  Pallas kernels  57.9 us (24%)
  local copies, waits for them, and re-layouts  16 us (7%)
  other arithmetic  7.64 us (3%)
    ppermute x7, waiting for transfers between devices, ring_gather(): k = lax.ppermute(k, 'seq', fwd)  48.8 us
    pallas_call x2, Pallas kernels, expert_group(): pl.pallas_call(functools.partial(group_kernel, first, count, pieces, chun...  33 us
    ppermute x6, starting transfers between devices, back(): lax.ppermute(self.shard, 'seq', line_pairs(self.seq_count, d))  17.1 us
    ppermute x2, waiting for transfers between devices, back(): other = lax.ppermute(own, 'seq', self.cross)  17 us
    pallas_call x2, Pallas kernels, attention(): pl.pallas_call(functools.partial(attention_kernel, degree, feat // HD, le...  14.1 us
    ppermute x6, starting transfers between devices, over_lines(): lax.ppermute(self.parts[d], 'seq', line_pairs(self.seq_count, d))  11 us
    ppermute x7, starting transfers between devices, ring_gather(): k = lax.ppermute(k, 'seq', fwd)  10.7 us
    ppermute x6, waiting for transfers between devices, back(): lax.ppermute(self.shard, 'seq', line_pairs(self.seq_count, d))  9 us
  transfers between devices with their start and end apart: 60, of which 20 were waited for; matrix products, arithmetic and copies ran while one was open for 8% of the time, Pallas kernels for 15%

profile of v3, /device:TPU:0, one launch (start us, length us, event | category | flops | bytes accessed | tf_op | source)
XLA Modules:
  0.0 239.6 jit_solution(7605312754685548522)
XLA Ops:
  1.2 2.6 %collective-permute-start.3 = (bf16[128,2048]{1,0:T(8,128)(2,1)}, bf16[128,2048]{1,0:T(8,128)(2,1)S(1)}, u32[]{:S(2)}, u32[]{:S(2)}) collective-permute-start(bf16[128,2048]{1,0:T(8,128)(2,1)} %refs_0_.3), channel_id=1, source_target_pairs={{0,8},{2,10},{8,16},{10,18},{16,24},{18,26},{24,28},{26,30},{28,20... | collective-permute-start | bytes 1572872 | tf_op jit(solution)/shard_map/ppermute | solution.py:74
  3.8 1.5 collective-permute-start
  6.7 1.2 dynamic_slice.13
  9.7 6.8 %collective-permute-done.3.refs_1_ = bf16[128,2048]{1,0:T(8,128)(2,1)S(1)} collective-permute-done((bf16[128,2048]{1,0:T(8,128)(2,1)}, bf16[128,2048]{1,0:T(8,128)(2,1)S(1)}, u32[]{:S(2)}, u32[]{:S(2)}) %collective-permute-start.3) | collective-permute-done | bytes 524320 | tf_op jit(solution)/shard_map/ppermute | solution.py:74
  16.5 1.8 collective-permute-start.4
  18.3 1.2 collective-permute-done.18.refs_17_
  20.7 9.5 %collective-permute-done.4.refs_2_ = bf16[128,2048]{1,0:T(8,128)(2,1)S(1)} collective-permute-done((bf16[128,2048]{1,0:T(8,128)(2,1)S(1)}, bf16[128,2048]{1,0:T(8,128)(2,1)S(1)}, u32[]{:S(2)}, u32[]{:S(2)}) %collective-permute-start.4) | collective-permute-done | bytes 524320 | tf_op jit(solution)/shard_map/ppermute | solution.py:74
  30.2 1.6 collective-permute-start.5
  33.9 9.5 %collective-permute-done.5.refs_3_ = bf16[128,2048]{1,0:T(8,128)(2,1)} collective-permute-done((bf16[128,2048]{1,0:T(8,128)(2,1)S(1)}, bf16[128,2048]{1,0:T(8,128)(2,1)}, u32[]{:S(2)}, u32[]{:S(2)}) %collective-permute-start.5) | collective-permute-done | bytes 524320 | tf_op jit(solution)/shard_map/ppermute | solution.py:74
  43.4 1.4 collective-permute-start.6
  46.0 1.2 constant_dynamic-update-slice_fusion.3
  47.3 1.1 constant_dynamic-update-slice_fusion.1
  49.1 6.8 %collective-permute-done.6.refs_4_ = bf16[128,2048]{1,0:T(8,128)(2,1)} collective-permute-done((bf16[128,2048]{1,0:T(8,128)(2,1)}, bf16[128,2048]{1,0:T(8,128)(2,1)}, u32[]{:S(2)}, u32[]{:S(2)}) %collective-permute-start.6) | collective-permute-done | bytes 524320 | tf_op jit(solution)/shard_map/ppermute | solution.py:74
  55.8 1.1 collective-permute-start.7
  58.8 9.1 %collective-permute-done.7.refs_5_ = bf16[128,2048]{1,0:T(8,128)(2,1)} collective-permute-done((bf16[128,2048]{1,0:T(8,128)(2,1)}, bf16[128,2048]{1,0:T(8,128)(2,1)}, u32[]{:S(2)}, u32[]{:S(2)}) %collective-permute-start.7) | collective-permute-done | bytes 524320 | tf_op jit(solution)/shard_map/ppermute | solution.py:74
  67.9 1.1 collective-permute-start.8
  70.8 4.2 %reduce-window.6 = s32[8,16,128]{2,1,0:T(8,128)S(1)} reduce-window(s32[8,16,128]{2,1,0:T(8,128)} %copy.43, s32[]{:T(128)} %constant.144.clone.1), window={size=1x1x128 pad=0_0x0_0x127_0}, to_apply=%region_1.2 | reduce-window | flops 2080768 | bytes 131076 | tf_op jit(solution)/shard_map/reduce-window
  75.6 2.9 %collective-permute-done.8.refs_6_ = bf16[128,2048]{1,0:T(8,128)(2,1)} collective-permute-done((bf16[128,2048]{1,0:T(8,128)(2,1)}, bf16[128,2048]{1,0:T(8,128)(2,1)}, u32[]{:S(2)}, u32[]{:S(2)}) %collective-permute-start.8) | collective-permute-done | bytes 524320 | tf_op jit(solution)/shard_map/ppermute | solution.py:74
  79.5 1.1 collective-permute-start.24
  86.0 4.2 %collective-permute-done.9.refs_7_ = bf16[128,2048]{1,0:T(8,128)(2,1)} collective-permute-done((bf16[128,2048]{1,0:T(8,128)(2,1)}, bf16[128,2048]{1,0:T(8,128)(2,1)}, u32[]{:S(2)}, u32[]{:S(2)}) %collective-permute-start.9) | collective-permute-done | bytes 524320 | tf_op jit(solution)/shard_map/ppermute | solution.py:74
  91.1 1.1 constant_dynamic-update-slice_fusion.2.refs_1_
  95.0 7.0 %attention.2 = bf16[1024,128]{1,0:T(8,128)(2,1)S(1)} custom-call(s32[32]{0:T(128)S(1)} %squeeze.37.local, s32[32]{0:T(128)S(1)} %get-tuple-element.81.korder, s32[17]{0:T(128)S(1)} %get-tuple-element.94.kbegin, s32[32]{0:T(128)S(1)} %get-tuple-element.79.vorder, s32[17]{0:T(128)S(1)} %get-tuple-element.66.vbegin, bf16[128,2048]{1,0:T(8,128)(2,1)S(1)} %copy-done.2, ...), custom_call_target="tpu_custom_call" | custom-call | flops 268435456 | bytes 2621440 | tf_op jit(solution)/shard_map/attention/pallas_call | solution.py:160
  102.1 1.6 collective-permute-start.33
  103.7 7.0 %attention.3 = bf16[1024,128]{1,0:T(8,128)(2,1)S(1)} custom-call(s32[32]{0:T(128)S(1)} %squeeze.43.local, s32[32]{0:T(128)S(1)} %get-tuple-element.82.korder, s32[17]{0:T(128)S(1)} %get-tuple-element.93.kbegin, s32[32]{0:T(128)S(1)} %get-tuple-element.80.vorder, s32[17]{0:T(128)S(1)} %get-tuple-element.67.vbegin, bf16[128,2048]{1,0:T(8,128)(2,1)S(1)} %copy-done.2, ...), custom_call_target="tpu_custom_call" | custom-call | flops 268435456 | bytes 2621440 | tf_op jit(solution)/shard_map/attention/pallas_call | solution.py:160
  111.4 7.7 %collective-permute-done.34 = bf16[1024,128]{1,0:T(8,128)(2,1)S(1)} collective-permute-done((bf16[1024,128]{1,0:T(8,128)(2,1)S(1)}, bf16[1024,128]{1,0:T(8,128)(2,1)S(1)}, u32[]{:S(2)}, u32[]{:S(2)}) %collective-permute-start.34) | collective-permute-done | bytes 262176 | tf_op jit(solution)/shard_map/ppermute | solution.py:703
  119.1 16.8 %experts.2 = (bf16[2048,256]{1,0:T(8,128)(2,1)S(1)}, bf16[1024,512]{1,0:T(8,128)(2,1)S(1)}, bf16[1024,512]{1,0:T(8,128)(2,1)}, bf16[1,512,512]{2,1,0:T(8,128)(2,...) custom-call(s32[8]{0:T(128)S(1)} %slice_reduce_fusion.5.counts, ...), custom_call_target="tpu_custom_call" | custom-call | flops 1000 | bytes 1000 | tf_op jit(solution)/shard_map/experts/pallas_call | solution.py:389
  138.4 1.4 collective-permute-done.35.refs_1_
  139.9 1.8 collective-permute-start.40
  141.7 16.2 %experts.3 = (bf16[1024,512]{1,0:T(8,128)(2,1)S(1)}, bf16[1024,512]{1,0:T(8,128)(2,1)S(1)}, bf16[1,512,512]{2,1,0:T(8,128)(2,1)S(1)}, bf16[1,512,512]{2,1,0:T(8,...) custom-call(s32[8]{0:T(128)S(1)} %slice_reduce_fusion.5.counts, ...), custom_call_target="tpu_custom_call" | custom-call | flops 1000 | bytes 1000 | tf_op jit(solution)/shard_map/experts/pallas_call | solution.py:389
  158.9 2.7 %collective-permute-start.36 = (bf16[1024,512]{1,0:T(8,128)(2,1)S(1)}, bf16[1024,512]{1,0:T(8,128)(2,1)S(1)}, u32[]{:S(2)}, u32[]{:S(2)}) collective-permute-start(bf16[1024,512]{1,0:T(8,128)(2,1)S(1)} %get-tuple-element.42), channel_id=1, source_target_pairs={{0,1},{1,0},{2,3},{3,2},{4,5},{5,4},{6,7},{7,6},{8,9},{9,8},{10,11... | collective-permute-start | bytes 3145736 | tf_op jit(solution)/shard_map/ppermute | solution.py:724
  163.1 2.6 %collective-permute-start.51 = (bf16[1,128,512]{2,1,0:T(8,128)(2,1)S(1)}, bf16[1,128,512]{2,1,0:T(8,128)(2,1)S(1)}, u32[]{:S(2)}, u32[]{:S(2)}) collective-permute-start(bf16[1,128,512]{2,1,0:T(8,128)(2,1)S(1)} %get-tuple-element.59), channel_id=1, source_target_pairs={{0,8},{2,10},{4,12},{6,14},{8,16},{10,18},{12,20},{14,22},{16,24},... | collective-permute-start | bytes 393224 | tf_op jit(solution)/shard_map/ppermute | solution.py:540
  165.7 1.5 collective-permute-start.52
  167.2 1.4 collective-permute-start.53
  168.6 7.8 %collective-permute-done.41.refs_2_ = bf16[1,512,512]{2,1,0:T(8,128)(2,1)S(1)} collective-permute-done((bf16[1,512,512]{2,1,0:T(8,128)(2,1)S(1)}, bf16[1,512,512]{2,1,0:T(8,128)(2,1)S(1)}, u32[]{:S(2)}, u32[]{:S(2)}) %collective-permute-start.41) | collective-permute-done | bytes 524320 | tf_op jit(solution)/shard_map/ppermute | solution.py:530
  177.1 1.1 collective-permute-start.42
  178.2 3.0 %collective-permute-start.43 = (bf16[1,128,512]{2,1,0:T(8,128)(2,1)S(1)}, bf16[1,128,512]{2,1,0:T(8,128)(2,1)S(1)}, u32[]{:S(2)}, u32[]{:S(2)}) collective-permute-start(bf16[1,128,512]{2,1,0:T(8,128)(2,1)S(1)} %get-tuple-element.56), channel_id=1, source_target_pairs={{0,16},{2,18},{4,20},{6,22},{8,24},{10,26},{12,28},{14,30},{16,0},... | collective-permute-start | bytes 393224 | tf_op jit(solution)/shard_map/ppermute | solution.py:540
  181.2 1.3 collective-permute-start.44
  182.9 2.5 %collective-permute-done.42 = bf16[1,128,512]{2,1,0:T(8,128)(2,1)S(1)} collective-permute-done((bf16[1,128,512]{2,1,0:T(8,128)(2,1)S(1)}, bf16[1,128,512]{2,1,0:T(8,128)(2,1)S(1)}, u32[]{:S(2)}, u32[]{:S(2)}) %collective-permute-start.42) | collective-permute-done | bytes 131104 | tf_op jit(solution)/shard_map/ppermute | solution.py:540
  185.3 10.5 %collective-permute-start.55 = (bf16[1,128,512]{2,1,0:T(8,128)(2,1)S(1)}, bf16[1,128,512]{2,1,0:T(8,128)(2,1)S(1)}, u32[]{:S(2)}, u32[]{:S(2)}) collective-permute-start(bf16[1,128,512]{2,1,0:T(8,128)(2,1)S(1)} %add_convert_fusion.refs_0_), channel_id=1, source_target_pairs={{0,16},{2,18},{4,20},{6,22},{8,24},{10,26},{12,28},{14,30},{16,0},... | collective-permute-start | bytes 393224 | tf_op jit(solution)/shard_map/ppermute | solution.py:546
  196.8 3.0 %collective-permute-start.47 = (bf16[1,128,512]{2,1,0:T(8,128)(2,1)S(1)}, bf16[1,128,512]{2,1,0:T(8,128)(2,1)S(1)}, u32[]{:S(2)}, u32[]{:S(2)}) collective-permute-start(bf16[1,128,512]{2,1,0:T(8,128)(2,1)S(1)} %add_convert_fusion.1.refs_0_), channel_id=1, source_target_pairs={{0,24},{2,26},{4,28},{6,30},{8,0},{10,2},{12,4},{14,6},{16,8},{18,... | collective-permute-start | bytes 393224 | tf_op jit(solution)/shard_map/ppermute | solution.py:546
  200.4 1.9 collective-permute-start.45
  202.3 1.9 at_home.1
  204.2 4.7 %collective-permute-done.55.refs_2_ = bf16[1,128,512]{2,1,0:T(8,128)(2,1)S(1)} collective-permute-done((bf16[1,128,512]{2,1,0:T(8,128)(2,1)S(1)}, bf16[1,128,512]{2,1,0:T(8,128)(2,1)S(1)}, u32[]{:S(2)}, u32[]{:S(2)}) %collective-permute-start.55) | collective-permute-done | bytes 131104 | tf_op jit(solution)/shard_map/ppermute | solution.py:546
  210.1 4.3 %collective-permute-done.46.refs_2_ = bf16[1,128,512]{2,1,0:T(8,128)(2,1)S(1)} collective-permute-done((bf16[1,128,512]{2,1,0:T(8,128)(2,1)S(1)}, bf16[1,128,512]{2,1,0:T(8,128)(2,1)S(1)}, u32[]{:S(2)}, u32[]{:S(2)}) %collective-permute-start.46) | collective-permute-done | bytes 131104 | tf_op jit(solution)/shard_map/ppermute | solution.py:546
  214.6 10.1 %collective-permute-done.57.refs_1_ = bf16[4,1,128,512]{3,2,1,0:T(8,128)(2,1)S(1)} collective-permute-done((bf16[4,1,128,512]{3,2,1,0:T(8,128)(2,1)S(1)}, bf16[4,1,128,512]{3,2,1,0:T(8,128)(2,1)S(1)}, u32[]{:S(2)}, u32[]{:S(2)}) %collective-permute-start.57) | collective-permute-done | bytes 524320 | tf_op jit(solution)/shard_map/ppermute | solution.py:548
  225.2 6.9 %collective-permute-done.48.refs_1_ = bf16[4,1,128,512]{3,2,1,0:T(8,128)(2,1)S(1)} collective-permute-done((bf16[4,1,128,512]{3,2,1,0:T(8,128)(2,1)S(1)}, bf16[4,1,128,512]{3,2,1,0:T(8,128)(2,1)S(1)}, u32[]{:S(2)}, u32[]{:S(2)}) %collective-permute-start.48) | collective-permute-done | bytes 524320 | tf_op jit(solution)/shard_map/ppermute | solution.py:548
  232.3 3.0 %unpack.2 = (f32[8,256,512]{2,1,0:T(8,128)}, f32[8,512,256]{2,1,0:T(8,128)}) custom-call(s32[4]{0:T(128)S(1)} %get-tuple-element.83.where, s32[1]{0:T(128)} %bitcast.8.line, bf16[4,1,128,512]{3,2,1,0:T(8,128)(2,1)S(1)} %stack_pieces.3.refs_0_, bf16[4,1,128,512]{3,2,1,0:T(8,128)(2,1)S(1)} %collective-permute-done.57.refs_1_, ...), custom_call_target="tpu_custom_call" | custom-call | flops 201326592 | bytes 6291456 | tf_op jit(solution)/shard_map/unpack/pallas_call | solution.py:576
  235.3 4.2 %unpack.3 = (f32[8,256,512]{2,1,0:T(8,128)}, f32[8,512,256]{2,1,0:T(8,128)}) custom-call(s32[4]{0:T(128)S(1)} %get-tuple-element.84.where, s32[1]{0:T(128)} %bitcast.8.line, bf16[4,1,128,512]{3,2,1,0:T(8,128)(2,1)S(1)} %stack_pieces.2.refs_0_, ...), custom_call_target="tpu_custom_call", output_to_operand_aliasing={{0}: (6, {}), {1}: (7, {})} | custom-call | flops 201326592 | bytes 6291456 | tf_op jit(solution)/shard_map/unpack/pallas_call | solution.py:576
  (209 shorter events, 33.0 us)
Async XLA Ops:
  0.6 47.7 %collective-permute-start.10 = (bf16[128,2048]{1,0:T(8,128)(2,1)}, bf16[128,2048]{1,0:T(8,128)(2,1)S(1)}, u32[]{:S(2)}, u32[]{:S(2)}) collective-permute-start(bf16[128,2048]{1,0:T(8,128)(2,1)} %refs_0_.3), channel_id=1, source_target_pairs={{0,2},{2,0},{4,6},{6,4},{8,10},{10,8},{12,14},{14,12},{16,18},{18,... | collective-permute-start | bytes 1572872 | tf_op jit(solution)/shard_map/ppermute | solution.py:78
  1.2 15.3 %collective-permute-start.3 = (bf16[128,2048]{1,0:T(8,128)(2,1)}, bf16[128,2048]{1,0:T(8,128)(2,1)S(1)}, u32[]{:S(2)}, u32[]{:S(2)}) collective-permute-start(bf16[128,2048]{1,0:T(8,128)(2,1)} %refs_0_.3), channel_id=1, source_target_pairs={{0,8},{2,10},{8,16},{10,18},{16,24},{18,26},{24,28},{26,30},{28,20... | collective-permute-start | bytes 1572872 | tf_op jit(solution)/shard_map/ppermute | solution.py:74
  3.8 29.5 %collective-permute-start = (s32[2,1024]{1,0:T(2,128)}, s32[2,1024]{1,0:T(2,128)S(1)}, u32[]{:S(2)}, u32[]{:S(2)}) collective-permute-start(s32[2,1024]{1,0:T(2,128)} %bitcast.38), channel_id=1, source_target_pairs={{0,1},{1,0},{2,3},{3,2},{4,5},{5,4},{6,7},{7,6},{8,9},{9,8},{10,11... | collective-permute-start | bytes 24584 | tf_op jit(solution)/shard_map/ppermute | solution.py:62
  5.3 28.0 %collective-permute-start.1 = (bf16[1024,256]{1,0:T(8,128)(2,1)}, bf16[1024,256]{1,0:T(8,128)(2,1)}, u32[]{:S(2)}, u32[]{:S(2)}) collective-permute-start(bf16[1024,256]{1,0:T(8,128)(2,1)} %refs_1_.1), channel_id=1, source_target_pairs={{0,1},{1,0},{2,3},{3,2},{4,5},{5,4},{6,7},{7,6},{8,9},{9,8},{10,11... | collective-permute-start | bytes 1572872 | tf_op jit(solution)/shard_map/ppermute | solution.py:62
  5.8 13.6 %collective-permute-start.18 = (bf16[128,2048]{1,0:T(8,128)(2,1)}, bf16[128,2048]{1,0:T(8,128)(2,1)S(1)}, u32[]{:S(2)}, u32[]{:S(2)}) collective-permute-start(bf16[128,2048]{1,0:T(8,128)(2,1)} %refs_16_.3), channel_id=1, source_target_pairs={{0,4},{2,6},{8,0},{10,2},{16,8},{18,10},{24,16},{26,18},{28,24},{3... | collective-permute-start | bytes 1572872 | tf_op jit(solution)/shard_map/ppermute | solution.py:75
  16.5 13.8 %collective-permute-start.4 = (bf16[128,2048]{1,0:T(8,128)(2,1)S(1)}, bf16[128,2048]{1,0:T(8,128)(2,1)S(1)}, u32[]{:S(2)}, u32[]{:S(2)}) collective-permute-start(bf16[128,2048]{1,0:T(8,128)(2,1)S(1)} %collective-permute-done.3.refs_1_), channel_id=1, source_target_pairs={{0,8},{2,10},{8,16},{10,18},{16,24},{18,26},{24,28},{26,30},{28,20... | collective-permute-start | bytes 1572872 | tf_op jit(solution)/shard_map/ppermute | solution.py:74
  19.5 12.7 %collective-permute-start.19 = (bf16[128,2048]{1,0:T(8,128)(2,1)S(1)}, bf16[128,2048]{1,0:T(8,128)(2,1)}, u32[]{:S(2)}, u32[]{:S(2)}) collective-permute-start(bf16[128,2048]{1,0:T(8,128)(2,1)S(1)} %collective-permute-done.18.refs_17_), channel_id=1, source_target_pairs={{0,4},{2,6},{8,0},{10,2},{16,8},{18,10},{24,16},{26,18},{28,24},{3... | collective-permute-start | bytes 1572872 | tf_op jit(solution)/shard_map/ppermute | solution.py:75
  30.2 13.1 %collective-permute-start.5 = (bf16[128,2048]{1,0:T(8,128)(2,1)S(1)}, bf16[128,2048]{1,0:T(8,128)(2,1)}, u32[]{:S(2)}, u32[]{:S(2)}) collective-permute-start(bf16[128,2048]{1,0:T(8,128)(2,1)S(1)} %collective-permute-done.4.refs_2_), channel_id=1, source_target_pairs={{0,8},{2,10},{8,16},{10,18},{16,24},{18,26},{24,28},{26,30},{28,20... | collective-permute-start | bytes 1572872 | tf_op jit(solution)/shard_map/ppermute | solution.py:74
  32.2 12.6 %collective-permute-start.20 = (bf16[128,2048]{1,0:T(8,128)(2,1)}, bf16[128,2048]{1,0:T(8,128)(2,1)}, u32[]{:S(2)}, u32[]{:S(2)}) collective-permute-start(bf16[128,2048]{1,0:T(8,128)(2,1)} %collective-permute-done.19.refs_18_), channel_id=1, source_target_pairs={{0,4},{2,6},{8,0},{10,2},{16,8},{18,10},{24,16},{26,18},{28,24},{3... | collective-permute-start | bytes 1572872 | tf_op jit(solution)/shard_map/ppermute | solution.py:75
  33.3 15.2 %collective-permute-start.25 = (bf16[128,2048]{1,0:T(8,128)(2,1)}, bf16[128,2048]{1,0:T(8,128)(2,1)}, u32[]{:S(2)}, u32[]{:S(2)}) collective-permute-start(bf16[128,2048]{1,0:T(8,128)(2,1)} %refs_16_.3), channel_id=1, source_target_pairs={{0,2},{2,0},{4,6},{6,4},{8,10},{10,8},{12,14},{14,12},{16,18},{18,... | collective-permute-start | bytes 1572872 | tf_op jit(solution)/shard_map/ppermute | solution.py:79
  33.4 15.6 %collective-permute-start.11 = (bf16[128,2048]{1,0:T(8,128)(2,1)S(1)}, bf16[128,2048]{1,0:T(8,128)(2,1)}, u32[]{:S(2)}, u32[]{:S(2)}) collective-permute-start(bf16[128,2048]{1,0:T(8,128)(2,1)S(1)} %collective-permute-done.3.refs_1_), channel_id=1, source_target_pairs={{0,2},{2,0},{4,6},{6,4},{8,10},{10,8},{12,14},{14,12},{16,18},{18,... | collective-permute-start | bytes 1572872 | tf_op jit(solution)/shard_map/ppermute | solution.py:78
  43.4 12.4 %collective-permute-start.6 = (bf16[128,2048]{1,0:T(8,128)(2,1)}, bf16[128,2048]{1,0:T(8,128)(2,1)}, u32[]{:S(2)}, u32[]{:S(2)}) collective-permute-start(bf16[128,2048]{1,0:T(8,128)(2,1)} %collective-permute-done.5.refs_3_), channel_id=1, source_target_pairs={{0,8},{2,10},{8,16},{10,18},{16,24},{18,26},{24,28},{26,30},{28,20... | collective-permute-start | bytes 1572872 | tf_op jit(solution)/shard_map/ppermute | solution.py:74
  44.8 12.2 %collective-permute-start.21 = (bf16[128,2048]{1,0:T(8,128)(2,1)}, bf16[128,2048]{1,0:T(8,128)(2,1)}, u32[]{:S(2)}, u32[]{:S(2)}) collective-permute-start(bf16[128,2048]{1,0:T(8,128)(2,1)} %collective-permute-done.20.refs_19_), channel_id=1, source_target_pairs={{0,4},{2,6},{8,0},{10,2},{16,8},{18,10},{24,16},{26,18},{28,24},{3... | collective-permute-start | bytes 1572872 | tf_op jit(solution)/shard_map/ppermute | solution.py:75
  48.4 9.7 %collective-permute-start.26 = (bf16[128,2048]{1,0:T(8,128)(2,1)S(1)}, bf16[128,2048]{1,0:T(8,128)(2,1)S(1)}, u32[]{:S(2)}, u32[]{:S(2)}) collective-permute-start(bf16[128,2048]{1,0:T(8,128)(2,1)S(1)} %copy-done.19), channel_id=1, source_target_pairs={{0,2},{2,0},{4,6},{6,4},{8,10},{10,8},{12,14},{14,12},{16,18},{18,... | collective-permute-start | bytes 1572872 | tf_op jit(solution)/shard_map/ppermute | solution.py:79
  48.5 9.7 %collective-permute-start.12 = (bf16[128,2048]{1,0:T(8,128)(2,1)S(1)}, bf16[128,2048]{1,0:T(8,128)(2,1)S(1)}, u32[]{:S(2)}, u32[]{:S(2)}) collective-permute-start(bf16[128,2048]{1,0:T(8,128)(2,1)S(1)} %copy-done.5), channel_id=1, source_target_pairs={{0,2},{2,0},{4,6},{6,4},{8,10},{10,8},{12,14},{14,12},{16,18},{18,... | collective-permute-start | bytes 1572872 | tf_op jit(solution)/shard_map/ppermute | solution.py:78
  49.0 9.7 %collective-permute-start.27 = (bf16[128,2048]{1,0:T(8,128)(2,1)}, bf16[128,2048]{1,0:T(8,128)(2,1)S(1)}, u32[]{:S(2)}, u32[]{:S(2)}) collective-permute-start(bf16[128,2048]{1,0:T(8,128)(2,1)} %collective-permute-done.19.refs_18_), channel_id=1, source_target_pairs={{0,2},{2,0},{4,6},{6,4},{8,10},{10,8},{12,14},{14,12},{16,18},{18,... | collective-permute-start | bytes 1572872 | tf_op jit(solution)/shard_map/ppermute | solution.py:79
  55.8 12.1 %collective-permute-start.7 = (bf16[128,2048]{1,0:T(8,128)(2,1)}, bf16[128,2048]{1,0:T(8,128)(2,1)}, u32[]{:S(2)}, u32[]{:S(2)}) collective-permute-start(bf16[128,2048]{1,0:T(8,128)(2,1)} %collective-permute-done.6.refs_4_), channel_id=1, source_target_pairs={{0,8},{2,10},{8,16},{10,18},{16,24},{18,26},{24,28},{26,30},{28,20... | collective-permute-start | bytes 1572872 | tf_op jit(solution)/shard_map/ppermute | solution.py:74
  57.0 12.1 %collective-permute-start.22 = (bf16[128,2048]{1,0:T(8,128)(2,1)}, bf16[128,2048]{1,0:T(8,128)(2,1)}, u32[]{:S(2)}, u32[]{:S(2)}) collective-permute-start(bf16[128,2048]{1,0:T(8,128)(2,1)} %collective-permute-done.21.refs_20_), channel_id=1, source_target_pairs={{0,4},{2,6},{8,0},{10,2},{16,8},{18,10},{24,16},{26,18},{28,24},{3... | collective-permute-start | bytes 1572872 | tf_op jit(solution)/shard_map/ppermute | solution.py:75
  58.1 16.8 %collective-permute-start.13 = (bf16[128,2048]{1,0:T(8,128)(2,1)}, bf16[128,2048]{1,0:T(8,128)(2,1)}, u32[]{:S(2)}, u32[]{:S(2)}) collective-permute-start(bf16[128,2048]{1,0:T(8,128)(2,1)} %collective-permute-done.5.refs_3_), channel_id=1, source_target_pairs={{0,2},{2,0},{4,6},{6,4},{8,10},{10,8},{12,14},{14,12},{16,18},{18,... | collective-permute-start | bytes 1572872 | tf_op jit(solution)/shard_map/ppermute | solution.py:78
  58.2 16.8 %collective-permute-start.28 = (bf16[128,2048]{1,0:T(8,128)(2,1)}, bf16[128,2048]{1,0:T(8,128)(2,1)}, u32[]{:S(2)}, u32[]{:S(2)}) collective-permute-start(bf16[128,2048]{1,0:T(8,128)(2,1)} %collective-permute-done.20.refs_19_), channel_id=1, source_target_pairs={{0,2},{2,0},{4,6},{6,4},{8,10},{10,8},{12,14},{14,12},{16,18},{18,... | collective-permute-start | bytes 1572872 | tf_op jit(solution)/shard_map/ppermute | solution.py:79
  58.7 16.8 %collective-permute-start.14 = (bf16[128,2048]{1,0:T(8,128)(2,1)}, bf16[128,2048]{1,0:T(8,128)(2,1)}, u32[]{:S(2)}, u32[]{:S(2)}) collective-permute-start(bf16[128,2048]{1,0:T(8,128)(2,1)} %collective-permute-done.6.refs_4_), channel_id=1, source_target_pairs={{0,2},{2,0},{4,6},{6,4},{8,10},{10,8},{12,14},{14,12},{16,18},{18,... | collective-permute-start | bytes 1572872 | tf_op jit(solution)/shard_map/ppermute | solution.py:78
  67.9 10.7 %collective-permute-start.8 = (bf16[128,2048]{1,0:T(8,128)(2,1)}, bf16[128,2048]{1,0:T(8,128)(2,1)}, u32[]{:S(2)}, u32[]{:S(2)}) collective-permute-start(bf16[128,2048]{1,0:T(8,128)(2,1)} %collective-permute-done.7.refs_5_), channel_id=1, source_target_pairs={{0,8},{2,10},{8,16},{10,18},{16,24},{18,26},{24,28},{26,30},{28,20... | collective-permute-start | bytes 1572872 | tf_op jit(solution)/shard_map/ppermute | solution.py:74
  69.1 10.4 %collective-permute-start.23 = (bf16[128,2048]{1,0:T(8,128)(2,1)}, bf16[128,2048]{1,0:T(8,128)(2,1)}, u32[]{:S(2)}, u32[]{:S(2)}) collective-permute-start(bf16[128,2048]{1,0:T(8,128)(2,1)} %collective-permute-done.22.refs_21_), channel_id=1, source_target_pairs={{0,4},{2,6},{8,0},{10,2},{16,8},{18,10},{24,16},{26,18},{28,24},{3... | collective-permute-start | bytes 1572872 | tf_op jit(solution)/shard_map/ppermute | solution.py:75
  75.0 9.6 %collective-permute-start.29 = (bf16[128,2048]{1,0:T(8,128)(2,1)}, bf16[128,2048]{1,0:T(8,128)(2,1)}, u32[]{:S(2)}, u32[]{:S(2)}) collective-permute-start(bf16[128,2048]{1,0:T(8,128)(2,1)} %collective-permute-done.21.refs_20_), channel_id=1, source_target_pairs={{0,2},{2,0},{4,6},{6,4},{8,10},{10,8},{12,14},{14,12},{16,18},{18,... | collective-permute-start | bytes 1572872 | tf_op jit(solution)/shard_map/ppermute | solution.py:79
  75.0 10.5 %collective-permute-start.15 = (bf16[128,2048]{1,0:T(8,128)(2,1)}, bf16[128,2048]{1,0:T(8,128)(2,1)}, u32[]{:S(2)}, u32[]{:S(2)}) collective-permute-start(bf16[128,2048]{1,0:T(8,128)(2,1)} %collective-permute-done.7.refs_5_), channel_id=1, source_target_pairs={{0,2},{2,0},{4,6},{6,4},{8,10},{10,8},{12,14},{14,12},{16,18},{18,... | collective-permute-start | bytes 1572872 | tf_op jit(solution)/shard_map/ppermute | solution.py:78
  75.5 10.0 %collective-permute-start.30 = (bf16[128,2048]{1,0:T(8,128)(2,1)}, bf16[128,2048]{1,0:T(8,128)(2,1)}, u32[]{:S(2)}, u32[]{:S(2)}) collective-permute-start(bf16[128,2048]{1,0:T(8,128)(2,1)} %collective-permute-done.22.refs_21_), channel_id=1, source_target_pairs={{0,2},{2,0},{4,6},{6,4},{8,10},{10,8},{12,14},{14,12},{16,18},{18,... | collective-permute-start | bytes 1572872 | tf_op jit(solution)/shard_map/ppermute | solution.py:79
  78.6 11.6 %collective-permute-start.9 = (bf16[128,2048]{1,0:T(8,128)(2,1)}, bf16[128,2048]{1,0:T(8,128)(2,1)}, u32[]{:S(2)}, u32[]{:S(2)}) collective-permute-start(bf16[128,2048]{1,0:T(8,128)(2,1)} %collective-permute-done.8.refs_6_), channel_id=1, source_target_pairs={{0,8},{2,10},{8,16},{10,18},{16,24},{18,26},{24,28},{26,30},{28,20... | collective-permute-start | bytes 1572872 | tf_op jit(solution)/shard_map/ppermute | solution.py:74
  79.5 11.6 %collective-permute-start.24 = (bf16[128,2048]{1,0:T(8,128)(2,1)}, bf16[128,2048]{1,0:T(8,128)(2,1)}, u32[]{:S(2)}, u32[]{:S(2)}) collective-permute-start(bf16[128,2048]{1,0:T(8,128)(2,1)} %collective-permute-done.23.refs_22_), channel_id=1, source_target_pairs={{0,4},{2,6},{8,0},{10,2},{16,8},{18,10},{24,16},{26,18},{28,24},{3... | collective-permute-start | bytes 1572872 | tf_op jit(solution)/shard_map/ppermute | solution.py:75
  84.6 26.7 %collective-permute-start.2 = (bf16[1024,256]{1,0:T(8,128)(2,1)}, bf16[1024,256]{1,0:T(8,128)(2,1)S(1)}, u32[]{:S(2)}, u32[]{:S(2)}) collective-permute-start(bf16[1024,256]{1,0:T(8,128)(2,1)} %param.17), channel_id=1, source_target_pairs={{0,1},{1,0},{2,3},{3,2},{4,5},{5,4},{6,7},{7,6},{8,9},{9,8},{10,11... | collective-permute-start | bytes 1572872 | tf_op jit(solution)/shard_map/ppermute | solution.py:62
  137.9 23.7 %collective-permute-start.39 = (bf16[1,512,512]{2,1,0:T(8,128)(2,1)S(1)}, bf16[1,512,512]{2,1,0:T(8,128)(2,1)S(1)}, u32[]{:S(2)}, u32[]{:S(2)}) collective-permute-start(bf16[1,512,512]{2,1,0:T(8,128)(2,1)S(1)} %get-tuple-element.50), channel_id=1, source_target_pairs={{0,2},{2,0},{4,6},{6,4},{8,10},{10,8},{12,14},{14,12},{16,18},{18,... | collective-permute-start | bytes 1572872 | tf_op jit(solution)/shard_map/ppermute | solution.py:528
  139.9 21.7 %collective-permute-start.40 = (bf16[1,512,512]{2,1,0:T(8,128)(2,1)S(1)}, bf16[1,512,512]{2,1,0:T(8,128)(2,1)S(1)}, u32[]{:S(2)}, u32[]{:S(2)}) collective-permute-start(bf16[1,512,512]{2,1,0:T(8,128)(2,1)S(1)} %get-tuple-element.51), channel_id=1, source_target_pairs={{0,4},{2,6},{4,0},{6,2},{8,12},{10,14},{12,8},{14,10},{16,20},{18,... | collective-permute-start | bytes 1572872 | tf_op jit(solution)/shard_map/ppermute | solution.py:530
  158.9 41.5 %collective-permute-start.36 = (bf16[1024,512]{1,0:T(8,128)(2,1)S(1)}, bf16[1024,512]{1,0:T(8,128)(2,1)S(1)}, u32[]{:S(2)}, u32[]{:S(2)}) collective-permute-start(bf16[1024,512]{1,0:T(8,128)(2,1)S(1)} %get-tuple-element.42), channel_id=1, source_target_pairs={{0,1},{1,0},{2,3},{3,2},{4,5},{5,4},{6,7},{7,6},{8,9},{9,8},{10,11... | collective-permute-start | bytes 3145736 | tf_op jit(solution)/shard_map/ppermute | solution.py:724
  162.4 14.0 %collective-permute-start.41 = (bf16[1,512,512]{2,1,0:T(8,128)(2,1)S(1)}, bf16[1,512,512]{2,1,0:T(8,128)(2,1)S(1)}, u32[]{:S(2)}, u32[]{:S(2)}) collective-permute-start(bf16[1,512,512]{2,1,0:T(8,128)(2,1)S(1)} %get-tuple-element.53), channel_id=1, source_target_pairs={{0,4},{2,6},{4,0},{6,2},{8,12},{10,14},{12,8},{14,10},{16,20},{18,... | collective-permute-start | bytes 1572872 | tf_op jit(solution)/shard_map/ppermute | solution.py:530
  163.1 15.1 %collective-permute-start.51 = (bf16[1,128,512]{2,1,0:T(8,128)(2,1)S(1)}, bf16[1,128,512]{2,1,0:T(8,128)(2,1)S(1)}, u32[]{:S(2)}, u32[]{:S(2)}) collective-permute-start(bf16[1,128,512]{2,1,0:T(8,128)(2,1)S(1)} %get-tuple-element.59), channel_id=1, source_target_pairs={{0,8},{2,10},{4,12},{6,14},{8,16},{10,18},{12,20},{14,22},{16,24},... | collective-permute-start | bytes 393224 | tf_op jit(solution)/shard_map/ppermute | solution.py:540
  165.7 15.5 %collective-permute-start.52 = (bf16[1,128,512]{2,1,0:T(8,128)(2,1)S(1)}, bf16[1,128,512]{2,1,0:T(8,128)(2,1)S(1)}, u32[]{:S(2)}, u32[]{:S(2)}) collective-permute-start(bf16[1,128,512]{2,1,0:T(8,128)(2,1)S(1)} %get-tuple-element.60), channel_id=1, source_target_pairs={{0,16},{2,18},{4,20},{6,22},{8,24},{10,26},{12,28},{14,30},{16,0},... | collective-permute-start | bytes 393224 | tf_op jit(solution)/shard_map/ppermute | solution.py:540
  167.2 15.4 %collective-permute-start.53 = (bf16[1,128,512]{2,1,0:T(8,128)(2,1)S(1)}, bf16[1,128,512]{2,1,0:T(8,128)(2,1)S(1)}, u32[]{:S(2)}, u32[]{:S(2)}) collective-permute-start(bf16[1,128,512]{2,1,0:T(8,128)(2,1)S(1)} %get-tuple-element.61), channel_id=1, source_target_pairs={{0,24},{2,26},{4,28},{6,30},{8,0},{10,2},{12,4},{14,6},{16,8},{18,... | collective-permute-start | bytes 393224 | tf_op jit(solution)/shard_map/ppermute | solution.py:540
  178.2 17.7 %collective-permute-start.43 = (bf16[1,128,512]{2,1,0:T(8,128)(2,1)S(1)}, bf16[1,128,512]{2,1,0:T(8,128)(2,1)S(1)}, u32[]{:S(2)}, u32[]{:S(2)}) collective-permute-start(bf16[1,128,512]{2,1,0:T(8,128)(2,1)S(1)} %get-tuple-element.56), channel_id=1, source_target_pairs={{0,16},{2,18},{4,20},{6,22},{8,24},{10,26},{12,28},{14,30},{16,0},... | collective-permute-start | bytes 393224 | tf_op jit(solution)/shard_map/ppermute | solution.py:540
  181.2 15.6 %collective-permute-start.44 = (bf16[1,128,512]{2,1,0:T(8,128)(2,1)S(1)}, bf16[1,128,512]{2,1,0:T(8,128)(2,1)S(1)}, u32[]{:S(2)}, u32[]{:S(2)}) collective-permute-start(bf16[1,128,512]{2,1,0:T(8,128)(2,1)S(1)} %get-tuple-element.57), channel_id=1, source_target_pairs={{0,24},{2,26},{4,28},{6,30},{8,0},{10,2},{12,4},{14,6},{16,8},{18,... | collective-permute-start | bytes 393224 | tf_op jit(solution)/shard_map/ppermute | solution.py:540
  182.6 17.2 %collective-permute-start.56 = (bf16[1,128,512]{2,1,0:T(8,128)(2,1)S(1)}, bf16[1,128,512]{2,1,0:T(8,128)(2,1)S(1)}, u32[]{:S(2)}, u32[]{:S(2)}) collective-permute-start(bf16[1,128,512]{2,1,0:T(8,128)(2,1)S(1)} %add_convert_fusion.refs_0_), channel_id=1, source_target_pairs={{0,24},{2,26},{4,28},{6,30},{8,0},{10,2},{12,4},{14,6},{16,8},{18,... | collective-permute-start | bytes 393224 | tf_op jit(solution)/shard_map/ppermute | solution.py:546
  185.3 23.6 %collective-permute-start.55 = (bf16[1,128,512]{2,1,0:T(8,128)(2,1)S(1)}, bf16[1,128,512]{2,1,0:T(8,128)(2,1)S(1)}, u32[]{:S(2)}, u32[]{:S(2)}) collective-permute-start(bf16[1,128,512]{2,1,0:T(8,128)(2,1)S(1)} %add_convert_fusion.refs_0_), channel_id=1, source_target_pairs={{0,16},{2,18},{4,20},{6,22},{8,24},{10,26},{12,28},{14,30},{16,0},... | collective-permute-start | bytes 393224 | tf_op jit(solution)/shard_map/ppermute | solution.py:546
  195.9 13.1 %collective-permute-start.54 = (bf16[1,128,512]{2,1,0:T(8,128)(2,1)S(1)}, bf16[1,128,512]{2,1,0:T(8,128)(2,1)S(1)}, u32[]{:S(2)}, u32[]{:S(2)}) collective-permute-start(bf16[1,128,512]{2,1,0:T(8,128)(2,1)S(1)} %add_convert_fusion.refs_0_), channel_id=1, source_target_pairs={{0,8},{2,10},{4,12},{6,14},{8,16},{10,18},{12,20},{14,22},{16,24},... | collective-permute-start | bytes 393224 | tf_op jit(solution)/shard_map/ppermute | solution.py:546
  196.8 13.3 %collective-permute-start.47 = (bf16[1,128,512]{2,1,0:T(8,128)(2,1)S(1)}, bf16[1,128,512]{2,1,0:T(8,128)(2,1)S(1)}, u32[]{:S(2)}, u32[]{:S(2)}) collective-permute-start(bf16[1,128,512]{2,1,0:T(8,128)(2,1)S(1)} %add_convert_fusion.1.refs_0_), channel_id=1, source_target_pairs={{0,24},{2,26},{4,28},{6,30},{8,0},{10,2},{12,4},{14,6},{16,8},{18,... | collective-permute-start | bytes 393224 | tf_op jit(solution)/shard_map/ppermute | solution.py:546
  199.8 14.6 %collective-permute-start.46 = (bf16[1,128,512]{2,1,0:T(8,128)(2,1)S(1)}, bf16[1,128,512]{2,1,0:T(8,128)(2,1)S(1)}, u32[]{:S(2)}, u32[]{:S(2)}) collective-permute-start(bf16[1,128,512]{2,1,0:T(8,128)(2,1)S(1)} %add_convert_fusion.1.refs_0_), channel_id=1, source_target_pairs={{0,16},{2,18},{4,20},{6,22},{8,24},{10,26},{12,28},{14,30},{16,0},... | collective-permute-start | bytes 393224 | tf_op jit(solution)/shard_map/ppermute | solution.py:546
  200.4 14.0 %collective-permute-start.45 = (bf16[1,128,512]{2,1,0:T(8,128)(2,1)S(1)}, bf16[1,128,512]{2,1,0:T(8,128)(2,1)S(1)}, u32[]{:S(2)}, u32[]{:S(2)}) collective-permute-start(bf16[1,128,512]{2,1,0:T(8,128)(2,1)S(1)} %add_convert_fusion.1.refs_0_), channel_id=1, source_target_pairs={{0,8},{2,10},{4,12},{6,14},{8,16},{10,18},{12,20},{14,22},{16,24},... | collective-permute-start | bytes 393224 | tf_op jit(solution)/shard_map/ppermute | solution.py:546
  210.1 14.6 %collective-permute-start.57 = (bf16[4,1,128,512]{3,2,1,0:T(8,128)(2,1)S(1)}, bf16[4,1,128,512]{3,2,1,0:T(8,128)(2,1)S(1)}, u32[]{:S(2)}, u32[]{:S(2)}) collective-permute-start(bf16[4,1,128,512]{3,2,1,0:T(8,128)(2,1)S(1)} %stack_pieces.3.refs_0_), channel_id=1, source_target_pairs={{0,4},{2,6},{4,0},{6,2},{8,12},{10,14},{12,8},{14,10},{16,20},{18,... | collective-permute-start | bytes 1572872 | tf_op jit(solution)/shard_map/ppermute | solution.py:548
  214.4 17.7 %collective-permute-start.48 = (bf16[4,1,128,512]{3,2,1,0:T(8,128)(2,1)S(1)}, bf16[4,1,128,512]{3,2,1,0:T(8,128)(2,1)S(1)}, u32[]{:S(2)}, u32[]{:S(2)}) collective-permute-start(bf16[4,1,128,512]{3,2,1,0:T(8,128)(2,1)S(1)} %stack_pieces.2.refs_0_), channel_id=1, source_target_pairs={{0,4},{2,6},{4,0},{6,2},{8,12},{10,14},{12,8},{14,10},{16,20},{18,... | collective-permute-start | bytes 1572872 | tf_op jit(solution)/shard_map/ppermute | solution.py:548
  214.6 17.7 %collective-permute-start.58 = (bf16[4,1,128,512]{3,2,1,0:T(8,128)(2,1)S(1)}, bf16[4,1,128,512]{3,2,1,0:T(8,128)(2,1)S(1)}, u32[]{:S(2)}, u32[]{:S(2)}) collective-permute-start(bf16[4,1,128,512]{3,2,1,0:T(8,128)(2,1)S(1)} %stack_pieces.3.refs_0_), channel_id=1, source_target_pairs={{0,2},{2,0},{4,6},{6,4},{8,10},{10,8},{12,14},{14,12},{16,18},{18,... | collective-permute-start | bytes 1572872 | tf_op jit(solution)/shard_map/ppermute | solution.py:549
  224.7 10.7 %collective-permute-start.49 = (bf16[4,1,128,512]{3,2,1,0:T(8,128)(2,1)S(1)}, bf16[4,1,128,512]{3,2,1,0:T(8,128)(2,1)}, u32[]{:S(2)}, u32[]{:S(2)}) collective-permute-start(bf16[4,1,128,512]{3,2,1,0:T(8,128)(2,1)S(1)} %stack_pieces.2.refs_0_), channel_id=1, source_target_pairs={{0,2},{2,0},{4,6},{6,4},{8,10},{10,8},{12,14},{14,12},{16,18},{18,... | collective-permute-start | bytes 1572872 | tf_op jit(solution)/shard_map/ppermute | solution.py:549
  (43 other events, 635.5 us)

commit v4 on v3

--- a/solution.py
+++ b/solution.py
@@ -19,11 +19,10 @@
 
 bf16 = jnp.bfloat16
 f32 = jnp.float32
-VMEM_BYTES = 48 * 1024 * 1024
-
-
-def params(**kw):
-    return pltpu.CompilerParams(vmem_limit_bytes=VMEM_BYTES, **kw)
+
+
+def params(mebibytes=32):
+    return pltpu.CompilerParams(vmem_limit_bytes=mebibytes * 1024 * 1024)
 
 
 def contract(a, b, da, db):
@@ -168,7 +167,7 @@
             scratch_shapes=[pltpu.VMEM((count, feat, degree * block_len), bf16)] * 2 + [pltpu.SemaphoreType.DMA((2,))],
         ),
         out_shape=jax.ShapeDtypeStruct((count * block_len, feat), bf16),
-        compiler_params=params(),
+        compiler_params=params(56),
         cost_estimate=pl.CostEstimate(
             flops=4 * count * block_len * degree * block_len * feat,
             bytes_accessed=2 * count * feat * block_len * (2 * degree + 2),
@@ -176,6 +175,16 @@
         ),
         name="attention",
     )(*[t[call] for t in tables], queries, *keys, *values)
+
+
+def place_of(part, line, lines):
+    differ = jnp.bitwise_xor(part, line)
+    place = 0
+    step = 1
+    while step < lines:
+        place = place * 2 + jnp.bitwise_and(lax.div(differ, step), 1)
+        step *= 2
+    return place
 
 
 def window_base(starts, i, e):
@@ -203,7 +212,7 @@
     return jnp.concatenate([one_hot(rank[e : e + 1, :], window_base(starts, i, e)) for e in range(first, first + count)], 0)
 
 
-def group_kernel(first, count, pieces, chunk, lines, owners, counts, ids, perm, starts, order, line, *refs):
+def group_kernel(first, count, pieces, after, chunk, lines, owners, counts, ids, perm, starts, order, place, *refs):
     refs = list(refs)
     rank_ref, cot_ref, gain_ref, router_ref, win_ref, wout_ref, rcol_ref = [refs.pop(0) for _ in range(7)]
     if pieces:
@@ -214,7 +223,7 @@
     else:
         stream_ref = refs.pop(0)
         partial_refs = [refs.pop(0) for _ in range(owners)]
-        refs.pop(0)
+        del refs[: after]
     if pieces:
         out_stream = refs.pop(0)
     out_refs = [refs.pop(0) for _ in range(owners)]
@@ -226,7 +235,7 @@
     def _():
         slots[...] = jnp.zeros_like(slots)
 
-        def place(i, carry):
+        def dispatch(i, carry):
             at = pl.ds(pl.multiple_of(i * chunk, chunk), chunk)
             if pieces:
                 projected = jnp.dot(atts[0][at, :], projs[0][...], preferred_element_type=f32)
@@ -262,7 +271,7 @@
 
             return carry
 
-        lax.fori_loop(0, nodes // chunk, place, 0)
+        lax.fori_loop(0, nodes // chunk, dispatch, 0)
 
     e = step + first
     tiles = (counts[e] + TILE - 1) // TILE
@@ -302,24 +311,33 @@
     lax.fori_loop(0, tiles, one, 0)
 
     ff = acc_in.shape[1]
-    part = 2 * width // lines
-
-    def write(grad_ref):
+
+    def write(grad_ref, with_in, with_out):
+        part = grad_ref.shape[1] // lines
         for p in range(lines):
-            where = lax.rem(p - line[0] + lines, lines)
-            at = pl.ds(pl.multiple_of(where * part, part), part)
+            at = pl.ds(pl.multiple_of(place_of(p, place[0], lines) * part, part), part)
             low = p * part
-            if low < width:
+            if with_in and low < width:
                 grad_ref[0, at, :] = acc_in[low : low + part, :].astype(bf16)
             else:
-                low = low - width
+                low = low - width if with_in else low
                 for j in range(ff // width):
                     cols = slice(j * width, (j + 1) * width)
                     grad_ref[0, at, cols] = acc_out[j * width + low : j * width + low + part, :].astype(bf16)
 
-    each = count // len(grad_refs)
-    for k, grad_ref in enumerate(grad_refs):
-        pl.when((step >= k * each) & (step < (k + 1) * each))(functools.partial(write, grad_ref))
+    if count > 2:
+        each = count // 4
+        for k, grad_ref in enumerate(grad_refs):
+            pl.when((step >= k * each) & (step < (k + 1) * each))(functools.partial(write, grad_ref, True, True))
+    else:
+        for k in range(2):
+            for column in range(2):
+
+                @pl.when((step == k) & (place[1] == column))
+                def _(k=k, column=column):
+                    other, own = grad_refs[2 * k], grad_refs[2 * k + 1]
+                    write((own, other)[column], True, False)
+                    write((other, own)[column], False, True)
 
     @pl.when(step == count - 1)
     def _():
@@ -355,7 +373,7 @@
 
 
 def expert_group(scalars, common, weights, first, count, head, tail, lines, slot_rows, chunk):
-    counts, ids, perm, starts, order, line = scalars
+    counts, ids, perm, starts, order, place = scalars
     rank, cotangent, gain, router = common
     w_in, w_out, columns = weights
     nodes, width = cotangent.shape
@@ -374,20 +392,19 @@
         pieces = len(atts)
     else:
         stream, partials, after = tail
-        extra = [stream, *partials, after]
-        specs += [whole(stream)] + [whole(p) for p in partials] + [pl.BlockSpec(memory_space=pl.ANY)]
+        extra = [stream, *partials, *after]
+        specs += [whole(stream)] + [whole(p) for p in partials] + [pl.BlockSpec(memory_space=pl.ANY)] * len(after)
         pieces = 0
     out_shape += [jax.ShapeDtypeStruct((nodes // owners, 2 * width), bf16)] * owners
     out_specs = [pl.BlockSpec(o.shape, lambda i, *_: (0, 0)) for o in out_shape]
-    parts = 4 if count % 4 == 0 else count
-    each = count // parts
-    out_shape += [jax.ShapeDtypeStruct((each, 2 * width, ff), bf16)] * parts
-    for k in range(parts):
-        out_specs.append(
-            pl.BlockSpec((1, 2 * width, ff), lambda i, *_, k=k: (jnp.clip(i - k * each, 0, each - 1), 0, 0))
-        )
+    each = max(1, count // 4)
+    block = (1, 2 * width if count > 2 else width, ff)
+    out_shape += [jax.ShapeDtypeStruct((each,) + block[1:], bf16)] * 4
+    for k in range(4):
+        first_step = k * each if count > 2 else k // 2
+        out_specs.append(pl.BlockSpec(block, lambda i, *_, at=first_step: (jnp.clip(i - at, 0, each - 1), 0, 0)))
     return pl.pallas_call(
-        functools.partial(group_kernel, first, count, pieces, chunk, lines, owners),
+        functools.partial(group_kernel, first, count, pieces, 0 if head else len(after), chunk, lines, owners),
         grid_spec=pltpu.PrefetchScalarGridSpec(
             num_scalar_prefetch=6,
             grid=(count,),
@@ -404,7 +421,7 @@
         compiler_params=params(),
         cost_estimate=pl.CostEstimate(flops=1000, bytes_accessed=1000, transcendentals=0),
         name="experts",
-    )(counts, ids, perm, starts, order, line, *args, *extra)
+    )(counts, ids, perm, starts, order, place, *args, *extra)
 
 
 def home_kernel(parts, stream_ref, cot_ref, gain_ref, *refs):
@@ -422,12 +439,12 @@
     grad_ref[...] = grad.astype(bf16)
 
 
-def at_home(me, stream, cotangent, gain, parts, chunk):
+def at_home(me, stream, cotangent, gain, parts, chunk, after):
     tok_dev, width = cotangent.shape
     steps = tok_dev // chunk
     fresh = lambda w: pl.BlockSpec((chunk, w), lambda i, me: (i, 0))
     return pl.pallas_call(
-        lambda me, *refs: home_kernel(len(parts), *refs),
+        lambda me, *refs: home_kernel(len(parts), *refs[:-3], *refs[-2:]),
         grid_spec=pltpu.PrefetchScalarGridSpec(
             num_scalar_prefetch=1,
             grid=(steps,),
@@ -436,7 +453,8 @@
                 fresh(width),
                 pl.BlockSpec(gain.shape, lambda i, me: (0, 0)),
             ]
-            + [fresh(2 * width) for _ in parts],
+            + [fresh(2 * width) for _ in parts]
+            + [pl.BlockSpec(memory_space=pl.ANY)],
             out_specs=[fresh(width), fresh(width)],
         ),
         out_shape=[jax.ShapeDtypeStruct((tok_dev, width), bf16)] * 2,
@@ -445,12 +463,11 @@
             flops=EAGER * tok_dev * width * 1000, bytes_accessed=tok_dev * width * 16, transcendentals=0
         ),
         name="at_home",
-    )(me.reshape(1), stream, cotangent, gain, *parts)
+    )(me.reshape(1), stream, cotangent, gain, *parts, after)
 
 
 def line_pairs(seq_count, d):
-    lines = seq_count // 4
-    return [(z * 4 + r, ((z + d) % lines) * 4 + r) for z in range(lines) for r in range(4)]
+    return [(z * 4 + r, (z ^ d) * 4 + r) for z in range(seq_count // 4) for r in range(4)]
 
 
 def seq_place():
@@ -458,61 +475,49 @@
     return s % 2, (s // 2) % 2, s // 4
 
 
-def add_bf16(*terms):
-    total = terms[0].astype(f32)
-    for t in terms[1:]:
-        total = total + t.astype(f32)
-    return total.astype(bf16)
-
-
-def token_spec():
-    return pl.BlockSpec((8, 128), lambda i: (0, 0)), jax.ShapeDtypeStruct((8, 128), f32)
-
-
 def sum_kernel(terms, cuts, *refs):
-    outs = refs[-1 - cuts : -1]
     total = refs[0][...].astype(f32)
     for r in refs[1:terms]:
         total = total + r[...].astype(f32)
     total = total.astype(bf16)
     part = total.shape[1] // cuts
-    for k, out in enumerate(outs):
+    for k, out in enumerate(refs[len(refs) - cuts :]):
         out[...] = total[:, k * part : (k + 1) * part]
-    refs[-1][...] = jnp.zeros_like(refs[-1])
 
 
 def sum_blocks(terms, cuts, after, name):
     shape = terms[0].shape
     whole = lambda s: pl.BlockSpec(s, lambda i: (0, 0, 0))
     piece = (shape[0], shape[1] // cuts, shape[2])
-    token, token_shape = token_spec()
-    found = pl.pallas_call(
+    return pl.pallas_call(
         functools.partial(sum_kernel, len(terms), cuts),
         grid=(1,),
         in_specs=[whole(shape)] * len(terms) + [pl.BlockSpec(memory_space=pl.ANY)] * len(after),
-        out_specs=[whole(piece)] * cuts + [token],
-        out_shape=[jax.ShapeDtypeStruct(piece, bf16)] * cuts + [token_shape],
-        compiler_params=params(),
+        out_specs=[whole(piece)] * cuts,
+        out_shape=[jax.ShapeDtypeStruct(piece, bf16)] * cuts,
+        compiler_params=params(16),
         cost_estimate=pl.CostEstimate(flops=1000, bytes_accessed=1000, transcendentals=0),
         name=name,
     )(*terms, *after)
-    return found[:-1], found[-1]
 
 
 def stack_kernel(count, *refs):
+    rows = refs[0].shape[0]
     for k in range(count):
-        refs[-1][k] = refs[k][...]
+        refs[-1][k * rows : (k + 1) * rows] = refs[k][...]
 
 
 def stack_pieces(pieces, after):
     shape = pieces[0].shape
+    whole = lambda s: pl.BlockSpec(s, lambda i: (0, 0, 0, 0))
+    stacked = (len(pieces) * shape[0],) + shape[1:]
     return pl.pallas_call(
         functools.partial(stack_kernel, len(pieces)),
         grid=(1,),
-        in_specs=[pl.BlockSpec(shape, lambda i: (0, 0, 0))] * len(pieces) + [pl.BlockSpec(memory_space=pl.ANY)] * len(after),
-        out_specs=pl.BlockSpec((len(pieces),) + shape, lambda i: (0, 0, 0, 0)),
-        out_shape=jax.ShapeDtypeStruct((len(pieces),) + shape, bf16),
-        compiler_params=params(),
+        in_specs=[whole(shape)] * len(pieces) + [pl.BlockSpec(memory_space=pl.ANY)] * len(after),
+        out_specs=whole(stacked),
+        out_shape=jax.ShapeDtypeStruct(stacked, bf16),
+        compiler_params=params(16),
         cost_estimate=pl.CostEstimate(flops=1000, bytes_accessed=1000, transcendentals=0),
         name="stack_pieces",
     )(*pieces, *after)
@@ -521,108 +526,122 @@
 class SeqSum:
     def __init__(self, grads, seq_count):
         self.grads, self.seq_count, self.lines = grads, seq_count, seq_count // 4
-        self.sib = sibling_pairs(seq_count)
         self.cross = [(i, i ^ 2) for i in range(seq_count)]
+        self.got = [self.to_sibling(g) for g in grads[:2]]
+        bits = self.lines.bit_length() - 1
+        self.left = [self.over_core, self.over_x]
+        self.left += [functools.partial(self.over_line, 1 << k) for k in range(bits)]
+        self.left += [functools.partial(self.back_line, 1 << k) for k in reversed(range(bits))]
+
+    def step(self, after):
+        return [self.left.pop(0)(after)]
+
+    def to_sibling(self, x):
+        return lax.ppermute(x, "seq", sibling_pairs(self.seq_count))
+
+    def to_line(self, x, step):
+        return lax.ppermute(x, "seq", line_pairs(self.seq_count, step))
 
     def over_core(self, after):
-        self.got = [lax.ppermute(g, "seq", self.sib) for g in self.grads[:2]]
-        (first,), token = sum_blocks([self.grads[2], self.got[0]], 1, after, "sum_core")
+        (first,) = sum_blocks([self.grads[2], self.got[0]], 1, after, "sum_core")
         self.crossed = lax.ppermute(first, "seq", self.cross)
-        return token
-
-    def over_x(self):
-        self.parts, token = sum_blocks([self.grads[3], self.got[1], self.crossed], self.lines, [], "sum_x")
-        return token
-
-    def over_lines(self):
-        shard = self.parts[0].astype(f32)
-        for d in range(1, self.lines):
-            shard = shard + lax.ppermute(self.parts[d], "seq", line_pairs(self.seq_count, d)).astype(f32)
-        self.shard = shard.astype(bf16)
-
-    def back(self, after):
-        pieces = [self.shard]
-        for d in range(1, self.lines):
-            pieces.append(lax.ppermute(self.shard, "seq", line_pairs(self.seq_count, d)))
-        own = stack_pieces(pieces, after)
-        other = lax.ppermute(own, "seq", self.cross)
-        return [own, other, lax.ppermute(own, "seq", self.sib), lax.ppermute(other, "seq", self.sib)]
-
-
-def unpack_kernel(lines, each, width, where, line, *refs):
-    win_ref, wout_ref = refs[-2:]
+        return first
+
+    def over_x(self, after):
+        self.kept, sent = sum_blocks([self.grads[3], self.got[1], self.crossed], 2, after, "sum_x")
+        self.arriving = self.to_line(sent, 1)
+        return sent
+
+    def over_line(self, step, after):
+        if 2 * step < self.lines:
+            self.kept, sent = sum_blocks([self.kept, self.arriving], 2, after, "sum_line")
+            self.arriving = self.to_line(sent, 2 * step)
+            return sent
+        (shard,) = sum_blocks([self.kept, self.arriving], 1, after, "sum_line")
+        self.own = shard[None]
+        self.arriving = self.to_line(self.own, step)
+        return shard
+
+    def back_line(self, step, after):
+        self.own = stack_pieces([self.own, self.arriving], after)
+        if step > 1:
+            self.arriving = self.to_line(self.own, step // 2)
+        else:
+            self.other = lax.ppermute(self.own, "seq", self.cross)
+        return self.own
+
+    def blocks(self, after):
+        other = stack_pieces([self.other], after) if after else self.other
+        return [self.own, other, self.to_sibling(self.own), self.to_sibling(other)]
+
+
+def step_order(sums):
+    left = [len(s.left) for s in sums]
+    order = []
+    while any(left):
+        for g in range(len(sums)):
+            if left[g]:
+                order.append(g)
+                left[g] -= 1
+    return order
+
+
+def unpack_kernel(lines, each, width, where, place, *refs):
+    win_ref, wout_ref, token_ref = refs[-3:]
+    token_ref[...] = jnp.zeros_like(token_ref)
     step = pl.program_id(0)
-    for a in range(4):
-        for i in range(each):
-
-            @pl.when(step == a * each + i)
-            def _(a=a, i=i):
-                for p in range(lines):
-                    block = refs[a][lax.rem(line[0] - p + lines, lines), i].astype(f32)
-                    part, ff = block.shape
-                    low = p * part
-                    if low < width:
-                        win_ref[0, low : low + part, :] = block
-                    else:
-                        low = low - width
-                        for j in range(ff // width):
-                            wout_ref[0, j * width + low : j * width + low + part, :] = block[:, j * width : (j + 1) * width]
-
-
-def unpack(where, line, blocks, experts, width, ff, into):
+
+    def read(ref, i, with_in, with_out):
+        for p in range(lines):
+            block = ref[place_of(p, place[0], lines), i].astype(f32)
+            part, ff = block.shape
+            low = p * part
+            if with_in and low < width:
+                win_ref[0, low : low + part, :] = block
+            else:
+                low = low - width if with_in else low
+                for j in range(ff // width):
+                    wout_ref[0, j * width + low : j * width + low + part, :] = block[:, j * width : (j + 1) * width]
+
+    if refs[0].shape[2] * lines > width:
+        for a in range(4):
+            for i in range(each):
+                pl.when(step == a * each + i)(functools.partial(read, refs[a], i, True, True))
+    else:
+        for k in range(2):
+            for column in range(2):
+
+                @pl.when((step == k) & (place[1] == column))
+                def _(k=k, column=column):
+                    own, other = refs[2 * k], refs[2 * k + 1]
+                    read((own, other)[column], 0, True, False)
+                    read((other, own)[column], 0, False, True)
+
+
+def unpack(where, place, blocks, experts, width, ff, into):
     lines, each = blocks[0].shape[:2]
     whole = pl.BlockSpec(blocks[0].shape, lambda i, *_: (0, 0, 0, 0))
-    out = lambda *shape: pl.BlockSpec((1,) + shape, lambda i, where, line: (where[i], 0, 0))
+    out = lambda *shape: pl.BlockSpec((1,) + shape, lambda i, where, place: (where[i], 0, 0))
     return pl.pallas_call(
         functools.partial(unpack_kernel, lines, each, width),
         grid_spec=pltpu.PrefetchScalarGridSpec(
             num_scalar_prefetch=2,
-            grid=(4 * each,),
+            grid=where.shape,
             in_specs=[whole] * 4 + [pl.BlockSpec(memory_space=pl.ANY)] * len(into),
-            out_specs=[out(width, ff), out(ff, width)],
+            out_specs=[out(width, ff), out(ff, width), pl.BlockSpec((8, 128), lambda i, *_: (0, 0))],
         ),
         out_shape=[
             jax.ShapeDtypeStruct((experts, width, ff), f32),
             jax.ShapeDtypeStruct((experts, ff, width), f32),
+            jax.ShapeDtypeStruct((8, 128), f32),
         ],
         input_output_aliases={6 + i: i for i in range(len(into))},
-        compiler_params=params(),
-        cost_estimate=pl.CostEstimate(flops=EAGER * 4 * each * 2 * width * ff * 6, bytes_accessed=4 * each * 2 * width * ff * 6, transcendentals=0),
+        compiler_params=params(16),
+        cost_estimate=pl.CostEstimate(
+            flops=EAGER * where.shape[0] * 2 * width * ff * 6, bytes_accessed=where.shape[0] * 2 * width * ff * 6, transcendentals=0
+        ),
         name="unpack",
-    )(where, line, *blocks, *into)
-
-
-def sum_any(grads, seq_count):
-    lines = seq_count // 4
-    core, column, line = seq_place()
-    sib = sibling_pairs(seq_count)
-    cross = [(i, i ^ 2) for i in range(seq_count)]
-
-    def halve(a, which, pairs):
-        h = a.shape[0] // 2
-        mine = lax.dynamic_slice_in_dim(a, which * h, h, 0)
-        other = lax.dynamic_slice_in_dim(a, (1 - which) * h, h, 0)
-        return add_bf16(mine, lax.ppermute(other, "seq", pairs))
-
-    a = halve(halve(grads, core, sib), column, cross)
-    q = a.shape[0] // lines
-    total = lax.dynamic_slice_in_dim(a, line * q, q, 0).astype(f32)
-    for d in range(1, lines):
-        part = lax.dynamic_slice_in_dim(a, lax.rem(line + d, lines) * q, q, 0)
-        total = total + lax.ppermute(part, "seq", line_pairs(seq_count, d)).astype(f32)
-    shard = total.astype(bf16)
-
-    out = jnp.zeros((q * lines,) + a.shape[1:], bf16)
-    out = lax.dynamic_update_slice_in_dim(out, shard, line * q, 0)
-    for d in range(1, lines):
-        got = lax.ppermute(shard, "seq", line_pairs(seq_count, d))
-        out = lax.dynamic_update_slice_in_dim(out, got, lax.rem(line - d + lines, lines) * q, 0)
-
-    def double(a, which, pairs):
-        got = lax.ppermute(a, "seq", pairs)
-        return jnp.where(which == 0, jnp.concatenate([a, got], 0), jnp.concatenate([got, a], 0))
-
-    return double(double(out, column, cross), core, sib)
+    )(where, place, *blocks, *into)
 
 
 def shards(
@@ -662,23 +681,23 @@
     cotangent_all = gather_expert_axis(cotangent, exp_count)
     ids_all = gather_expert_axis(expert_ids.T, exp_count, 1)
     gain = norm_gain.reshape(1, width)
-    core, column, line_at = seq_place()
+    core, column, line = seq_place()
     lines = seq_count // 4
-    line = line_at.reshape(1).astype(jnp.int32)
-    groups = 2 if experts % 8 == 0 else 1
-    per_group = experts // groups
-    tuned = per_group % 4 == 0 and (2 * width) % (16 * lines) == 0 and lines > 1
-    each = per_group // 4
-    at = jnp.arange(experts, dtype=jnp.int32)
-    first_of = lambda dest, i: at // per_group * per_group + dest * each + i
-    dests = jnp.stack([(1 - core) * 2 + 1 - column, (1 - core) * 2 + column, core * 2 + 1 - column, core * 2 + column])
-    outs = jnp.stack([core * 2 + column, core * 2 + 1 - column, (1 - core) * 2 + column, (1 - core) * 2 + 1 - column])
-    if tuned:
-        perm = first_of(jnp.tile(jnp.repeat(dests, each), groups), at % each).astype(jnp.int32)
-        where = first_of(jnp.tile(jnp.repeat(outs, each), groups), at % each).astype(jnp.int32)
-    else:
-        perm = at
-        line = jnp.zeros_like(line)
+    place = jnp.stack([line, column]).astype(jnp.int32)
+    groups = [4] * (experts // 4)
+    groups += [2] * ((experts - sum(groups)) // 2)
+    dests = [(1 - core, 1 - column), (1 - core, column), (core, 1 - column), (core, column)]
+    perm, wheres, first = [], [], 0
+    for count in groups:
+        if count == 4:
+            perm += [first + 2 * c + x for c, x in dests]
+            wheres.append([first + 2 * c + x for c, x in (dests[3], dests[2], dests[1], dests[0])])
+        else:
+            perm += [first + 1 - core, first + core]
+            wheres.append([first + core, first + 1 - core])
+        first += count
+    perm = jnp.stack(perm).astype(jnp.int32)
+    wheres = [jnp.stack(w).astype(jnp.int32) for w in wheres]
     local_ids = me * experts + perm
     hot = jnp.sum((ids_all[None, :, :] == local_ids[:, None, None]).astype(jnp.int32), 1)
     running = jnp.cumsum(hot, 1)
@@ -703,39 +722,33 @@
             pieces[d].append(lax.ppermute(part, "expert", shift_pairs(exp_count, d)))
     atts = [jnp.concatenate(p, 0) for p in pieces]
 
-    scalars = (counts, local_ids, perm, starts, owner_order, line)
+    scalars = (counts, local_ids, perm, starts, owner_order, place)
     common = (rank, cotangent_all, gain, router)
     weights = (expert_in, expert_out, columns)
-    into, sums, after, stream, partials = [], [], None, None, None
-    for g in range(groups):
+    sums, last, stream, partials, first = [], [], None, None, 0
+    for g, count in enumerate(groups):
         head = (residual_all, atts, projs) if g == 0 else None
-        tail = (stream, partials, after)
-        found = list(
-            expert_group(scalars, common, weights, g * per_group, per_group, head, tail, lines, slot_rows, chunk)
-        )
+        found = list(expert_group(scalars, common, weights, first, count, head, (stream, partials, last), lines, slot_rows, chunk))
+        first += count
         if g == 0:
             stream = found.pop(0)
         partials, grads = found[:exp_count], found[exp_count:]
-        if tuned:
-            sums.append(SeqSum(grads, seq_count))
-            after = sums[-1].over_core([sums[-2].over_x()] if g > 0 else [])
-        else:
-            into.append(sum_any(jnp.concatenate(grads, 0).reshape(per_group * 2 * width, ff), seq_count))
+        sums.append(SeqSum(grads, seq_count))
+        if g == 0:
+            last = sums[0].step(last)
     parts = partials[:1] + [lax.ppermute(partials[d], "expert", shift_pairs(exp_count, d)) for d in range(1, exp_count)]
-    layer_out, grad_stream = at_home(me, stream, cotangent, gain, parts, chunk)
-    if tuned:
-        sums[-1].over_x()
-        for g, each_sum in enumerate(sums):
-            each_sum.over_lines()
-            blocks = each_sum.back([layer_out] if g == 0 else [])
-            into = unpack(where[g * per_group : (g + 1) * per_group], line, blocks, experts, width, ff, into)
-    if tuned:
-        grad_w_in, grad_w_out = into
-    else:
-        total = jnp.concatenate(into, 0).reshape(experts, 2 * width, ff).astype(f32)
-        grad_w_in = total[:, :width, :]
-        grad_w_out = jnp.concatenate([total[:, width:, j * width : (j + 1) * width] for j in range(ff // width)], 1)
-
+    steps = step_order(sums)
+    for k, g in enumerate(steps):
+        last = sums[g].step(last)
+        if k == len(steps) // 2:
+            layer_out, grad_stream = at_home(me, stream, cotangent, gain, parts, chunk, last[0])
+            last = [layer_out]
+    into, token = [], []
+    for g, each_sum in enumerate(sums):
+        blocks = each_sum.blocks(token if g == len(sums) - 1 else [])
+        *into, done = unpack(wheres[g], place, blocks, experts, width, ff, into)
+        token = [done]
+    grad_w_in, grad_w_out = into
     return layer_out, grad_stream, grad_w_in, grad_w_out
 
 

time: 240 us -> 231 us (0.963)
  starting transfers between devices: 59.2 us -> 46.5 us
  waiting for transfers between devices: 97.5 us -> 102 us
    ppermute x22 -> x18, waiting for transfers between devices: 29.9 us -> 42 us  [the longest x8 29.4 us: to_line(): return lax.ppermute(x, 'seq', line_pairs(self.seq_count, step))]
    ppermute x22 -> x18, starting transfers between devices: 30.4 us -> 19.4 us  [the longest x8 17.6 us: to_line(): return lax.ppermute(x, 'seq', line_pairs(self.seq_count, step))]
    pallas_call x2, Pallas kernels: 14.1 us -> 17.2 us  [attention(): pl.pallas_call(functools.partial(attention_kernel, degree, feat // HD, le...]
    ppermute x2, waiting for transfers between devices: 7.79 us -> 4.76 us  [over_core(): self.crossed = lax.ppermute(first, 'seq', self.cross)]
    unnamed x65 -> x51, local copies, waits for them, and re-layouts: 6.48 us -> 3.47 us
    pallas_call x3, Pallas kernels: 34.9 us -> 32.1 us  [the longest x2 30.1 us: expert_group(): pl.pallas_call(functools.partial(group_kernel, first, count, pieces, 0 if...]
  transfers between devices with their start and end apart: 60 -> 56, of which waited for: 20 -> 24; matrix products, arithmetic and copies ran while one was open for 8% -> 10% of each run, Pallas kernels for 15% -> 17%
where the time goes in v4:
time: 231 us
  waiting for transfers between devices  102 us (44%)
  Pallas kernels  56.3 us (24%)
  starting transfers between devices  46.5 us (20%)
  local copies, waits for them, and re-layouts  15.9 us (7%)
  other arithmetic  8.15 us (4%)
    ppermute x7, waiting for transfers between devices, ring_gather(): k = lax.ppermute(k, 'seq', fwd)  47.2 us
    pallas_call x2, Pallas kernels, expert_group(): pl.pallas_call(functools.partial(group_kernel, first, count, pieces, 0 if...  30.1 us
    ppermute x8, waiting for transfers between devices, to_line(): return lax.ppermute(x, 'seq', line_pairs(self.seq_count, step))  29.4 us
    ppermute x8, starting transfers between devices, to_line(): return lax.ppermute(x, 'seq', line_pairs(self.seq_count, step))  17.6 us
    pallas_call x2, Pallas kernels, attention(): pl.pallas_call(functools.partial(attention_kernel, degree, feat // HD, le...  17.2 us
    ppermute x7, starting transfers between devices, ring_gather(): k = lax.ppermute(k, 'seq', fwd)  10.9 us
    ppermute x2, waiting for transfers between devices, back_line(): self.other = lax.ppermute(self.own, 'seq', self.cross)  9.41 us
    pallas_call x2, Pallas kernels, unpack(): pl.pallas_call(functools.partial(unpack_kernel, lines, each, width), grid...  6.08 us
  transfers between devices with their start and end apart: 56, of which 24 were waited for; matrix products, arithmetic and copies ran while one was open for 10% of the time, Pallas kernels for 17%

profile of v4, /device:TPU:0, one launch (start us, length us, event | category | flops | bytes accessed | tf_op | source)
XLA Modules:
  0.0 230.6 jit_solution(16148120506529481374)
XLA Ops:
  1.2 2.6 %collective-permute-start.3 = (bf16[128,2048]{1,0:T(8,128)(2,1)}, bf16[128,2048]{1,0:T(8,128)(2,1)}, u32[]{:S(2)}, u32[]{:S(2)}) collective-permute-start(bf16[128,2048]{1,0:T(8,128)(2,1)} %refs_0_.3), channel_id=1, source_target_pairs={{0,8},{2,10},{8,16},{10,18},{16,24},{18,26},{24,28},{26,30},{28,20... | collective-permute-start | bytes 1572872 | tf_op jit(solution)/shard_map/ppermute | solution.py:73
  3.8 1.5 collective-permute-start
  6.7 1.2 dynamic_slice.13
  9.6 6.9 %collective-permute-done.3.refs_1_ = bf16[128,2048]{1,0:T(8,128)(2,1)} collective-permute-done((bf16[128,2048]{1,0:T(8,128)(2,1)}, bf16[128,2048]{1,0:T(8,128)(2,1)}, u32[]{:S(2)}, u32[]{:S(2)}) %collective-permute-start.3) | collective-permute-done | bytes 524320 | tf_op jit(solution)/shard_map/ppermute | solution.py:73
  16.6 1.8 collective-permute-start.4
  20.3 10.1 %collective-permute-done.4.refs_2_ = bf16[128,2048]{1,0:T(8,128)(2,1)S(1)} collective-permute-done((bf16[128,2048]{1,0:T(8,128)(2,1)}, bf16[128,2048]{1,0:T(8,128)(2,1)S(1)}, u32[]{:S(2)}, u32[]{:S(2)}) %collective-permute-start.4) | collective-permute-done | bytes 524320 | tf_op jit(solution)/shard_map/ppermute | solution.py:73
  30.5 1.6 collective-permute-start.5
  34.0 9.4 %collective-permute-done.5.refs_3_ = bf16[128,2048]{1,0:T(8,128)(2,1)} collective-permute-done((bf16[128,2048]{1,0:T(8,128)(2,1)S(1)}, bf16[128,2048]{1,0:T(8,128)(2,1)}, u32[]{:S(2)}, u32[]{:S(2)}) %collective-permute-start.5) | collective-permute-done | bytes 524320 | tf_op jit(solution)/shard_map/ppermute | solution.py:73
  43.4 1.4 collective-permute-start.6
  47.2 1.2 constant_dynamic-update-slice_fusion.1
  49.1 6.5 %collective-permute-done.6.refs_4_ = bf16[128,2048]{1,0:T(8,128)(2,1)} collective-permute-done((bf16[128,2048]{1,0:T(8,128)(2,1)}, bf16[128,2048]{1,0:T(8,128)(2,1)}, u32[]{:S(2)}, u32[]{:S(2)}) %collective-permute-start.6) | collective-permute-done | bytes 524320 | tf_op jit(solution)/shard_map/ppermute | solution.py:73
  55.6 1.3 collective-permute-start.7
  60.2 7.5 %collective-permute-done.7.refs_5_ = bf16[128,2048]{1,0:T(8,128)(2,1)} collective-permute-done((bf16[128,2048]{1,0:T(8,128)(2,1)}, bf16[128,2048]{1,0:T(8,128)(2,1)}, u32[]{:S(2)}, u32[]{:S(2)}) %collective-permute-start.7) | collective-permute-done | bytes 524320 | tf_op jit(solution)/shard_map/ppermute | solution.py:73
  67.7 1.3 collective-permute-start.8
  70.0 3.8 %reduce-window.6 = s32[8,16,128]{2,1,0:T(8,128)} reduce-window(s32[8,16,128]{2,1,0:T(8,128)S(1)} %copy.43, s32[]{:T(128)} %constant.111.clone.1), window={size=1x1x128 pad=0_0x0_0x127_0}, to_apply=%region_1.2 | reduce-window | flops 2080768 | bytes 131076 | tf_op jit(solution)/shard_map/reduce-window
  74.4 4.1 %collective-permute-done.8.refs_6_ = bf16[128,2048]{1,0:T(8,128)(2,1)} collective-permute-done((bf16[128,2048]{1,0:T(8,128)(2,1)}, bf16[128,2048]{1,0:T(8,128)(2,1)}, u32[]{:S(2)}, u32[]{:S(2)}) %collective-permute-start.8) | collective-permute-done | bytes 524320 | tf_op jit(solution)/shard_map/ppermute | solution.py:73
  79.4 1.1 collective-permute-start.24
  80.5 1.1 slice_reduce_fusion
  86.7 2.6 %collective-permute-done.9.refs_7_ = bf16[128,2048]{1,0:T(8,128)(2,1)} collective-permute-done((bf16[128,2048]{1,0:T(8,128)(2,1)}, bf16[128,2048]{1,0:T(8,128)(2,1)}, u32[]{:S(2)}, u32[]{:S(2)}) %collective-permute-start.9) | collective-permute-done | bytes 524320 | tf_op jit(solution)/shard_map/ppermute | solution.py:73
  93.1 8.5 %attention.2 = bf16[1024,128]{1,0:T(8,128)(2,1)} custom-call(s32[32]{0:T(128)} %squeeze.37.local, s32[32]{0:T(128)} %get-tuple-element.75.korder, s32[17]{0:T(128)} %get-tuple-element.84.kbegin, s32[32]{0:T(128)} %get-tuple-element.73.vorder, s32[17]{0:T(128)} %get-tuple-element.60.vbegin, bf16[128,2048]{1,0:T(8,128)(2,1)} %q_ref.3, ...), custom_call_target="tpu_custom_call" | custom-call | flops 268435456 | bytes 2621440 | tf_op jit(solution)/shard_map/attention/pallas_call | solution.py:159
  101.6 1.6 collective-permute-start.33
  103.2 8.7 %attention.3 = bf16[1024,128]{1,0:T(8,128)(2,1)} custom-call(s32[32]{0:T(128)} %squeeze.43.local, s32[32]{0:T(128)} %get-tuple-element.76.korder, s32[17]{0:T(128)} %get-tuple-element.83.kbegin, s32[32]{0:T(128)} %get-tuple-element.74.vorder, s32[17]{0:T(128)} %get-tuple-element.61.vbegin, bf16[128,2048]{1,0:T(8,128)(2,1)} %q_ref.3, ...), custom_call_target="tpu_custom_call" | custom-call | flops 268435456 | bytes 2621440 | tf_op jit(solution)/shard_map/attention/pallas_call | solution.py:159
  112.5 1.1 constant_dynamic-update-slice_fusion.refs_7_
  114.6 5.6 %collective-permute-done.34 = bf16[1024,128]{1,0:T(8,128)(2,1)S(1)} collective-permute-done((bf16[1024,128]{1,0:T(8,128)(2,1)}, bf16[1024,128]{1,0:T(8,128)(2,1)S(1)}, u32[]{:S(2)}, u32[]{:S(2)}) %collective-permute-start.34) | collective-permute-done | bytes 262176 | tf_op jit(solution)/shard_map/ppermute | solution.py:722
  120.3 15.0 %experts.2 = (bf16[2048,256]{1,0:T(8,128)(2,1)S(1)}, bf16[1024,512]{1,0:T(8,128)(2,1)S(1)}, bf16[1024,512]{1,0:T(8,128)(2,1)S(1)}, bf16[1,512,512]{2,1,0:T(8,128...) custom-call(s32[8]{0:T(128)S(1)} %slice_reduce_fusion.5.counts, ...), custom_call_target="tpu_custom_call" | custom-call | flops 1000 | bytes 1000 | tf_op jit(solution)/shard_map/experts/pallas_call | solution.py:406
  135.8 1.4 collective-permute-done.35.refs_1_
  138.4 15.1 %experts.3 = (bf16[1024,512]{1,0:T(8,128)(2,1)S(1)}, bf16[1024,512]{1,0:T(8,128)(2,1)S(1)}, bf16[1,512,512]{2,1,0:T(8,128)(2,1)S(1)}, bf16[1,512,512]{2,1,0:T(8,...) custom-call(s32[8]{0:T(128)S(1)} %slice_reduce_fusion.5.counts, ...), custom_call_target="tpu_custom_call" | custom-call | flops 1000 | bytes 1000 | tf_op jit(solution)/shard_map/experts/pallas_call | solution.py:406
  153.6 1.6 collective-permute-start.36
  155.7 1.1 collective-permute-start.41
  156.8 1.6 collective-permute-start.42
  158.4 6.7 %collective-permute-done.42.refs_1_ = bf16[1,256,512]{2,1,0:T(8,128)(2,1)S(1)} collective-permute-done((bf16[1,256,512]{2,1,0:T(8,128)(2,1)S(1)}, bf16[1,256,512]{2,1,0:T(8,128)(2,1)S(1)}, u32[]{:S(2)}, u32[]{:S(2)}) %collective-permute-start.42) | collective-permute-done | bytes 262176 | tf_op jit(solution)/shard_map/ppermute | solution.py:543
  165.1 4.8 %collective-permute-done.41.refs_2_ = bf16[1,512,512]{2,1,0:T(8,128)(2,1)S(1)} collective-permute-done((bf16[1,512,512]{2,1,0:T(8,128)(2,1)S(1)}, bf16[1,512,512]{2,1,0:T(8,128)(2,1)S(1)}, u32[]{:S(2)}, u32[]{:S(2)}) %collective-permute-start.41) | collective-permute-done | bytes 524320 | tf_op jit(solution)/shard_map/ppermute | solution.py:547
  171.1 3.7 %collective-permute-start.44 = (bf16[1,128,512]{2,1,0:T(8,128)(2,1)S(1)}, bf16[1,128,512]{2,1,0:T(8,128)(2,1)S(1)}, u32[]{:S(2)}, u32[]{:S(2)}) collective-permute-start(bf16[1,128,512]{2,1,0:T(8,128)(2,1)S(1)} %get-tuple-element.47.refs_3_), channel_id=1, source_target_pairs={{0,16},{2,18},{4,20},{6,22},{8,24},{10,26},{12,28},{14,30},{16,0},... | collective-permute-start | bytes 393224 | tf_op jit(solution)/shard_map/ppermute | solution.py:543
  174.8 4.7 %collective-permute-done.44.refs_1_ = bf16[1,128,512]{2,1,0:T(8,128)(2,1)S(1)} collective-permute-done((bf16[1,128,512]{2,1,0:T(8,128)(2,1)S(1)}, bf16[1,128,512]{2,1,0:T(8,128)(2,1)S(1)}, u32[]{:S(2)}, u32[]{:S(2)}) %collective-permute-start.44) | collective-permute-done | bytes 131104 | tf_op jit(solution)/shard_map/ppermute | solution.py:543
  179.5 3.4 %collective-permute-start.46 = (bf16[1,1,128,512]{3,2,1,0:T(8,128)(2,1)S(1)}, bf16[1,1,128,512]{3,2,1,0:T(8,128)(2,1)S(1)}, u32[]{:S(2)}, u32[]{:S(2)}) collective-permute-start(bf16[1,1,128,512]{3,2,1,0:T(8,128)(2,1)S(1)} %bitcast.38), channel_id=1, source_target_pairs={{0,16},{2,18},{4,20},{6,22},{8,24},{10,26},{12,28},{14,30},{16,0},... | collective-permute-start | bytes 393224 | tf_op jit(solution)/shard_map/ppermute | solution.py:543
  183.0 1.9 at_home.1
  185.0 2.6 %collective-permute-done.46.refs_1_ = bf16[1,1,128,512]{3,2,1,0:T(8,128)(2,1)S(1)} collective-permute-done((bf16[1,1,128,512]{3,2,1,0:T(8,128)(2,1)S(1)}, bf16[1,1,128,512]{3,2,1,0:T(8,128)(2,1)S(1)}, u32[]{:S(2)}, u32[]{:S(2)}) %collective-permute-start.46) | collective-permute-done | bytes 131104 | tf_op jit(solution)/shard_map/ppermute | solution.py:543
  188.6 2.5 %collective-permute-start.48 = (bf16[2,1,128,512]{3,2,1,0:T(8,128)(2,1)S(1)}, bf16[2,1,128,512]{3,2,1,0:T(8,128)(2,1)S(1)}, u32[]{:S(2)}, u32[]{:S(2)}) collective-permute-start(bf16[2,1,128,512]{3,2,1,0:T(8,128)(2,1)S(1)} %stack_pieces.5.refs_2_.refs_0_), channel_id=1, source_target_pairs={{0,8},{2,10},{4,12},{6,14},{8,0},{10,2},{12,4},{14,6},{16,24},{18,... | collective-permute-start | bytes 786440 | tf_op jit(solution)/shard_map/ppermute | solution.py:543
  191.1 2.4 %collective-permute-start.45 = (bf16[1,128,512]{2,1,0:T(8,128)(2,1)S(1)}, bf16[1,128,512]{2,1,0:T(8,128)(2,1)S(1)}, u32[]{:S(2)}, u32[]{:S(2)}) collective-permute-start(bf16[1,128,512]{2,1,0:T(8,128)(2,1)S(1)} %get-tuple-element.51.refs_5_), channel_id=1, source_target_pairs={{0,16},{2,18},{4,20},{6,22},{8,24},{10,26},{12,28},{14,30},{16,0},... | collective-permute-start | bytes 393224 | tf_op jit(solution)/shard_map/ppermute | solution.py:543
  193.5 4.8 %collective-permute-done.45.refs_1_ = bf16[1,128,512]{2,1,0:T(8,128)(2,1)S(1)} collective-permute-done((bf16[1,128,512]{2,1,0:T(8,128)(2,1)S(1)}, bf16[1,128,512]{2,1,0:T(8,128)(2,1)S(1)}, u32[]{:S(2)}, u32[]{:S(2)}) %collective-permute-start.45) | collective-permute-done | bytes 131104 | tf_op jit(solution)/shard_map/ppermute | solution.py:543
  199.6 2.7 %collective-permute-start.47 = (bf16[1,1,128,512]{3,2,1,0:T(8,128)(2,1)S(1)}, bf16[1,1,128,512]{3,2,1,0:T(8,128)(2,1)S(1)}, u32[]{:S(2)}, u32[]{:S(2)}) collective-permute-start(bf16[1,1,128,512]{3,2,1,0:T(8,128)(2,1)S(1)} %bitcast.40), channel_id=1, source_target_pairs={{0,16},{2,18},{4,20},{6,22},{8,24},{10,26},{12,28},{14,30},{16,0},... | collective-permute-start | bytes 393224 | tf_op jit(solution)/shard_map/ppermute | solution.py:543
  202.3 6.1 %collective-permute-done.47.refs_1_ = bf16[1,1,128,512]{3,2,1,0:T(8,128)(2,1)S(1)} collective-permute-done((bf16[1,1,128,512]{3,2,1,0:T(8,128)(2,1)S(1)}, bf16[1,1,128,512]{3,2,1,0:T(8,128)(2,1)S(1)}, u32[]{:S(2)}, u32[]{:S(2)}) %collective-permute-start.47) | collective-permute-done | bytes 131104 | tf_op jit(solution)/shard_map/ppermute | solution.py:543
  208.7 2.4 %collective-permute-done.51.refs_1_ = bf16[4,1,128,512]{3,2,1,0:T(8,128)(2,1)S(1)} collective-permute-done((bf16[4,1,128,512]{3,2,1,0:T(8,128)(2,1)S(1)}, bf16[4,1,128,512]{3,2,1,0:T(8,128)(2,1)S(1)}, u32[]{:S(2)}, u32[]{:S(2)}) %collective-permute-start.51) | collective-permute-done | bytes 524320 | tf_op jit(solution)/shard_map/ppermute | solution.py:570
  211.1 3.8 %collective-permute-done.49.refs_1_ = bf16[2,1,128,512]{3,2,1,0:T(8,128)(2,1)S(1)} collective-permute-done((bf16[2,1,128,512]{3,2,1,0:T(8,128)(2,1)S(1)}, bf16[2,1,128,512]{3,2,1,0:T(8,128)(2,1)S(1)}, u32[]{:S(2)}, u32[]{:S(2)}) %collective-permute-start.49) | collective-permute-done | bytes 262176 | tf_op jit(solution)/shard_map/ppermute | solution.py:543
  215.4 3.0 %unpack.2 = (f32[8,256,512]{2,1,0:T(8,128)}, f32[8,512,256]{2,1,0:T(8,128)}, f32[8,128]{1,0:T(8,128)S(1)}) custom-call(s32[4]{0:T(128)S(1)} %pad_add_fusion.2.where, s32[2]{0:T(128)S(1)} %get-tuple-element.80.place, bf16[4,1,128,512]{3,2,1,0:T(8,128)(2,1)S(1)} %stack_pieces.6.refs_2_.refs_0_, bf16[4,1,128,512]{3,2,1,0:T(8,128)(2,1)S(1)} %collective-permute-done.51.refs_1_, ...), custom_call_target="tpu_custom_call" | custom-call | flops 201326592 | bytes 6291456 | tf_op jit(solution)/shard_map/unpack/pallas_call | solution.py:625
  218.5 7.0 %collective-permute-done.50.refs_0_ = bf16[4,1,128,512]{3,2,1,0:T(8,128)(2,1)S(1)} collective-permute-done((bf16[4,1,128,512]{3,2,1,0:T(8,128)(2,1)S(1)}, bf16[4,1,128,512]{3,2,1,0:T(8,128)(2,1)S(1)}, u32[]{:S(2)}, u32[]{:S(2)}) %collective-permute-start.50) | collective-permute-done | bytes 524320 | tf_op jit(solution)/shard_map/ppermute | solution.py:570
  225.7 1.8 collective-permute-done.55.refs_3_
  227.5 3.0 %unpack.3 = (f32[8,256,512]{2,1,0:T(8,128)}, f32[8,512,256]{2,1,0:T(8,128)}, f32[8,128]{1,0:T(8,128)}) custom-call(s32[4]{0:T(128)S(1)} %pad_add_fusion.1.where, s32[2]{0:T(128)S(1)} %get-tuple-element.80.place, bf16[4,1,128,512]{3,2,1,0:T(8,128)(2,1)S(1)} %stack_pieces.8.refs_0_, ...), custom_call_target="tpu_custom_call", output_to_operand_aliasing={{0}: (6, {}), {1}: (7, {})} | custom-call | flops 201326592 | bytes 6291456 | tf_op jit(solution)/shard_map/unpack/pallas_call | solution.py:625
  (188 shorter events, 33.5 us)
Async XLA Ops:
  0.6 47.8 %collective-permute-start.10 = (bf16[128,2048]{1,0:T(8,128)(2,1)}, bf16[128,2048]{1,0:T(8,128)(2,1)}, u32[]{:S(2)}, u32[]{:S(2)}) collective-permute-start(bf16[128,2048]{1,0:T(8,128)(2,1)} %refs_0_.3), channel_id=1, source_target_pairs={{0,2},{2,0},{4,6},{6,4},{8,10},{10,8},{12,14},{14,12},{16,18},{18,... | collective-permute-start | bytes 1572872 | tf_op jit(solution)/shard_map/ppermute | solution.py:77
  1.2 15.4 %collective-permute-start.3 = (bf16[128,2048]{1,0:T(8,128)(2,1)}, bf16[128,2048]{1,0:T(8,128)(2,1)}, u32[]{:S(2)}, u32[]{:S(2)}) collective-permute-start(bf16[128,2048]{1,0:T(8,128)(2,1)} %refs_0_.3), channel_id=1, source_target_pairs={{0,8},{2,10},{8,16},{10,18},{16,24},{18,26},{24,28},{26,30},{28,20... | collective-permute-start | bytes 1572872 | tf_op jit(solution)/shard_map/ppermute | solution.py:73
  3.8 29.6 %collective-permute-start = (s32[2,1024]{1,0:T(2,128)}, s32[2,1024]{1,0:T(2,128)S(1)}, u32[]{:S(2)}, u32[]{:S(2)}) collective-permute-start(s32[2,1024]{1,0:T(2,128)} %bitcast.49), channel_id=1, source_target_pairs={{0,1},{1,0},{2,3},{3,2},{4,5},{5,4},{6,7},{7,6},{8,9},{9,8},{10,11... | collective-permute-start | bytes 24584 | tf_op jit(solution)/shard_map/ppermute | solution.py:61
  5.3 28.2 %collective-permute-start.1 = (bf16[1024,256]{1,0:T(8,128)(2,1)}, bf16[1024,256]{1,0:T(8,128)(2,1)S(1)}, u32[]{:S(2)}, u32[]{:S(2)}) collective-permute-start(bf16[1024,256]{1,0:T(8,128)(2,1)} %refs_1_.1), channel_id=1, source_target_pairs={{0,1},{1,0},{2,3},{3,2},{4,5},{5,4},{6,7},{7,6},{8,9},{9,8},{10,11... | collective-permute-start | bytes 1572872 | tf_op jit(solution)/shard_map/ppermute | solution.py:61
  5.8 13.6 %collective-permute-start.18 = (bf16[128,2048]{1,0:T(8,128)(2,1)}, bf16[128,2048]{1,0:T(8,128)(2,1)S(1)}, u32[]{:S(2)}, u32[]{:S(2)}) collective-permute-start(bf16[128,2048]{1,0:T(8,128)(2,1)} %refs_16_.3), channel_id=1, source_target_pairs={{0,4},{2,6},{8,0},{10,2},{16,8},{18,10},{24,16},{26,18},{28,24},{3... | collective-permute-start | bytes 1572872 | tf_op jit(solution)/shard_map/ppermute | solution.py:74
  16.6 13.9 %collective-permute-start.4 = (bf16[128,2048]{1,0:T(8,128)(2,1)}, bf16[128,2048]{1,0:T(8,128)(2,1)S(1)}, u32[]{:S(2)}, u32[]{:S(2)}) collective-permute-start(bf16[128,2048]{1,0:T(8,128)(2,1)} %collective-permute-done.3.refs_1_), channel_id=1, source_target_pairs={{0,8},{2,10},{8,16},{10,18},{16,24},{18,26},{24,28},{26,30},{28,20... | collective-permute-start | bytes 1572872 | tf_op jit(solution)/shard_map/ppermute | solution.py:73
  19.5 12.6 %collective-permute-start.19 = (bf16[128,2048]{1,0:T(8,128)(2,1)S(1)}, bf16[128,2048]{1,0:T(8,128)(2,1)S(1)}, u32[]{:S(2)}, u32[]{:S(2)}) collective-permute-start(bf16[128,2048]{1,0:T(8,128)(2,1)S(1)} %collective-permute-done.18.refs_17_), channel_id=1, source_target_pairs={{0,4},{2,6},{8,0},{10,2},{16,8},{18,10},{24,16},{26,18},{28,24},{3... | collective-permute-start | bytes 1572872 | tf_op jit(solution)/shard_map/ppermute | solution.py:74
  30.5 12.9 %collective-permute-start.5 = (bf16[128,2048]{1,0:T(8,128)(2,1)S(1)}, bf16[128,2048]{1,0:T(8,128)(2,1)}, u32[]{:S(2)}, u32[]{:S(2)}) collective-permute-start(bf16[128,2048]{1,0:T(8,128)(2,1)S(1)} %collective-permute-done.4.refs_2_), channel_id=1, source_target_pairs={{0,8},{2,10},{8,16},{10,18},{16,24},{18,26},{24,28},{26,30},{28,20... | collective-permute-start | bytes 1572872 | tf_op jit(solution)/shard_map/ppermute | solution.py:73
  32.1 12.7 %collective-permute-start.20 = (bf16[128,2048]{1,0:T(8,128)(2,1)S(1)}, bf16[128,2048]{1,0:T(8,128)(2,1)}, u32[]{:S(2)}, u32[]{:S(2)}) collective-permute-start(bf16[128,2048]{1,0:T(8,128)(2,1)S(1)} %collective-permute-done.19.refs_18_), channel_id=1, source_target_pairs={{0,4},{2,6},{8,0},{10,2},{16,8},{18,10},{24,16},{26,18},{28,24},{3... | collective-permute-start | bytes 1572872 | tf_op jit(solution)/shard_map/ppermute | solution.py:74
  33.4 15.1 %collective-permute-start.25 = (bf16[128,2048]{1,0:T(8,128)(2,1)S(1)}, bf16[128,2048]{1,0:T(8,128)(2,1)}, u32[]{:S(2)}, u32[]{:S(2)}) collective-permute-start(bf16[128,2048]{1,0:T(8,128)(2,1)S(1)} %copy-done.6), channel_id=1, source_target_pairs={{0,2},{2,0},{4,6},{6,4},{8,10},{10,8},{12,14},{14,12},{16,18},{18,... | collective-permute-start | bytes 1572872 | tf_op jit(solution)/shard_map/ppermute | solution.py:78
  33.5 15.5 %collective-permute-start.11 = (bf16[128,2048]{1,0:T(8,128)(2,1)}, bf16[128,2048]{1,0:T(8,128)(2,1)}, u32[]{:S(2)}, u32[]{:S(2)}) collective-permute-start(bf16[128,2048]{1,0:T(8,128)(2,1)} %collective-permute-done.3.refs_1_), channel_id=1, source_target_pairs={{0,2},{2,0},{4,6},{6,4},{8,10},{10,8},{12,14},{14,12},{16,18},{18,... | collective-permute-start | bytes 1572872 | tf_op jit(solution)/shard_map/ppermute | solution.py:77
  43.4 12.2 %collective-permute-start.6 = (bf16[128,2048]{1,0:T(8,128)(2,1)}, bf16[128,2048]{1,0:T(8,128)(2,1)}, u32[]{:S(2)}, u32[]{:S(2)}) collective-permute-start(bf16[128,2048]{1,0:T(8,128)(2,1)} %collective-permute-done.5.refs_3_), channel_id=1, source_target_pairs={{0,8},{2,10},{8,16},{10,18},{16,24},{18,26},{24,28},{26,30},{28,20... | collective-permute-start | bytes 1572872 | tf_op jit(solution)/shard_map/ppermute | solution.py:73
  44.8 12.1 %collective-permute-start.21 = (bf16[128,2048]{1,0:T(8,128)(2,1)}, bf16[128,2048]{1,0:T(8,128)(2,1)}, u32[]{:S(2)}, u32[]{:S(2)}) collective-permute-start(bf16[128,2048]{1,0:T(8,128)(2,1)} %collective-permute-done.20.refs_19_), channel_id=1, source_target_pairs={{0,4},{2,6},{8,0},{10,2},{16,8},{18,10},{24,16},{26,18},{28,24},{3... | collective-permute-start | bytes 1572872 | tf_op jit(solution)/shard_map/ppermute | solution.py:74
  48.4 11.1 %collective-permute-start.26 = (bf16[128,2048]{1,0:T(8,128)(2,1)S(1)}, bf16[128,2048]{1,0:T(8,128)(2,1)S(1)}, u32[]{:S(2)}, u32[]{:S(2)}) collective-permute-start(bf16[128,2048]{1,0:T(8,128)(2,1)S(1)} %copy-done.8), channel_id=1, source_target_pairs={{0,2},{2,0},{4,6},{6,4},{8,10},{10,8},{12,14},{14,12},{16,18},{18,... | collective-permute-start | bytes 1572872 | tf_op jit(solution)/shard_map/ppermute | solution.py:78
  48.5 11.1 %collective-permute-start.12 = (bf16[128,2048]{1,0:T(8,128)(2,1)S(1)}, bf16[128,2048]{1,0:T(8,128)(2,1)S(1)}, u32[]{:S(2)}, u32[]{:S(2)}) collective-permute-start(bf16[128,2048]{1,0:T(8,128)(2,1)S(1)} %copy-done.10), channel_id=1, source_target_pairs={{0,2},{2,0},{4,6},{6,4},{8,10},{10,8},{12,14},{14,12},{16,18},{18,... | collective-permute-start | bytes 1572872 | tf_op jit(solution)/shard_map/ppermute | solution.py:77
  49.0 11.1 %collective-permute-start.27 = (bf16[128,2048]{1,0:T(8,128)(2,1)}, bf16[128,2048]{1,0:T(8,128)(2,1)S(1)}, u32[]{:S(2)}, u32[]{:S(2)}) collective-permute-start(bf16[128,2048]{1,0:T(8,128)(2,1)} %copy-done.11), channel_id=1, source_target_pairs={{0,2},{2,0},{4,6},{6,4},{8,10},{10,8},{12,14},{14,12},{16,18},{18,... | collective-permute-start | bytes 1572872 | tf_op jit(solution)/shard_map/ppermute | solution.py:78
  55.6 12.1 %collective-permute-start.7 = (bf16[128,2048]{1,0:T(8,128)(2,1)}, bf16[128,2048]{1,0:T(8,128)(2,1)}, u32[]{:S(2)}, u32[]{:S(2)}) collective-permute-start(bf16[128,2048]{1,0:T(8,128)(2,1)} %collective-permute-done.6.refs_4_), channel_id=1, source_target_pairs={{0,8},{2,10},{8,16},{10,18},{16,24},{18,26},{24,28},{26,30},{28,20... | collective-permute-start | bytes 1572872 | tf_op jit(solution)/shard_map/ppermute | solution.py:73
  56.9 12.1 %collective-permute-start.22 = (bf16[128,2048]{1,0:T(8,128)(2,1)}, bf16[128,2048]{1,0:T(8,128)(2,1)}, u32[]{:S(2)}, u32[]{:S(2)}) collective-permute-start(bf16[128,2048]{1,0:T(8,128)(2,1)} %collective-permute-done.21.refs_20_), channel_id=1, source_target_pairs={{0,4},{2,6},{8,0},{10,2},{16,8},{18,10},{24,16},{26,18},{28,24},{3... | collective-permute-start | bytes 1572872 | tf_op jit(solution)/shard_map/ppermute | solution.py:74
  59.6 14.2 %collective-permute-start.13 = (bf16[128,2048]{1,0:T(8,128)(2,1)}, bf16[128,2048]{1,0:T(8,128)(2,1)}, u32[]{:S(2)}, u32[]{:S(2)}) collective-permute-start(bf16[128,2048]{1,0:T(8,128)(2,1)} %collective-permute-done.5.refs_3_), channel_id=1, source_target_pairs={{0,2},{2,0},{4,6},{6,4},{8,10},{10,8},{12,14},{14,12},{16,18},{18,... | collective-permute-start | bytes 1572872 | tf_op jit(solution)/shard_map/ppermute | solution.py:77
  59.6 14.2 %collective-permute-start.28 = (bf16[128,2048]{1,0:T(8,128)(2,1)}, bf16[128,2048]{1,0:T(8,128)(2,1)}, u32[]{:S(2)}, u32[]{:S(2)}) collective-permute-start(bf16[128,2048]{1,0:T(8,128)(2,1)} %collective-permute-done.20.refs_19_), channel_id=1, source_target_pairs={{0,2},{2,0},{4,6},{6,4},{8,10},{10,8},{12,14},{14,12},{16,18},{18,... | collective-permute-start | bytes 1572872 | tf_op jit(solution)/shard_map/ppermute | solution.py:78
  60.1 14.2 %collective-permute-start.14 = (bf16[128,2048]{1,0:T(8,128)(2,1)}, bf16[128,2048]{1,0:T(8,128)(2,1)}, u32[]{:S(2)}, u32[]{:S(2)}) collective-permute-start(bf16[128,2048]{1,0:T(8,128)(2,1)} %collective-permute-done.6.refs_4_), channel_id=1, source_target_pairs={{0,2},{2,0},{4,6},{6,4},{8,10},{10,8},{12,14},{14,12},{16,18},{18,... | collective-permute-start | bytes 1572872 | tf_op jit(solution)/shard_map/ppermute | solution.py:77
  67.7 10.8 %collective-permute-start.8 = (bf16[128,2048]{1,0:T(8,128)(2,1)}, bf16[128,2048]{1,0:T(8,128)(2,1)}, u32[]{:S(2)}, u32[]{:S(2)}) collective-permute-start(bf16[128,2048]{1,0:T(8,128)(2,1)} %collective-permute-done.7.refs_5_), channel_id=1, source_target_pairs={{0,8},{2,10},{8,16},{10,18},{16,24},{18,26},{24,28},{26,30},{28,20... | collective-permute-start | bytes 1572872 | tf_op jit(solution)/shard_map/ppermute | solution.py:73
  68.9 10.4 %collective-permute-start.23 = (bf16[128,2048]{1,0:T(8,128)(2,1)}, bf16[128,2048]{1,0:T(8,128)(2,1)}, u32[]{:S(2)}, u32[]{:S(2)}) collective-permute-start(bf16[128,2048]{1,0:T(8,128)(2,1)} %collective-permute-done.22.refs_21_), channel_id=1, source_target_pairs={{0,4},{2,6},{8,0},{10,2},{16,8},{18,10},{24,16},{26,18},{28,24},{3... | collective-permute-start | bytes 1572872 | tf_op jit(solution)/shard_map/ppermute | solution.py:74
  73.8 11.5 %collective-permute-start.29 = (bf16[128,2048]{1,0:T(8,128)(2,1)}, bf16[128,2048]{1,0:T(8,128)(2,1)}, u32[]{:S(2)}, u32[]{:S(2)}) collective-permute-start(bf16[128,2048]{1,0:T(8,128)(2,1)} %collective-permute-done.21.refs_20_), channel_id=1, source_target_pairs={{0,2},{2,0},{4,6},{6,4},{8,10},{10,8},{12,14},{14,12},{16,18},{18,... | collective-permute-start | bytes 1572872 | tf_op jit(solution)/shard_map/ppermute | solution.py:78
  73.8 12.4 %collective-permute-start.15 = (bf16[128,2048]{1,0:T(8,128)(2,1)}, bf16[128,2048]{1,0:T(8,128)(2,1)}, u32[]{:S(2)}, u32[]{:S(2)}) collective-permute-start(bf16[128,2048]{1,0:T(8,128)(2,1)} %collective-permute-done.7.refs_5_), channel_id=1, source_target_pairs={{0,2},{2,0},{4,6},{6,4},{8,10},{10,8},{12,14},{14,12},{16,18},{18,... | collective-permute-start | bytes 1572872 | tf_op jit(solution)/shard_map/ppermute | solution.py:77
  74.3 11.9 %collective-permute-start.30 = (bf16[128,2048]{1,0:T(8,128)(2,1)}, bf16[128,2048]{1,0:T(8,128)(2,1)}, u32[]{:S(2)}, u32[]{:S(2)}) collective-permute-start(bf16[128,2048]{1,0:T(8,128)(2,1)} %collective-permute-done.22.refs_21_), channel_id=1, source_target_pairs={{0,2},{2,0},{4,6},{6,4},{8,10},{10,8},{12,14},{14,12},{16,18},{18,... | collective-permute-start | bytes 1572872 | tf_op jit(solution)/shard_map/ppermute | solution.py:78
  78.5 10.9 %collective-permute-start.9 = (bf16[128,2048]{1,0:T(8,128)(2,1)}, bf16[128,2048]{1,0:T(8,128)(2,1)}, u32[]{:S(2)}, u32[]{:S(2)}) collective-permute-start(bf16[128,2048]{1,0:T(8,128)(2,1)} %collective-permute-done.8.refs_6_), channel_id=1, source_target_pairs={{0,8},{2,10},{8,16},{10,18},{16,24},{18,26},{24,28},{26,30},{28,20... | collective-permute-start | bytes 1572872 | tf_op jit(solution)/shard_map/ppermute | solution.py:73
  79.4 10.8 %collective-permute-start.24 = (bf16[128,2048]{1,0:T(8,128)(2,1)}, bf16[128,2048]{1,0:T(8,128)(2,1)}, u32[]{:S(2)}, u32[]{:S(2)}) collective-permute-start(bf16[128,2048]{1,0:T(8,128)(2,1)} %collective-permute-done.23.refs_22_), channel_id=1, source_target_pairs={{0,4},{2,6},{8,0},{10,2},{16,8},{18,10},{24,16},{26,18},{28,24},{3... | collective-permute-start | bytes 1572872 | tf_op jit(solution)/shard_map/ppermute | solution.py:74
  85.3 27.1 %collective-permute-start.2 = (bf16[1024,256]{1,0:T(8,128)(2,1)}, bf16[1024,256]{1,0:T(8,128)(2,1)}, u32[]{:S(2)}, u32[]{:S(2)}) collective-permute-start(bf16[1024,256]{1,0:T(8,128)(2,1)} %param.17), channel_id=1, source_target_pairs={{0,1},{1,0},{2,3},{3,2},{4,5},{5,4},{6,7},{7,6},{8,9},{9,8},{10,11... | collective-permute-start | bytes 1572872 | tf_op jit(solution)/shard_map/ppermute | solution.py:61
  101.6 13.0 %collective-permute-start.33 = (bf16[1024,128]{1,0:T(8,128)(2,1)}, bf16[1024,128]{1,0:T(8,128)(2,1)S(1)}, u32[]{:S(2)}, u32[]{:S(2)}) collective-permute-start(bf16[1024,128]{1,0:T(8,128)(2,1)} %attention.2), channel_id=1, source_target_pairs={{0,1},{1,0},{2,3},{3,2},{4,5},{5,4},{6,7},{7,6},{8,9},{9,8},{10,11... | collective-permute-start | bytes 786440 | tf_op jit(solution)/shard_map/ppermute | solution.py:722
  111.9 8.3 %collective-permute-start.34 = (bf16[1024,128]{1,0:T(8,128)(2,1)}, bf16[1024,128]{1,0:T(8,128)(2,1)S(1)}, u32[]{:S(2)}, u32[]{:S(2)}) collective-permute-start(bf16[1024,128]{1,0:T(8,128)(2,1)} %attention.3), channel_id=1, source_target_pairs={{0,1},{1,0},{2,3},{3,2},{4,5},{5,4},{6,7},{7,6},{8,9},{9,8},{10,11... | collective-permute-start | bytes 786440 | tf_op jit(solution)/shard_map/ppermute | solution.py:722
  135.3 20.0 %collective-permute-start.39 = (bf16[1,512,512]{2,1,0:T(8,128)(2,1)S(1)}, bf16[1,512,512]{2,1,0:T(8,128)(2,1)S(1)}, u32[]{:S(2)}, u32[]{:S(2)}) collective-permute-start(bf16[1,512,512]{2,1,0:T(8,128)(2,1)S(1)} %get-tuple-element.44), channel_id=1, source_target_pairs={{0,2},{2,0},{4,6},{6,4},{8,10},{10,8},{12,14},{14,12},{16,18},{18,... | collective-permute-start | bytes 1572872 | tf_op jit(solution)/shard_map/ppermute | solution.py:540
  137.4 18.0 %collective-permute-start.40 = (bf16[1,512,512]{2,1,0:T(8,128)(2,1)S(1)}, bf16[1,512,512]{2,1,0:T(8,128)(2,1)S(1)}, u32[]{:S(2)}, u32[]{:S(2)}) collective-permute-start(bf16[1,512,512]{2,1,0:T(8,128)(2,1)S(1)} %sum_core.2.refs_10_.refs_3_), channel_id=1, source_target_pairs={{0,4},{2,6},{4,0},{6,2},{8,12},{10,14},{12,8},{14,10},{16,20},{18,... | collective-permute-start | bytes 1572872 | tf_op jit(solution)/shard_map/ppermute | solution.py:547
  153.6 29.4 %collective-permute-start.36 = (bf16[1024,512]{1,0:T(8,128)(2,1)S(1)}, bf16[1024,512]{1,0:T(8,128)(2,1)S(1)}, u32[]{:S(2)}, u32[]{:S(2)}) collective-permute-start(bf16[1024,512]{1,0:T(8,128)(2,1)S(1)} %get-tuple-element.38), channel_id=1, source_target_pairs={{0,1},{1,0},{2,3},{3,2},{4,5},{5,4},{6,7},{7,6},{8,9},{9,8},{10,11... | collective-permute-start | bytes 3145736 | tf_op jit(solution)/shard_map/ppermute | solution.py:739
  155.2 10.0 %collective-permute-start.37 = (bf16[1,512,512]{2,1,0:T(8,128)(2,1)S(1)}, bf16[1,512,512]{2,1,0:T(8,128)(2,1)S(1)}, u32[]{:S(2)}, u32[]{:S(2)}) collective-permute-start(bf16[1,512,512]{2,1,0:T(8,128)(2,1)S(1)} %get-tuple-element.40), channel_id=1, source_target_pairs={{0,2},{2,0},{4,6},{6,4},{8,10},{10,8},{12,14},{14,12},{16,18},{18,... | collective-permute-start | bytes 1572872 | tf_op jit(solution)/shard_map/ppermute | solution.py:540
  155.7 14.2 %collective-permute-start.41 = (bf16[1,512,512]{2,1,0:T(8,128)(2,1)S(1)}, bf16[1,512,512]{2,1,0:T(8,128)(2,1)S(1)}, u32[]{:S(2)}, u32[]{:S(2)}) collective-permute-start(bf16[1,512,512]{2,1,0:T(8,128)(2,1)S(1)} %sum_core.3.refs_2_), channel_id=1, source_target_pairs={{0,4},{2,6},{4,0},{6,2},{8,12},{10,14},{12,8},{14,10},{16,20},{18,... | collective-permute-start | bytes 1572872 | tf_op jit(solution)/shard_map/ppermute | solution.py:547
  156.8 8.3 %collective-permute-start.42 = (bf16[1,256,512]{2,1,0:T(8,128)(2,1)S(1)}, bf16[1,256,512]{2,1,0:T(8,128)(2,1)S(1)}, u32[]{:S(2)}, u32[]{:S(2)}) collective-permute-start(bf16[1,256,512]{2,1,0:T(8,128)(2,1)S(1)} %get-tuple-element.45.refs_2_), channel_id=1, source_target_pairs={{0,8},{2,10},{4,12},{6,14},{8,0},{10,2},{12,4},{14,6},{16,24},{18,... | collective-permute-start | bytes 786440 | tf_op jit(solution)/shard_map/ppermute | solution.py:543
  170.1 12.8 %collective-permute-start.43 = (bf16[1,256,512]{2,1,0:T(8,128)(2,1)S(1)}, bf16[1,256,512]{2,1,0:T(8,128)(2,1)S(1)}, u32[]{:S(2)}, u32[]{:S(2)}) collective-permute-start(bf16[1,256,512]{2,1,0:T(8,128)(2,1)S(1)} %get-tuple-element.49.refs_2_), channel_id=1, source_target_pairs={{0,8},{2,10},{4,12},{6,14},{8,0},{10,2},{12,4},{14,6},{16,24},{18,... | collective-permute-start | bytes 786440 | tf_op jit(solution)/shard_map/ppermute | solution.py:543
  171.1 8.4 %collective-permute-start.44 = (bf16[1,128,512]{2,1,0:T(8,128)(2,1)S(1)}, bf16[1,128,512]{2,1,0:T(8,128)(2,1)S(1)}, u32[]{:S(2)}, u32[]{:S(2)}) collective-permute-start(bf16[1,128,512]{2,1,0:T(8,128)(2,1)S(1)} %get-tuple-element.47.refs_3_), channel_id=1, source_target_pairs={{0,16},{2,18},{4,20},{6,22},{8,24},{10,26},{12,28},{14,30},{16,0},... | collective-permute-start | bytes 393224 | tf_op jit(solution)/shard_map/ppermute | solution.py:543
  179.5 8.1 %collective-permute-start.46 = (bf16[1,1,128,512]{3,2,1,0:T(8,128)(2,1)S(1)}, bf16[1,1,128,512]{3,2,1,0:T(8,128)(2,1)S(1)}, u32[]{:S(2)}, u32[]{:S(2)}) collective-permute-start(bf16[1,1,128,512]{3,2,1,0:T(8,128)(2,1)S(1)} %bitcast.38), channel_id=1, source_target_pairs={{0,16},{2,18},{4,20},{6,22},{8,24},{10,26},{12,28},{14,30},{16,0},... | collective-permute-start | bytes 393224 | tf_op jit(solution)/shard_map/ppermute | solution.py:543
  188.6 10.4 %collective-permute-start.48 = (bf16[2,1,128,512]{3,2,1,0:T(8,128)(2,1)S(1)}, bf16[2,1,128,512]{3,2,1,0:T(8,128)(2,1)S(1)}, u32[]{:S(2)}, u32[]{:S(2)}) collective-permute-start(bf16[2,1,128,512]{3,2,1,0:T(8,128)(2,1)S(1)} %stack_pieces.5.refs_2_.refs_0_), channel_id=1, source_target_pairs={{0,8},{2,10},{4,12},{6,14},{8,0},{10,2},{12,4},{14,6},{16,24},{18,... | collective-permute-start | bytes 786440 | tf_op jit(solution)/shard_map/ppermute | solution.py:543
  191.1 7.2 %collective-permute-start.45 = (bf16[1,128,512]{2,1,0:T(8,128)(2,1)S(1)}, bf16[1,128,512]{2,1,0:T(8,128)(2,1)S(1)}, u32[]{:S(2)}, u32[]{:S(2)}) collective-permute-start(bf16[1,128,512]{2,1,0:T(8,128)(2,1)S(1)} %get-tuple-element.51.refs_5_), channel_id=1, source_target_pairs={{0,16},{2,18},{4,20},{6,22},{8,24},{10,26},{12,28},{14,30},{16,0},... | collective-permute-start | bytes 393224 | tf_op jit(solution)/shard_map/ppermute | solution.py:543
  199.1 12.0 %collective-permute-start.51 = (bf16[4,1,128,512]{3,2,1,0:T(8,128)(2,1)S(1)}, bf16[4,1,128,512]{3,2,1,0:T(8,128)(2,1)S(1)}, u32[]{:S(2)}, u32[]{:S(2)}) collective-permute-start(bf16[4,1,128,512]{3,2,1,0:T(8,128)(2,1)S(1)} %stack_pieces.6.refs_2_.refs_0_), channel_id=1, source_target_pairs={{0,4},{2,6},{4,0},{6,2},{8,12},{10,14},{12,8},{14,10},{16,20},{18,... | collective-permute-start | bytes 1572872 | tf_op jit(solution)/shard_map/ppermute | solution.py:570
  199.6 8.8 %collective-permute-start.47 = (bf16[1,1,128,512]{3,2,1,0:T(8,128)(2,1)S(1)}, bf16[1,1,128,512]{3,2,1,0:T(8,128)(2,1)S(1)}, u32[]{:S(2)}, u32[]{:S(2)}) collective-permute-start(bf16[1,1,128,512]{3,2,1,0:T(8,128)(2,1)S(1)} %bitcast.40), channel_id=1, source_target_pairs={{0,16},{2,18},{4,20},{6,22},{8,24},{10,26},{12,28},{14,30},{16,0},... | collective-permute-start | bytes 393224 | tf_op jit(solution)/shard_map/ppermute | solution.py:543
  208.4 6.4 %collective-permute-start.49 = (bf16[2,1,128,512]{3,2,1,0:T(8,128)(2,1)S(1)}, bf16[2,1,128,512]{3,2,1,0:T(8,128)(2,1)S(1)}, u32[]{:S(2)}, u32[]{:S(2)}) collective-permute-start(bf16[2,1,128,512]{3,2,1,0:T(8,128)(2,1)S(1)} %stack_pieces.7.refs_0_.refs_2_), channel_id=1, source_target_pairs={{0,8},{2,10},{4,12},{6,14},{8,0},{10,2},{12,4},{14,6},{16,24},{18,... | collective-permute-start | bytes 786440 | tf_op jit(solution)/shard_map/ppermute | solution.py:543
  208.7 6.7 %collective-permute-start.52 = (bf16[4,1,128,512]{3,2,1,0:T(8,128)(2,1)S(1)}, bf16[4,1,128,512]{3,2,1,0:T(8,128)(2,1)S(1)}, u32[]{:S(2)}, u32[]{:S(2)}) collective-permute-start(bf16[4,1,128,512]{3,2,1,0:T(8,128)(2,1)S(1)} %stack_pieces.6.refs_2_.refs_0_), channel_id=1, source_target_pairs={{0,2},{2,0},{4,6},{6,4},{8,10},{10,8},{12,14},{14,12},{16,18},{18,... | collective-permute-start | bytes 1572872 | tf_op jit(solution)/shard_map/ppermute | solution.py:540
  214.9 10.6 %collective-permute-start.50 = (bf16[4,1,128,512]{3,2,1,0:T(8,128)(2,1)S(1)}, bf16[4,1,128,512]{3,2,1,0:T(8,128)(2,1)S(1)}, u32[]{:S(2)}, u32[]{:S(2)}) collective-permute-start(bf16[4,1,128,512]{3,2,1,0:T(8,128)(2,1)S(1)} %stack_pieces.8.refs_0_), channel_id=1, source_target_pairs={{0,4},{2,6},{4,0},{6,2},{8,12},{10,14},{12,8},{14,10},{16,20},{18,... | collective-permute-start | bytes 1572872 | tf_op jit(solution)/shard_map/ppermute | solution.py:570
  215.4 10.3 %collective-permute-start.54 = (bf16[4,1,128,512]{3,2,1,0:T(8,128)(2,1)S(1)}, bf16[4,1,128,512]{3,2,1,0:T(8,128)(2,1)S(1)}, u32[]{:S(2)}, u32[]{:S(2)}) collective-permute-start(bf16[4,1,128,512]{3,2,1,0:T(8,128)(2,1)S(1)} %stack_pieces.8.refs_0_), channel_id=1, source_target_pairs={{0,2},{2,0},{4,6},{6,4},{8,10},{10,8},{12,14},{14,12},{16,18},{18,... | collective-permute-start | bytes 1572872 | tf_op jit(solution)/shard_map/ppermute | solution.py:540
  (32 other events, 405.3 us)

commit v5 on v4

--- a/solution.py
+++ b/solution.py
@@ -212,7 +212,7 @@
     return jnp.concatenate([one_hot(rank[e : e + 1, :], window_base(starts, i, e)) for e in range(first, first + count)], 0)
 
 
-def group_kernel(first, count, pieces, after, chunk, lines, owners, counts, ids, perm, starts, order, place, *refs):
+def group_kernel(first, count, pieces, after, chunk, lines, counts, ids, perm, starts, place, *refs):
     refs = list(refs)
     rank_ref, cot_ref, gain_ref, router_ref, win_ref, wout_ref, rcol_ref = [refs.pop(0) for _ in range(7)]
     if pieces:
@@ -222,11 +222,10 @@
         stream_ref = None
     else:
         stream_ref = refs.pop(0)
-        partial_refs = [refs.pop(0) for _ in range(owners)]
-        del refs[: after]
+        del refs[:after]
     if pieces:
         out_stream = refs.pop(0)
-    out_refs = [refs.pop(0) for _ in range(owners)]
+    out_rows = refs.pop(0)
     grad_refs, (rows_ref, slots, acc_in, acc_out) = refs[:-4], refs[-4:]
     nodes, width = cot_ref.shape
     step = pl.program_id(0)
@@ -304,11 +303,18 @@
         produced = jnp.dot(hidden, w_out, preferred_element_type=f32).astype(bf16).astype(f32)
         grad_rows = contract(grad_pre, w_in, 1, 1).astype(bf16).astype(f32)
         grad_logit = jnp.sum(cot_wide * produced, 1, keepdims=True) * gate * (1.0 - gate)
-        slots[step, at, :width] = (gate * produced).astype(bf16)
-        slots[step, at, width:] = (grad_rows + grad_logit * column).astype(bf16)
+        out_rows[0, at, :width] = (gate * produced).astype(bf16)
+        out_rows[0, at, width:] = (grad_rows + grad_logit * column).astype(bf16)
         return carry
 
     lax.fori_loop(0, tiles, one, 0)
+
+    def blank(t, carry):
+        at = pl.ds(pl.multiple_of(t * WINDOW, WINDOW), WINDOW)
+        out_rows[0, at, :] = jnp.zeros((WINDOW, 2 * width), bf16)
+        return carry
+
+    lax.fori_loop(tiles * TILE // WINDOW, out_rows.shape[1] // WINDOW, blank, 0)
 
     ff = acc_in.shape[1]
 
@@ -339,46 +345,13 @@
                     write((own, other)[column], True, False)
                     write((other, own)[column], False, True)
 
-    @pl.when(step == count - 1)
-    def _():
-        chunks = nodes // chunk // owners
-
-        for d in range(owners):
-
-            def gather(c, carry, d=d):
-                i = order[d] * chunks + c
-                rank = rank_ref[:, pl.ds(pl.multiple_of(i * chunk, chunk), chunk)]
-                windows = [slots[e, pl.ds(window_base(starts, i, first + e), WINDOW), :] for e in range(count)]
-                total = contract(stack_hot(starts, rank, i, first, count), jnp.concatenate(windows, 0), 0, 0)
-
-                def further(total):
-                    for e in range(count):
-
-                        def more(w, acc, e=e):
-                            base = pl.multiple_of(window_base(starts, i, first + e) + w * WINDOW, 16)
-                            hot = one_hot(rank[first + e : first + e + 1, :], base)
-                            return acc + contract(hot, slots[e, pl.ds(base, WINDOW), :], 0, 0)
-
-                        total = lax.fori_loop(1, further_windows(starts, i, first + e), more, total)
-                    return total
-
-                total = lax.cond(any_further(starts, i, first, count), further, lambda total: total, total)
-                at = pl.ds(pl.multiple_of(c * chunk, chunk), chunk)
-                if not pieces:
-                    total = total + partial_refs[d][at, :].astype(f32)
-                out_refs[d][at, :] = total.astype(bf16)
-                return carry
-
-            lax.fori_loop(0, chunks, gather, 0)
-
 
 def expert_group(scalars, common, weights, first, count, head, tail, lines, slot_rows, chunk):
-    counts, ids, perm, starts, order, place = scalars
+    counts, ids, perm, starts, place = scalars
     rank, cotangent, gain, router = common
     w_in, w_out, columns = weights
     nodes, width = cotangent.shape
     ff = w_in.shape[2]
-    owners = order.shape[0]
     whole = lambda a: pl.BlockSpec(a.shape, lambda i, *_: (0,) * a.ndim)
     listed = lambda *shape: pl.BlockSpec((1,) + shape, lambda i, c, d, perm, *_: (perm[i + first], 0, 0))
     args = [rank, cotangent, gain, router, w_in, w_out, columns]
@@ -391,12 +364,13 @@
         out_shape.append(jax.ShapeDtypeStruct((nodes, width), bf16))
         pieces = len(atts)
     else:
-        stream, partials, after = tail
-        extra = [stream, *partials, *after]
-        specs += [whole(stream)] + [whole(p) for p in partials] + [pl.BlockSpec(memory_space=pl.ANY)] * len(after)
+        stream, after = tail
+        extra = [stream, *after]
+        specs += [whole(stream)] + [pl.BlockSpec(memory_space=pl.ANY)] * len(after)
         pieces = 0
-    out_shape += [jax.ShapeDtypeStruct((nodes // owners, 2 * width), bf16)] * owners
     out_specs = [pl.BlockSpec(o.shape, lambda i, *_: (0, 0)) for o in out_shape]
+    out_shape.append(jax.ShapeDtypeStruct((count, slot_rows, 2 * width), bf16))
+    out_specs.append(pl.BlockSpec((1, slot_rows, 2 * width), lambda i, *_: (i, 0, 0)))
     each = max(1, count // 4)
     block = (1, 2 * width if count > 2 else width, ff)
     out_shape += [jax.ShapeDtypeStruct((each,) + block[1:], bf16)] * 4
@@ -404,9 +378,9 @@
         first_step = k * each if count > 2 else k // 2
         out_specs.append(pl.BlockSpec(block, lambda i, *_, at=first_step: (jnp.clip(i - at, 0, each - 1), 0, 0)))
     return pl.pallas_call(
-        functools.partial(group_kernel, first, count, pieces, 0 if head else len(after), chunk, lines, owners),
+        functools.partial(group_kernel, first, count, pieces, 0 if head else len(after), chunk, lines),
         grid_spec=pltpu.PrefetchScalarGridSpec(
-            num_scalar_prefetch=6,
+            num_scalar_prefetch=5,
             grid=(count,),
             in_specs=specs,
             out_specs=out_specs,
@@ -421,11 +395,63 @@
         compiler_params=params(),
         cost_estimate=pl.CostEstimate(flops=1000, bytes_accessed=1000, transcendentals=0),
         name="experts",
-    )(counts, ids, perm, starts, order, place, *args, *extra)
+    )(counts, ids, perm, starts, place, *args, *extra)
+
+
+def combine_kernel(parts, owners, chunk, starts, order, rank_ref, *refs):
+    rows_refs, out_refs = refs[:parts], refs[len(refs) - owners :]
+    held = [(r, j) for r in rows_refs for j in range(r.shape[0])]
+    experts = len(held)
+    chunks = out_refs[0].shape[0] // chunk
+
+    for d in range(owners):
+
+        def gather(c, carry, d=d):
+            i = order[d] * chunks + c
+            rank = rank_ref[:, pl.ds(pl.multiple_of(i * chunk, chunk), chunk)]
+            windows = [r[j, pl.ds(window_base(starts, i, e), WINDOW), :] for e, (r, j) in enumerate(held)]
+            total = contract(stack_hot(starts, rank, i, 0, experts), jnp.concatenate(windows, 0), 0, 0)
+
+            def further(total):
+                for e, (r, j) in enumerate(held):
+
+                    def more(w, acc, e=e, r=r, j=j):
+                        base = pl.multiple_of(window_base(starts, i, e) + w * WINDOW, 16)
+                        return acc + contract(one_hot(rank[e : e + 1, :], base), r[j, pl.ds(base, WINDOW), :], 0, 0)
+
+                    total = lax.fori_loop(1, further_windows(starts, i, e), more, total)
+                return total
+
+            total = lax.cond(any_further(starts, i, 0, experts), further, lambda total: total, total)
+            out_refs[d][pl.ds(pl.multiple_of(c * chunk, chunk), chunk), :] = total.astype(bf16)
+            return carry
+
+        lax.fori_loop(0, chunks, gather, 0)
+
+
+def combine(starts, order, rank, rows_parts, chunk, after):
+    owners = order.shape[0]
+    nodes, double = rank.shape[1], rows_parts[0].shape[2]
+    whole = lambda a: pl.BlockSpec(a.shape, lambda i, *_: (0,) * a.ndim)
+    out = jax.ShapeDtypeStruct((nodes // owners, double), bf16)
+    return pl.pallas_call(
+        functools.partial(combine_kernel, len(rows_parts), owners, chunk),
+        grid_spec=pltpu.PrefetchScalarGridSpec(
+            num_scalar_prefetch=2,
+            grid=(1,),
+            in_specs=[whole(rank)] + [whole(r) for r in rows_parts] + [pl.BlockSpec(memory_space=pl.ANY)] * len(after),
+            out_specs=[whole(out)] * owners,
+        ),
+        out_shape=[out] * owners,
+        compiler_params=params(),
+        cost_estimate=pl.CostEstimate(flops=EAGER * 10**9, bytes_accessed=10**7, transcendentals=0),
+        name="combine",
+    )(starts, order, rank, *rows_parts, *after)
 
 
 def home_kernel(parts, stream_ref, cot_ref, gain_ref, *refs):
-    layer_ref, grad_ref = refs[parts:]
+    layer_ref, grad_ref, token_ref = refs[parts:]
+    token_ref[...] = jnp.zeros_like(token_ref)
     total = refs[0][...].astype(f32)
     for g in refs[1:parts]:
         total = total + g[...].astype(f32)
@@ -444,7 +470,7 @@
     steps = tok_dev // chunk
     fresh = lambda w: pl.BlockSpec((chunk, w), lambda i, me: (i, 0))
     return pl.pallas_call(
-        lambda me, *refs: home_kernel(len(parts), *refs[:-3], *refs[-2:]),
+        lambda me, *refs: home_kernel(len(parts), *refs[:-4], *refs[-3:]),
         grid_spec=pltpu.PrefetchScalarGridSpec(
             num_scalar_prefetch=1,
             grid=(steps,),
@@ -455,9 +481,9 @@
             ]
             + [fresh(2 * width) for _ in parts]
             + [pl.BlockSpec(memory_space=pl.ANY)],
-            out_specs=[fresh(width), fresh(width)],
-        ),
-        out_shape=[jax.ShapeDtypeStruct((tok_dev, width), bf16)] * 2,
+            out_specs=[fresh(width), fresh(width), pl.BlockSpec((8, 128), lambda i, me: (0, 0))],
+        ),
+        out_shape=[jax.ShapeDtypeStruct((tok_dev, width), bf16)] * 2 + [jax.ShapeDtypeStruct((8, 128), f32)],
         compiler_params=params(),
         cost_estimate=pl.CostEstimate(
             flops=EAGER * tok_dev * width * 1000, bytes_accessed=tok_dev * width * 16, transcendentals=0
@@ -722,30 +748,33 @@
             pieces[d].append(lax.ppermute(part, "expert", shift_pairs(exp_count, d)))
     atts = [jnp.concatenate(p, 0) for p in pieces]
 
-    scalars = (counts, local_ids, perm, starts, owner_order, place)
+    scalars = (counts, local_ids, perm, starts, place)
     common = (rank, cotangent_all, gain, router)
     weights = (expert_in, expert_out, columns)
-    sums, last, stream, partials, first = [], [], None, None, 0
+    sums, last, stream, rows_parts, first = [], [], None, [], 0
     for g, count in enumerate(groups):
         head = (residual_all, atts, projs) if g == 0 else None
-        found = list(expert_group(scalars, common, weights, first, count, head, (stream, partials, last), lines, slot_rows, chunk))
+        found = list(expert_group(scalars, common, weights, first, count, head, (stream, last), lines, slot_rows, chunk))
         first += count
         if g == 0:
             stream = found.pop(0)
-        partials, grads = found[:exp_count], found[exp_count:]
-        sums.append(SeqSum(grads, seq_count))
+        rows_parts.append(found[0])
+        sums.append(SeqSum(found[1:], seq_count))
         if g == 0:
             last = sums[0].step(last)
-    parts = partials[:1] + [lax.ppermute(partials[d], "expert", shift_pairs(exp_count, d)) for d in range(1, exp_count)]
     steps = step_order(sums)
     for k, g in enumerate(steps):
         last = sums[g].step(last)
-        if k == len(steps) // 2:
-            layer_out, grad_stream = at_home(me, stream, cotangent, gain, parts, chunk, last[0])
-            last = [layer_out]
+        if k == len(groups) - 1:
+            partials = list(combine(starts, owner_order, rank, rows_parts, chunk, last))
+            last = [partials[0]]
+            parts = partials[:1] + [
+                lax.ppermute(partials[d], "expert", shift_pairs(exp_count, d)) for d in range(1, exp_count)
+            ]
+    layer_out, grad_stream, home = at_home(me, stream, cotangent, gain, parts, chunk, last[0])
     into, token = [], []
     for g, each_sum in enumerate(sums):
-        blocks = each_sum.blocks(token if g == len(sums) - 1 else [])
+        blocks = each_sum.blocks(token + [home] if g == len(sums) - 1 else [])
         *into, done = unpack(wheres[g], place, blocks, experts, width, ff, into)
         token = [done]
     grad_w_in, grad_w_out = into

time: 231 us -> 218 us (0.944)
  waiting for transfers between devices: 102 us -> 92.7 us
  Pallas kernels: 56.3 us -> 53.1 us
    ppermute x8, waiting for transfers between devices: 29.4 us -> 19.9 us  [to_line(): return lax.ppermute(x, 'seq', line_pairs(self.seq_count, step))]
    pallas_call x2, Pallas kernels: 30.1 us -> 21.1 us  [expert_group(): pl.pallas_call(functools.partial(group_kernel, first, count, pieces, 0 if...]
    pallas_call x1 -> x2, Pallas kernels: 1.94 us -> 7.74 us  [the longest x1 5.83 us: combine(): pl.pallas_call(functools.partial(combine_kernel, len(rows_parts), owners,...]
    ppermute x8, starting transfers between devices: 17.6 us -> 14.9 us  [to_line(): return lax.ppermute(x, 'seq', line_pairs(self.seq_count, step))]
  transfers between devices with their start and end apart: 56 -> 56, of which waited for: 24 -> 22; matrix products, arithmetic and copies ran while one was open for 10% -> 10% of each run, Pallas kernels for 17% -> 18%
where the time goes in v5:
time: 218 us; the launch traced here: 216 us
  waiting for transfers between devices  92.7 us (43%)
  Pallas kernels  53.1 us (24%)
  starting transfers between devices  45.6 us (21%)
  local copies, waits for them, and re-layouts  14.7 us (7%)
  other arithmetic  8.15 us (4%)
    ppermute x7, waiting for transfers between devices, ring_gather(): k = lax.ppermute(k, 'seq', fwd)  47.3 us
    pallas_call x2, Pallas kernels, expert_group(): pl.pallas_call(functools.partial(group_kernel, first, count, pieces, 0 if...  21.1 us
    ppermute x8, waiting for transfers between devices, to_line(): return lax.ppermute(x, 'seq', line_pairs(self.seq_count, step))  19.9 us
    pallas_call x2, Pallas kernels, attention(): pl.pallas_call(functools.partial(attention_kernel, degree, feat // HD, le...  17.2 us
    ppermute x8, starting transfers between devices, to_line(): return lax.ppermute(x, 'seq', line_pairs(self.seq_count, step))  14.9 us
    ppermute x7, starting transfers between devices, ring_gather(): k = lax.ppermute(k, 'seq', fwd)  10.9 us
    ppermute x2, waiting for transfers between devices, back_line(): self.other = lax.ppermute(self.own, 'seq', self.cross)  8.35 us
    pallas_call x2, Pallas kernels, unpack(): pl.pallas_call(functools.partial(unpack_kernel, lines, each, width), grid...  6.07 us
  transfers between devices with their start and end apart: 56, of which 22 were waited for; matrix products, arithmetic and copies ran while one was open for 10% of the time, Pallas kernels for 18%

profile of v5, /device:TPU:0, one launch (start us, length us, event | category | flops | bytes accessed | tf_op | source)
XLA Modules:
  0.0 215.5 jit_solution(14745661946788744041)
XLA Ops:
  1.2 2.6 %collective-permute-start.3 = (bf16[128,2048]{1,0:T(8,128)(2,1)}, bf16[128,2048]{1,0:T(8,128)(2,1)}, u32[]{:S(2)}, u32[]{:S(2)}) collective-permute-start(bf16[128,2048]{1,0:T(8,128)(2,1)} %refs_0_.3), channel_id=1, source_target_pairs={{0,8},{2,10},{8,16},{10,18},{16,24},{18,26},{24,28},{26,30},{28,20... | collective-permute-start | bytes 1572872 | tf_op jit(solution)/shard_map/ppermute | solution.py:73
  3.8 1.5 collective-permute-start
  6.7 1.2 dynamic_slice.13
  9.6 6.9 %collective-permute-done.3.refs_1_ = bf16[128,2048]{1,0:T(8,128)(2,1)} collective-permute-done((bf16[128,2048]{1,0:T(8,128)(2,1)}, bf16[128,2048]{1,0:T(8,128)(2,1)}, u32[]{:S(2)}, u32[]{:S(2)}) %collective-permute-start.3) | collective-permute-done | bytes 524320 | tf_op jit(solution)/shard_map/ppermute | solution.py:73
  16.6 1.8 collective-permute-start.4
  20.3 10.1 %collective-permute-done.4.refs_2_ = bf16[128,2048]{1,0:T(8,128)(2,1)S(1)} collective-permute-done((bf16[128,2048]{1,0:T(8,128)(2,1)}, bf16[128,2048]{1,0:T(8,128)(2,1)S(1)}, u32[]{:S(2)}, u32[]{:S(2)}) %collective-permute-start.4) | collective-permute-done | bytes 524320 | tf_op jit(solution)/shard_map/ppermute | solution.py:73
  30.5 1.6 collective-permute-start.5
  34.0 9.4 %collective-permute-done.5.refs_3_ = bf16[128,2048]{1,0:T(8,128)(2,1)} collective-permute-done((bf16[128,2048]{1,0:T(8,128)(2,1)S(1)}, bf16[128,2048]{1,0:T(8,128)(2,1)}, u32[]{:S(2)}, u32[]{:S(2)}) %collective-permute-start.5) | collective-permute-done | bytes 524320 | tf_op jit(solution)/shard_map/ppermute | solution.py:73
  43.4 1.4 collective-permute-start.6
  47.1 1.2 constant_dynamic-update-slice_fusion.1
  49.0 6.6 %collective-permute-done.6.refs_4_ = bf16[128,2048]{1,0:T(8,128)(2,1)} collective-permute-done((bf16[128,2048]{1,0:T(8,128)(2,1)}, bf16[128,2048]{1,0:T(8,128)(2,1)}, u32[]{:S(2)}, u32[]{:S(2)}) %collective-permute-start.6) | collective-permute-done | bytes 524320 | tf_op jit(solution)/shard_map/ppermute | solution.py:73
  55.6 1.3 collective-permute-start.7
  60.1 7.6 %collective-permute-done.7.refs_5_ = bf16[128,2048]{1,0:T(8,128)(2,1)} collective-permute-done((bf16[128,2048]{1,0:T(8,128)(2,1)}, bf16[128,2048]{1,0:T(8,128)(2,1)}, u32[]{:S(2)}, u32[]{:S(2)}) %collective-permute-start.7) | collective-permute-done | bytes 524320 | tf_op jit(solution)/shard_map/ppermute | solution.py:73
  67.7 1.3 collective-permute-start.8
  70.0 3.8 %reduce-window.6 = s32[8,16,128]{2,1,0:T(8,128)} reduce-window(s32[8,16,128]{2,1,0:T(8,128)S(1)} %copy.46, s32[]{:T(128)} %constant.111.clone.1), window={size=1x1x128 pad=0_0x0_0x127_0}, to_apply=%region_1.2 | reduce-window | flops 2080768 | bytes 131076 | tf_op jit(solution)/shard_map/reduce-window
  74.4 4.1 %collective-permute-done.8.refs_6_ = bf16[128,2048]{1,0:T(8,128)(2,1)} collective-permute-done((bf16[128,2048]{1,0:T(8,128)(2,1)}, bf16[128,2048]{1,0:T(8,128)(2,1)}, u32[]{:S(2)}, u32[]{:S(2)}) %collective-permute-start.8) | collective-permute-done | bytes 524320 | tf_op jit(solution)/shard_map/ppermute | solution.py:73
  79.4 1.1 collective-permute-start.24
  80.5 1.1 slice_reduce_fusion
  86.7 2.6 %collective-permute-done.9.refs_7_ = bf16[128,2048]{1,0:T(8,128)(2,1)} collective-permute-done((bf16[128,2048]{1,0:T(8,128)(2,1)}, bf16[128,2048]{1,0:T(8,128)(2,1)}, u32[]{:S(2)}, u32[]{:S(2)}) %collective-permute-start.9) | collective-permute-done | bytes 524320 | tf_op jit(solution)/shard_map/ppermute | solution.py:73
  93.1 8.5 %attention.2 = bf16[1024,128]{1,0:T(8,128)(2,1)} custom-call(s32[32]{0:T(128)} %squeeze.37.local, s32[32]{0:T(128)} %get-tuple-element.77.korder, s32[17]{0:T(128)} %get-tuple-element.84.kbegin, s32[32]{0:T(128)} %get-tuple-element.75.vorder, s32[17]{0:T(128)} %get-tuple-element.62.vbegin, bf16[128,2048]{1,0:T(8,128)(2,1)} %q_ref.3, ...), custom_call_target="tpu_custom_call" | custom-call | flops 268435456 | bytes 2621440 | tf_op jit(solution)/shard_map/attention/pallas_call | solution.py:159
  101.6 1.6 collective-permute-start.33
  103.2 8.7 %attention.3 = bf16[1024,128]{1,0:T(8,128)(2,1)} custom-call(s32[32]{0:T(128)} %squeeze.43.local, s32[32]{0:T(128)} %get-tuple-element.78.korder, s32[17]{0:T(128)} %get-tuple-element.83.kbegin, s32[32]{0:T(128)} %get-tuple-element.76.vorder, s32[17]{0:T(128)} %get-tuple-element.63.vbegin, bf16[128,2048]{1,0:T(8,128)(2,1)} %q_ref.3, ...), custom_call_target="tpu_custom_call" | custom-call | flops 268435456 | bytes 2621440 | tf_op jit(solution)/shard_map/attention/pallas_call | solution.py:159
  112.5 1.1 constant_dynamic-update-slice_fusion.refs_7_
  114.6 5.6 %collective-permute-done.34 = bf16[1024,128]{1,0:T(8,128)(2,1)S(1)} collective-permute-done((bf16[1024,128]{1,0:T(8,128)(2,1)}, bf16[1024,128]{1,0:T(8,128)(2,1)S(1)}, u32[]{:S(2)}, u32[]{:S(2)}) %collective-permute-start.34) | collective-permute-done | bytes 262176 | tf_op jit(solution)/shard_map/ppermute | solution.py:748
  120.3 11.2 %experts.2 = (bf16[2048,256]{1,0:T(8,128)(2,1)S(1)}, bf16[4,640,512]{2,1,0:T(8,128)(2,1)S(1)}, bf16[1,512,512]{2,1,0:T(8,128)(2,1)S(1)}, bf16[1,512,512]{2,1,0:T...) custom-call(s32[8]{0:T(128)S(1)} %slice_reduce_fusion.5.counts, ...), custom_call_target="tpu_custom_call" | custom-call | flops 1000 | bytes 1000 | tf_op jit(solution)/shard_map/experts/pallas_call | solution.py:380
  132.1 1.4 collective-permute-done.35.refs_1_
  134.6 9.9 %experts.3 = (bf16[4,640,512]{2,1,0:T(8,128)(2,1)S(1)}, bf16[1,512,512]{2,1,0:T(8,128)(2,1)S(1)}, bf16[1,512,512]{2,1,0:T(8,128)(2,1)S(1)}, bf16[1,512,512]{2,1,0:T(8,128)(2,1)S(1)}, bf16[1,512,512]{2,1,0:T(8,128)(2,1)S(1)}) custom-call(s32[8]{0:T(128)S(1)} %slice_reduce_fusion.5.counts, s32[8]{0:T(128)S(1)} %broadcast_add_fusion.ids, s32[8]{0:T(128)S(1)} %stack.58.perm, ...), custom_call_target="tpu_custom_call" | custom-call | flops 1000 | bytes 1000 | tf_op jit(solution)/shard_map/experts/pallas_call | solution.py:380
  145.5 2.1 collective-permute-done.38.refs_2_
  147.9 1.6 collective-permute-start.42
  150.7 5.8 %combine.1 = (bf16[1024,512]{1,0:T(8,128)(2,1)S(1)}, bf16[1024,512]{1,0:T(8,128)(2,1)S(1)}) custom-call(s32[9,8]{1,0:T(8,128)S(1)} %copy.52.starts, s32[2]{0:T(128)S(1)} %compare_select_fusion.1.order, s32[8,2048]{1,0:T(8,128)S(1)} %add_select_fusion.refs_0_.rank_ref, bf16[4,640,512]{2,1,0:T(8,128)(2,1)S(1)} %get-tuple-element.34.refs_0_, ...), custom_call_target="tpu_custom_call" | custom-call | flops 32000000000 | bytes 10000000 | tf_op jit(solution)/shard_map/combine/pallas_call | solution.py:437
  156.6 2.7 %collective-permute-start.44 = (bf16[1,128,512]{2,1,0:T(8,128)(2,1)S(1)}, bf16[1,128,512]{2,1,0:T(8,128)(2,1)S(1)}, u32[]{:S(2)}, u32[]{:S(2)}) collective-permute-start(bf16[1,128,512]{2,1,0:T(8,128)(2,1)S(1)} %get-tuple-element.48.refs_3_), channel_id=1, source_target_pairs={{0,16},{2,18},{4,20},{6,22},{8,24},{10,26},{12,28},{14,30},{16,0},... | collective-permute-start | bytes 393224 | tf_op jit(solution)/shard_map/ppermute | solution.py:569
  159.2 3.3 %collective-permute-done.41.refs_2_ = bf16[1,512,512]{2,1,0:T(8,128)(2,1)S(1)} collective-permute-done((bf16[1,512,512]{2,1,0:T(8,128)(2,1)S(1)}, bf16[1,512,512]{2,1,0:T(8,128)(2,1)S(1)}, u32[]{:S(2)}, u32[]{:S(2)}) %collective-permute-start.41) | collective-permute-done | bytes 524320 | tf_op jit(solution)/shard_map/ppermute | solution.py:573
  163.5 1.3 collective-permute-start.39
  164.8 1.9 collective-permute-start.46
  166.7 6.5 %collective-permute-done.43.refs_1_ = bf16[1,256,512]{2,1,0:T(8,128)(2,1)S(1)} collective-permute-done((bf16[1,256,512]{2,1,0:T(8,128)(2,1)S(1)}, bf16[1,256,512]{2,1,0:T(8,128)(2,1)S(1)}, u32[]{:S(2)}, u32[]{:S(2)}) %collective-permute-start.43) | collective-permute-done | bytes 262176 | tf_op jit(solution)/shard_map/ppermute | solution.py:569
  173.3 1.3 collective-permute-start.48
  174.6 1.7 collective-permute-start.45
  176.4 4.3 %collective-permute-done.45.refs_1_ = bf16[1,128,512]{2,1,0:T(8,128)(2,1)S(1)} collective-permute-done((bf16[1,128,512]{2,1,0:T(8,128)(2,1)S(1)}, bf16[1,128,512]{2,1,0:T(8,128)(2,1)S(1)}, u32[]{:S(2)}, u32[]{:S(2)}) %collective-permute-start.45) | collective-permute-done | bytes 131104 | tf_op jit(solution)/shard_map/ppermute | solution.py:569
  181.4 1.1 collective-permute-start.51
  182.6 2.0 collective-permute-start.47
  184.5 4.1 %collective-permute-done.47.refs_1_ = bf16[1,1,128,512]{3,2,1,0:T(8,128)(2,1)S(1)} collective-permute-done((bf16[1,1,128,512]{3,2,1,0:T(8,128)(2,1)S(1)}, bf16[1,1,128,512]{3,2,1,0:T(8,128)(2,1)S(1)}, u32[]{:S(2)}, u32[]{:S(2)}) %collective-permute-start.47) | collective-permute-done | bytes 131104 | tf_op jit(solution)/shard_map/ppermute | solution.py:569
  188.7 3.0 %collective-permute-start.49 = (bf16[2,1,128,512]{3,2,1,0:T(8,128)(2,1)S(1)}, bf16[2,1,128,512]{3,2,1,0:T(8,128)(2,1)S(1)}, u32[]{:S(2)}, u32[]{:S(2)}) collective-permute-start(bf16[2,1,128,512]{3,2,1,0:T(8,128)(2,1)S(1)} %stack_pieces.7.refs_0_.refs_2_), channel_id=1, source_target_pairs={{0,8},{2,10},{4,12},{6,14},{8,0},{10,2},{12,4},{14,6},{16,24},{18,... | collective-permute-start | bytes 786440 | tf_op jit(solution)/shard_map/ppermute | solution.py:569
  191.7 4.3 %collective-permute-done.49.refs_1_ = bf16[2,1,128,512]{3,2,1,0:T(8,128)(2,1)S(1)} collective-permute-done((bf16[2,1,128,512]{3,2,1,0:T(8,128)(2,1)S(1)}, bf16[2,1,128,512]{3,2,1,0:T(8,128)(2,1)S(1)}, u32[]{:S(2)}, u32[]{:S(2)}) %collective-permute-start.49) | collective-permute-done | bytes 262176 | tf_op jit(solution)/shard_map/ppermute | solution.py:569
  197.2 1.9 at_home.1
  199.1 3.0 %unpack.2 = (f32[8,256,512]{2,1,0:T(8,128)}, f32[8,512,256]{2,1,0:T(8,128)}, f32[8,128]{1,0:T(8,128)S(1)}) custom-call(s32[4]{0:T(128)S(1)} %pad_add_fusion.2.where, s32[2]{0:T(128)S(1)} %pad_add_fusion.place, bf16[4,1,128,512]{3,2,1,0:T(8,128)(2,1)S(1)} %stack_pieces.6.refs_2_.refs_0_, bf16[4,1,128,512]{3,2,1,0:T(8,128)(2,1)S(1)} %collective-permute-done.51.refs_1_, ...), custom_call_target="tpu_custom_call" | custom-call | flops 201326592 | bytes 6291456 | tf_op jit(solution)/shard_map/unpack/pallas_call | solution.py:651
  202.1 8.3 %collective-permute-done.50.refs_0_ = bf16[4,1,128,512]{3,2,1,0:T(8,128)(2,1)S(1)} collective-permute-done((bf16[4,1,128,512]{3,2,1,0:T(8,128)(2,1)S(1)}, bf16[4,1,128,512]{3,2,1,0:T(8,128)(2,1)S(1)}, u32[]{:S(2)}, u32[]{:S(2)}) %collective-permute-start.50) | collective-permute-done | bytes 524320 | tf_op jit(solution)/shard_map/ppermute | solution.py:596
  210.7 1.8 collective-permute-done.55.refs_3_
  212.5 3.0 %unpack.3 = (f32[8,256,512]{2,1,0:T(8,128)}, f32[8,512,256]{2,1,0:T(8,128)}, f32[8,128]{1,0:T(8,128)}) custom-call(s32[4]{0:T(128)S(1)} %pad_add_fusion.1.where, s32[2]{0:T(128)S(1)} %pad_add_fusion.place, bf16[4,1,128,512]{3,2,1,0:T(8,128)(2,1)S(1)} %stack_pieces.8.refs_5_.refs_0_, ...), custom_call_target="tpu_custom_call", output_to_operand_aliasing={{0}: (6, {}), {1}: (7, {})} | custom-call | flops 201326592 | bytes 6291456 | tf_op jit(solution)/shard_map/unpack/pallas_call | solution.py:651
  (188 shorter events, 33.7 us)
Async XLA Ops:
  0.6 47.7 %collective-permute-start.10 = (bf16[128,2048]{1,0:T(8,128)(2,1)}, bf16[128,2048]{1,0:T(8,128)(2,1)}, u32[]{:S(2)}, u32[]{:S(2)}) collective-permute-start(bf16[128,2048]{1,0:T(8,128)(2,1)} %refs_0_.3), channel_id=1, source_target_pairs={{0,2},{2,0},{4,6},{6,4},{8,10},{10,8},{12,14},{14,12},{16,18},{18,... | collective-permute-start | bytes 1572872 | tf_op jit(solution)/shard_map/ppermute | solution.py:77
  1.2 15.4 %collective-permute-start.3 = (bf16[128,2048]{1,0:T(8,128)(2,1)}, bf16[128,2048]{1,0:T(8,128)(2,1)}, u32[]{:S(2)}, u32[]{:S(2)}) collective-permute-start(bf16[128,2048]{1,0:T(8,128)(2,1)} %refs_0_.3), channel_id=1, source_target_pairs={{0,8},{2,10},{8,16},{10,18},{16,24},{18,26},{24,28},{26,30},{28,20... | collective-permute-start | bytes 1572872 | tf_op jit(solution)/shard_map/ppermute | solution.py:73
  3.8 29.6 %collective-permute-start = (s32[2,1024]{1,0:T(2,128)}, s32[2,1024]{1,0:T(2,128)S(1)}, u32[]{:S(2)}, u32[]{:S(2)}) collective-permute-start(s32[2,1024]{1,0:T(2,128)} %bitcast.49), channel_id=1, source_target_pairs={{0,1},{1,0},{2,3},{3,2},{4,5},{5,4},{6,7},{7,6},{8,9},{9,8},{10,11... | collective-permute-start | bytes 24584 | tf_op jit(solution)/shard_map/ppermute | solution.py:61
  5.3 28.2 %collective-permute-start.1 = (bf16[1024,256]{1,0:T(8,128)(2,1)}, bf16[1024,256]{1,0:T(8,128)(2,1)S(1)}, u32[]{:S(2)}, u32[]{:S(2)}) collective-permute-start(bf16[1024,256]{1,0:T(8,128)(2,1)} %refs_1_.1), channel_id=1, source_target_pairs={{0,1},{1,0},{2,3},{3,2},{4,5},{5,4},{6,7},{7,6},{8,9},{9,8},{10,11... | collective-permute-start | bytes 1572872 | tf_op jit(solution)/shard_map/ppermute | solution.py:61
  5.8 13.6 %collective-permute-start.18 = (bf16[128,2048]{1,0:T(8,128)(2,1)}, bf16[128,2048]{1,0:T(8,128)(2,1)S(1)}, u32[]{:S(2)}, u32[]{:S(2)}) collective-permute-start(bf16[128,2048]{1,0:T(8,128)(2,1)} %refs_16_.3), channel_id=1, source_target_pairs={{0,4},{2,6},{8,0},{10,2},{16,8},{18,10},{24,16},{26,18},{28,24},{3... | collective-permute-start | bytes 1572872 | tf_op jit(solution)/shard_map/ppermute | solution.py:74
  16.6 13.9 %collective-permute-start.4 = (bf16[128,2048]{1,0:T(8,128)(2,1)}, bf16[128,2048]{1,0:T(8,128)(2,1)S(1)}, u32[]{:S(2)}, u32[]{:S(2)}) collective-permute-start(bf16[128,2048]{1,0:T(8,128)(2,1)} %collective-permute-done.3.refs_1_), channel_id=1, source_target_pairs={{0,8},{2,10},{8,16},{10,18},{16,24},{18,26},{24,28},{26,30},{28,20... | collective-permute-start | bytes 1572872 | tf_op jit(solution)/shard_map/ppermute | solution.py:73
  19.5 12.6 %collective-permute-start.19 = (bf16[128,2048]{1,0:T(8,128)(2,1)S(1)}, bf16[128,2048]{1,0:T(8,128)(2,1)S(1)}, u32[]{:S(2)}, u32[]{:S(2)}) collective-permute-start(bf16[128,2048]{1,0:T(8,128)(2,1)S(1)} %collective-permute-done.18.refs_17_), channel_id=1, source_target_pairs={{0,4},{2,6},{8,0},{10,2},{16,8},{18,10},{24,16},{26,18},{28,24},{3... | collective-permute-start | bytes 1572872 | tf_op jit(solution)/shard_map/ppermute | solution.py:74
  30.5 12.9 %collective-permute-start.5 = (bf16[128,2048]{1,0:T(8,128)(2,1)S(1)}, bf16[128,2048]{1,0:T(8,128)(2,1)}, u32[]{:S(2)}, u32[]{:S(2)}) collective-permute-start(bf16[128,2048]{1,0:T(8,128)(2,1)S(1)} %collective-permute-done.4.refs_2_), channel_id=1, source_target_pairs={{0,8},{2,10},{8,16},{10,18},{16,24},{18,26},{24,28},{26,30},{28,20... | collective-permute-start | bytes 1572872 | tf_op jit(solution)/shard_map/ppermute | solution.py:73
  32.1 12.7 %collective-permute-start.20 = (bf16[128,2048]{1,0:T(8,128)(2,1)S(1)}, bf16[128,2048]{1,0:T(8,128)(2,1)}, u32[]{:S(2)}, u32[]{:S(2)}) collective-permute-start(bf16[128,2048]{1,0:T(8,128)(2,1)S(1)} %collective-permute-done.19.refs_18_), channel_id=1, source_target_pairs={{0,4},{2,6},{8,0},{10,2},{16,8},{18,10},{24,16},{26,18},{28,24},{3... | collective-permute-start | bytes 1572872 | tf_op jit(solution)/shard_map/ppermute | solution.py:74
  33.4 15.0 %collective-permute-start.25 = (bf16[128,2048]{1,0:T(8,128)(2,1)S(1)}, bf16[128,2048]{1,0:T(8,128)(2,1)}, u32[]{:S(2)}, u32[]{:S(2)}) collective-permute-start(bf16[128,2048]{1,0:T(8,128)(2,1)S(1)} %copy-done.5), channel_id=1, source_target_pairs={{0,2},{2,0},{4,6},{6,4},{8,10},{10,8},{12,14},{14,12},{16,18},{18,... | collective-permute-start | bytes 1572872 | tf_op jit(solution)/shard_map/ppermute | solution.py:78
  33.5 15.4 %collective-permute-start.11 = (bf16[128,2048]{1,0:T(8,128)(2,1)}, bf16[128,2048]{1,0:T(8,128)(2,1)}, u32[]{:S(2)}, u32[]{:S(2)}) collective-permute-start(bf16[128,2048]{1,0:T(8,128)(2,1)} %collective-permute-done.3.refs_1_), channel_id=1, source_target_pairs={{0,2},{2,0},{4,6},{6,4},{8,10},{10,8},{12,14},{14,12},{16,18},{18,... | collective-permute-start | bytes 1572872 | tf_op jit(solution)/shard_map/ppermute | solution.py:77
  43.4 12.2 %collective-permute-start.6 = (bf16[128,2048]{1,0:T(8,128)(2,1)}, bf16[128,2048]{1,0:T(8,128)(2,1)}, u32[]{:S(2)}, u32[]{:S(2)}) collective-permute-start(bf16[128,2048]{1,0:T(8,128)(2,1)} %collective-permute-done.5.refs_3_), channel_id=1, source_target_pairs={{0,8},{2,10},{8,16},{10,18},{16,24},{18,26},{24,28},{26,30},{28,20... | collective-permute-start | bytes 1572872 | tf_op jit(solution)/shard_map/ppermute | solution.py:73
  44.8 12.1 %collective-permute-start.21 = (bf16[128,2048]{1,0:T(8,128)(2,1)}, bf16[128,2048]{1,0:T(8,128)(2,1)}, u32[]{:S(2)}, u32[]{:S(2)}) collective-permute-start(bf16[128,2048]{1,0:T(8,128)(2,1)} %collective-permute-done.20.refs_19_), channel_id=1, source_target_pairs={{0,4},{2,6},{8,0},{10,2},{16,8},{18,10},{24,16},{26,18},{28,24},{3... | collective-permute-start | bytes 1572872 | tf_op jit(solution)/shard_map/ppermute | solution.py:74
  48.3 11.2 %collective-permute-start.26 = (bf16[128,2048]{1,0:T(8,128)(2,1)S(1)}, bf16[128,2048]{1,0:T(8,128)(2,1)S(1)}, u32[]{:S(2)}, u32[]{:S(2)}) collective-permute-start(bf16[128,2048]{1,0:T(8,128)(2,1)S(1)} %copy-done.7), channel_id=1, source_target_pairs={{0,2},{2,0},{4,6},{6,4},{8,10},{10,8},{12,14},{14,12},{16,18},{18,... | collective-permute-start | bytes 1572872 | tf_op jit(solution)/shard_map/ppermute | solution.py:78
  48.4 11.1 %collective-permute-start.12 = (bf16[128,2048]{1,0:T(8,128)(2,1)S(1)}, bf16[128,2048]{1,0:T(8,128)(2,1)S(1)}, u32[]{:S(2)}, u32[]{:S(2)}) collective-permute-start(bf16[128,2048]{1,0:T(8,128)(2,1)S(1)} %copy-done.9), channel_id=1, source_target_pairs={{0,2},{2,0},{4,6},{6,4},{8,10},{10,8},{12,14},{14,12},{16,18},{18,... | collective-permute-start | bytes 1572872 | tf_op jit(solution)/shard_map/ppermute | solution.py:77
  48.9 11.1 %collective-permute-start.27 = (bf16[128,2048]{1,0:T(8,128)(2,1)}, bf16[128,2048]{1,0:T(8,128)(2,1)S(1)}, u32[]{:S(2)}, u32[]{:S(2)}) collective-permute-start(bf16[128,2048]{1,0:T(8,128)(2,1)} %copy-done.10), channel_id=1, source_target_pairs={{0,2},{2,0},{4,6},{6,4},{8,10},{10,8},{12,14},{14,12},{16,18},{18,... | collective-permute-start | bytes 1572872 | tf_op jit(solution)/shard_map/ppermute | solution.py:78
  55.6 12.1 %collective-permute-start.7 = (bf16[128,2048]{1,0:T(8,128)(2,1)}, bf16[128,2048]{1,0:T(8,128)(2,1)}, u32[]{:S(2)}, u32[]{:S(2)}) collective-permute-start(bf16[128,2048]{1,0:T(8,128)(2,1)} %collective-permute-done.6.refs_4_), channel_id=1, source_target_pairs={{0,8},{2,10},{8,16},{10,18},{16,24},{18,26},{24,28},{26,30},{28,20... | collective-permute-start | bytes 1572872 | tf_op jit(solution)/shard_map/ppermute | solution.py:73
  56.9 12.1 %collective-permute-start.22 = (bf16[128,2048]{1,0:T(8,128)(2,1)}, bf16[128,2048]{1,0:T(8,128)(2,1)}, u32[]{:S(2)}, u32[]{:S(2)}) collective-permute-start(bf16[128,2048]{1,0:T(8,128)(2,1)} %collective-permute-done.21.refs_20_), channel_id=1, source_target_pairs={{0,4},{2,6},{8,0},{10,2},{16,8},{18,10},{24,16},{26,18},{28,24},{3... | collective-permute-start | bytes 1572872 | tf_op jit(solution)/shard_map/ppermute | solution.py:74
  59.5 14.3 %collective-permute-start.13 = (bf16[128,2048]{1,0:T(8,128)(2,1)}, bf16[128,2048]{1,0:T(8,128)(2,1)}, u32[]{:S(2)}, u32[]{:S(2)}) collective-permute-start(bf16[128,2048]{1,0:T(8,128)(2,1)} %collective-permute-done.5.refs_3_), channel_id=1, source_target_pairs={{0,2},{2,0},{4,6},{6,4},{8,10},{10,8},{12,14},{14,12},{16,18},{18,... | collective-permute-start | bytes 1572872 | tf_op jit(solution)/shard_map/ppermute | solution.py:77
  59.5 14.3 %collective-permute-start.28 = (bf16[128,2048]{1,0:T(8,128)(2,1)}, bf16[128,2048]{1,0:T(8,128)(2,1)}, u32[]{:S(2)}, u32[]{:S(2)}) collective-permute-start(bf16[128,2048]{1,0:T(8,128)(2,1)} %collective-permute-done.20.refs_19_), channel_id=1, source_target_pairs={{0,2},{2,0},{4,6},{6,4},{8,10},{10,8},{12,14},{14,12},{16,18},{18,... | collective-permute-start | bytes 1572872 | tf_op jit(solution)/shard_map/ppermute | solution.py:78
  60.0 14.3 %collective-permute-start.14 = (bf16[128,2048]{1,0:T(8,128)(2,1)}, bf16[128,2048]{1,0:T(8,128)(2,1)}, u32[]{:S(2)}, u32[]{:S(2)}) collective-permute-start(bf16[128,2048]{1,0:T(8,128)(2,1)} %collective-permute-done.6.refs_4_), channel_id=1, source_target_pairs={{0,2},{2,0},{4,6},{6,4},{8,10},{10,8},{12,14},{14,12},{16,18},{18,... | collective-permute-start | bytes 1572872 | tf_op jit(solution)/shard_map/ppermute | solution.py:77
  67.7 10.8 %collective-permute-start.8 = (bf16[128,2048]{1,0:T(8,128)(2,1)}, bf16[128,2048]{1,0:T(8,128)(2,1)}, u32[]{:S(2)}, u32[]{:S(2)}) collective-permute-start(bf16[128,2048]{1,0:T(8,128)(2,1)} %collective-permute-done.7.refs_5_), channel_id=1, source_target_pairs={{0,8},{2,10},{8,16},{10,18},{16,24},{18,26},{24,28},{26,30},{28,20... | collective-permute-start | bytes 1572872 | tf_op jit(solution)/shard_map/ppermute | solution.py:73
  68.9 10.4 %collective-permute-start.23 = (bf16[128,2048]{1,0:T(8,128)(2,1)}, bf16[128,2048]{1,0:T(8,128)(2,1)}, u32[]{:S(2)}, u32[]{:S(2)}) collective-permute-start(bf16[128,2048]{1,0:T(8,128)(2,1)} %collective-permute-done.22.refs_21_), channel_id=1, source_target_pairs={{0,4},{2,6},{8,0},{10,2},{16,8},{18,10},{24,16},{26,18},{28,24},{3... | collective-permute-start | bytes 1572872 | tf_op jit(solution)/shard_map/ppermute | solution.py:74
  73.8 11.5 %collective-permute-start.29 = (bf16[128,2048]{1,0:T(8,128)(2,1)}, bf16[128,2048]{1,0:T(8,128)(2,1)}, u32[]{:S(2)}, u32[]{:S(2)}) collective-permute-start(bf16[128,2048]{1,0:T(8,128)(2,1)} %collective-permute-done.21.refs_20_), channel_id=1, source_target_pairs={{0,2},{2,0},{4,6},{6,4},{8,10},{10,8},{12,14},{14,12},{16,18},{18,... | collective-permute-start | bytes 1572872 | tf_op jit(solution)/shard_map/ppermute | solution.py:78
  73.8 12.4 %collective-permute-start.15 = (bf16[128,2048]{1,0:T(8,128)(2,1)}, bf16[128,2048]{1,0:T(8,128)(2,1)}, u32[]{:S(2)}, u32[]{:S(2)}) collective-permute-start(bf16[128,2048]{1,0:T(8,128)(2,1)} %collective-permute-done.7.refs_5_), channel_id=1, source_target_pairs={{0,2},{2,0},{4,6},{6,4},{8,10},{10,8},{12,14},{14,12},{16,18},{18,... | collective-permute-start | bytes 1572872 | tf_op jit(solution)/shard_map/ppermute | solution.py:77
  74.3 11.9 %collective-permute-start.30 = (bf16[128,2048]{1,0:T(8,128)(2,1)}, bf16[128,2048]{1,0:T(8,128)(2,1)}, u32[]{:S(2)}, u32[]{:S(2)}) collective-permute-start(bf16[128,2048]{1,0:T(8,128)(2,1)} %collective-permute-done.22.refs_21_), channel_id=1, source_target_pairs={{0,2},{2,0},{4,6},{6,4},{8,10},{10,8},{12,14},{14,12},{16,18},{18,... | collective-permute-start | bytes 1572872 | tf_op jit(solution)/shard_map/ppermute | solution.py:78
  78.5 10.9 %collective-permute-start.9 = (bf16[128,2048]{1,0:T(8,128)(2,1)}, bf16[128,2048]{1,0:T(8,128)(2,1)}, u32[]{:S(2)}, u32[]{:S(2)}) collective-permute-start(bf16[128,2048]{1,0:T(8,128)(2,1)} %collective-permute-done.8.refs_6_), channel_id=1, source_target_pairs={{0,8},{2,10},{8,16},{10,18},{16,24},{18,26},{24,28},{26,30},{28,20... | collective-permute-start | bytes 1572872 | tf_op jit(solution)/shard_map/ppermute | solution.py:73
  79.4 10.8 %collective-permute-start.24 = (bf16[128,2048]{1,0:T(8,128)(2,1)}, bf16[128,2048]{1,0:T(8,128)(2,1)}, u32[]{:S(2)}, u32[]{:S(2)}) collective-permute-start(bf16[128,2048]{1,0:T(8,128)(2,1)} %collective-permute-done.23.refs_22_), channel_id=1, source_target_pairs={{0,4},{2,6},{8,0},{10,2},{16,8},{18,10},{24,16},{26,18},{28,24},{3... | collective-permute-start | bytes 1572872 | tf_op jit(solution)/shard_map/ppermute | solution.py:74
  85.3 27.2 %collective-permute-start.2 = (bf16[1024,256]{1,0:T(8,128)(2,1)}, bf16[1024,256]{1,0:T(8,128)(2,1)}, u32[]{:S(2)}, u32[]{:S(2)}) collective-permute-start(bf16[1024,256]{1,0:T(8,128)(2,1)} %param.17), channel_id=1, source_target_pairs={{0,1},{1,0},{2,3},{3,2},{4,5},{5,4},{6,7},{7,6},{8,9},{9,8},{10,11... | collective-permute-start | bytes 1572872 | tf_op jit(solution)/shard_map/ppermute | solution.py:61
  101.6 13.0 %collective-permute-start.33 = (bf16[1024,128]{1,0:T(8,128)(2,1)}, bf16[1024,128]{1,0:T(8,128)(2,1)S(1)}, u32[]{:S(2)}, u32[]{:S(2)}) collective-permute-start(bf16[1024,128]{1,0:T(8,128)(2,1)} %attention.2), channel_id=1, source_target_pairs={{0,1},{1,0},{2,3},{3,2},{4,5},{5,4},{6,7},{7,6},{8,9},{9,8},{10,11... | collective-permute-start | bytes 786440 | tf_op jit(solution)/shard_map/ppermute | solution.py:748
  111.9 8.3 %collective-permute-start.34 = (bf16[1024,128]{1,0:T(8,128)(2,1)}, bf16[1024,128]{1,0:T(8,128)(2,1)S(1)}, u32[]{:S(2)}, u32[]{:S(2)}) collective-permute-start(bf16[1024,128]{1,0:T(8,128)(2,1)} %attention.3), channel_id=1, source_target_pairs={{0,1},{1,0},{2,3},{3,2},{4,5},{5,4},{6,7},{7,6},{8,9},{9,8},{10,11... | collective-permute-start | bytes 786440 | tf_op jit(solution)/shard_map/ppermute | solution.py:748
  131.6 13.9 %collective-permute-start.37 = (bf16[1,512,512]{2,1,0:T(8,128)(2,1)S(1)}, bf16[1,512,512]{2,1,0:T(8,128)(2,1)S(1)}, u32[]{:S(2)}, u32[]{:S(2)}) collective-permute-start(bf16[1,512,512]{2,1,0:T(8,128)(2,1)S(1)} %get-tuple-element.41), channel_id=1, source_target_pairs={{0,2},{2,0},{4,6},{6,4},{8,10},{10,8},{12,14},{14,12},{16,18},{18,... | collective-permute-start | bytes 1572872 | tf_op jit(solution)/shard_map/ppermute | solution.py:566
  133.6 14.0 %collective-permute-start.38 = (bf16[1,512,512]{2,1,0:T(8,128)(2,1)S(1)}, bf16[1,512,512]{2,1,0:T(8,128)(2,1)S(1)}, u32[]{:S(2)}, u32[]{:S(2)}) collective-permute-start(bf16[1,512,512]{2,1,0:T(8,128)(2,1)S(1)} %sum_core.2.refs_8_.refs_3_), channel_id=1, source_target_pairs={{0,4},{2,6},{4,0},{6,2},{8,12},{10,14},{12,8},{14,10},{16,20},{18,... | collective-permute-start | bytes 1572872 | tf_op jit(solution)/shard_map/ppermute | solution.py:573
  145.4 13.8 %collective-permute-start.40 = (bf16[1,512,512]{2,1,0:T(8,128)(2,1)S(1)}, bf16[1,512,512]{2,1,0:T(8,128)(2,1)S(1)}, u32[]{:S(2)}, u32[]{:S(2)}) collective-permute-start(bf16[1,512,512]{2,1,0:T(8,128)(2,1)S(1)} %get-tuple-element.46), channel_id=1, source_target_pairs={{0,2},{2,0},{4,6},{6,4},{8,10},{10,8},{12,14},{14,12},{16,18},{18,... | collective-permute-start | bytes 1572872 | tf_op jit(solution)/shard_map/ppermute | solution.py:566
  147.9 8.6 %collective-permute-start.42 = (bf16[1,256,512]{2,1,0:T(8,128)(2,1)S(1)}, bf16[1,256,512]{2,1,0:T(8,128)(2,1)S(1)}, u32[]{:S(2)}, u32[]{:S(2)}) collective-permute-start(bf16[1,256,512]{2,1,0:T(8,128)(2,1)S(1)} %get-tuple-element.42.refs_2_), channel_id=1, source_target_pairs={{0,8},{2,10},{4,12},{6,14},{8,0},{10,2},{12,4},{14,6},{16,24},{18,... | collective-permute-start | bytes 786440 | tf_op jit(solution)/shard_map/ppermute | solution.py:569
  149.6 12.9 %collective-permute-start.41 = (bf16[1,512,512]{2,1,0:T(8,128)(2,1)S(1)}, bf16[1,512,512]{2,1,0:T(8,128)(2,1)S(1)}, u32[]{:S(2)}, u32[]{:S(2)}) collective-permute-start(bf16[1,512,512]{2,1,0:T(8,128)(2,1)S(1)} %sum_core.3.refs_2_), channel_id=1, source_target_pairs={{0,4},{2,6},{4,0},{6,2},{8,12},{10,14},{12,8},{14,10},{16,20},{18,... | collective-permute-start | bytes 1572872 | tf_op jit(solution)/shard_map/ppermute | solution.py:573
  156.6 8.2 %collective-permute-start.44 = (bf16[1,128,512]{2,1,0:T(8,128)(2,1)S(1)}, bf16[1,128,512]{2,1,0:T(8,128)(2,1)S(1)}, u32[]{:S(2)}, u32[]{:S(2)}) collective-permute-start(bf16[1,128,512]{2,1,0:T(8,128)(2,1)S(1)} %get-tuple-element.48.refs_3_), channel_id=1, source_target_pairs={{0,16},{2,18},{4,20},{6,22},{8,24},{10,26},{12,28},{14,30},{16,0},... | collective-permute-start | bytes 393224 | tf_op jit(solution)/shard_map/ppermute | solution.py:569
  162.8 10.4 %collective-permute-start.43 = (bf16[1,256,512]{2,1,0:T(8,128)(2,1)S(1)}, bf16[1,256,512]{2,1,0:T(8,128)(2,1)S(1)}, u32[]{:S(2)}, u32[]{:S(2)}) collective-permute-start(bf16[1,256,512]{2,1,0:T(8,128)(2,1)S(1)} %get-tuple-element.50.refs_2_), channel_id=1, source_target_pairs={{0,8},{2,10},{4,12},{6,14},{8,0},{10,2},{12,4},{14,6},{16,24},{18,... | collective-permute-start | bytes 786440 | tf_op jit(solution)/shard_map/ppermute | solution.py:569
  163.5 33.7 %collective-permute-start.39 = (bf16[1024,512]{1,0:T(8,128)(2,1)S(1)}, bf16[1024,512]{1,0:T(8,128)(2,1)S(1)}, u32[]{:S(2)}, u32[]{:S(2)}) collective-permute-start(bf16[1024,512]{1,0:T(8,128)(2,1)S(1)} %get-tuple-element.44), channel_id=1, source_target_pairs={{0,1},{1,0},{2,3},{3,2},{4,5},{5,4},{6,7},{7,6},{8,9},{9,8},{10,11... | collective-permute-start | bytes 3145736 | tf_op jit(solution)/shard_map/ppermute | solution.py:772
  164.8 8.5 %collective-permute-start.46 = (bf16[1,1,128,512]{3,2,1,0:T(8,128)(2,1)S(1)}, bf16[1,1,128,512]{3,2,1,0:T(8,128)(2,1)S(1)}, u32[]{:S(2)}, u32[]{:S(2)}) collective-permute-start(bf16[1,1,128,512]{3,2,1,0:T(8,128)(2,1)S(1)} %bitcast.38), channel_id=1, source_target_pairs={{0,16},{2,18},{4,20},{6,22},{8,24},{10,26},{12,28},{14,30},{16,0},... | collective-permute-start | bytes 393224 | tf_op jit(solution)/shard_map/ppermute | solution.py:569
  173.3 8.1 %collective-permute-start.48 = (bf16[2,1,128,512]{3,2,1,0:T(8,128)(2,1)S(1)}, bf16[2,1,128,512]{3,2,1,0:T(8,128)(2,1)S(1)}, u32[]{:S(2)}, u32[]{:S(2)}) collective-permute-start(bf16[2,1,128,512]{3,2,1,0:T(8,128)(2,1)S(1)} %stack_pieces.5.refs_2_.refs_0_), channel_id=1, source_target_pairs={{0,8},{2,10},{4,12},{6,14},{8,0},{10,2},{12,4},{14,6},{16,24},{18,... | collective-permute-start | bytes 786440 | tf_op jit(solution)/shard_map/ppermute | solution.py:569
  174.6 6.0 %collective-permute-start.45 = (bf16[1,128,512]{2,1,0:T(8,128)(2,1)S(1)}, bf16[1,128,512]{2,1,0:T(8,128)(2,1)S(1)}, u32[]{:S(2)}, u32[]{:S(2)}) collective-permute-start(bf16[1,128,512]{2,1,0:T(8,128)(2,1)S(1)} %get-tuple-element.53.refs_2_), channel_id=1, source_target_pairs={{0,16},{2,18},{4,20},{6,22},{8,24},{10,26},{12,28},{14,30},{16,0},... | collective-permute-start | bytes 393224 | tf_op jit(solution)/shard_map/ppermute | solution.py:569
  181.4 15.6 %collective-permute-start.51 = (bf16[4,1,128,512]{3,2,1,0:T(8,128)(2,1)S(1)}, bf16[4,1,128,512]{3,2,1,0:T(8,128)(2,1)S(1)}, u32[]{:S(2)}, u32[]{:S(2)}) collective-permute-start(bf16[4,1,128,512]{3,2,1,0:T(8,128)(2,1)S(1)} %stack_pieces.6.refs_2_.refs_0_), channel_id=1, source_target_pairs={{0,4},{2,6},{4,0},{6,2},{8,12},{10,14},{12,8},{14,10},{16,20},{18,... | collective-permute-start | bytes 1572872 | tf_op jit(solution)/shard_map/ppermute | solution.py:596
  182.6 6.1 %collective-permute-start.47 = (bf16[1,1,128,512]{3,2,1,0:T(8,128)(2,1)S(1)}, bf16[1,1,128,512]{3,2,1,0:T(8,128)(2,1)S(1)}, u32[]{:S(2)}, u32[]{:S(2)}) collective-permute-start(bf16[1,1,128,512]{3,2,1,0:T(8,128)(2,1)S(1)} %bitcast.40), channel_id=1, source_target_pairs={{0,16},{2,18},{4,20},{6,22},{8,24},{10,26},{12,28},{14,30},{16,0},... | collective-permute-start | bytes 393224 | tf_op jit(solution)/shard_map/ppermute | solution.py:569
  188.7 7.3 %collective-permute-start.49 = (bf16[2,1,128,512]{3,2,1,0:T(8,128)(2,1)S(1)}, bf16[2,1,128,512]{3,2,1,0:T(8,128)(2,1)S(1)}, u32[]{:S(2)}, u32[]{:S(2)}) collective-permute-start(bf16[2,1,128,512]{3,2,1,0:T(8,128)(2,1)S(1)} %stack_pieces.7.refs_0_.refs_2_), channel_id=1, source_target_pairs={{0,8},{2,10},{4,12},{6,14},{8,0},{10,2},{12,4},{14,6},{16,24},{18,... | collective-permute-start | bytes 786440 | tf_op jit(solution)/shard_map/ppermute | solution.py:569
  191.7 7.4 %collective-permute-start.52 = (bf16[4,1,128,512]{3,2,1,0:T(8,128)(2,1)S(1)}, bf16[4,1,128,512]{3,2,1,0:T(8,128)(2,1)S(1)}, u32[]{:S(2)}, u32[]{:S(2)}) collective-permute-start(bf16[4,1,128,512]{3,2,1,0:T(8,128)(2,1)S(1)} %stack_pieces.6.refs_2_.refs_0_), channel_id=1, source_target_pairs={{0,2},{2,0},{4,6},{6,4},{8,10},{10,8},{12,14},{14,12},{16,18},{18,... | collective-permute-start | bytes 1572872 | tf_op jit(solution)/shard_map/ppermute | solution.py:566
  196.0 14.6 %collective-permute-start.54 = (bf16[4,1,128,512]{3,2,1,0:T(8,128)(2,1)S(1)}, bf16[4,1,128,512]{3,2,1,0:T(8,128)(2,1)S(1)}, u32[]{:S(2)}, u32[]{:S(2)}) collective-permute-start(bf16[4,1,128,512]{3,2,1,0:T(8,128)(2,1)S(1)} %stack_pieces.8.refs_5_.refs_0_), channel_id=1, source_target_pairs={{0,2},{2,0},{4,6},{6,4},{8,10},{10,8},{12,14},{14,12},{16,18},{18,... | collective-permute-start | bytes 1572872 | tf_op jit(solution)/shard_map/ppermute | solution.py:566
  196.1 14.3 %collective-permute-start.50 = (bf16[4,1,128,512]{3,2,1,0:T(8,128)(2,1)S(1)}, bf16[4,1,128,512]{3,2,1,0:T(8,128)(2,1)S(1)}, u32[]{:S(2)}, u32[]{:S(2)}) collective-permute-start(bf16[4,1,128,512]{3,2,1,0:T(8,128)(2,1)S(1)} %stack_pieces.8.refs_5_.refs_0_), channel_id=1, source_target_pairs={{0,4},{2,6},{4,0},{6,2},{8,12},{10,14},{12,8},{14,10},{16,20},{18,... | collective-permute-start | bytes 1572872 | tf_op jit(solution)/shard_map/ppermute | solution.py:596
  (31 other events, 404.8 us)

commit v6 on v5

--- a/solution.py
+++ b/solution.py
@@ -89,7 +89,7 @@
     return order, begin
 
 
-def block_tables(block_list, blk_seq, seq_count, calls):
+def block_tables(block_list, blk_seq, seq_count, cuts):
     order = ring_order(seq_count)
     n = len(order)
     inverse = [0] * n
@@ -99,15 +99,20 @@
     me = lax.axis_index("seq")
     place = inverse[me // 2]
     owner = block_list // blk_seq
-    local = (block_list % blk_seq).reshape(calls, -1)
+    local = block_list % blk_seq
     other = inverse[owner // 2]
     flag = ((owner ^ me) & 1) * n
-    kslot = (flag + lax.rem(place - other + n, n)).reshape(calls, -1)
-    vslot = (flag + lax.rem(other - place + n, n)).reshape(calls, -1)
-    return (local,) + sorted_entries(kslot, 2 * n) + sorted_entries(vslot, 2 * n)
-
-
-def attention_kernel(degree, heads, sources, local, korder, kbegin, vorder, vbegin, q_ref, *refs):
+    kslot = flag + lax.rem(place - other + n, n)
+    vslot = flag + lax.rem(other - place + n, n)
+    tables = []
+    for low, high in zip(cuts[:-1], cuts[1:]):
+        entries = [x[low:high].reshape(1, -1) for x in (local, kslot, vslot)]
+        found = (entries[0],) + sorted_entries(entries[1], 2 * n) + sorted_entries(entries[2], 2 * n)
+        tables.append([x[0] for x in found])
+    return tables
+
+
+def attention_kernel(degree, heads, sources, first, local, korder, kbegin, vorder, vbegin, q_ref, *refs):
     k_refs, v_refs = refs[:sources], refs[sources : 2 * sources]
     out_ref, k_all, v_all, sems = refs[2 * sources :]
     block_len = k_all.shape[2] // degree
@@ -137,7 +142,8 @@
 
     def one_block(b, carry):
         nodes = pl.ds(pl.multiple_of(b * block_len, block_len), block_len)
-        q = jnp.concatenate([q_ref[:, nodes]] * heads, 1)
+        asked = pl.ds(pl.multiple_of((b + first) * block_len, block_len), block_len)
+        q = jnp.concatenate([q_ref[:, asked]] * heads, 1)
         scores = contract(k_all[b], jnp.where(diagonal, q, jnp.zeros_like(q)), 0, 0)
         top = jnp.max(scores, 0, keepdims=True)
         probs = jnp.exp2((scores - top) * factor)
@@ -151,17 +157,17 @@
         return carry
 
     count = k_all.shape[0]
-    lax.fori_loop(0, count, one_block, 0, unroll=4 if count % 4 == 0 else 1)
-
-
-def attention(queries, keys, values, tables, call, count, block_len, degree):
+    lax.fori_loop(0, count, one_block, 0, unroll=next(u for u in (4, 3, 2, 1) if count % u == 0))
+
+
+def attention(queries, keys, values, tables, first, count, block_len, degree):
     feat = queries.shape[0]
     return pl.pallas_call(
-        functools.partial(attention_kernel, degree, feat // HD, len(keys)),
+        functools.partial(attention_kernel, degree, feat // HD, len(keys), first),
         grid_spec=pltpu.PrefetchScalarGridSpec(
             num_scalar_prefetch=5,
             grid=(1,),
-            in_specs=[pl.BlockSpec((feat, count * block_len), lambda i, *_: (0, call))]
+            in_specs=[pl.BlockSpec(queries.shape, lambda i, *_: (0, 0))]
             + [pl.BlockSpec(memory_space=pl.ANY)] * (2 * len(keys)),
             out_specs=pl.BlockSpec((count * block_len, feat), lambda i, *_: (0, 0)),
             scratch_shapes=[pltpu.VMEM((count, feat, degree * block_len), bf16)] * 2 + [pltpu.SemaphoreType.DMA((2,))],
@@ -174,7 +180,7 @@
             transcendentals=count * block_len * degree * block_len * feat // HD,
         ),
         name="attention",
-    )(*[t[call] for t in tables], queries, *keys, *values)
+    )(*tables, queries, *keys, *values)
 
 
 def place_of(part, line, lines):
@@ -596,9 +602,12 @@
             self.other = lax.ppermute(self.own, "seq", self.cross)
         return self.own
 
-    def blocks(self, after):
+    def near_blocks(self):
+        return [self.own, self.to_sibling(self.own)]
+
+    def far_blocks(self, after):
         other = stack_pieces([self.other], after) if after else self.other
-        return [self.own, other, self.to_sibling(self.own), self.to_sibling(other)]
+        return [other, self.to_sibling(other)]
 
 
 def step_order(sums):
@@ -612,7 +621,7 @@
     return order
 
 
-def unpack_kernel(lines, each, width, where, place, *refs):
+def unpack_kernel(blocks, lines, each, width, where, place, *refs):
     win_ref, wout_ref, token_ref = refs[-3:]
     token_ref[...] = jnp.zeros_like(token_ref)
     step = pl.program_id(0)
@@ -630,7 +639,7 @@
                     wout_ref[0, j * width + low : j * width + low + part, :] = block[:, j * width : (j + 1) * width]
 
     if refs[0].shape[2] * lines > width:
-        for a in range(4):
+        for a in range(blocks):
             for i in range(each):
                 pl.when(step == a * each + i)(functools.partial(read, refs[a], i, True, True))
     else:
@@ -649,11 +658,11 @@
     whole = pl.BlockSpec(blocks[0].shape, lambda i, *_: (0, 0, 0, 0))
     out = lambda *shape: pl.BlockSpec((1,) + shape, lambda i, where, place: (where[i], 0, 0))
     return pl.pallas_call(
-        functools.partial(unpack_kernel, lines, each, width),
+        functools.partial(unpack_kernel, len(blocks), lines, each, width),
         grid_spec=pltpu.PrefetchScalarGridSpec(
             num_scalar_prefetch=2,
             grid=where.shape,
-            in_specs=[whole] * 4 + [pl.BlockSpec(memory_space=pl.ANY)] * len(into),
+            in_specs=[whole] * len(blocks) + [pl.BlockSpec(memory_space=pl.ANY)] * len(into),
             out_specs=[out(width, ff), out(ff, width), pl.BlockSpec((8, 128), lambda i, *_: (0, 0))],
         ),
         out_shape=[
@@ -661,7 +670,7 @@
             jax.ShapeDtypeStruct((experts, ff, width), f32),
             jax.ShapeDtypeStruct((8, 128), f32),
         ],
-        input_output_aliases={6 + i: i for i in range(len(into))},
+        input_output_aliases={2 + len(blocks) + i: i for i in range(len(into))},
         compiler_params=params(16),
         cost_estimate=pl.CostEstimate(
             flops=EAGER * where.shape[0] * 2 * width * ff * 6, bytes_accessed=where.shape[0] * 2 * width * ff * 6, transcendentals=0
@@ -699,9 +708,9 @@
     capacity = 2 * tok_dev * topk // expert_total * exp_count
     slot_rows = capacity + WINDOW
 
-    calls = 2 if blk_seq % 2 == 0 else 1
+    cuts = [0, blk_seq * 5 // 8, blk_seq]
     keys, values = ring_gather(key_cols, value_cols, seq_count)
-    tables = block_tables(block_list, blk_seq, seq_count, calls)
+    tables = block_tables(block_list, blk_seq, seq_count, cuts)
 
     residual_all = gather_expert_axis(residual, exp_count)
     cotangent_all = gather_expert_axis(cotangent, exp_count)
@@ -739,10 +748,9 @@
     ]
     owner_order = lax.rem(me + jnp.arange(exp_count, dtype=jnp.int32), exp_count)
 
-    per_call = blk_seq // calls
     pieces = [[] for _ in range(exp_count)]
-    for c in range(calls):
-        part = attention(query_cols, keys, values, tables, c, per_call, block_len, degree)
+    for table, low, high in zip(tables, cuts[:-1], cuts[1:]):
+        part = attention(query_cols, keys, values, table, low, high - low, block_len, degree)
         pieces[0].append(part)
         for d in range(1, exp_count):
             pieces[d].append(lax.ppermute(part, "expert", shift_pairs(exp_count, d)))
@@ -772,11 +780,22 @@
                 lax.ppermute(partials[d], "expert", shift_pairs(exp_count, d)) for d in range(1, exp_count)
             ]
     layer_out, grad_stream, home = at_home(me, stream, cotangent, gain, parts, chunk, last[0])
-    into, token = [], []
-    for g, each_sum in enumerate(sums):
-        blocks = each_sum.blocks(token + [home] if g == len(sums) - 1 else [])
-        *into, done = unpack(wheres[g], place, blocks, experts, width, ff, into)
-        token = [done]
+    into, done = [], []
+    for g, (count, each_sum) in enumerate(zip(groups, sums)):
+        where, after = wheres[g], []
+        if g == len(groups) - 1:
+            after = done + [home]
+            if count > 2:
+                near = jnp.concatenate([where[: count // 4], where[count // 2 : 3 * count // 4]])
+                *into, token = unpack(near, place, each_sum.near_blocks(), experts, width, ff, into)
+                where = jnp.concatenate([where[count // 4 : count // 2], where[3 * count // 4 :]])
+                after = [token, home]
+        blocks = each_sum.far_blocks(after)
+        if where is wheres[g]:
+            own, other = each_sum.near_blocks(), blocks
+            blocks = [own[0], other[0], own[1], other[1]]
+        *into, token = unpack(where, place, blocks, experts, width, ff, into)
+        done = [token]
     grad_w_in, grad_w_out = into
     return layer_out, grad_stream, grad_w_in, grad_w_out
 

time: 218 us -> 214 us (0.982)
  local copies, waits for them, and re-layouts: 14.7 us -> 9.68 us
  Pallas kernels: 53.1 us -> 57.2 us
  waiting for transfers between devices: 92.7 us -> 88.8 us
    ppermute x2, waiting for transfers between devices: 8.35 us -> 5.57 us  [back_line(): self.other = lax.ppermute(self.own, 'seq', self.cross)]
    squeeze x4 -> x0, local copies, waits for them, and re-layouts: 2.33 us -> none  [attention(): t[call]]
    pallas_call x2 -> x3, Pallas kernels: 6.07 us -> 7.01 us  [unpack(): pl.pallas_call(functools.partial(unpack_kernel, len(blocks), lines, each,...]
  transfers between devices with their start and end apart: 56 -> 56, of which waited for: 22 -> 22; matrix products, arithmetic and copies ran while one was open for 10% -> 8% of each run, Pallas kernels for 18% -> 20%
where the time goes in v6:
time: 214 us; the launch traced here: 213 us
  waiting for transfers between devices  88.8 us (41%)
  Pallas kernels  57.2 us (27%)
  starting transfers between devices  46.7 us (22%)
  local copies, waits for them, and re-layouts  9.68 us (5%)
  other arithmetic  9.28 us (4%)
    ppermute x7, waiting for transfers between devices, ring_gather(): k = lax.ppermute(k, 'seq', fwd)  48.7 us
    pallas_call x2, Pallas kernels, expert_group(): pl.pallas_call(functools.partial(group_kernel, first, count, pieces, 0 if...  23.1 us
    ppermute x8, waiting for transfers between devices, to_line(): return lax.ppermute(x, 'seq', line_pairs(self.seq_count, step))  19.4 us
    pallas_call x2, Pallas kernels, attention(): pl.pallas_call(functools.partial(attention_kernel, degree, feat // HD, le...  18.5 us
    ppermute x8, starting transfers between devices, to_line(): return lax.ppermute(x, 'seq', line_pairs(self.seq_count, step))  16.2 us
    ppermute x7, starting transfers between devices, ring_gather(): k = lax.ppermute(k, 'seq', fwd)  10.1 us
    pallas_call x3, Pallas kernels, unpack(): pl.pallas_call(functools.partial(unpack_kernel, len(blocks), lines, each,...  7.01 us
    pallas_call x1, Pallas kernels, combine(): pl.pallas_call(functools.partial(combine_kernel, len(rows_parts), owners,...  5.82 us
  transfers between devices with their start and end apart: 56, of which 22 were waited for; matrix products, arithmetic and copies ran while one was open for 8% of the time, Pallas kernels for 20%

profile of v6, /device:TPU:0, one launch (start us, length us, event | category | flops | bytes accessed | tf_op | source)
XLA Modules:
  0.0 212.9 jit_solution(14571798307797946672)
XLA Ops:
  0.6 3.1 %collective-permute-start.3 = (bf16[128,2048]{1,0:T(8,128)(2,1)}, bf16[128,2048]{1,0:T(8,128)(2,1)S(1)}, u32[]{:S(2)}, u32[]{:S(2)}) collective-permute-start(bf16[128,2048]{1,0:T(8,128)(2,1)} %refs_0_.3), channel_id=1, source_target_pairs={{0,8},{2,10},{8,16},{10,18},{16,24},{18,26},{24,28},{26,30},{28,20... | collective-permute-start | bytes 1572872 | tf_op jit(solution)/shard_map/ppermute | solution.py:73
  3.7 2.0 collective-permute-start
  6.5 9.3 %collective-permute-done.3.refs_1_ = bf16[128,2048]{1,0:T(8,128)(2,1)S(1)} collective-permute-done((bf16[128,2048]{1,0:T(8,128)(2,1)}, bf16[128,2048]{1,0:T(8,128)(2,1)S(1)}, u32[]{:S(2)}, u32[]{:S(2)}) %collective-permute-start.3) | collective-permute-done | bytes 524320 | tf_op jit(solution)/shard_map/ppermute | solution.py:73
  15.8 1.8 collective-permute-start.4
  17.9 1.2 dynamic_slice.13
  20.8 8.3 %collective-permute-done.4.refs_2_ = bf16[128,2048]{1,0:T(8,128)(2,1)} collective-permute-done((bf16[128,2048]{1,0:T(8,128)(2,1)S(1)}, bf16[128,2048]{1,0:T(8,128)(2,1)}, u32[]{:S(2)}, u32[]{:S(2)}) %collective-permute-start.4) | collective-permute-done | bytes 524320 | tf_op jit(solution)/shard_map/ppermute | solution.py:73
  29.1 1.5 collective-permute-start.5
  32.9 8.8 %collective-permute-done.5.refs_3_ = bf16[128,2048]{1,0:T(8,128)(2,1)} collective-permute-done((bf16[128,2048]{1,0:T(8,128)(2,1)}, bf16[128,2048]{1,0:T(8,128)(2,1)}, u32[]{:S(2)}, u32[]{:S(2)}) %collective-permute-start.5) | collective-permute-done | bytes 524320 | tf_op jit(solution)/shard_map/ppermute | solution.py:73
  41.7 1.2 collective-permute-start.6
  45.1 1.2 fusion.8
  46.4 1.2 fusion.10
  49.4 4.4 %collective-permute-done.6.refs_4_ = bf16[128,2048]{1,0:T(8,128)(2,1)} collective-permute-done((bf16[128,2048]{1,0:T(8,128)(2,1)}, bf16[128,2048]{1,0:T(8,128)(2,1)}, u32[]{:S(2)}, u32[]{:S(2)}) %collective-permute-start.6) | collective-permute-done | bytes 524320 | tf_op jit(solution)/shard_map/ppermute | solution.py:73
  54.6 1.3 collective-permute-start.22
  59.4 6.5 %collective-permute-done.7.refs_5_ = bf16[128,2048]{1,0:T(8,128)(2,1)} collective-permute-done((bf16[128,2048]{1,0:T(8,128)(2,1)}, bf16[128,2048]{1,0:T(8,128)(2,1)}, u32[]{:S(2)}, u32[]{:S(2)}) %collective-permute-start.7) | collective-permute-done | bytes 524320 | tf_op jit(solution)/shard_map/ppermute | solution.py:73
  66.7 1.3 collective-permute-start.23
  68.1 2.3 %reduce-window.6 = s32[8,16,128]{2,1,0:T(8,128)S(1)} reduce-window(s32[8,16,128]{2,1,0:T(8,128)S(1)} %copy.39, s32[]{:T(128)} %constant.111.clone.1), window={size=1x1x128 pad=0_0x0_0x127_0}, to_apply=%region_1.2 | reduce-window | flops 2080768 | bytes 131076 | tf_op jit(solution)/shard_map/reduce-window
  71.1 6.1 %collective-permute-done.8.refs_6_ = bf16[128,2048]{1,0:T(8,128)(2,1)} collective-permute-done((bf16[128,2048]{1,0:T(8,128)(2,1)}, bf16[128,2048]{1,0:T(8,128)(2,1)}, u32[]{:S(2)}, u32[]{:S(2)}) %collective-permute-start.8) | collective-permute-done | bytes 524320 | tf_op jit(solution)/shard_map/ppermute | solution.py:73
  81.8 5.3 %collective-permute-done.9.refs_7_ = bf16[128,2048]{1,0:T(8,128)(2,1)} collective-permute-done((bf16[128,2048]{1,0:T(8,128)(2,1)}, bf16[128,2048]{1,0:T(8,128)(2,1)}, u32[]{:S(2)}, u32[]{:S(2)}) %collective-permute-start.9) | collective-permute-done | bytes 524320 | tf_op jit(solution)/shard_map/ppermute | solution.py:73
  87.7 1.1 constant_dynamic-update-slice_fusion.2.refs_1_
  90.8 10.5 %attention.2 = bf16[1280,128]{1,0:T(8,128)(2,1)} custom-call(s32[40]{0:T(128)} %squeeze_reshape.6.local, s32[40]{0:T(128)} %get-tuple-element.78.korder, s32[17]{0:T(128)} %get-tuple-element.79.kbegin, s32[40]{0:T(128)} %get-tuple-element.77.vorder, s32[17]{0:T(128)} %get-tuple-element.80.vbegin, bf16[128,2048]{1,0:T(8,128)(2,1)} %q_ref.3, ...), custom_call_target="tpu_custom_call" | custom-call | flops 335544320 | bytes 3276800 | tf_op jit(solution)/shard_map/attention/pallas_call | solution.py:165
  101.3 1.4 collective-permute-start.33
  102.8 8.0 %attention.3 = bf16[768,128]{1,0:T(8,128)(2,1)} custom-call(s32[24]{0:T(128)} %squeeze_reshape.7.local, s32[24]{0:T(128)} %get-tuple-element.74.korder, s32[17]{0:T(128)} %get-tuple-element.75.kbegin, s32[24]{0:T(128)} %get-tuple-element.73.vorder, s32[17]{0:T(128)} %get-tuple-element.76.vbegin, bf16[128,2048]{1,0:T(8,128)(2,1)} %q_ref.3, ...), custom_call_target="tpu_custom_call" | custom-call | flops 201326592 | bytes 1966080 | tf_op jit(solution)/shard_map/attention/pallas_call | solution.py:165
  112.6 5.2 %collective-permute-done.34 = bf16[768,128]{1,0:T(8,128)(2,1)S(1)} collective-permute-done((bf16[768,128]{1,0:T(8,128)(2,1)}, bf16[768,128]{1,0:T(8,128)(2,1)S(1)}, u32[]{:S(2)}, u32[]{:S(2)}) %collective-permute-start.34) | collective-permute-done | bytes 196640 | tf_op jit(solution)/shard_map/ppermute | solution.py:756
  117.9 12.2 %experts.2 = (bf16[2048,256]{1,0:T(8,128)(2,1)S(1)}, bf16[4,640,512]{2,1,0:T(8,128)(2,1)S(1)}, bf16[1,512,512]{2,1,0:T(8,128)(2,1)S(1)}, bf16[1,512,512]{2,1,0:T...) custom-call(s32[8]{0:T(128)S(1)} %slice_reduce_fusion.1.counts, ...), custom_call_target="tpu_custom_call" | custom-call | flops 1000 | bytes 1000 | tf_op jit(solution)/shard_map/experts/pallas_call | solution.py:386
  130.6 1.4 collective-permute-done.35.refs_1_
  133.2 10.9 %experts.3 = (bf16[4,640,512]{2,1,0:T(8,128)(2,1)S(1)}, bf16[1,512,512]{2,1,0:T(8,128)(2,1)S(1)}, bf16[1,512,512]{2,1,0:T(8,128)(2,1)S(1)}, bf16[1,512,512]{2,1,0:T(8,128)(2,1)S(1)}, bf16[1,512,512]{2,1,0:T(8,128)(2,1)S(1)}) custom-call(s32[8]{0:T(128)S(1)} %slice_reduce_fusion.1.counts, s32[8]{0:T(128)S(1)} %broadcast_add_fusion.ids, s32[8]{0:T(128)S(1)} %stack.55.perm, ...), custom_call_target="tpu_custom_call" | custom-call | flops 1000 | bytes 1000 | tf_op jit(solution)/shard_map/experts/pallas_call | solution.py:386
  144.6 1.5 collective-permute-done.38.refs_2_
  146.4 1.7 collective-permute-start.42
  149.1 5.8 %combine.1 = (bf16[1024,512]{1,0:T(8,128)(2,1)S(1)}, bf16[1024,512]{1,0:T(8,128)(2,1)S(1)}) custom-call(s32[9,8]{1,0:T(8,128)S(1)} %copy.45.starts, s32[2]{0:T(128)S(1)} %compare_select_fusion.1.order, s32[8,2048]{1,0:T(8,128)S(1)} %add_select_fusion.refs_0_.rank_ref, bf16[4,640,512]{2,1,0:T(8,128)(2,1)S(1)} %get-tuple-element.36.refs_0_, ...), custom_call_target="tpu_custom_call" | custom-call | flops 32000000000 | bytes 10000000 | tf_op jit(solution)/shard_map/combine/pallas_call | solution.py:443
  155.1 2.6 %collective-permute-start.44 = (bf16[1,128,512]{2,1,0:T(8,128)(2,1)S(1)}, bf16[1,128,512]{2,1,0:T(8,128)(2,1)S(1)}, u32[]{:S(2)}, u32[]{:S(2)}) collective-permute-start(bf16[1,128,512]{2,1,0:T(8,128)(2,1)S(1)} %get-tuple-element.50.refs_3_), channel_id=1, source_target_pairs={{0,16},{2,18},{4,20},{6,22},{8,24},{10,26},{12,28},{14,30},{16,0},... | collective-permute-start | bytes 393224 | tf_op jit(solution)/shard_map/ppermute | solution.py:575
  157.7 3.4 %collective-permute-done.41.refs_2_ = bf16[1,512,512]{2,1,0:T(8,128)(2,1)S(1)} collective-permute-done((bf16[1,512,512]{2,1,0:T(8,128)(2,1)S(1)}, bf16[1,512,512]{2,1,0:T(8,128)(2,1)S(1)}, u32[]{:S(2)}, u32[]{:S(2)}) %collective-permute-start.41) | collective-permute-done | bytes 524320 | tf_op jit(solution)/shard_map/ppermute | solution.py:579
  163.3 2.1 %collective-permute-start.46 = (bf16[1,1,128,512]{3,2,1,0:T(8,128)(2,1)S(1)}, bf16[1,1,128,512]{3,2,1,0:T(8,128)(2,1)S(1)}, u32[]{:S(2)}, u32[]{:S(2)}) collective-permute-start(bf16[1,1,128,512]{3,2,1,0:T(8,128)(2,1)S(1)} %bitcast.33), channel_id=1, source_target_pairs={{0,16},{2,18},{4,20},{6,22},{8,24},{10,26},{12,28},{14,30},{16,0},... | collective-permute-start | bytes 393224 | tf_op jit(solution)/shard_map/ppermute | solution.py:575
  165.4 6.1 %collective-permute-done.43.refs_1_ = bf16[1,256,512]{2,1,0:T(8,128)(2,1)S(1)} collective-permute-done((bf16[1,256,512]{2,1,0:T(8,128)(2,1)S(1)}, bf16[1,256,512]{2,1,0:T(8,128)(2,1)S(1)}, u32[]{:S(2)}, u32[]{:S(2)}) %collective-permute-start.43) | collective-permute-done | bytes 262176 | tf_op jit(solution)/shard_map/ppermute | solution.py:575
  171.7 1.4 collective-permute-start.48
  173.0 2.2 %collective-permute-start.45 = (bf16[1,128,512]{2,1,0:T(8,128)(2,1)S(1)}, bf16[1,128,512]{2,1,0:T(8,128)(2,1)S(1)}, u32[]{:S(2)}, u32[]{:S(2)}) collective-permute-start(bf16[1,128,512]{2,1,0:T(8,128)(2,1)S(1)} %get-tuple-element.55.refs_2_), channel_id=1, source_target_pairs={{0,16},{2,18},{4,20},{6,22},{8,24},{10,26},{12,28},{14,30},{16,0},... | collective-permute-start | bytes 393224 | tf_op jit(solution)/shard_map/ppermute | solution.py:575
  175.3 3.8 %collective-permute-done.45.refs_1_ = bf16[1,128,512]{2,1,0:T(8,128)(2,1)S(1)} collective-permute-done((bf16[1,128,512]{2,1,0:T(8,128)(2,1)S(1)}, bf16[1,128,512]{2,1,0:T(8,128)(2,1)S(1)}, u32[]{:S(2)}, u32[]{:S(2)}) %collective-permute-start.45) | collective-permute-done | bytes 131104 | tf_op jit(solution)/shard_map/ppermute | solution.py:575
  180.2 1.1 collective-permute-start.52
  181.3 2.5 %collective-permute-start.47 = (bf16[1,1,128,512]{3,2,1,0:T(8,128)(2,1)S(1)}, bf16[1,1,128,512]{3,2,1,0:T(8,128)(2,1)S(1)}, u32[]{:S(2)}, u32[]{:S(2)}) collective-permute-start(bf16[1,1,128,512]{3,2,1,0:T(8,128)(2,1)S(1)} %bitcast.35), channel_id=1, source_target_pairs={{0,16},{2,18},{4,20},{6,22},{8,24},{10,26},{12,28},{14,30},{16,0},... | collective-permute-start | bytes 393224 | tf_op jit(solution)/shard_map/ppermute | solution.py:575
  183.8 3.4 %collective-permute-done.47.refs_1_ = bf16[1,1,128,512]{3,2,1,0:T(8,128)(2,1)S(1)} collective-permute-done((bf16[1,1,128,512]{3,2,1,0:T(8,128)(2,1)S(1)}, bf16[1,1,128,512]{3,2,1,0:T(8,128)(2,1)S(1)}, u32[]{:S(2)}, u32[]{:S(2)}) %collective-permute-start.47) | collective-permute-done | bytes 131104 | tf_op jit(solution)/shard_map/ppermute | solution.py:575
  187.2 2.9 %collective-permute-start.49 = (bf16[2,1,128,512]{3,2,1,0:T(8,128)(2,1)S(1)}, bf16[2,1,128,512]{3,2,1,0:T(8,128)(2,1)S(1)}, u32[]{:S(2)}, u32[]{:S(2)}) collective-permute-start(bf16[2,1,128,512]{3,2,1,0:T(8,128)(2,1)S(1)} %stack_pieces.7.refs_0_.refs_2_), channel_id=1, source_target_pairs={{0,8},{2,10},{4,12},{6,14},{8,0},{10,2},{12,4},{14,6},{16,24},{18,... | collective-permute-start | bytes 786440 | tf_op jit(solution)/shard_map/ppermute | solution.py:575
  190.3 4.2 %collective-permute-done.49.refs_1_ = bf16[2,1,128,512]{3,2,1,0:T(8,128)(2,1)S(1)} collective-permute-done((bf16[2,1,128,512]{3,2,1,0:T(8,128)(2,1)S(1)}, bf16[2,1,128,512]{3,2,1,0:T(8,128)(2,1)S(1)}, u32[]{:S(2)}, u32[]{:S(2)}) %collective-permute-start.49) | collective-permute-done | bytes 262176 | tf_op jit(solution)/shard_map/ppermute | solution.py:575
  194.6 1.7 collective-permute-start.50
  196.5 1.9 at_home.1
  198.4 3.0 %unpack.3 = (f32[8,256,512]{2,1,0:T(8,128)}, f32[8,512,256]{2,1,0:T(8,128)}, f32[8,128]{1,0:T(8,128)}) custom-call(s32[4]{0:T(128)S(1)} %pad_add_fusion.3.where, s32[2]{0:T(128)S(1)} %pad_add_fusion.place, bf16[4,1,128,512]{3,2,1,0:T(8,128)(2,1)S(1)} %stack_pieces.6.refs_2_.refs_0_, bf16[4,1,128,512]{3,2,1,0:T(8,128)(2,1)S(1)} %collective-permute-done.52.refs_1_, ...), custom_call_target="tpu_custom_call" | custom-call | flops 201326592 | bytes 6291456 | tf_op jit(solution)/shard_map/unpack/pallas_call | solution.py:660
  201.4 2.0 unpack.4
  203.4 5.6 %collective-permute-done.50.refs_0_ = bf16[4,1,128,512]{3,2,1,0:T(8,128)(2,1)S(1)} collective-permute-done((bf16[4,1,128,512]{3,2,1,0:T(8,128)(2,1)S(1)}, bf16[4,1,128,512]{3,2,1,0:T(8,128)(2,1)S(1)}, u32[]{:S(2)}, u32[]{:S(2)}) %collective-permute-start.50) | collective-permute-done | bytes 524320 | tf_op jit(solution)/shard_map/ppermute | solution.py:602
  209.1 1.8 collective-permute-done.55.refs_1_
  211.0 2.0 unpack.5
  (186 shorter events, 31.4 us)
Async XLA Ops:
  0.6 15.1 %collective-permute-start.3 = (bf16[128,2048]{1,0:T(8,128)(2,1)}, bf16[128,2048]{1,0:T(8,128)(2,1)S(1)}, u32[]{:S(2)}, u32[]{:S(2)}) collective-permute-start(bf16[128,2048]{1,0:T(8,128)(2,1)} %refs_0_.3), channel_id=1, source_target_pairs={{0,8},{2,10},{8,16},{10,18},{16,24},{18,26},{24,28},{26,30},{28,20... | collective-permute-start | bytes 1572872 | tf_op jit(solution)/shard_map/ppermute | solution.py:73
  3.7 13.9 %collective-permute-start.18 = (bf16[128,2048]{1,0:T(8,128)(2,1)}, bf16[128,2048]{1,0:T(8,128)(2,1)}, u32[]{:S(2)}, u32[]{:S(2)}) collective-permute-start(bf16[128,2048]{1,0:T(8,128)(2,1)} %refs_16_.3), channel_id=1, source_target_pairs={{0,4},{2,6},{8,0},{10,2},{16,8},{18,10},{24,16},{26,18},{28,24},{3... | collective-permute-start | bytes 1572872 | tf_op jit(solution)/shard_map/ppermute | solution.py:74
  3.7 43.9 %collective-permute-start.10 = (bf16[128,2048]{1,0:T(8,128)(2,1)}, bf16[128,2048]{1,0:T(8,128)(2,1)S(1)}, u32[]{:S(2)}, u32[]{:S(2)}) collective-permute-start(bf16[128,2048]{1,0:T(8,128)(2,1)} %refs_0_.3), channel_id=1, source_target_pairs={{0,2},{2,0},{4,6},{6,4},{8,10},{10,8},{12,14},{14,12},{16,18},{18,... | collective-permute-start | bytes 1572872 | tf_op jit(solution)/shard_map/ppermute | solution.py:77
  3.7 28.5 %collective-permute-start = (s32[2,1024]{1,0:T(2,128)}, s32[2,1024]{1,0:T(2,128)S(1)}, u32[]{:S(2)}, u32[]{:S(2)}) collective-permute-start(s32[2,1024]{1,0:T(2,128)} %bitcast.47), channel_id=1, source_target_pairs={{0,1},{1,0},{2,3},{3,2},{4,5},{5,4},{6,7},{7,6},{8,9},{9,8},{10,11... | collective-permute-start | bytes 24584 | tf_op jit(solution)/shard_map/ppermute | solution.py:61
  5.7 26.6 %collective-permute-start.1 = (bf16[1024,256]{1,0:T(8,128)(2,1)}, bf16[1024,256]{1,0:T(8,128)(2,1)S(1)}, u32[]{:S(2)}, u32[]{:S(2)}) collective-permute-start(bf16[1024,256]{1,0:T(8,128)(2,1)} %refs_1_.1), channel_id=1, source_target_pairs={{0,1},{1,0},{2,3},{3,2},{4,5},{5,4},{6,7},{7,6},{8,9},{9,8},{10,11... | collective-permute-start | bytes 1572872 | tf_op jit(solution)/shard_map/ppermute | solution.py:61
  15.8 13.3 %collective-permute-start.4 = (bf16[128,2048]{1,0:T(8,128)(2,1)S(1)}, bf16[128,2048]{1,0:T(8,128)(2,1)}, u32[]{:S(2)}, u32[]{:S(2)}) collective-permute-start(bf16[128,2048]{1,0:T(8,128)(2,1)S(1)} %collective-permute-done.3.refs_1_), channel_id=1, source_target_pairs={{0,8},{2,10},{8,16},{10,18},{16,24},{18,26},{24,28},{26,30},{28,20... | collective-permute-start | bytes 1572872 | tf_op jit(solution)/shard_map/ppermute | solution.py:73
  17.6 13.0 %collective-permute-start.19 = (bf16[128,2048]{1,0:T(8,128)(2,1)}, bf16[128,2048]{1,0:T(8,128)(2,1)}, u32[]{:S(2)}, u32[]{:S(2)}) collective-permute-start(bf16[128,2048]{1,0:T(8,128)(2,1)} %collective-permute-done.18.refs_17_), channel_id=1, source_target_pairs={{0,4},{2,6},{8,0},{10,2},{16,8},{18,10},{24,16},{26,18},{28,24},{3... | collective-permute-start | bytes 1572872 | tf_op jit(solution)/shard_map/ppermute | solution.py:74
  29.1 12.6 %collective-permute-start.5 = (bf16[128,2048]{1,0:T(8,128)(2,1)}, bf16[128,2048]{1,0:T(8,128)(2,1)}, u32[]{:S(2)}, u32[]{:S(2)}) collective-permute-start(bf16[128,2048]{1,0:T(8,128)(2,1)} %collective-permute-done.4.refs_2_), channel_id=1, source_target_pairs={{0,8},{2,10},{8,16},{10,18},{16,24},{18,26},{24,28},{26,30},{28,20... | collective-permute-start | bytes 1572872 | tf_op jit(solution)/shard_map/ppermute | solution.py:73
  30.6 12.3 %collective-permute-start.20 = (bf16[128,2048]{1,0:T(8,128)(2,1)}, bf16[128,2048]{1,0:T(8,128)(2,1)}, u32[]{:S(2)}, u32[]{:S(2)}) collective-permute-start(bf16[128,2048]{1,0:T(8,128)(2,1)} %collective-permute-done.19.refs_18_), channel_id=1, source_target_pairs={{0,4},{2,6},{8,0},{10,2},{16,8},{18,10},{24,16},{26,18},{28,24},{3... | collective-permute-start | bytes 1572872 | tf_op jit(solution)/shard_map/ppermute | solution.py:74
  32.3 15.4 %collective-permute-start.25 = (bf16[128,2048]{1,0:T(8,128)(2,1)S(1)}, bf16[128,2048]{1,0:T(8,128)(2,1)S(1)}, u32[]{:S(2)}, u32[]{:S(2)}) collective-permute-start(bf16[128,2048]{1,0:T(8,128)(2,1)S(1)} %copy-done.5), channel_id=1, source_target_pairs={{0,2},{2,0},{4,6},{6,4},{8,10},{10,8},{12,14},{14,12},{16,18},{18,... | collective-permute-start | bytes 1572872 | tf_op jit(solution)/shard_map/ppermute | solution.py:78
  32.4 15.8 %collective-permute-start.11 = (bf16[128,2048]{1,0:T(8,128)(2,1)S(1)}, bf16[128,2048]{1,0:T(8,128)(2,1)S(1)}, u32[]{:S(2)}, u32[]{:S(2)}) collective-permute-start(bf16[128,2048]{1,0:T(8,128)(2,1)S(1)} %collective-permute-done.3.refs_1_), channel_id=1, source_target_pairs={{0,2},{2,0},{4,6},{6,4},{8,10},{10,8},{12,14},{14,12},{16,18},{18,... | collective-permute-start | bytes 1572872 | tf_op jit(solution)/shard_map/ppermute | solution.py:77
  41.7 12.1 %collective-permute-start.6 = (bf16[128,2048]{1,0:T(8,128)(2,1)}, bf16[128,2048]{1,0:T(8,128)(2,1)}, u32[]{:S(2)}, u32[]{:S(2)}) collective-permute-start(bf16[128,2048]{1,0:T(8,128)(2,1)} %collective-permute-done.5.refs_3_), channel_id=1, source_target_pairs={{0,8},{2,10},{8,16},{10,18},{16,24},{18,26},{24,28},{26,30},{28,20... | collective-permute-start | bytes 1572872 | tf_op jit(solution)/shard_map/ppermute | solution.py:73
  42.9 11.7 %collective-permute-start.21 = (bf16[128,2048]{1,0:T(8,128)(2,1)}, bf16[128,2048]{1,0:T(8,128)(2,1)}, u32[]{:S(2)}, u32[]{:S(2)}) collective-permute-start(bf16[128,2048]{1,0:T(8,128)(2,1)} %collective-permute-done.20.refs_19_), channel_id=1, source_target_pairs={{0,4},{2,6},{8,0},{10,2},{16,8},{18,10},{24,16},{26,18},{28,24},{3... | collective-permute-start | bytes 1572872 | tf_op jit(solution)/shard_map/ppermute | solution.py:74
  47.6 11.1 %collective-permute-start.26 = (bf16[128,2048]{1,0:T(8,128)(2,1)}, bf16[128,2048]{1,0:T(8,128)(2,1)}, u32[]{:S(2)}, u32[]{:S(2)}) collective-permute-start(bf16[128,2048]{1,0:T(8,128)(2,1)} %collective-permute-done.18.refs_17_), channel_id=1, source_target_pairs={{0,2},{2,0},{4,6},{6,4},{8,10},{10,8},{12,14},{14,12},{16,18},{18,... | collective-permute-start | bytes 1572872 | tf_op jit(solution)/shard_map/ppermute | solution.py:78
  47.7 11.1 %collective-permute-start.12 = (bf16[128,2048]{1,0:T(8,128)(2,1)}, bf16[128,2048]{1,0:T(8,128)(2,1)}, u32[]{:S(2)}, u32[]{:S(2)}) collective-permute-start(bf16[128,2048]{1,0:T(8,128)(2,1)} %collective-permute-done.4.refs_2_), channel_id=1, source_target_pairs={{0,2},{2,0},{4,6},{6,4},{8,10},{10,8},{12,14},{14,12},{16,18},{18,... | collective-permute-start | bytes 1572872 | tf_op jit(solution)/shard_map/ppermute | solution.py:77
  48.6 10.7 %collective-permute-start.27 = (bf16[128,2048]{1,0:T(8,128)(2,1)}, bf16[128,2048]{1,0:T(8,128)(2,1)}, u32[]{:S(2)}, u32[]{:S(2)}) collective-permute-start(bf16[128,2048]{1,0:T(8,128)(2,1)} %collective-permute-done.19.refs_18_), channel_id=1, source_target_pairs={{0,2},{2,0},{4,6},{6,4},{8,10},{10,8},{12,14},{14,12},{16,18},{18,... | collective-permute-start | bytes 1572872 | tf_op jit(solution)/shard_map/ppermute | solution.py:78
  53.8 12.1 %collective-permute-start.7 = (bf16[128,2048]{1,0:T(8,128)(2,1)}, bf16[128,2048]{1,0:T(8,128)(2,1)}, u32[]{:S(2)}, u32[]{:S(2)}) collective-permute-start(bf16[128,2048]{1,0:T(8,128)(2,1)} %collective-permute-done.6.refs_4_), channel_id=1, source_target_pairs={{0,8},{2,10},{8,16},{10,18},{16,24},{18,26},{24,28},{26,30},{28,20... | collective-permute-start | bytes 1572872 | tf_op jit(solution)/shard_map/ppermute | solution.py:73
  54.6 12.1 %collective-permute-start.22 = (bf16[128,2048]{1,0:T(8,128)(2,1)}, bf16[128,2048]{1,0:T(8,128)(2,1)}, u32[]{:S(2)}, u32[]{:S(2)}) collective-permute-start(bf16[128,2048]{1,0:T(8,128)(2,1)} %collective-permute-done.21.refs_20_), channel_id=1, source_target_pairs={{0,4},{2,6},{8,0},{10,2},{16,8},{18,10},{24,16},{26,18},{28,24},{3... | collective-permute-start | bytes 1572872 | tf_op jit(solution)/shard_map/ppermute | solution.py:74
  58.7 11.7 %collective-permute-start.13 = (bf16[128,2048]{1,0:T(8,128)(2,1)}, bf16[128,2048]{1,0:T(8,128)(2,1)}, u32[]{:S(2)}, u32[]{:S(2)}) collective-permute-start(bf16[128,2048]{1,0:T(8,128)(2,1)} %collective-permute-done.5.refs_3_), channel_id=1, source_target_pairs={{0,2},{2,0},{4,6},{6,4},{8,10},{10,8},{12,14},{14,12},{16,18},{18,... | collective-permute-start | bytes 1572872 | tf_op jit(solution)/shard_map/ppermute | solution.py:77
  58.8 11.7 %collective-permute-start.28 = (bf16[128,2048]{1,0:T(8,128)(2,1)}, bf16[128,2048]{1,0:T(8,128)(2,1)}, u32[]{:S(2)}, u32[]{:S(2)}) collective-permute-start(bf16[128,2048]{1,0:T(8,128)(2,1)} %collective-permute-done.20.refs_19_), channel_id=1, source_target_pairs={{0,2},{2,0},{4,6},{6,4},{8,10},{10,8},{12,14},{14,12},{16,18},{18,... | collective-permute-start | bytes 1572872 | tf_op jit(solution)/shard_map/ppermute | solution.py:78
  59.3 11.7 %collective-permute-start.14 = (bf16[128,2048]{1,0:T(8,128)(2,1)}, bf16[128,2048]{1,0:T(8,128)(2,1)}, u32[]{:S(2)}, u32[]{:S(2)}) collective-permute-start(bf16[128,2048]{1,0:T(8,128)(2,1)} %collective-permute-done.6.refs_4_), channel_id=1, source_target_pairs={{0,2},{2,0},{4,6},{6,4},{8,10},{10,8},{12,14},{14,12},{16,18},{18,... | collective-permute-start | bytes 1572872 | tf_op jit(solution)/shard_map/ppermute | solution.py:77
  65.9 11.3 %collective-permute-start.8 = (bf16[128,2048]{1,0:T(8,128)(2,1)}, bf16[128,2048]{1,0:T(8,128)(2,1)}, u32[]{:S(2)}, u32[]{:S(2)}) collective-permute-start(bf16[128,2048]{1,0:T(8,128)(2,1)} %collective-permute-done.7.refs_5_), channel_id=1, source_target_pairs={{0,8},{2,10},{8,16},{10,18},{16,24},{18,26},{24,28},{26,30},{28,20... | collective-permute-start | bytes 1572872 | tf_op jit(solution)/shard_map/ppermute | solution.py:73
  66.7 11.6 %collective-permute-start.23 = (bf16[128,2048]{1,0:T(8,128)(2,1)}, bf16[128,2048]{1,0:T(8,128)(2,1)}, u32[]{:S(2)}, u32[]{:S(2)}) collective-permute-start(bf16[128,2048]{1,0:T(8,128)(2,1)} %collective-permute-done.22.refs_21_), channel_id=1, source_target_pairs={{0,4},{2,6},{8,0},{10,2},{16,8},{18,10},{24,16},{26,18},{28,24},{3... | collective-permute-start | bytes 1572872 | tf_op jit(solution)/shard_map/ppermute | solution.py:74
  70.4 9.8 %collective-permute-start.29 = (bf16[128,2048]{1,0:T(8,128)(2,1)}, bf16[128,2048]{1,0:T(8,128)(2,1)}, u32[]{:S(2)}, u32[]{:S(2)}) collective-permute-start(bf16[128,2048]{1,0:T(8,128)(2,1)} %collective-permute-done.21.refs_20_), channel_id=1, source_target_pairs={{0,2},{2,0},{4,6},{6,4},{8,10},{10,8},{12,14},{14,12},{16,18},{18,... | collective-permute-start | bytes 1572872 | tf_op jit(solution)/shard_map/ppermute | solution.py:78
  70.5 10.7 %collective-permute-start.15 = (bf16[128,2048]{1,0:T(8,128)(2,1)}, bf16[128,2048]{1,0:T(8,128)(2,1)}, u32[]{:S(2)}, u32[]{:S(2)}) collective-permute-start(bf16[128,2048]{1,0:T(8,128)(2,1)} %collective-permute-done.7.refs_5_), channel_id=1, source_target_pairs={{0,2},{2,0},{4,6},{6,4},{8,10},{10,8},{12,14},{14,12},{16,18},{18,... | collective-permute-start | bytes 1572872 | tf_op jit(solution)/shard_map/ppermute | solution.py:77
  71.0 10.3 %collective-permute-start.30 = (bf16[128,2048]{1,0:T(8,128)(2,1)}, bf16[128,2048]{1,0:T(8,128)(2,1)}, u32[]{:S(2)}, u32[]{:S(2)}) collective-permute-start(bf16[128,2048]{1,0:T(8,128)(2,1)} %collective-permute-done.22.refs_21_), channel_id=1, source_target_pairs={{0,2},{2,0},{4,6},{6,4},{8,10},{10,8},{12,14},{14,12},{16,18},{18,... | collective-permute-start | bytes 1572872 | tf_op jit(solution)/shard_map/ppermute | solution.py:78
  77.2 9.9 %collective-permute-start.9 = (bf16[128,2048]{1,0:T(8,128)(2,1)}, bf16[128,2048]{1,0:T(8,128)(2,1)}, u32[]{:S(2)}, u32[]{:S(2)}) collective-permute-start(bf16[128,2048]{1,0:T(8,128)(2,1)} %collective-permute-done.8.refs_6_), channel_id=1, source_target_pairs={{0,8},{2,10},{8,16},{10,18},{16,24},{18,26},{24,28},{26,30},{28,20... | collective-permute-start | bytes 1572872 | tf_op jit(solution)/shard_map/ppermute | solution.py:73
  78.2 9.5 %collective-permute-start.24 = (bf16[128,2048]{1,0:T(8,128)(2,1)}, bf16[128,2048]{1,0:T(8,128)(2,1)}, u32[]{:S(2)}, u32[]{:S(2)}) collective-permute-start(bf16[128,2048]{1,0:T(8,128)(2,1)} %collective-permute-done.23.refs_22_), channel_id=1, source_target_pairs={{0,4},{2,6},{8,0},{10,2},{16,8},{18,10},{24,16},{26,18},{28,24},{3... | collective-permute-start | bytes 1572872 | tf_op jit(solution)/shard_map/ppermute | solution.py:74
  80.3 22.5 %collective-permute-start.2 = (bf16[1024,256]{1,0:T(8,128)(2,1)}, bf16[1024,256]{1,0:T(8,128)(2,1)S(1)}, u32[]{:S(2)}, u32[]{:S(2)}) collective-permute-start(bf16[1024,256]{1,0:T(8,128)(2,1)} %param.17), channel_id=1, source_target_pairs={{0,1},{1,0},{2,3},{3,2},{4,5},{5,4},{6,7},{7,6},{8,9},{9,8},{10,11... | collective-permute-start | bytes 1572872 | tf_op jit(solution)/shard_map/ppermute | solution.py:61
  81.3 7.6 %collective-permute-start.16 = (bf16[128,2048]{1,0:T(8,128)(2,1)}, bf16[128,2048]{1,0:T(8,128)(2,1)S(1)}, u32[]{:S(2)}, u32[]{:S(2)}) collective-permute-start(bf16[128,2048]{1,0:T(8,128)(2,1)} %collective-permute-done.8.refs_6_), channel_id=1, source_target_pairs={{0,2},{2,0},{4,6},{6,4},{8,10},{10,8},{12,14},{14,12},{16,18},{18,... | collective-permute-start | bytes 1572872 | tf_op jit(solution)/shard_map/ppermute | solution.py:77
  81.3 7.6 %collective-permute-start.31 = (bf16[128,2048]{1,0:T(8,128)(2,1)}, bf16[128,2048]{1,0:T(8,128)(2,1)S(1)}, u32[]{:S(2)}, u32[]{:S(2)}) collective-permute-start(bf16[128,2048]{1,0:T(8,128)(2,1)} %collective-permute-done.23.refs_22_), channel_id=1, source_target_pairs={{0,2},{2,0},{4,6},{6,4},{8,10},{10,8},{12,14},{14,12},{16,18},{18,... | collective-permute-start | bytes 1572872 | tf_op jit(solution)/shard_map/ppermute | solution.py:78
  101.3 16.5 %collective-permute-start.33 = (bf16[1280,128]{1,0:T(8,128)(2,1)}, bf16[1280,128]{1,0:T(8,128)(2,1)S(1)}, u32[]{:S(2)}, u32[]{:S(2)}) collective-permute-start(bf16[1280,128]{1,0:T(8,128)(2,1)} %attention.2), channel_id=1, source_target_pairs={{0,1},{1,0},{2,3},{3,2},{4,5},{5,4},{6,7},{7,6},{8,9},{9,8},{10,11... | collective-permute-start | bytes 983048 | tf_op jit(solution)/shard_map/ppermute | solution.py:756
  110.8 7.0 %collective-permute-start.34 = (bf16[768,128]{1,0:T(8,128)(2,1)}, bf16[768,128]{1,0:T(8,128)(2,1)S(1)}, u32[]{:S(2)}, u32[]{:S(2)}) collective-permute-start(bf16[768,128]{1,0:T(8,128)(2,1)} %attention.3), channel_id=1, source_target_pairs={{0,1},{1,0},{2,3},{3,2},{4,5},{5,4},{6,7},{7,6},{8,9},{9,8},{10,11... | collective-permute-start | bytes 589832 | tf_op jit(solution)/shard_map/ppermute | solution.py:756
  130.1 14.5 %collective-permute-start.37 = (bf16[1,512,512]{2,1,0:T(8,128)(2,1)S(1)}, bf16[1,512,512]{2,1,0:T(8,128)(2,1)S(1)}, u32[]{:S(2)}, u32[]{:S(2)}) collective-permute-start(bf16[1,512,512]{2,1,0:T(8,128)(2,1)S(1)} %get-tuple-element.43), channel_id=1, source_target_pairs={{0,2},{2,0},{4,6},{6,4},{8,10},{10,8},{12,14},{14,12},{16,18},{18,... | collective-permute-start | bytes 1572872 | tf_op jit(solution)/shard_map/ppermute | solution.py:572
  132.1 14.0 %collective-permute-start.38 = (bf16[1,512,512]{2,1,0:T(8,128)(2,1)S(1)}, bf16[1,512,512]{2,1,0:T(8,128)(2,1)S(1)}, u32[]{:S(2)}, u32[]{:S(2)}) collective-permute-start(bf16[1,512,512]{2,1,0:T(8,128)(2,1)S(1)} %sum_core.2.refs_8_.refs_3_), channel_id=1, source_target_pairs={{0,4},{2,6},{4,0},{6,2},{8,12},{10,14},{12,8},{14,10},{16,20},{18,... | collective-permute-start | bytes 1572872 | tf_op jit(solution)/shard_map/ppermute | solution.py:579
  144.2 13.5 %collective-permute-start.40 = (bf16[1,512,512]{2,1,0:T(8,128)(2,1)S(1)}, bf16[1,512,512]{2,1,0:T(8,128)(2,1)S(1)}, u32[]{:S(2)}, u32[]{:S(2)}) collective-permute-start(bf16[1,512,512]{2,1,0:T(8,128)(2,1)S(1)} %get-tuple-element.48), channel_id=1, source_target_pairs={{0,2},{2,0},{4,6},{6,4},{8,10},{10,8},{12,14},{14,12},{16,18},{18,... | collective-permute-start | bytes 1572872 | tf_op jit(solution)/shard_map/ppermute | solution.py:572
  146.4 8.6 %collective-permute-start.42 = (bf16[1,256,512]{2,1,0:T(8,128)(2,1)S(1)}, bf16[1,256,512]{2,1,0:T(8,128)(2,1)S(1)}, u32[]{:S(2)}, u32[]{:S(2)}) collective-permute-start(bf16[1,256,512]{2,1,0:T(8,128)(2,1)S(1)} %get-tuple-element.44.refs_2_), channel_id=1, source_target_pairs={{0,8},{2,10},{4,12},{6,14},{8,0},{10,2},{12,4},{14,6},{16,24},{18,... | collective-permute-start | bytes 786440 | tf_op jit(solution)/shard_map/ppermute | solution.py:575
  148.1 12.9 %collective-permute-start.41 = (bf16[1,512,512]{2,1,0:T(8,128)(2,1)S(1)}, bf16[1,512,512]{2,1,0:T(8,128)(2,1)S(1)}, u32[]{:S(2)}, u32[]{:S(2)}) collective-permute-start(bf16[1,512,512]{2,1,0:T(8,128)(2,1)S(1)} %sum_core.3.refs_2_), channel_id=1, source_target_pairs={{0,4},{2,6},{4,0},{6,2},{8,12},{10,14},{12,8},{14,10},{16,20},{18,... | collective-permute-start | bytes 1572872 | tf_op jit(solution)/shard_map/ppermute | solution.py:579
  155.1 8.2 %collective-permute-start.44 = (bf16[1,128,512]{2,1,0:T(8,128)(2,1)S(1)}, bf16[1,128,512]{2,1,0:T(8,128)(2,1)S(1)}, u32[]{:S(2)}, u32[]{:S(2)}) collective-permute-start(bf16[1,128,512]{2,1,0:T(8,128)(2,1)S(1)} %get-tuple-element.50.refs_3_), channel_id=1, source_target_pairs={{0,16},{2,18},{4,20},{6,22},{8,24},{10,26},{12,28},{14,30},{16,0},... | collective-permute-start | bytes 393224 | tf_op jit(solution)/shard_map/ppermute | solution.py:575
  161.3 10.3 %collective-permute-start.43 = (bf16[1,256,512]{2,1,0:T(8,128)(2,1)S(1)}, bf16[1,256,512]{2,1,0:T(8,128)(2,1)S(1)}, u32[]{:S(2)}, u32[]{:S(2)}) collective-permute-start(bf16[1,256,512]{2,1,0:T(8,128)(2,1)S(1)} %get-tuple-element.52.refs_2_), channel_id=1, source_target_pairs={{0,8},{2,10},{4,12},{6,14},{8,0},{10,2},{12,4},{14,6},{16,24},{18,... | collective-permute-start | bytes 786440 | tf_op jit(solution)/shard_map/ppermute | solution.py:575
  162.0 34.4 %collective-permute-start.39 = (bf16[1024,512]{1,0:T(8,128)(2,1)S(1)}, bf16[1024,512]{1,0:T(8,128)(2,1)S(1)}, u32[]{:S(2)}, u32[]{:S(2)}) collective-permute-start(bf16[1024,512]{1,0:T(8,128)(2,1)S(1)} %get-tuple-element.46), channel_id=1, source_target_pairs={{0,1},{1,0},{2,3},{3,2},{4,5},{5,4},{6,7},{7,6},{8,9},{9,8},{10,11... | collective-permute-start | bytes 3145736 | tf_op jit(solution)/shard_map/ppermute | solution.py:780
  163.3 8.4 %collective-permute-start.46 = (bf16[1,1,128,512]{3,2,1,0:T(8,128)(2,1)S(1)}, bf16[1,1,128,512]{3,2,1,0:T(8,128)(2,1)S(1)}, u32[]{:S(2)}, u32[]{:S(2)}) collective-permute-start(bf16[1,1,128,512]{3,2,1,0:T(8,128)(2,1)S(1)} %bitcast.33), channel_id=1, source_target_pairs={{0,16},{2,18},{4,20},{6,22},{8,24},{10,26},{12,28},{14,30},{16,0},... | collective-permute-start | bytes 393224 | tf_op jit(solution)/shard_map/ppermute | solution.py:575
  171.7 8.5 %collective-permute-start.48 = (bf16[2,1,128,512]{3,2,1,0:T(8,128)(2,1)S(1)}, bf16[2,1,128,512]{3,2,1,0:T(8,128)(2,1)S(1)}, u32[]{:S(2)}, u32[]{:S(2)}) collective-permute-start(bf16[2,1,128,512]{3,2,1,0:T(8,128)(2,1)S(1)} %stack_pieces.5.refs_2_.refs_0_), channel_id=1, source_target_pairs={{0,8},{2,10},{4,12},{6,14},{8,0},{10,2},{12,4},{14,6},{16,24},{18,... | collective-permute-start | bytes 786440 | tf_op jit(solution)/shard_map/ppermute | solution.py:575
  180.2 16.1 %collective-permute-start.52 = (bf16[4,1,128,512]{3,2,1,0:T(8,128)(2,1)S(1)}, bf16[4,1,128,512]{3,2,1,0:T(8,128)(2,1)S(1)}, u32[]{:S(2)}, u32[]{:S(2)}) collective-permute-start(bf16[4,1,128,512]{3,2,1,0:T(8,128)(2,1)S(1)} %stack_pieces.6.refs_2_.refs_0_), channel_id=1, source_target_pairs={{0,4},{2,6},{4,0},{6,2},{8,12},{10,14},{12,8},{14,10},{16,20},{18,... | collective-permute-start | bytes 1572872 | tf_op jit(solution)/shard_map/ppermute | solution.py:602
  187.2 7.3 %collective-permute-start.49 = (bf16[2,1,128,512]{3,2,1,0:T(8,128)(2,1)S(1)}, bf16[2,1,128,512]{3,2,1,0:T(8,128)(2,1)S(1)}, u32[]{:S(2)}, u32[]{:S(2)}) collective-permute-start(bf16[2,1,128,512]{3,2,1,0:T(8,128)(2,1)S(1)} %stack_pieces.7.refs_0_.refs_2_), channel_id=1, source_target_pairs={{0,8},{2,10},{4,12},{6,14},{8,0},{10,2},{12,4},{14,6},{16,24},{18,... | collective-permute-start | bytes 786440 | tf_op jit(solution)/shard_map/ppermute | solution.py:575
  190.3 8.1 %collective-permute-start.53 = (bf16[4,1,128,512]{3,2,1,0:T(8,128)(2,1)S(1)}, bf16[4,1,128,512]{3,2,1,0:T(8,128)(2,1)S(1)}, u32[]{:S(2)}, u32[]{:S(2)}) collective-permute-start(bf16[4,1,128,512]{3,2,1,0:T(8,128)(2,1)S(1)} %stack_pieces.6.refs_2_.refs_0_), channel_id=1, source_target_pairs={{0,2},{2,0},{4,6},{6,4},{8,10},{10,8},{12,14},{14,12},{16,18},{18,... | collective-permute-start | bytes 1572872 | tf_op jit(solution)/shard_map/ppermute | solution.py:572
  194.5 6.9 %collective-permute-start.51 = (bf16[4,1,128,512]{3,2,1,0:T(8,128)(2,1)S(1)}, bf16[4,1,128,512]{3,2,1,0:T(8,128)(2,1)S(1)}, u32[]{:S(2)}, u32[]{:S(2)}) collective-permute-start(bf16[4,1,128,512]{3,2,1,0:T(8,128)(2,1)S(1)} %stack_pieces.8.refs_5_.refs_0_), channel_id=1, source_target_pairs={{0,2},{2,0},{4,6},{6,4},{8,10},{10,8},{12,14},{14,12},{16,18},{18,... | collective-permute-start | bytes 1572872 | tf_op jit(solution)/shard_map/ppermute | solution.py:572
  194.6 14.3 %collective-permute-start.50 = (bf16[4,1,128,512]{3,2,1,0:T(8,128)(2,1)S(1)}, bf16[4,1,128,512]{3,2,1,0:T(8,128)(2,1)S(1)}, u32[]{:S(2)}, u32[]{:S(2)}) collective-permute-start(bf16[4,1,128,512]{3,2,1,0:T(8,128)(2,1)S(1)} %stack_pieces.8.refs_5_.refs_0_), channel_id=1, source_target_pairs={{0,4},{2,6},{4,0},{6,2},{8,12},{10,14},{12,8},{14,10},{16,20},{18,... | collective-permute-start | bytes 1572872 | tf_op jit(solution)/shard_map/ppermute | solution.py:602
  (27 other events, 319.8 us)

commit v7 on v6

--- a/solution.py
+++ b/solution.py
@@ -243,9 +243,14 @@
         def dispatch(i, carry):
             at = pl.ds(pl.multiple_of(i * chunk, chunk), chunk)
             if pieces:
-                projected = jnp.dot(atts[0][at, :], projs[0][...], preferred_element_type=f32)
-                for a, w in zip(atts[1:], projs[1:]):
-                    projected = projected + jnp.dot(a[at, :], w[...], preferred_element_type=f32)
+                if atts[0].shape[1] % 128 == 0:
+                    gathered = jnp.concatenate([a[at, :] for a in atts], 1)
+                    weights = jnp.concatenate([w[...] for w in projs], 0)
+                    projected = jnp.dot(gathered, weights, preferred_element_type=f32)
+                else:
+                    projected = jnp.dot(atts[0][at, :], projs[0][...], preferred_element_type=f32)
+                    for a, w in zip(atts[1:], projs[1:]):
+                        projected = projected + jnp.dot(a[at, :], w[...], preferred_element_type=f32)
                 stream = (res_ref[at, :].astype(f32) + projected).astype(bf16)
                 out_stream[at, :] = stream
             else:

time: 214 us -> 216 us (level)
  waiting for transfers between devices: 88.8 us -> 95.4 us
  starting transfers between devices: 46.7 us -> 44.3 us
    ppermute x8, starting transfers between devices: 16.2 us -> 11.2 us  [to_line(): return lax.ppermute(x, 'seq', line_pairs(self.seq_count, step))]
    ppermute x8, waiting for transfers between devices: 19.4 us -> 23.7 us  [to_line(): return lax.ppermute(x, 'seq', line_pairs(self.seq_count, step))]
  transfers between devices with their start and end apart: 56 -> 56, of which waited for: 22 -> 23; matrix products, arithmetic and copies ran while one was open for 8% -> 8% of each run, Pallas kernels for 20% -> 20%
where the time goes in v7:
time: 216 us
  waiting for transfers between devices  95.4 us (44%)
  Pallas kernels  55.5 us (26%)
  starting transfers between devices  44.3 us (21%)
  local copies, waits for them, and re-layouts  9.68 us (4%)
  other arithmetic  9.28 us (4%)
    ppermute x7, waiting for transfers between devices, ring_gather(): k = lax.ppermute(k, 'seq', fwd)  48.7 us
    ppermute x8, waiting for transfers between devices, to_line(): return lax.ppermute(x, 'seq', line_pairs(self.seq_count, step))  23.7 us
    pallas_call x2, Pallas kernels, expert_group(): pl.pallas_call(functools.partial(group_kernel, first, count, pieces, 0 if...  21.3 us
    pallas_call x2, Pallas kernels, attention(): pl.pallas_call(functools.partial(attention_kernel, degree, feat // HD, le...  18.5 us
    ppermute x8, starting transfers between devices, to_line(): return lax.ppermute(x, 'seq', line_pairs(self.seq_count, step))  11.2 us
    ppermute x7, starting transfers between devices, ring_gather(): k = lax.ppermute(k, 'seq', fwd)  10.1 us
    pallas_call x3, Pallas kernels, unpack(): pl.pallas_call(functools.partial(unpack_kernel, len(blocks), lines, each,...  7.01 us
    ppermute x2, waiting for transfers between devices, back_line(): self.other = lax.ppermute(self.own, 'seq', self.cross)  6.67 us
  transfers between devices with their start and end apart: 56, of which 23 were waited for; matrix products, arithmetic and copies ran while one was open for 8% of the time, Pallas kernels for 20%

profile of v7, /device:TPU:0, one launch (start us, length us, event | category | flops | bytes accessed | tf_op | source)
XLA Modules:
  0.0 215.5 jit_solution(7552500732655375014)
XLA Ops:
  0.6 3.1 %collective-permute-start.3 = (bf16[128,2048]{1,0:T(8,128)(2,1)}, bf16[128,2048]{1,0:T(8,128)(2,1)S(1)}, u32[]{:S(2)}, u32[]{:S(2)}) collective-permute-start(bf16[128,2048]{1,0:T(8,128)(2,1)} %refs_0_.3), channel_id=1, source_target_pairs={{0,8},{2,10},{8,16},{10,18},{16,24},{18,26},{24,28},{26,30},{28,20... | collective-permute-start | bytes 1572872 | tf_op jit(solution)/shard_map/ppermute | solution.py:73
  3.7 2.0 collective-permute-start
  6.5 9.3 %collective-permute-done.3.refs_1_ = bf16[128,2048]{1,0:T(8,128)(2,1)S(1)} collective-permute-done((bf16[128,2048]{1,0:T(8,128)(2,1)}, bf16[128,2048]{1,0:T(8,128)(2,1)S(1)}, u32[]{:S(2)}, u32[]{:S(2)}) %collective-permute-start.3) | collective-permute-done | bytes 524320 | tf_op jit(solution)/shard_map/ppermute | solution.py:73
  15.8 1.8 collective-permute-start.4
  17.9 1.2 dynamic_slice.13
  20.8 8.3 %collective-permute-done.4.refs_2_ = bf16[128,2048]{1,0:T(8,128)(2,1)} collective-permute-done((bf16[128,2048]{1,0:T(8,128)(2,1)S(1)}, bf16[128,2048]{1,0:T(8,128)(2,1)}, u32[]{:S(2)}, u32[]{:S(2)}) %collective-permute-start.4) | collective-permute-done | bytes 524320 | tf_op jit(solution)/shard_map/ppermute | solution.py:73
  29.1 1.5 collective-permute-start.5
  32.9 8.8 %collective-permute-done.5.refs_3_ = bf16[128,2048]{1,0:T(8,128)(2,1)} collective-permute-done((bf16[128,2048]{1,0:T(8,128)(2,1)}, bf16[128,2048]{1,0:T(8,128)(2,1)}, u32[]{:S(2)}, u32[]{:S(2)}) %collective-permute-start.5) | collective-permute-done | bytes 524320 | tf_op jit(solution)/shard_map/ppermute | solution.py:73
  41.7 1.2 collective-permute-start.6
  45.1 1.2 fusion.8
  46.4 1.2 fusion.10
  49.4 4.4 %collective-permute-done.6.refs_4_ = bf16[128,2048]{1,0:T(8,128)(2,1)} collective-permute-done((bf16[128,2048]{1,0:T(8,128)(2,1)}, bf16[128,2048]{1,0:T(8,128)(2,1)}, u32[]{:S(2)}, u32[]{:S(2)}) %collective-permute-start.6) | collective-permute-done | bytes 524320 | tf_op jit(solution)/shard_map/ppermute | solution.py:73
  54.6 1.3 collective-permute-start.22
  57.6 1.1 constant_dynamic-update-slice_fusion.1
  59.4 6.5 %collective-permute-done.7.refs_5_ = bf16[128,2048]{1,0:T(8,128)(2,1)} collective-permute-done((bf16[128,2048]{1,0:T(8,128)(2,1)}, bf16[128,2048]{1,0:T(8,128)(2,1)}, u32[]{:S(2)}, u32[]{:S(2)}) %collective-permute-start.7) | collective-permute-done | bytes 524320 | tf_op jit(solution)/shard_map/ppermute | solution.py:73
  66.7 1.3 collective-permute-start.23
  68.1 2.3 %reduce-window.6 = s32[8,16,128]{2,1,0:T(8,128)S(1)} reduce-window(s32[8,16,128]{2,1,0:T(8,128)S(1)} %copy.39, s32[]{:T(128)} %constant.111.clone.1), window={size=1x1x128 pad=0_0x0_0x127_0}, to_apply=%region_1.2 | reduce-window | flops 2080768 | bytes 131076 | tf_op jit(solution)/shard_map/reduce-window
  71.1 6.1 %collective-permute-done.8.refs_6_ = bf16[128,2048]{1,0:T(8,128)(2,1)} collective-permute-done((bf16[128,2048]{1,0:T(8,128)(2,1)}, bf16[128,2048]{1,0:T(8,128)(2,1)}, u32[]{:S(2)}, u32[]{:S(2)}) %collective-permute-start.8) | collective-permute-done | bytes 524320 | tf_op jit(solution)/shard_map/ppermute | solution.py:73
  78.2 1.1 collective-permute-start.24
  81.8 5.3 %collective-permute-done.9.refs_7_ = bf16[128,2048]{1,0:T(8,128)(2,1)} collective-permute-done((bf16[128,2048]{1,0:T(8,128)(2,1)}, bf16[128,2048]{1,0:T(8,128)(2,1)}, u32[]{:S(2)}, u32[]{:S(2)}) %collective-permute-start.9) | collective-permute-done | bytes 524320 | tf_op jit(solution)/shard_map/ppermute | solution.py:73
  87.7 1.1 constant_dynamic-update-slice_fusion.2.refs_1_
  90.8 10.5 %attention.2 = bf16[1280,128]{1,0:T(8,128)(2,1)} custom-call(s32[40]{0:T(128)} %squeeze_reshape.6.local, s32[40]{0:T(128)} %get-tuple-element.78.korder, s32[17]{0:T(128)} %get-tuple-element.79.kbegin, s32[40]{0:T(128)} %get-tuple-element.77.vorder, s32[17]{0:T(128)} %get-tuple-element.80.vbegin, bf16[128,2048]{1,0:T(8,128)(2,1)} %q_ref.3, ...), custom_call_target="tpu_custom_call" | custom-call | flops 335544320 | bytes 3276800 | tf_op jit(solution)/shard_map/attention/pallas_call | solution.py:165
  101.3 1.4 collective-permute-start.33
  102.8 8.0 %attention.3 = bf16[768,128]{1,0:T(8,128)(2,1)} custom-call(s32[24]{0:T(128)} %squeeze_reshape.7.local, s32[24]{0:T(128)} %get-tuple-element.74.korder, s32[17]{0:T(128)} %get-tuple-element.75.kbegin, s32[24]{0:T(128)} %get-tuple-element.73.vorder, s32[17]{0:T(128)} %get-tuple-element.76.vbegin, bf16[128,2048]{1,0:T(8,128)(2,1)} %q_ref.3, ...), custom_call_target="tpu_custom_call" | custom-call | flops 201326592 | bytes 1966080 | tf_op jit(solution)/shard_map/attention/pallas_call | solution.py:165
  112.6 5.3 %collective-permute-done.34 = bf16[768,128]{1,0:T(8,128)(2,1)S(1)} collective-permute-done((bf16[768,128]{1,0:T(8,128)(2,1)}, bf16[768,128]{1,0:T(8,128)(2,1)S(1)}, u32[]{:S(2)}, u32[]{:S(2)}) %collective-permute-start.34) | collective-permute-done | bytes 196640 | tf_op jit(solution)/shard_map/ppermute | solution.py:761
  117.9 11.3 %experts.2 = (bf16[2048,256]{1,0:T(8,128)(2,1)S(1)}, bf16[4,640,512]{2,1,0:T(8,128)(2,1)S(1)}, bf16[1,512,512]{2,1,0:T(8,128)(2,1)S(1)}, bf16[1,512,512]{2,1,0:T...) custom-call(s32[8]{0:T(128)S(1)} %slice_reduce_fusion.1.counts, ...), custom_call_target="tpu_custom_call" | custom-call | flops 1000 | bytes 1000 | tf_op jit(solution)/shard_map/experts/pallas_call | solution.py:391
  129.8 1.4 collective-permute-done.35.refs_1_
  132.3 9.9 %experts.3 = (bf16[4,640,512]{2,1,0:T(8,128)(2,1)S(1)}, bf16[1,512,512]{2,1,0:T(8,128)(2,1)S(1)}, bf16[1,512,512]{2,1,0:T(8,128)(2,1)S(1)}, bf16[1,512,512]{2,1,0:T(8,128)(2,1)S(1)}, bf16[1,512,512]{2,1,0:T(8,128)(2,1)S(1)}) custom-call(s32[8]{0:T(128)S(1)} %slice_reduce_fusion.1.counts, s32[8]{0:T(128)S(1)} %broadcast_add_fusion.ids, s32[8]{0:T(128)S(1)} %stack.55.perm, ...), custom_call_target="tpu_custom_call" | custom-call | flops 1000 | bytes 1000 | tf_op jit(solution)/shard_map/experts/pallas_call | solution.py:391
  142.8 2.5 %collective-permute-done.38.refs_2_ = bf16[1,512,512]{2,1,0:T(8,128)(2,1)S(1)} collective-permute-done((bf16[1,512,512]{2,1,0:T(8,128)(2,1)S(1)}, bf16[1,512,512]{2,1,0:T(8,128)(2,1)S(1)}, u32[]{:S(2)}, u32[]{:S(2)}) %collective-permute-start.38) | collective-permute-done | bytes 524320 | tf_op jit(solution)/shard_map/ppermute | solution.py:584
  145.6 2.6 %collective-permute-start.42 = (bf16[1,256,512]{2,1,0:T(8,128)(2,1)S(1)}, bf16[1,256,512]{2,1,0:T(8,128)(2,1)S(1)}, u32[]{:S(2)}, u32[]{:S(2)}) collective-permute-start(bf16[1,256,512]{2,1,0:T(8,128)(2,1)S(1)} %get-tuple-element.44.refs_2_), channel_id=1, source_target_pairs={{0,8},{2,10},{4,12},{6,14},{8,0},{10,2},{12,4},{14,6},{16,24},{18,... | collective-permute-start | bytes 786440 | tf_op jit(solution)/shard_map/ppermute | solution.py:580
  148.2 1.0 collective-permute-start.41
  149.3 5.8 %combine.1 = (bf16[1024,512]{1,0:T(8,128)(2,1)S(1)}, bf16[1024,512]{1,0:T(8,128)(2,1)S(1)}) custom-call(s32[9,8]{1,0:T(8,128)S(1)} %copy.45.starts, s32[2]{0:T(128)S(1)} %compare_select_fusion.1.order, s32[8,2048]{1,0:T(8,128)S(1)} %add_select_fusion.refs_0_.rank_ref, bf16[4,640,512]{2,1,0:T(8,128)(2,1)S(1)} %get-tuple-element.36.refs_0_, ...), custom_call_target="tpu_custom_call" | custom-call | flops 32000000000 | bytes 10000000 | tf_op jit(solution)/shard_map/combine/pallas_call | solution.py:448
  155.2 2.6 %collective-permute-start.44 = (bf16[1,128,512]{2,1,0:T(8,128)(2,1)S(1)}, bf16[1,128,512]{2,1,0:T(8,128)(2,1)S(1)}, u32[]{:S(2)}, u32[]{:S(2)}) collective-permute-start(bf16[1,128,512]{2,1,0:T(8,128)(2,1)S(1)} %get-tuple-element.50.refs_3_), channel_id=1, source_target_pairs={{0,16},{2,18},{4,20},{6,22},{8,24},{10,26},{12,28},{14,30},{16,0},... | collective-permute-start | bytes 393224 | tf_op jit(solution)/shard_map/ppermute | solution.py:580
  157.8 3.4 %collective-permute-done.41.refs_2_ = bf16[1,512,512]{2,1,0:T(8,128)(2,1)S(1)} collective-permute-done((bf16[1,512,512]{2,1,0:T(8,128)(2,1)S(1)}, bf16[1,512,512]{2,1,0:T(8,128)(2,1)S(1)}, u32[]{:S(2)}, u32[]{:S(2)}) %collective-permute-start.41) | collective-permute-done | bytes 524320 | tf_op jit(solution)/shard_map/ppermute | solution.py:584
  163.0 2.3 %collective-permute-start.46 = (bf16[1,1,128,512]{3,2,1,0:T(8,128)(2,1)S(1)}, bf16[1,1,128,512]{3,2,1,0:T(8,128)(2,1)S(1)}, u32[]{:S(2)}, u32[]{:S(2)}) collective-permute-start(bf16[1,1,128,512]{3,2,1,0:T(8,128)(2,1)S(1)} %bitcast.33), channel_id=1, source_target_pairs={{0,16},{2,18},{4,20},{6,22},{8,24},{10,26},{12,28},{14,30},{16,0},... | collective-permute-start | bytes 393224 | tf_op jit(solution)/shard_map/ppermute | solution.py:580
  165.3 6.3 %collective-permute-done.43.refs_1_ = bf16[1,256,512]{2,1,0:T(8,128)(2,1)S(1)} collective-permute-done((bf16[1,256,512]{2,1,0:T(8,128)(2,1)S(1)}, bf16[1,256,512]{2,1,0:T(8,128)(2,1)S(1)}, u32[]{:S(2)}, u32[]{:S(2)}) %collective-permute-start.43) | collective-permute-done | bytes 262176 | tf_op jit(solution)/shard_map/ppermute | solution.py:580
  171.7 1.7 collective-permute-start.48
  173.4 1.0 collective-permute-start.45
  174.4 4.9 %collective-permute-done.45.refs_1_ = bf16[1,128,512]{2,1,0:T(8,128)(2,1)S(1)} collective-permute-done((bf16[1,128,512]{2,1,0:T(8,128)(2,1)S(1)}, bf16[1,128,512]{2,1,0:T(8,128)(2,1)S(1)}, u32[]{:S(2)}, u32[]{:S(2)}) %collective-permute-start.45) | collective-permute-done | bytes 131104 | tf_op jit(solution)/shard_map/ppermute | solution.py:580
  179.7 4.7 %collective-permute-start.52 = (bf16[4,1,128,512]{3,2,1,0:T(8,128)(2,1)S(1)}, bf16[4,1,128,512]{3,2,1,0:T(8,128)(2,1)S(1)}, u32[]{:S(2)}, u32[]{:S(2)}) collective-permute-start(bf16[4,1,128,512]{3,2,1,0:T(8,128)(2,1)S(1)} %stack_pieces.6.refs_2_.refs_0_), channel_id=1, source_target_pairs={{0,4},{2,6},{4,0},{6,2},{8,12},{10,14},{12,8},{14,10},{16,20},{18,... | collective-permute-start | bytes 1572872 | tf_op jit(solution)/shard_map/ppermute | solution.py:607
  185.0 5.6 %collective-permute-done.47.refs_1_ = bf16[1,1,128,512]{3,2,1,0:T(8,128)(2,1)S(1)} collective-permute-done((bf16[1,1,128,512]{3,2,1,0:T(8,128)(2,1)S(1)}, bf16[1,1,128,512]{3,2,1,0:T(8,128)(2,1)S(1)}, u32[]{:S(2)}, u32[]{:S(2)}) %collective-permute-start.47) | collective-permute-done | bytes 131104 | tf_op jit(solution)/shard_map/ppermute | solution.py:580
  190.9 6.2 %collective-permute-done.49.refs_1_ = bf16[2,1,128,512]{3,2,1,0:T(8,128)(2,1)S(1)} collective-permute-done((bf16[2,1,128,512]{3,2,1,0:T(8,128)(2,1)S(1)}, bf16[2,1,128,512]{3,2,1,0:T(8,128)(2,1)S(1)}, u32[]{:S(2)}, u32[]{:S(2)}) %collective-permute-start.49) | collective-permute-done | bytes 262176 | tf_op jit(solution)/shard_map/ppermute | solution.py:580
  197.7 1.9 at_home.1
  199.8 3.0 %unpack.3 = (f32[8,256,512]{2,1,0:T(8,128)}, f32[8,512,256]{2,1,0:T(8,128)}, f32[8,128]{1,0:T(8,128)}) custom-call(s32[4]{0:T(128)S(1)} %pad_add_fusion.3.where, s32[2]{0:T(128)S(1)} %pad_add_fusion.place, bf16[4,1,128,512]{3,2,1,0:T(8,128)(2,1)S(1)} %stack_pieces.6.refs_2_.refs_0_, bf16[4,1,128,512]{3,2,1,0:T(8,128)(2,1)S(1)} %collective-permute-done.52.refs_1_, ...), custom_call_target="tpu_custom_call" | custom-call | flops 201326592 | bytes 6291456 | tf_op jit(solution)/shard_map/unpack/pallas_call | solution.py:665
  202.9 2.0 unpack.4
  204.8 6.7 %collective-permute-done.50.refs_0_ = bf16[4,1,128,512]{3,2,1,0:T(8,128)(2,1)S(1)} collective-permute-done((bf16[4,1,128,512]{3,2,1,0:T(8,128)(2,1)S(1)}, bf16[4,1,128,512]{3,2,1,0:T(8,128)(2,1)S(1)}, u32[]{:S(2)}, u32[]{:S(2)}) %collective-permute-start.50) | collective-permute-done | bytes 524320 | tf_op jit(solution)/shard_map/ppermute | solution.py:607
  211.7 1.8 collective-permute-done.55.refs_1_
  213.5 2.0 unpack.5
  (186 shorter events, 28.2 us)
Async XLA Ops:
  0.6 15.1 %collective-permute-start.3 = (bf16[128,2048]{1,0:T(8,128)(2,1)}, bf16[128,2048]{1,0:T(8,128)(2,1)S(1)}, u32[]{:S(2)}, u32[]{:S(2)}) collective-permute-start(bf16[128,2048]{1,0:T(8,128)(2,1)} %refs_0_.3), channel_id=1, source_target_pairs={{0,8},{2,10},{8,16},{10,18},{16,24},{18,26},{24,28},{26,30},{28,20... | collective-permute-start | bytes 1572872 | tf_op jit(solution)/shard_map/ppermute | solution.py:73
  3.7 13.9 %collective-permute-start.18 = (bf16[128,2048]{1,0:T(8,128)(2,1)}, bf16[128,2048]{1,0:T(8,128)(2,1)}, u32[]{:S(2)}, u32[]{:S(2)}) collective-permute-start(bf16[128,2048]{1,0:T(8,128)(2,1)} %refs_16_.3), channel_id=1, source_target_pairs={{0,4},{2,6},{8,0},{10,2},{16,8},{18,10},{24,16},{26,18},{28,24},{3... | collective-permute-start | bytes 1572872 | tf_op jit(solution)/shard_map/ppermute | solution.py:74
  3.7 43.9 %collective-permute-start.10 = (bf16[128,2048]{1,0:T(8,128)(2,1)}, bf16[128,2048]{1,0:T(8,128)(2,1)S(1)}, u32[]{:S(2)}, u32[]{:S(2)}) collective-permute-start(bf16[128,2048]{1,0:T(8,128)(2,1)} %refs_0_.3), channel_id=1, source_target_pairs={{0,2},{2,0},{4,6},{6,4},{8,10},{10,8},{12,14},{14,12},{16,18},{18,... | collective-permute-start | bytes 1572872 | tf_op jit(solution)/shard_map/ppermute | solution.py:77
  3.7 28.5 %collective-permute-start = (s32[2,1024]{1,0:T(2,128)}, s32[2,1024]{1,0:T(2,128)S(1)}, u32[]{:S(2)}, u32[]{:S(2)}) collective-permute-start(s32[2,1024]{1,0:T(2,128)} %bitcast.47), channel_id=1, source_target_pairs={{0,1},{1,0},{2,3},{3,2},{4,5},{5,4},{6,7},{7,6},{8,9},{9,8},{10,11... | collective-permute-start | bytes 24584 | tf_op jit(solution)/shard_map/ppermute | solution.py:61
  5.7 26.6 %collective-permute-start.1 = (bf16[1024,256]{1,0:T(8,128)(2,1)}, bf16[1024,256]{1,0:T(8,128)(2,1)S(1)}, u32[]{:S(2)}, u32[]{:S(2)}) collective-permute-start(bf16[1024,256]{1,0:T(8,128)(2,1)} %refs_1_.1), channel_id=1, source_target_pairs={{0,1},{1,0},{2,3},{3,2},{4,5},{5,4},{6,7},{7,6},{8,9},{9,8},{10,11... | collective-permute-start | bytes 1572872 | tf_op jit(solution)/shard_map/ppermute | solution.py:61
  15.8 13.3 %collective-permute-start.4 = (bf16[128,2048]{1,0:T(8,128)(2,1)S(1)}, bf16[128,2048]{1,0:T(8,128)(2,1)}, u32[]{:S(2)}, u32[]{:S(2)}) collective-permute-start(bf16[128,2048]{1,0:T(8,128)(2,1)S(1)} %collective-permute-done.3.refs_1_), channel_id=1, source_target_pairs={{0,8},{2,10},{8,16},{10,18},{16,24},{18,26},{24,28},{26,30},{28,20... | collective-permute-start | bytes 1572872 | tf_op jit(solution)/shard_map/ppermute | solution.py:73
  17.6 13.0 %collective-permute-start.19 = (bf16[128,2048]{1,0:T(8,128)(2,1)}, bf16[128,2048]{1,0:T(8,128)(2,1)}, u32[]{:S(2)}, u32[]{:S(2)}) collective-permute-start(bf16[128,2048]{1,0:T(8,128)(2,1)} %collective-permute-done.18.refs_17_), channel_id=1, source_target_pairs={{0,4},{2,6},{8,0},{10,2},{16,8},{18,10},{24,16},{26,18},{28,24},{3... | collective-permute-start | bytes 1572872 | tf_op jit(solution)/shard_map/ppermute | solution.py:74
  29.1 12.6 %collective-permute-start.5 = (bf16[128,2048]{1,0:T(8,128)(2,1)}, bf16[128,2048]{1,0:T(8,128)(2,1)}, u32[]{:S(2)}, u32[]{:S(2)}) collective-permute-start(bf16[128,2048]{1,0:T(8,128)(2,1)} %collective-permute-done.4.refs_2_), channel_id=1, source_target_pairs={{0,8},{2,10},{8,16},{10,18},{16,24},{18,26},{24,28},{26,30},{28,20... | collective-permute-start | bytes 1572872 | tf_op jit(solution)/shard_map/ppermute | solution.py:73
  30.6 12.3 %collective-permute-start.20 = (bf16[128,2048]{1,0:T(8,128)(2,1)}, bf16[128,2048]{1,0:T(8,128)(2,1)}, u32[]{:S(2)}, u32[]{:S(2)}) collective-permute-start(bf16[128,2048]{1,0:T(8,128)(2,1)} %collective-permute-done.19.refs_18_), channel_id=1, source_target_pairs={{0,4},{2,6},{8,0},{10,2},{16,8},{18,10},{24,16},{26,18},{28,24},{3... | collective-permute-start | bytes 1572872 | tf_op jit(solution)/shard_map/ppermute | solution.py:74
  32.3 15.4 %collective-permute-start.25 = (bf16[128,2048]{1,0:T(8,128)(2,1)S(1)}, bf16[128,2048]{1,0:T(8,128)(2,1)S(1)}, u32[]{:S(2)}, u32[]{:S(2)}) collective-permute-start(bf16[128,2048]{1,0:T(8,128)(2,1)S(1)} %copy-done.5), channel_id=1, source_target_pairs={{0,2},{2,0},{4,6},{6,4},{8,10},{10,8},{12,14},{14,12},{16,18},{18,... | collective-permute-start | bytes 1572872 | tf_op jit(solution)/shard_map/ppermute | solution.py:78
  32.4 15.8 %collective-permute-start.11 = (bf16[128,2048]{1,0:T(8,128)(2,1)S(1)}, bf16[128,2048]{1,0:T(8,128)(2,1)S(1)}, u32[]{:S(2)}, u32[]{:S(2)}) collective-permute-start(bf16[128,2048]{1,0:T(8,128)(2,1)S(1)} %collective-permute-done.3.refs_1_), channel_id=1, source_target_pairs={{0,2},{2,0},{4,6},{6,4},{8,10},{10,8},{12,14},{14,12},{16,18},{18,... | collective-permute-start | bytes 1572872 | tf_op jit(solution)/shard_map/ppermute | solution.py:77
  41.7 12.1 %collective-permute-start.6 = (bf16[128,2048]{1,0:T(8,128)(2,1)}, bf16[128,2048]{1,0:T(8,128)(2,1)}, u32[]{:S(2)}, u32[]{:S(2)}) collective-permute-start(bf16[128,2048]{1,0:T(8,128)(2,1)} %collective-permute-done.5.refs_3_), channel_id=1, source_target_pairs={{0,8},{2,10},{8,16},{10,18},{16,24},{18,26},{24,28},{26,30},{28,20... | collective-permute-start | bytes 1572872 | tf_op jit(solution)/shard_map/ppermute | solution.py:73
  42.9 11.7 %collective-permute-start.21 = (bf16[128,2048]{1,0:T(8,128)(2,1)}, bf16[128,2048]{1,0:T(8,128)(2,1)}, u32[]{:S(2)}, u32[]{:S(2)}) collective-permute-start(bf16[128,2048]{1,0:T(8,128)(2,1)} %collective-permute-done.20.refs_19_), channel_id=1, source_target_pairs={{0,4},{2,6},{8,0},{10,2},{16,8},{18,10},{24,16},{26,18},{28,24},{3... | collective-permute-start | bytes 1572872 | tf_op jit(solution)/shard_map/ppermute | solution.py:74
  47.6 11.1 %collective-permute-start.26 = (bf16[128,2048]{1,0:T(8,128)(2,1)}, bf16[128,2048]{1,0:T(8,128)(2,1)}, u32[]{:S(2)}, u32[]{:S(2)}) collective-permute-start(bf16[128,2048]{1,0:T(8,128)(2,1)} %collective-permute-done.18.refs_17_), channel_id=1, source_target_pairs={{0,2},{2,0},{4,6},{6,4},{8,10},{10,8},{12,14},{14,12},{16,18},{18,... | collective-permute-start | bytes 1572872 | tf_op jit(solution)/shard_map/ppermute | solution.py:78
  47.7 11.1 %collective-permute-start.12 = (bf16[128,2048]{1,0:T(8,128)(2,1)}, bf16[128,2048]{1,0:T(8,128)(2,1)}, u32[]{:S(2)}, u32[]{:S(2)}) collective-permute-start(bf16[128,2048]{1,0:T(8,128)(2,1)} %collective-permute-done.4.refs_2_), channel_id=1, source_target_pairs={{0,2},{2,0},{4,6},{6,4},{8,10},{10,8},{12,14},{14,12},{16,18},{18,... | collective-permute-start | bytes 1572872 | tf_op jit(solution)/shard_map/ppermute | solution.py:77
  48.6 10.7 %collective-permute-start.27 = (bf16[128,2048]{1,0:T(8,128)(2,1)}, bf16[128,2048]{1,0:T(8,128)(2,1)}, u32[]{:S(2)}, u32[]{:S(2)}) collective-permute-start(bf16[128,2048]{1,0:T(8,128)(2,1)} %collective-permute-done.19.refs_18_), channel_id=1, source_target_pairs={{0,2},{2,0},{4,6},{6,4},{8,10},{10,8},{12,14},{14,12},{16,18},{18,... | collective-permute-start | bytes 1572872 | tf_op jit(solution)/shard_map/ppermute | solution.py:78
  53.8 12.1 %collective-permute-start.7 = (bf16[128,2048]{1,0:T(8,128)(2,1)}, bf16[128,2048]{1,0:T(8,128)(2,1)}, u32[]{:S(2)}, u32[]{:S(2)}) collective-permute-start(bf16[128,2048]{1,0:T(8,128)(2,1)} %collective-permute-done.6.refs_4_), channel_id=1, source_target_pairs={{0,8},{2,10},{8,16},{10,18},{16,24},{18,26},{24,28},{26,30},{28,20... | collective-permute-start | bytes 1572872 | tf_op jit(solution)/shard_map/ppermute | solution.py:73
  54.6 12.1 %collective-permute-start.22 = (bf16[128,2048]{1,0:T(8,128)(2,1)}, bf16[128,2048]{1,0:T(8,128)(2,1)}, u32[]{:S(2)}, u32[]{:S(2)}) collective-permute-start(bf16[128,2048]{1,0:T(8,128)(2,1)} %collective-permute-done.21.refs_20_), channel_id=1, source_target_pairs={{0,4},{2,6},{8,0},{10,2},{16,8},{18,10},{24,16},{26,18},{28,24},{3... | collective-permute-start | bytes 1572872 | tf_op jit(solution)/shard_map/ppermute | solution.py:74
  58.7 11.7 %collective-permute-start.13 = (bf16[128,2048]{1,0:T(8,128)(2,1)}, bf16[128,2048]{1,0:T(8,128)(2,1)}, u32[]{:S(2)}, u32[]{:S(2)}) collective-permute-start(bf16[128,2048]{1,0:T(8,128)(2,1)} %collective-permute-done.5.refs_3_), channel_id=1, source_target_pairs={{0,2},{2,0},{4,6},{6,4},{8,10},{10,8},{12,14},{14,12},{16,18},{18,... | collective-permute-start | bytes 1572872 | tf_op jit(solution)/shard_map/ppermute | solution.py:77
  58.8 11.7 %collective-permute-start.28 = (bf16[128,2048]{1,0:T(8,128)(2,1)}, bf16[128,2048]{1,0:T(8,128)(2,1)}, u32[]{:S(2)}, u32[]{:S(2)}) collective-permute-start(bf16[128,2048]{1,0:T(8,128)(2,1)} %collective-permute-done.20.refs_19_), channel_id=1, source_target_pairs={{0,2},{2,0},{4,6},{6,4},{8,10},{10,8},{12,14},{14,12},{16,18},{18,... | collective-permute-start | bytes 1572872 | tf_op jit(solution)/shard_map/ppermute | solution.py:78
  59.3 11.7 %collective-permute-start.14 = (bf16[128,2048]{1,0:T(8,128)(2,1)}, bf16[128,2048]{1,0:T(8,128)(2,1)}, u32[]{:S(2)}, u32[]{:S(2)}) collective-permute-start(bf16[128,2048]{1,0:T(8,128)(2,1)} %collective-permute-done.6.refs_4_), channel_id=1, source_target_pairs={{0,2},{2,0},{4,6},{6,4},{8,10},{10,8},{12,14},{14,12},{16,18},{18,... | collective-permute-start | bytes 1572872 | tf_op jit(solution)/shard_map/ppermute | solution.py:77
  65.9 11.3 %collective-permute-start.8 = (bf16[128,2048]{1,0:T(8,128)(2,1)}, bf16[128,2048]{1,0:T(8,128)(2,1)}, u32[]{:S(2)}, u32[]{:S(2)}) collective-permute-start(bf16[128,2048]{1,0:T(8,128)(2,1)} %collective-permute-done.7.refs_5_), channel_id=1, source_target_pairs={{0,8},{2,10},{8,16},{10,18},{16,24},{18,26},{24,28},{26,30},{28,20... | collective-permute-start | bytes 1572872 | tf_op jit(solution)/shard_map/ppermute | solution.py:73
  66.7 11.6 %collective-permute-start.23 = (bf16[128,2048]{1,0:T(8,128)(2,1)}, bf16[128,2048]{1,0:T(8,128)(2,1)}, u32[]{:S(2)}, u32[]{:S(2)}) collective-permute-start(bf16[128,2048]{1,0:T(8,128)(2,1)} %collective-permute-done.22.refs_21_), channel_id=1, source_target_pairs={{0,4},{2,6},{8,0},{10,2},{16,8},{18,10},{24,16},{26,18},{28,24},{3... | collective-permute-start | bytes 1572872 | tf_op jit(solution)/shard_map/ppermute | solution.py:74
  70.4 9.8 %collective-permute-start.29 = (bf16[128,2048]{1,0:T(8,128)(2,1)}, bf16[128,2048]{1,0:T(8,128)(2,1)}, u32[]{:S(2)}, u32[]{:S(2)}) collective-permute-start(bf16[128,2048]{1,0:T(8,128)(2,1)} %collective-permute-done.21.refs_20_), channel_id=1, source_target_pairs={{0,2},{2,0},{4,6},{6,4},{8,10},{10,8},{12,14},{14,12},{16,18},{18,... | collective-permute-start | bytes 1572872 | tf_op jit(solution)/shard_map/ppermute | solution.py:78
  70.5 10.7 %collective-permute-start.15 = (bf16[128,2048]{1,0:T(8,128)(2,1)}, bf16[128,2048]{1,0:T(8,128)(2,1)}, u32[]{:S(2)}, u32[]{:S(2)}) collective-permute-start(bf16[128,2048]{1,0:T(8,128)(2,1)} %collective-permute-done.7.refs_5_), channel_id=1, source_target_pairs={{0,2},{2,0},{4,6},{6,4},{8,10},{10,8},{12,14},{14,12},{16,18},{18,... | collective-permute-start | bytes 1572872 | tf_op jit(solution)/shard_map/ppermute | solution.py:77
  71.0 10.3 %collective-permute-start.30 = (bf16[128,2048]{1,0:T(8,128)(2,1)}, bf16[128,2048]{1,0:T(8,128)(2,1)}, u32[]{:S(2)}, u32[]{:S(2)}) collective-permute-start(bf16[128,2048]{1,0:T(8,128)(2,1)} %collective-permute-done.22.refs_21_), channel_id=1, source_target_pairs={{0,2},{2,0},{4,6},{6,4},{8,10},{10,8},{12,14},{14,12},{16,18},{18,... | collective-permute-start | bytes 1572872 | tf_op jit(solution)/shard_map/ppermute | solution.py:78
  77.2 9.9 %collective-permute-start.9 = (bf16[128,2048]{1,0:T(8,128)(2,1)}, bf16[128,2048]{1,0:T(8,128)(2,1)}, u32[]{:S(2)}, u32[]{:S(2)}) collective-permute-start(bf16[128,2048]{1,0:T(8,128)(2,1)} %collective-permute-done.8.refs_6_), channel_id=1, source_target_pairs={{0,8},{2,10},{8,16},{10,18},{16,24},{18,26},{24,28},{26,30},{28,20... | collective-permute-start | bytes 1572872 | tf_op jit(solution)/shard_map/ppermute | solution.py:73
  78.2 9.5 %collective-permute-start.24 = (bf16[128,2048]{1,0:T(8,128)(2,1)}, bf16[128,2048]{1,0:T(8,128)(2,1)}, u32[]{:S(2)}, u32[]{:S(2)}) collective-permute-start(bf16[128,2048]{1,0:T(8,128)(2,1)} %collective-permute-done.23.refs_22_), channel_id=1, source_target_pairs={{0,4},{2,6},{8,0},{10,2},{16,8},{18,10},{24,16},{26,18},{28,24},{3... | collective-permute-start | bytes 1572872 | tf_op jit(solution)/shard_map/ppermute | solution.py:74
  80.3 22.5 %collective-permute-start.2 = (bf16[1024,256]{1,0:T(8,128)(2,1)}, bf16[1024,256]{1,0:T(8,128)(2,1)S(1)}, u32[]{:S(2)}, u32[]{:S(2)}) collective-permute-start(bf16[1024,256]{1,0:T(8,128)(2,1)} %param.17), channel_id=1, source_target_pairs={{0,1},{1,0},{2,3},{3,2},{4,5},{5,4},{6,7},{7,6},{8,9},{9,8},{10,11... | collective-permute-start | bytes 1572872 | tf_op jit(solution)/shard_map/ppermute | solution.py:61
  81.3 7.6 %collective-permute-start.16 = (bf16[128,2048]{1,0:T(8,128)(2,1)}, bf16[128,2048]{1,0:T(8,128)(2,1)S(1)}, u32[]{:S(2)}, u32[]{:S(2)}) collective-permute-start(bf16[128,2048]{1,0:T(8,128)(2,1)} %collective-permute-done.8.refs_6_), channel_id=1, source_target_pairs={{0,2},{2,0},{4,6},{6,4},{8,10},{10,8},{12,14},{14,12},{16,18},{18,... | collective-permute-start | bytes 1572872 | tf_op jit(solution)/shard_map/ppermute | solution.py:77
  81.3 7.6 %collective-permute-start.31 = (bf16[128,2048]{1,0:T(8,128)(2,1)}, bf16[128,2048]{1,0:T(8,128)(2,1)S(1)}, u32[]{:S(2)}, u32[]{:S(2)}) collective-permute-start(bf16[128,2048]{1,0:T(8,128)(2,1)} %collective-permute-done.23.refs_22_), channel_id=1, source_target_pairs={{0,2},{2,0},{4,6},{6,4},{8,10},{10,8},{12,14},{14,12},{16,18},{18,... | collective-permute-start | bytes 1572872 | tf_op jit(solution)/shard_map/ppermute | solution.py:78
  101.3 16.5 %collective-permute-start.33 = (bf16[1280,128]{1,0:T(8,128)(2,1)}, bf16[1280,128]{1,0:T(8,128)(2,1)S(1)}, u32[]{:S(2)}, u32[]{:S(2)}) collective-permute-start(bf16[1280,128]{1,0:T(8,128)(2,1)} %attention.2), channel_id=1, source_target_pairs={{0,1},{1,0},{2,3},{3,2},{4,5},{5,4},{6,7},{7,6},{8,9},{9,8},{10,11... | collective-permute-start | bytes 983048 | tf_op jit(solution)/shard_map/ppermute | solution.py:761
  110.8 7.0 %collective-permute-start.34 = (bf16[768,128]{1,0:T(8,128)(2,1)}, bf16[768,128]{1,0:T(8,128)(2,1)S(1)}, u32[]{:S(2)}, u32[]{:S(2)}) collective-permute-start(bf16[768,128]{1,0:T(8,128)(2,1)} %attention.3), channel_id=1, source_target_pairs={{0,1},{1,0},{2,3},{3,2},{4,5},{5,4},{6,7},{7,6},{8,9},{9,8},{10,11... | collective-permute-start | bytes 589832 | tf_op jit(solution)/shard_map/ppermute | solution.py:761
  129.3 13.5 %collective-permute-start.37 = (bf16[1,512,512]{2,1,0:T(8,128)(2,1)S(1)}, bf16[1,512,512]{2,1,0:T(8,128)(2,1)S(1)}, u32[]{:S(2)}, u32[]{:S(2)}) collective-permute-start(bf16[1,512,512]{2,1,0:T(8,128)(2,1)S(1)} %get-tuple-element.43), channel_id=1, source_target_pairs={{0,2},{2,0},{4,6},{6,4},{8,10},{10,8},{12,14},{14,12},{16,18},{18,... | collective-permute-start | bytes 1572872 | tf_op jit(solution)/shard_map/ppermute | solution.py:577
  131.3 14.0 %collective-permute-start.38 = (bf16[1,512,512]{2,1,0:T(8,128)(2,1)S(1)}, bf16[1,512,512]{2,1,0:T(8,128)(2,1)S(1)}, u32[]{:S(2)}, u32[]{:S(2)}) collective-permute-start(bf16[1,512,512]{2,1,0:T(8,128)(2,1)S(1)} %sum_core.2.refs_8_.refs_3_), channel_id=1, source_target_pairs={{0,4},{2,6},{4,0},{6,2},{8,12},{10,14},{12,8},{14,10},{16,20},{18,... | collective-permute-start | bytes 1572872 | tf_op jit(solution)/shard_map/ppermute | solution.py:584
  142.3 15.5 %collective-permute-start.40 = (bf16[1,512,512]{2,1,0:T(8,128)(2,1)S(1)}, bf16[1,512,512]{2,1,0:T(8,128)(2,1)S(1)}, u32[]{:S(2)}, u32[]{:S(2)}) collective-permute-start(bf16[1,512,512]{2,1,0:T(8,128)(2,1)S(1)} %get-tuple-element.48), channel_id=1, source_target_pairs={{0,2},{2,0},{4,6},{6,4},{8,10},{10,8},{12,14},{14,12},{16,18},{18,... | collective-permute-start | bytes 1572872 | tf_op jit(solution)/shard_map/ppermute | solution.py:577
  145.6 9.5 %collective-permute-start.42 = (bf16[1,256,512]{2,1,0:T(8,128)(2,1)S(1)}, bf16[1,256,512]{2,1,0:T(8,128)(2,1)S(1)}, u32[]{:S(2)}, u32[]{:S(2)}) collective-permute-start(bf16[1,256,512]{2,1,0:T(8,128)(2,1)S(1)} %get-tuple-element.44.refs_2_), channel_id=1, source_target_pairs={{0,8},{2,10},{4,12},{6,14},{8,0},{10,2},{12,4},{14,6},{16,24},{18,... | collective-permute-start | bytes 786440 | tf_op jit(solution)/shard_map/ppermute | solution.py:580
  148.2 12.9 %collective-permute-start.41 = (bf16[1,512,512]{2,1,0:T(8,128)(2,1)S(1)}, bf16[1,512,512]{2,1,0:T(8,128)(2,1)S(1)}, u32[]{:S(2)}, u32[]{:S(2)}) collective-permute-start(bf16[1,512,512]{2,1,0:T(8,128)(2,1)S(1)} %sum_core.3.refs_2_), channel_id=1, source_target_pairs={{0,4},{2,6},{4,0},{6,2},{8,12},{10,14},{12,8},{14,10},{16,20},{18,... | collective-permute-start | bytes 1572872 | tf_op jit(solution)/shard_map/ppermute | solution.py:584
  155.2 7.8 %collective-permute-start.44 = (bf16[1,128,512]{2,1,0:T(8,128)(2,1)S(1)}, bf16[1,128,512]{2,1,0:T(8,128)(2,1)S(1)}, u32[]{:S(2)}, u32[]{:S(2)}) collective-permute-start(bf16[1,128,512]{2,1,0:T(8,128)(2,1)S(1)} %get-tuple-element.50.refs_3_), channel_id=1, source_target_pairs={{0,16},{2,18},{4,20},{6,22},{8,24},{10,26},{12,28},{14,30},{16,0},... | collective-permute-start | bytes 393224 | tf_op jit(solution)/shard_map/ppermute | solution.py:580
  161.4 10.2 %collective-permute-start.43 = (bf16[1,256,512]{2,1,0:T(8,128)(2,1)S(1)}, bf16[1,256,512]{2,1,0:T(8,128)(2,1)S(1)}, u32[]{:S(2)}, u32[]{:S(2)}) collective-permute-start(bf16[1,256,512]{2,1,0:T(8,128)(2,1)S(1)} %get-tuple-element.52.refs_2_), channel_id=1, source_target_pairs={{0,8},{2,10},{4,12},{6,14},{8,0},{10,2},{12,4},{14,6},{16,24},{18,... | collective-permute-start | bytes 786440 | tf_op jit(solution)/shard_map/ppermute | solution.py:580
  161.7 35.9 %collective-permute-start.39 = (bf16[1024,512]{1,0:T(8,128)(2,1)S(1)}, bf16[1024,512]{1,0:T(8,128)(2,1)S(1)}, u32[]{:S(2)}, u32[]{:S(2)}) collective-permute-start(bf16[1024,512]{1,0:T(8,128)(2,1)S(1)} %get-tuple-element.46), channel_id=1, source_target_pairs={{0,1},{1,0},{2,3},{3,2},{4,5},{5,4},{6,7},{7,6},{8,9},{9,8},{10,11... | collective-permute-start | bytes 3145736 | tf_op jit(solution)/shard_map/ppermute | solution.py:785
  163.0 8.7 %collective-permute-start.46 = (bf16[1,1,128,512]{3,2,1,0:T(8,128)(2,1)S(1)}, bf16[1,1,128,512]{3,2,1,0:T(8,128)(2,1)S(1)}, u32[]{:S(2)}, u32[]{:S(2)}) collective-permute-start(bf16[1,1,128,512]{3,2,1,0:T(8,128)(2,1)S(1)} %bitcast.33), channel_id=1, source_target_pairs={{0,16},{2,18},{4,20},{6,22},{8,24},{10,26},{12,28},{14,30},{16,0},... | collective-permute-start | bytes 393224 | tf_op jit(solution)/shard_map/ppermute | solution.py:580
  171.7 8.0 %collective-permute-start.48 = (bf16[2,1,128,512]{3,2,1,0:T(8,128)(2,1)S(1)}, bf16[2,1,128,512]{3,2,1,0:T(8,128)(2,1)S(1)}, u32[]{:S(2)}, u32[]{:S(2)}) collective-permute-start(bf16[2,1,128,512]{3,2,1,0:T(8,128)(2,1)S(1)} %stack_pieces.5.refs_2_.refs_0_), channel_id=1, source_target_pairs={{0,8},{2,10},{4,12},{6,14},{8,0},{10,2},{12,4},{14,6},{16,24},{18,... | collective-permute-start | bytes 786440 | tf_op jit(solution)/shard_map/ppermute | solution.py:580
  179.7 17.6 %collective-permute-start.52 = (bf16[4,1,128,512]{3,2,1,0:T(8,128)(2,1)S(1)}, bf16[4,1,128,512]{3,2,1,0:T(8,128)(2,1)S(1)}, u32[]{:S(2)}, u32[]{:S(2)}) collective-permute-start(bf16[4,1,128,512]{3,2,1,0:T(8,128)(2,1)S(1)} %stack_pieces.6.refs_2_.refs_0_), channel_id=1, source_target_pairs={{0,4},{2,6},{4,0},{6,2},{8,12},{10,14},{12,8},{14,10},{16,20},{18,... | collective-permute-start | bytes 1572872 | tf_op jit(solution)/shard_map/ppermute | solution.py:607
  184.4 6.2 %collective-permute-start.47 = (bf16[1,1,128,512]{3,2,1,0:T(8,128)(2,1)S(1)}, bf16[1,1,128,512]{3,2,1,0:T(8,128)(2,1)S(1)}, u32[]{:S(2)}, u32[]{:S(2)}) collective-permute-start(bf16[1,1,128,512]{3,2,1,0:T(8,128)(2,1)S(1)} %bitcast.35), channel_id=1, source_target_pairs={{0,16},{2,18},{4,20},{6,22},{8,24},{10,26},{12,28},{14,30},{16,0},... | collective-permute-start | bytes 393224 | tf_op jit(solution)/shard_map/ppermute | solution.py:580
  190.6 6.4 %collective-permute-start.49 = (bf16[2,1,128,512]{3,2,1,0:T(8,128)(2,1)S(1)}, bf16[2,1,128,512]{3,2,1,0:T(8,128)(2,1)S(1)}, u32[]{:S(2)}, u32[]{:S(2)}) collective-permute-start(bf16[2,1,128,512]{3,2,1,0:T(8,128)(2,1)S(1)} %stack_pieces.7.refs_0_.refs_2_), channel_id=1, source_target_pairs={{0,8},{2,10},{4,12},{6,14},{8,0},{10,2},{12,4},{14,6},{16,24},{18,... | collective-permute-start | bytes 786440 | tf_op jit(solution)/shard_map/ppermute | solution.py:580
  190.8 8.7 %collective-permute-start.53 = (bf16[4,1,128,512]{3,2,1,0:T(8,128)(2,1)S(1)}, bf16[4,1,128,512]{3,2,1,0:T(8,128)(2,1)S(1)}, u32[]{:S(2)}, u32[]{:S(2)}) collective-permute-start(bf16[4,1,128,512]{3,2,1,0:T(8,128)(2,1)S(1)} %stack_pieces.6.refs_2_.refs_0_), channel_id=1, source_target_pairs={{0,2},{2,0},{4,6},{6,4},{8,10},{10,8},{12,14},{14,12},{16,18},{18,... | collective-permute-start | bytes 1572872 | tf_op jit(solution)/shard_map/ppermute | solution.py:577
  197.2 14.3 %collective-permute-start.50 = (bf16[4,1,128,512]{3,2,1,0:T(8,128)(2,1)S(1)}, bf16[4,1,128,512]{3,2,1,0:T(8,128)(2,1)S(1)}, u32[]{:S(2)}, u32[]{:S(2)}) collective-permute-start(bf16[4,1,128,512]{3,2,1,0:T(8,128)(2,1)S(1)} %stack_pieces.8.refs_5_.refs_0_), channel_id=1, source_target_pairs={{0,4},{2,6},{4,0},{6,2},{8,12},{10,14},{12,8},{14,10},{16,20},{18,... | collective-permute-start | bytes 1572872 | tf_op jit(solution)/shard_map/ppermute | solution.py:607
  (27 other events, 322.0 us)
